TPU v7x, 32 devices: a whole 2x2x4 slice. The times are simulated.
32 devices in a mesh: gx: 4 (over z), gy: 4 (over x, core), gz: 2 (over y).
Axes of the slice: x: 2, y: 2, z: 4, core: 2. Of those that a mesh axis runs over, the one named last changes fastest.
Arguments:
- local_solution: float32 [3, 68, 180, 256], P(None, 'gx', 'gy', 'gz'), may hold values from -6 to 6
- top_nodes: float32 [3, 68, 180, 2], P(None, 'gx', 'gy', 'gz'), may hold values from -6 to 6
- coarse_solution: float32 [3, 1024], P(None, 'gz'), may hold values from -6 to 6
- corner_dofs: int32 [4, 4, 2, 8], P('gx', 'gy', 'gz'), may hold values from 0 to 1023
- density: float32 [64, 176, 256], P('gx', 'gy', 'gz'), may hold values from 0.1 to 1
- element_stiffness: float32 [24, 24], replicated, may hold values from -0.15 to 4.5, as said below
Outputs:
- filtered_sens: float32 [64, 176, 256], P('gx', 'gy', 'gz')
- filtered_density: float32 [64, 176, 256], P('gx', 'gy', 'gz')
Inputs may be any that keep to these rules, and one draw needn't show every extreme that they name: element_stiffness is symmetric.
All inputs are finite; a program needn't handle non-finite values.
Results may differ from a plain program's by a relative error of at most 0.00005.
Values sent between devices are 32-bit elements; how exact they have to be, the bound alone decides.
No kernel may reach another device: no remote copies, remote signals or barrier semaphores. Data moves between devices by JAX's collectives and lax.ppermute only.
A program may use at most 64 MiB of HBM per device.

v0:
```python
import jax
import jax.numpy as jnp
from jax import lax
from jax.sharding import PartitionSpec as P

RADIUS = 3


penal_scale = -3.0 / 96.0


def with_halo(shard, sides, width):
    for axis, dim in sides:
        count, length = (lax.axis_size(axis), shard.shape[dim])
        up = [(i, (i + 1) % count) for i in range(count - 1)]
        down = [(j, i) for i, j in up]
        last = lax.slice_in_dim(shard, length - width, length, axis=dim)
        initial = lax.slice_in_dim(shard, 0, width, axis=dim)
        before = lax.ppermute(last, axis, up)
        after = lax.ppermute(initial, axis, down)
        shard = jnp.concatenate([before, shard, after], axis=dim)
    return shard


def recover(local_nodes, corner_vals, ratio_z):
    ex = local_nodes.shape[1] - 1
    ey = local_nodes.shape[2] - 1
    ratio_x = jnp.arange(ex + 1, dtype=jnp.float32) / ex
    ratio_y = jnp.arange(ey + 1, dtype=jnp.float32) / ey
    summed = local_nodes
    for corner in range(8):
        along_x = ratio_x if corner // 4 == 1 else 1.0 - ratio_x
        along_y = ratio_y if corner // 2 % 2 == 1 else 1.0 - ratio_y
        along_z = ratio_z if corner % 2 == 1 else 1.0 - ratio_z
        basis = along_x[:, None, None] * along_y[None, :, None] * along_z[None, None, :]
        summed = summed + basis[None] * corner_vals[:, corner][:, None, None, None]
    return summed


def average_rows(extended, dim, has_lower, has_upper):
    inner = extended.shape[dim] - 2
    own_rows = lax.slice_in_dim(extended, 1, inner + 1, axis=dim)
    rim_low = lax.slice_in_dim(extended, 0, 1, axis=dim)
    rim_high = lax.slice_in_dim(extended, inner + 1, inner + 2, axis=dim)
    shape_row = [1] * extended.ndim
    shape_row[dim] = inner
    rows = jnp.arange(inner, dtype=jnp.int32).reshape(shape_row)
    is_low = rows == 0
    is_high = rows == inner - 1
    factor = jnp.where(is_low & has_lower, 0.5, jnp.where(is_high & has_upper, 0.5, 1.0))
    rim_part = jnp.where(is_low, rim_low, 0.0) + jnp.where(is_high, rim_high, 0.0)
    return own_rows * factor + rim_part * 0.5


def element_energy(lower_nodes, upper_nodes, stiffness):
    ex = lower_nodes.shape[1] - 1
    ey = lower_nodes.shape[2] - 1

    def rows_energy(first_row):
        slab_low = lax.dynamic_slice_in_dim(lower_nodes, first_row, 5, axis=1)
        slab_up = lax.dynamic_slice_in_dim(upper_nodes, first_row, 5, axis=1)
        columns = []
        for corner in range(8):
            shift_x = corner // 4
            shift_y = corner // 2 % 2
            source = slab_up if corner % 2 == 1 else slab_low
            columns.append(source[:, shift_x : shift_x + 4, shift_y : shift_y + ey, :])
        vectors = jnp.stack(columns, axis=1)
        vectors = vectors.reshape((24,) + vectors.shape[2:])
        product = jnp.einsum(
            "ij,jabc->iabc",
            stiffness,
            vectors,
            precision=lax.Precision.HIGHEST,
            preferred_element_type=jnp.float32,
        )
        return jnp.sum(vectors * product, axis=0)

    starts = jnp.arange(ex // 4, dtype=jnp.int32) * 4
    energies = lax.map(rows_energy, starts)
    return energies.reshape((ex,) + energies.shape[2:])


def smooth(field, axis, count):
    summed = None
    for offset in range(-RADIUS, RADIUS + 1):
        term_piece = lax.slice_in_dim(field, RADIUS + offset, RADIUS + offset + count, axis=axis)
        term_value = float(RADIUS + 1 - abs(offset)) * term_piece
        summed = term_value if summed is None else summed + term_value
    return summed


def edge_counts(count, position, parts):
    places = position * count + jnp.arange(count, dtype=jnp.int32)
    summed = None
    for offset in range(-RADIUS, RADIUS + 1):
        inside = ((places + offset >= 0) & (places + offset < count * parts)).astype(jnp.float32)
        term_value = float(RADIUS + 1 - abs(offset)) * inside
        summed = term_value if summed is None else summed + term_value
    return summed


def local(local_solution, top_nodes, coarse_solution, corner_dofs, density, element_stiffness):
    wanted = corner_dofs.reshape(8)
    columns = lax.all_gather(coarse_solution, "gz", axis=1, tiled=True)
    matches = wanted[:, None] == jnp.arange(columns.shape[1], dtype=jnp.int32)[None, :]
    corner_vals = jnp.sum(jnp.where(matches[None], columns[:, None, :], 0.0), axis=2)
    depth = local_solution.shape[3]
    main_nodes = recover(local_solution, corner_vals, jnp.arange(depth, dtype=jnp.float32) / depth)
    top_plane = recover(top_nodes, corner_vals, jnp.ones((1,), jnp.float32))
    index_x = lax.axis_index("gx")
    index_y = lax.axis_index("gy")
    index_z = lax.axis_index("gz")
    lower_x = index_x > 0
    upper_x = index_x < lax.axis_size("gx") - 1
    lower_y = index_y > 0
    upper_y = index_y < lax.axis_size("gy") - 1
    extended = with_halo(main_nodes, (("gx", 1), ("gy", 2)), 1)
    extended = average_rows(extended, 1, lower_x, upper_x)
    main_avg = average_rows(extended, 2, lower_y, upper_y)
    planes = jnp.concatenate([main_nodes[:, :, :, 0:1], top_plane], axis=3)
    faces = with_halo(planes, (("gx", 1), ("gy", 2), ("gz", 3)), 1)
    faces = average_rows(faces, 1, lower_x, upper_x)
    faces = average_rows(faces, 2, lower_y, upper_y)
    low_factor = jnp.where(index_z > 0, 0.5, 1.0)
    high_factor = jnp.where(index_z < lax.axis_size("gz") - 1, 0.5, 1.0)
    first_plane = faces[:, :, :, 1:2] * low_factor + faces[:, :, :, 0:1] * 0.5
    last_plane = faces[:, :, :, 2:3] * high_factor + faces[:, :, :, 3:4] * 0.5
    plane_rows = jnp.arange(depth, dtype=jnp.int32)[None, None, None, :]
    lower_nodes = jnp.where(plane_rows == 0, first_plane, main_avg)
    upper_nodes = jnp.concatenate([lower_nodes[:, :, :, 1:], last_plane], axis=3)
    energy = element_energy(lower_nodes, upper_nodes, element_stiffness)
    sens = penal_scale * density * density * energy
    count_x, count_y, count_z = density.shape
    normalizer = (
        edge_counts(count_x, index_x, lax.axis_size("gx"))[:, None, None]
        * edge_counts(count_y, index_y, lax.axis_size("gy"))[None, :, None]
        * edge_counts(count_z, index_z, lax.axis_size("gz"))[None, None, :]
    )
    stacked = jnp.stack([density * sens, density])
    padded = with_halo(stacked, (("gx", 1), ("gy", 2), ("gz", 3)), RADIUS)
    smoothed = smooth(padded, 1, count_x)
    smoothed = smooth(smoothed, 2, count_y)
    smoothed = smooth(smoothed, 3, count_z)
    numerator = smoothed[0]
    smooth_density = smoothed[1]
    return (numerator / (density * normalizer), smooth_density / normalizer)


def solution(mesh):
    in_specs = (
        P(None, "gx", "gy", "gz"),
        P(None, "gx", "gy", "gz"),
        P(None, "gz"),
        P("gx", "gy", "gz", None),
        P("gx", "gy", "gz"),
        P(),
    )
    out_specs = (P("gx", "gy", "gz"), P("gx", "gy", "gz"))
    return jax.shard_map(local, mesh=mesh, in_specs=in_specs, out_specs=out_specs, check_vma=False)
```

profile of v0, /device:TPU:9, one launch (start us, length us, event | category | flops | bytes accessed | tf_op | source)
XLA Modules:
  0.0 128.8 jit_solution(15022249960729847419)
XLA Ops:
  0.7 3.4 %all_gather.3 = f32[3,1024]{1,0:T(4,128)S(1)} all-gather(f32[3,512]{1,0:T(4,128)} %param.10), channel_id=1, replica_groups=mesh['gx'=4,'gy'=4,'gz'=2] {'gz'}, dimensions={1}, use_global_device_ids=true | all-gather | bytes 18432 | tf_op jit(solution)/shard_map/all_gather | solution.py:105
  8.1 3.2 %collective-permute-start = (f32[3,1,45,2]{2,3,1,0:T(2,128)S(1)}, f32[3,1,45,2]{2,3,1,0:T(2,128)S(1)}, u32[]{:S(2)}, u32[]{:S(2)}) collective-permute-start(f32[3,1,45,2]{2,3,1,0:T(2,128)S(1)} %get-tuple-element.143), channel_id=1, source_target_pairs={{0,8},{8,16},{16,24},{1,9},{9,17},{17,25},{2,10},{10,18},{18,26},{... | collective-permute-start | bytes 3248 | tf_op jit(solution)/shard_map/ppermute | solution.py:19
  11.3 2.1 %collective-permute-start.1 = (f32[3,1,45,2]{2,3,1,0:T(2,128)S(1)}, f32[3,1,45,2]{2,3,1,0:T(2,128)S(1)}, u32[]{:S(2)}, u32[]{:S(2)}) collective-permute-start(f32[3,1,45,2]{2,3,1,0:T(2,128)S(1)} %get-tuple-element.144), channel_id=1, source_target_pairs={{8,0},{16,8},{24,16},{9,1},{17,9},{25,17},{10,2},{18,10},{26,18},{... | collective-permute-start | bytes 3248 | tf_op jit(solution)/shard_map/ppermute | solution.py:20
  13.4 3.2 %collective-permute-start.6 = (f32[3,1,45,128]{3,2,1,0:T(8,128)S(1)}, f32[3,1,45,128]{3,2,1,0:T(8,128)S(1)}, u32[]{:S(2)}, u32[]{:S(2)}) collective-permute-start(f32[3,1,45,128]{3,2,1,0:T(8,128)S(1)} %get-tuple-element.123), channel_id=1, source_target_pairs={{0,8},{8,16},{16,24},{1,9},{9,17},{17,25},{2,10},{10,18},{18,26},{... | collective-permute-start | bytes 207368 | tf_op jit(solution)/shard_map/ppermute | solution.py:19
  16.6 2.1 %collective-permute-start.7 = (f32[3,1,45,128]{3,2,1,0:T(8,128)S(1)}, f32[3,1,45,128]{3,2,1,0:T(8,128)S(1)}, u32[]{:S(2)}, u32[]{:S(2)}) collective-permute-start(f32[3,1,45,128]{3,2,1,0:T(8,128)S(1)} %get-tuple-element.124), channel_id=1, source_target_pairs={{8,0},{16,8},{24,16},{9,1},{17,9},{25,17},{10,2},{18,10},{26,18},{... | collective-permute-start | bytes 207368 | tf_op jit(solution)/shard_map/ppermute | solution.py:20
  20.0 5.9 %collective-permute-start.2 = (f32[3,19,1,2]{2,3,1,0:T(2,128)S(1)}, f32[3,19,1,2]{2,3,1,0:T(2,128)S(1)}, u32[]{:S(2)}, u32[]{:S(2)}) collective-permute-start(f32[3,19,1,2]{2,3,1,0:T(2,128)S(1)} %get-tuple-element.141), channel_id=1, source_target_pairs={{0,2},{2,4},{4,6},{1,3},{3,5},{5,7},{8,10},{10,12},{12,14},{9,11},... | collective-permute-start | bytes 1376 | tf_op jit(solution)/shard_map/ppermute | solution.py:19
  25.9 1.9 %collective-permute-start.3 = (f32[3,19,1,2]{2,3,1,0:T(2,128)S(1)}, f32[3,19,1,2]{2,3,1,0:T(2,128)S(1)}, u32[]{:S(2)}, u32[]{:S(2)}) collective-permute-start(f32[3,19,1,2]{2,3,1,0:T(2,128)S(1)} %get-tuple-element.142), channel_id=1, source_target_pairs={{2,0},{4,2},{6,4},{3,1},{5,3},{7,5},{10,8},{12,10},{14,12},{11,9},... | collective-permute-start | bytes 1376 | tf_op jit(solution)/shard_map/ppermute | solution.py:20
  27.9 3.5 %collective-permute-done.3 = f32[3,19,1,2]{2,3,1,0:T(2,128)S(1)} collective-permute-done((f32[3,19,1,2]{2,3,1,0:T(2,128)S(1)}, f32[3,19,1,2]{2,3,1,0:T(2,128)S(1)}, u32[]{:S(2)}, u32[]{:S(2)}) %collective-permute-start.3) | collective-permute-done | bytes 488 | tf_op jit(solution)/shard_map/ppermute | solution.py:20
  31.7 3.1 %collective-permute-start.4 = (f32[3,19,47,1]{2,3,1,0:T(1,128)S(1)}, f32[3,19,47,1]{2,3,1,0:T(1,128)S(1)}, u32[]{:S(2)}, u32[]{:S(2)}) collective-permute-start(f32[3,19,47,1]{2,3,1,0:T(1,128)S(1)} %get-tuple-element.139), channel_id=1, source_target_pairs={{0,1},{2,3},{4,5},{6,7},{8,9},{10,11},{12,13},{14,15},{16,17},{18,... | collective-permute-start | bytes 32156 | tf_op jit(solution)/shard_map/ppermute | solution.py:19
  36.2 3.3 %collective-permute-done.5 = f32[3,19,47,1]{2,3,1,0:T(1,128)S(1)} collective-permute-done((f32[3,19,47,1]{2,3,1,0:T(1,128)S(1)}, f32[3,19,47,1]{2,3,1,0:T(1,128)S(1)}, u32[]{:S(2)}, u32[]{:S(2)}) %collective-permute-start.5) | collective-permute-done | bytes 10748 | tf_op jit(solution)/shard_map/ppermute | solution.py:20
  40.7 3.3 %collective-permute-start.8 = (f32[3,19,1,128]{3,2,1,0:T(1,128)S(1)}, f32[3,19,1,128]{3,2,1,0:T(1,128)S(1)}, u32[]{:S(2)}, u32[]{:S(2)}) collective-permute-start(f32[3,19,1,128]{3,2,1,0:T(1,128)S(1)} %get-tuple-element.121), channel_id=1, source_target_pairs={{0,2},{2,4},{4,6},{1,3},{3,5},{5,7},{8,10},{10,12},{12,14},{9,11},... | collective-permute-start | bytes 87560 | tf_op jit(solution)/shard_map/ppermute | solution.py:19
  44.0 2.1 %collective-permute-start.9 = (f32[3,19,1,128]{3,2,1,0:T(1,128)S(1)}, f32[3,19,1,128]{3,2,1,0:T(1,128)S(1)}, u32[]{:S(2)}, u32[]{:S(2)}) collective-permute-start(f32[3,19,1,128]{3,2,1,0:T(1,128)S(1)} %get-tuple-element.122), channel_id=1, source_target_pairs={{2,0},{4,2},{6,4},{3,1},{5,3},{7,5},{10,8},{12,10},{14,12},{11,9},... | collective-permute-start | bytes 87560 | tf_op jit(solution)/shard_map/ppermute | solution.py:20
  46.2 1.6 %copy.284 = f32[3,17,45,1]{3,2,1,0:T(8,128)} copy(f32[3,17,45,1]{2,1,0,3:T(8,128)S(1)} %get-tuple-element.133) | data formatting | bytes 18360 | tf_op jit(solution)/shard_map/add | solution.py:128
  54.0 36.0 %while.10 = (s32[]{:T(128)}, f32[4,4,44,128]{3,1,0,2:T(4,128)S(1)}, s32[4]{0:T(128)}, f32[3,17,45,128]{3,0,2,1:T(4,128)S(1)}, f32[3,17,45,128]{3,2,1,0:T(8,128)S...) while((s32[]{:T(128)}, f32[4,4,44,128]{3,1,0,2:T(4,128)S(1)}, s32[4]{0:T(128)}, ...), condition=%wide.region_3.4_spmd, body=%wide.region_1.3_spmd.sunk | while | flops 156772352 | bytes 10021331 | solution.py:80
  58.6 4.4 %fusion.89 = f32[4,44,128]{2,1,0:T(8,128)S(1)} fusion(f32[3,8,4,44,128]{4,0,3,2,1:T(4,128)S(1)} %fusion.88, f32[24,24]{1,0:T(8,128)S(1)} %get-tuple-element.253), kind=kOutput, calls=%fused_computation.1.clone.1 | convolution fusion | flops 156772352 | bytes 2255104 | tf_op jit(solution)/shard_map/while/body/eval_jaxpr/ij,jabc->iabc/dot_general | solution.py:70
  67.6 4.4 %fusion.89 = f32[4,44,128]{2,1,0:T(8,128)S(1)} fusion(f32[3,8,4,44,128]{4,0,3,2,1:T(4,128)S(1)} %fusion.88, f32[24,24]{1,0:T(8,128)S(1)} %get-tuple-element.253), kind=kOutput, calls=%fused_computation.1.clone.1 | convolution fusion | flops 156772352 | bytes 2255104 | tf_op jit(solution)/shard_map/while/body/eval_jaxpr/ij,jabc->iabc/dot_general | solution.py:70
  76.6 4.4 %fusion.89 = f32[4,44,128]{2,1,0:T(8,128)S(1)} fusion(f32[3,8,4,44,128]{4,0,3,2,1:T(4,128)S(1)} %fusion.88, f32[24,24]{1,0:T(8,128)S(1)} %get-tuple-element.253), kind=kOutput, calls=%fused_computation.1.clone.1 | convolution fusion | flops 156772352 | bytes 2255104 | tf_op jit(solution)/shard_map/while/body/eval_jaxpr/ij,jabc->iabc/dot_general | solution.py:70
  85.6 4.4 %fusion.89 = f32[4,44,128]{2,1,0:T(8,128)S(1)} fusion(f32[3,8,4,44,128]{4,0,3,2,1:T(4,128)S(1)} %fusion.88, f32[24,24]{1,0:T(8,128)S(1)} %get-tuple-element.253), kind=kOutput, calls=%fused_computation.1.clone.1 | convolution fusion | flops 156772352 | bytes 2255104 | tf_op jit(solution)/shard_map/while/body/eval_jaxpr/ij,jabc->iabc/dot_general | solution.py:70
  90.2 3.2 %collective-permute-start.10 = (f32[2,3,44,128]{3,1,2,0:T(4,128)S(1)}, f32[2,3,44,128]{3,1,2,0:T(4,128)S(1)}, u32[]{:S(2)}, u32[]{:S(2)}) collective-permute-start(f32[2,3,44,128]{3,1,2,0:T(4,128)S(1)} %get-tuple-element.132), channel_id=1, source_target_pairs={{0,8},{8,16},{16,24},{1,9},{9,17},{17,25},{2,10},{10,18},{18,26},{... | collective-permute-start | bytes 405512 | tf_op jit(solution)/shard_map/ppermute | solution.py:19
  93.4 2.1 %collective-permute-start.11 = (f32[2,3,44,128]{3,1,2,0:T(4,128)S(1)}, f32[2,3,44,128]{3,1,2,0:T(4,128)S(1)}, u32[]{:S(2)}, u32[]{:S(2)}) collective-permute-start(f32[2,3,44,128]{3,1,2,0:T(4,128)S(1)} %get-tuple-element.131), channel_id=1, source_target_pairs={{8,0},{16,8},{24,16},{9,1},{17,9},{25,17},{10,2},{18,10},{26,18},{... | collective-permute-start | bytes 405512 | tf_op jit(solution)/shard_map/ppermute | solution.py:20
  95.6 1.4 %collective-permute-done.10 = f32[2,3,44,128]{3,1,2,0:T(4,128)S(1)} collective-permute-done((f32[2,3,44,128]{3,1,2,0:T(4,128)S(1)}, f32[2,3,44,128]{3,1,2,0:T(4,128)S(1)}, u32[]{:S(2)}, u32[]{:S(2)}) %collective-permute-start.10) | collective-permute-done | bytes 135200 | tf_op jit(solution)/shard_map/ppermute | solution.py:19
  97.7 2.5 %collective-permute-done.11 = f32[2,3,44,128]{3,1,2,0:T(4,128)S(1)} collective-permute-done((f32[2,3,44,128]{3,1,2,0:T(4,128)S(1)}, f32[2,3,44,128]{3,1,2,0:T(4,128)S(1)}, u32[]{:S(2)}, u32[]{:S(2)}) %collective-permute-start.11) | collective-permute-done | bytes 135200 | tf_op jit(solution)/shard_map/ppermute | solution.py:20
  100.4 3.2 %collective-permute-start.12 = (f32[2,22,3,128]{3,0,2,1:T(2,128)S(1)}, f32[2,22,3,128]{3,0,2,1:T(2,128)S(1)}, u32[]{:S(2)}, u32[]{:S(2)}) collective-permute-start(f32[2,22,3,128]{3,0,2,1:T(2,128)S(1)} %get-tuple-element.127), channel_id=1, source_target_pairs={{0,2},{2,4},{4,6},{1,3},{3,5},{5,7},{8,10},{10,12},{12,14},{9,11},... | collective-permute-start | bytes 202760 | tf_op jit(solution)/shard_map/ppermute | solution.py:19
  103.5 2.1 %collective-permute-start.13 = (f32[2,22,3,128]{3,0,2,1:T(2,128)S(1)}, f32[2,22,3,128]{3,0,2,1:T(2,128)S(1)}, u32[]{:S(2)}, u32[]{:S(2)}) collective-permute-start(f32[2,22,3,128]{3,0,2,1:T(2,128)S(1)} %get-tuple-element.128), channel_id=1, source_target_pairs={{2,0},{4,2},{6,4},{3,1},{5,3},{7,5},{10,8},{12,10},{14,12},{11,9},... | collective-permute-start | bytes 202760 | tf_op jit(solution)/shard_map/ppermute | solution.py:20
  105.8 3.4 %collective-permute-done.13 = f32[2,22,3,128]{3,0,2,1:T(2,128)S(1)} collective-permute-done((f32[2,22,3,128]{3,0,2,1:T(2,128)S(1)}, f32[2,22,3,128]{3,0,2,1:T(2,128)S(1)}, u32[]{:S(2)}, u32[]{:S(2)}) %collective-permute-start.13) | collective-permute-done | bytes 67616 | tf_op jit(solution)/shard_map/ppermute | solution.py:20
  109.6 2.2 %fusion.63 = (f32[2,22,50,3]{3,0,2,1:T(2,128)}, f32[2,22,50,3]{3,0,2,1:T(2,128)S(1)}) fusion(f32[2,22,50,128]{3,0,2,1:T(2,128)S(1)} %pad_maximum_fusion.3), kind=kLoop, calls=%fused_computation.198 | loop fusion | bytes 105600 | tf_op jit(solution)/shard_map/slice | solution.py:17
  111.9 1.7 %copy.306 = f32[2,22,50,3]{2,0,3,1:T(2,128)S(1)} copy(f32[2,22,50,3]{3,0,2,1:T(2,128)} %get-tuple-element.125) | data formatting | bytes 52800
  113.5 1.3 %collective-permute-start.14 = (f32[2,22,50,3]{2,0,3,1:T(2,128)S(1)}, f32[2,22,50,3]{2,0,3,1:T(2,128)S(1)}, u32[]{:S(2)}, u32[]{:S(2)}) collective-permute-start(f32[2,22,50,3]{2,0,3,1:T(2,128)S(1)} %copy.306), channel_id=1, source_target_pairs={{0,1},{2,3},{4,5},{6,7},{8,9},{10,11},{12,13},{14,15},{16,17},{18,... | collective-permute-start | bytes 79208 | tf_op jit(solution)/shard_map/ppermute | solution.py:19
  117.0 1.6 %copy.293 = f32[2,22,50,3]{3,1,2,0:T(8,128)} copy(f32[2,22,50,3]{2,0,3,1:T(2,128)S(1)} %collective-permute-done.14) | data formatting | bytes 52800 | tf_op jit(solution)/shard_map/ppermute | solution.py:19
  118.6 2.0 %collective-permute-done.15 = f32[2,22,50,3]{2,0,3,1:T(2,128)S(1)} collective-permute-done((f32[2,22,50,3]{2,0,3,1:T(2,128)S(1)}, f32[2,22,50,3]{2,0,3,1:T(2,128)S(1)}, u32[]{:S(2)}, u32[]{:S(2)}) %collective-permute-start.15) | collective-permute-done | bytes 26432 | tf_op jit(solution)/shard_map/ppermute | solution.py:20
  120.6 1.6 %copy.295 = f32[2,22,50,3]{3,1,2,0:T(8,128)} copy(f32[2,22,50,3]{2,0,3,1:T(2,128)S(1)} %collective-permute-done.15) | data formatting | bytes 52800 | tf_op jit(solution)/shard_map/ppermute | solution.py:20
  122.2 2.7 %pad_maximum_fusion = f32[2,22,50,134]{3,1,2,0:T(8,128)S(1)} fusion(f32[2,22,50,3]{3,1,2,0:T(8,128)} %copy.295, f32[2,22,50,128]{3,1,2,0:T(8,128)S(1)} %copy.294, f32[2,22,50,3]{3,1,2,0:T(8,128)} %copy.293), kind=kLoop, calls=%fused_computation.27 | loop fusion | flops 589600 | bytes 2358400 | tf_op jit(solution)/shard_map/concatenate | solution.py:21
  (135 shorter events, 32.2 us)
Async XLA Ops:
  5.3 1.3 %copy-start.2 = (f32[3,17,45,128]{3,2,1,0:T(8,128)S(1)}, f32[3,17,45,128]{3,2,1,0:T(8,128)}, u32[]{:S(2)}) copy-start(f32[3,17,45,128]{3,2,1,0:T(8,128)} %param.8) | copy-start | bytes 3525124
  6.6 1.2 copy-start.4
  8.1 11.7 %collective-permute-start = (f32[3,1,45,2]{2,3,1,0:T(2,128)S(1)}, f32[3,1,45,2]{2,3,1,0:T(2,128)S(1)}, u32[]{:S(2)}, u32[]{:S(2)}) collective-permute-start(f32[3,1,45,2]{2,3,1,0:T(2,128)S(1)} %get-tuple-element.143), channel_id=1, source_target_pairs={{0,8},{8,16},{16,24},{1,9},{9,17},{17,25},{2,10},{10,18},{18,26},{... | collective-permute-start | bytes 3248 | tf_op jit(solution)/shard_map/ppermute | solution.py:19
  11.3 8.5 %collective-permute-start.1 = (f32[3,1,45,2]{2,3,1,0:T(2,128)S(1)}, f32[3,1,45,2]{2,3,1,0:T(2,128)S(1)}, u32[]{:S(2)}, u32[]{:S(2)}) collective-permute-start(f32[3,1,45,2]{2,3,1,0:T(2,128)S(1)} %get-tuple-element.144), channel_id=1, source_target_pairs={{8,0},{16,8},{24,16},{9,1},{17,9},{25,17},{10,2},{18,10},{26,18},{... | collective-permute-start | bytes 3248 | tf_op jit(solution)/shard_map/ppermute | solution.py:20
  13.4 27.2 %collective-permute-start.6 = (f32[3,1,45,128]{3,2,1,0:T(8,128)S(1)}, f32[3,1,45,128]{3,2,1,0:T(8,128)S(1)}, u32[]{:S(2)}, u32[]{:S(2)}) collective-permute-start(f32[3,1,45,128]{3,2,1,0:T(8,128)S(1)} %get-tuple-element.123), channel_id=1, source_target_pairs={{0,8},{8,16},{16,24},{1,9},{9,17},{17,25},{2,10},{10,18},{18,26},{... | collective-permute-start | bytes 207368 | tf_op jit(solution)/shard_map/ppermute | solution.py:19
  16.6 24.0 %collective-permute-start.7 = (f32[3,1,45,128]{3,2,1,0:T(8,128)S(1)}, f32[3,1,45,128]{3,2,1,0:T(8,128)S(1)}, u32[]{:S(2)}, u32[]{:S(2)}) collective-permute-start(f32[3,1,45,128]{3,2,1,0:T(8,128)S(1)} %get-tuple-element.124), channel_id=1, source_target_pairs={{8,0},{16,8},{24,16},{9,1},{17,9},{25,17},{10,2},{18,10},{26,18},{... | collective-permute-start | bytes 207368 | tf_op jit(solution)/shard_map/ppermute | solution.py:20
  20.0 7.9 %collective-permute-start.2 = (f32[3,19,1,2]{2,3,1,0:T(2,128)S(1)}, f32[3,19,1,2]{2,3,1,0:T(2,128)S(1)}, u32[]{:S(2)}, u32[]{:S(2)}) collective-permute-start(f32[3,19,1,2]{2,3,1,0:T(2,128)S(1)} %get-tuple-element.141), channel_id=1, source_target_pairs={{0,2},{2,4},{4,6},{1,3},{3,5},{5,7},{8,10},{10,12},{12,14},{9,11},... | collective-permute-start | bytes 1376 | tf_op jit(solution)/shard_map/ppermute | solution.py:19
  25.9 5.5 %collective-permute-start.3 = (f32[3,19,1,2]{2,3,1,0:T(2,128)S(1)}, f32[3,19,1,2]{2,3,1,0:T(2,128)S(1)}, u32[]{:S(2)}, u32[]{:S(2)}) collective-permute-start(f32[3,19,1,2]{2,3,1,0:T(2,128)S(1)} %get-tuple-element.142), channel_id=1, source_target_pairs={{2,0},{4,2},{6,4},{3,1},{5,3},{7,5},{10,8},{12,10},{14,12},{11,9},... | collective-permute-start | bytes 1376 | tf_op jit(solution)/shard_map/ppermute | solution.py:20
  31.7 4.5 %collective-permute-start.4 = (f32[3,19,47,1]{2,3,1,0:T(1,128)S(1)}, f32[3,19,47,1]{2,3,1,0:T(1,128)S(1)}, u32[]{:S(2)}, u32[]{:S(2)}) collective-permute-start(f32[3,19,47,1]{2,3,1,0:T(1,128)S(1)} %get-tuple-element.139), channel_id=1, source_target_pairs={{0,1},{2,3},{4,5},{6,7},{8,9},{10,11},{12,13},{14,15},{16,17},{18,... | collective-permute-start | bytes 32156 | tf_op jit(solution)/shard_map/ppermute | solution.py:19
  34.9 4.6 %collective-permute-start.5 = (f32[3,19,47,1]{2,3,1,0:T(1,128)S(1)}, f32[3,19,47,1]{2,3,1,0:T(1,128)S(1)}, u32[]{:S(2)}, u32[]{:S(2)}) collective-permute-start(f32[3,19,47,1]{2,3,1,0:T(1,128)S(1)} %get-tuple-element.140), channel_id=1, source_target_pairs={{1,0},{3,2},{5,4},{7,6},{9,8},{11,10},{13,12},{15,14},{17,16},{19,... | collective-permute-start | bytes 32156 | tf_op jit(solution)/shard_map/ppermute | solution.py:20
  40.7 7.2 %collective-permute-start.8 = (f32[3,19,1,128]{3,2,1,0:T(1,128)S(1)}, f32[3,19,1,128]{3,2,1,0:T(1,128)S(1)}, u32[]{:S(2)}, u32[]{:S(2)}) collective-permute-start(f32[3,19,1,128]{3,2,1,0:T(1,128)S(1)} %get-tuple-element.121), channel_id=1, source_target_pairs={{0,2},{2,4},{4,6},{1,3},{3,5},{5,7},{8,10},{10,12},{12,14},{9,11},... | collective-permute-start | bytes 87560 | tf_op jit(solution)/shard_map/ppermute | solution.py:19
  44.0 5.2 %collective-permute-start.9 = (f32[3,19,1,128]{3,2,1,0:T(1,128)S(1)}, f32[3,19,1,128]{3,2,1,0:T(1,128)S(1)}, u32[]{:S(2)}, u32[]{:S(2)}) collective-permute-start(f32[3,19,1,128]{3,2,1,0:T(1,128)S(1)} %get-tuple-element.122), channel_id=1, source_target_pairs={{2,0},{4,2},{6,4},{3,1},{5,3},{7,5},{10,8},{12,10},{14,12},{11,9},... | collective-permute-start | bytes 87560 | tf_op jit(solution)/shard_map/ppermute | solution.py:20
  52.0 1.3 %copy-start.1 = (f32[3,17,45,1]{3,2,1,0:T(8,128)S(1)}, f32[3,17,45,1]{3,2,1,0:T(8,128)}, u32[]{:S(2)}) copy-start(f32[3,17,45,1]{3,2,1,0:T(8,128)} %copy.284) | copy-start | bytes 27544
  53.3 0.7 copy-start.3
  54.0 36.0 %copy-start = (f32[16,44,128]{2,0,1:T(8,128)S(1)}, f32[16,44,128]{2,0,1:T(8,128)}, u32[]{:S(2)}) copy-start(f32[16,44,128]{2,0,1:T(8,128)} %param.12) | copy-start | bytes 1081348
  90.2 6.8 %collective-permute-start.10 = (f32[2,3,44,128]{3,1,2,0:T(4,128)S(1)}, f32[2,3,44,128]{3,1,2,0:T(4,128)S(1)}, u32[]{:S(2)}, u32[]{:S(2)}) collective-permute-start(f32[2,3,44,128]{3,1,2,0:T(4,128)S(1)} %get-tuple-element.132), channel_id=1, source_target_pairs={{0,8},{8,16},{16,24},{1,9},{9,17},{17,25},{2,10},{10,18},{18,26},{... | collective-permute-start | bytes 405512 | tf_op jit(solution)/shard_map/ppermute | solution.py:19
  93.4 6.8 %collective-permute-start.11 = (f32[2,3,44,128]{3,1,2,0:T(4,128)S(1)}, f32[2,3,44,128]{3,1,2,0:T(4,128)S(1)}, u32[]{:S(2)}, u32[]{:S(2)}) collective-permute-start(f32[2,3,44,128]{3,1,2,0:T(4,128)S(1)} %get-tuple-element.131), channel_id=1, source_target_pairs={{8,0},{16,8},{24,16},{9,1},{17,9},{25,17},{10,2},{18,10},{26,18},{... | collective-permute-start | bytes 405512 | tf_op jit(solution)/shard_map/ppermute | solution.py:20
  95.6 10.1 %copy-start.5 = (f32[16]{0:T(128)S(1)}, f32[16]{0:T(128)}, u32[]{:S(2)}) copy-start(f32[16]{0:T(128)} %fusion.49) | copy-start | bytes 196
  100.4 5.4 %collective-permute-start.12 = (f32[2,22,3,128]{3,0,2,1:T(2,128)S(1)}, f32[2,22,3,128]{3,0,2,1:T(2,128)S(1)}, u32[]{:S(2)}, u32[]{:S(2)}) collective-permute-start(f32[2,22,3,128]{3,0,2,1:T(2,128)S(1)} %get-tuple-element.127), channel_id=1, source_target_pairs={{0,2},{2,4},{4,6},{1,3},{3,5},{5,7},{8,10},{10,12},{12,14},{9,11},... | collective-permute-start | bytes 202760 | tf_op jit(solution)/shard_map/ppermute | solution.py:19
  103.5 5.6 %collective-permute-start.13 = (f32[2,22,3,128]{3,0,2,1:T(2,128)S(1)}, f32[2,22,3,128]{3,0,2,1:T(2,128)S(1)}, u32[]{:S(2)}, u32[]{:S(2)}) collective-permute-start(f32[2,22,3,128]{3,0,2,1:T(2,128)S(1)} %get-tuple-element.128), channel_id=1, source_target_pairs={{2,0},{4,2},{6,4},{3,1},{5,3},{7,5},{10,8},{12,10},{14,12},{11,9},... | collective-permute-start | bytes 202760 | tf_op jit(solution)/shard_map/ppermute | solution.py:20
  113.5 3.5 %collective-permute-start.14 = (f32[2,22,50,3]{2,0,3,1:T(2,128)S(1)}, f32[2,22,50,3]{2,0,3,1:T(2,128)S(1)}, u32[]{:S(2)}, u32[]{:S(2)}) collective-permute-start(f32[2,22,50,3]{2,0,3,1:T(2,128)S(1)} %copy.306), channel_id=1, source_target_pairs={{0,1},{2,3},{4,5},{6,7},{8,9},{10,11},{12,13},{14,15},{16,17},{18,... | collective-permute-start | bytes 79208 | tf_op jit(solution)/shard_map/ppermute | solution.py:19
  115.6 5.0 %collective-permute-start.15 = (f32[2,22,50,3]{2,0,3,1:T(2,128)S(1)}, f32[2,22,50,3]{2,0,3,1:T(2,128)S(1)}, u32[]{:S(2)}, u32[]{:S(2)}) collective-permute-start(f32[2,22,50,3]{2,0,3,1:T(2,128)S(1)} %copy.307), channel_id=1, source_target_pairs={{1,0},{3,2},{5,4},{7,6},{9,8},{11,10},{13,12},{15,14},{17,16},{19,... | collective-permute-start | bytes 79208 | tf_op jit(solution)/shard_map/ppermute | solution.py:20
where the time goes:
time: 130 us; the launch traced here: 129 us
  starting transfers between devices  41.5 us (32%)
  local copies, waits for them, and re-layouts  25.9 us (20%)
  waiting for transfers between devices  17.5 us (13%)
  matrix products  17.4 us (13%)
  other arithmetic  13.8 us (11%)
  loops' own time  8.02 us (6%)
  blocking collectives  3.43 us (3%)
    ppermute x8, starting transfers between devices, with_halo(): before = lax.ppermute(last, axis, up)  26.5 us
    dot_general x4, matrix products, rows_energy(): jnp.einsum('ij,jabc->iabc', stiffness, vectors, precision=lax.Precision.H...  17.4 us
    ppermute x8, waiting for transfers between devices, with_halo(): after = lax.ppermute(initial, axis, down)  16 us
    ppermute x8, starting transfers between devices, with_halo(): after = lax.ppermute(initial, axis, down)  15 us
    another operation x1, loops' own time, element_energy(): energies = lax.map(rows_energy, starts)  8.02 us
    unnamed x16, local copies, waits for them, and re-layouts  5.19 us
    dynamic_slice x4, local copies, waits for them, and re-layouts, element_energy(): energies = lax.map(rows_energy, starts)  5.1 us
    while x28, local copies, waits for them, and re-layouts  3.96 us
  transfers between devices with their start and end apart: 16, of which 7 were waited for; matrix products, arithmetic and copies ran while one was open for 6% of the time, Pallas kernels for 0%

commit v1 on v0

v1 whole, which is shorter than its diff:
```python
import functools

import jax
import jax.numpy as jnp
from jax import lax
from jax.experimental import pallas as pl
from jax.experimental.pallas import tpu as pltpu
from jax.sharding import PartitionSpec as P

RADIUS = 3
F32 = jnp.float32
BF16 = jnp.bfloat16
SCALE = -3.0 / 96.0
HIGHEST = lax.Precision.HIGHEST
VM = pltpu.VMEM
SM = pltpu.SMEM

EX, EY, EZ = 16, 44, 128
NX, NY = EX + 1, EY + 1
XN, XE = NX + 2 * RADIUS, EX + 2 * RADIUS
ROWS = 48
QROWS = 56
XR = 24


def iota(shape, dim):
    return lax.broadcasted_iota(jnp.int32, shape, dim)


def one_hot(mask):
    return jnp.where(mask, 1.0, 0.0).astype(F32)


def halves(value):
    high = value.astype(BF16)
    return high, (value - high.astype(F32)).astype(BF16)


def corner_scalars(coarse_ref, dof_of, shared):
    width = coarse_ref.shape[2]
    own = lax.axis_index("gz")
    out = [[None] * 8 for _ in range(3)]
    for k in range(8):
        dof = dof_of(k)
        part = dof // width
        place = dof - part * width
        if shared:
            part = jnp.where(part == own, 0, 1)
        for c in range(3):
            out[c][k] = coarse_ref[part, c, place]
    return out


def plane_scalars(corners, c, i):
    wx = i / EX
    return [(1.0 - wx) * corners[c][m] + wx * corners[c][4 + m] for m in range(4)]


def plane_interp(corners, c, i, rows):
    low_low, low_high, high_low, high_high = plane_scalars(corners, c, i)
    rz = iota((1, EZ), 1).astype(F32) * (1.0 / EZ)
    ry = iota((rows, EZ), 0).astype(F32) * (1.0 / EY)
    first = low_low * (1.0 - rz) + low_high * rz
    second = high_low * (1.0 - rz) + high_high * rz
    return (1.0 - ry) * first + ry * second


def stiffness_rows(stiff, in_lanes):
    def target(m, r):
        s, c = r // 4, r % 4
        if in_lanes:
            return jnp.where(c < 3, 8 * c + 4 * (m % 2) + 2 * s + m // 2, -1)
        return jnp.where(c < 3, 8 * c + 2 * m + s, -1)

    row = iota((32, 24), 0)
    left = one_hot(iota((32, 24), 1) == target(row // 8, row % 8))
    col = iota((24, 64), 1)
    right = one_hot(iota((24, 64), 0) == target(col // 16, col % 8))
    full = jnp.dot(left, stiff, precision=HIGHEST, preferred_element_type=F32)
    full = jnp.dot(full, right, precision=HIGHEST, preferred_element_type=F32)
    high = full.astype(BF16).astype(F32)
    return jnp.concatenate([high, full - high], axis=0).astype(BF16)


def build_nodes(plane_of, planes, rows, w_ref, b_ref, first=0):
    for p in planes:
        base = (first + p) * rows * 8
        zero = jnp.zeros((rows, EZ), F32)
        for c in range(3):
            value = plane_of(c, p)
            w_ref[pl.ds(base + c, rows, stride=8), :] = value
            w_ref[pl.ds(base + 4 + c, rows, stride=8), :] = pltpu.roll(value, EZ - 1, 1)
        w_ref[pl.ds(base + 3, rows, stride=8), :] = zero
        w_ref[pl.ds(base + 7, rows, stride=8), :] = zero

    count = len(planes)

    def split(p, _):
        base = (first + p) * rows
        for r in range(rows):
            value = w_ref[pl.ds(pl.multiple_of((base + r) * 8, 8), 8), :]
            high = value.astype(BF16).astype(F32)
            b_ref[pl.ds(pl.multiple_of((base + r) * 16, 16), 16), :] = jnp.concatenate([high, value - high], axis=0).astype(BF16)
        return 0

    lax.fori_loop(0, count, split, 0)


def energy_planes(lhs, w_ref, b_ref, s_ref, e_ref, first, count, rows, starts, out_first):
    def step(i, _):
        base = (first + i) * rows
        for r in starts:
            right = []
            for t in (0, 1):
                here = pl.multiple_of((base + r + t) * 16, 16)
                there = pl.multiple_of((base + rows + r + t) * 16, 16)
                right.append(jnp.concatenate([b_ref[pl.ds(here, 32), :], b_ref[pl.ds(there, 32), :]], axis=0))
            product = jnp.dot(lhs, jnp.concatenate(right, axis=1), preferred_element_type=F32)
            product = product[0:32] + product[32:64]
            for t in (0, 1):
                here = pl.multiple_of((base + r + t) * 8, 8)
                there = pl.multiple_of((base + rows + r + t) * 8, 8)
                part = product[:, t * EZ : (t + 1) * EZ]
                low = w_ref[pl.ds(here, 16), :] * part[0:16]
                high = w_ref[pl.ds(there, 16), :] * part[16:32]
                both = low + high
                s_ref[pl.ds(pl.multiple_of((r + t) * 8, 8), 8), :] = both[0:8] + both[8:16]
        total = None
        for s in (0, 1, 2, 4, 5, 6):
            term = s_ref[pl.ds(s, rows, stride=8), :]
            total = term if total is None else total + term
        e_ref[out_first + i] = total
        return 0

    lax.fori_loop(0, count, step, 0)


def pack_kernel(local_ref, top_ref, dens_ref, dofs_ref, up_ref, down_ref):
    for out_ref, node, elem in ((up_ref, EX - RADIUS, EX - RADIUS), (down_ref, 0, 0)):
        out_ref[...] = jnp.zeros(out_ref.shape, F32)
        for c in range(3):
            for j in range(4):
                out_ref[c * 4 + j, 0:NY, :] = local_ref[c, node + j]
                out_ref[c * 4 + j, NY : NY + 1, 0:NY] = top_ref[c, node + j : node + j + 1, :]
        for j in range(3):
            out_ref[12 + j, 0:EY, :] = dens_ref[pl.ds(elem + j, EY, stride=EX), :]
        out_ref[12, EY : EY + 1, 0:8] = dofs_ref[...].astype(F32)


def own_kernel(shared, local_ref, stiff_ref, coarse_ref, dofs_ref, own_ref, e_ref, lhs_ref, w_ref, b_ref, s_ref):
    corners = corner_scalars(coarse_ref, lambda k: dofs_ref[k], shared)
    for i in range(NX):
        for c in range(3):
            own_ref[c * NX + i, 0:NY, :] = local_ref[c, i] + plane_interp(corners, c, i, NY)
            own_ref[c * NX + i, NY:ROWS, :] = jnp.zeros((ROWS - NY, EZ), F32)
    stiff = stiff_ref[...]
    lhs = stiffness_rows(stiff, False)
    lhs_ref[0] = lhs
    lhs_ref[1] = stiffness_rows(stiff, True)
    s_ref[...] = jnp.zeros(s_ref.shape, F32)
    build_nodes(lambda c, p: own_ref[c * NX + p + 1], range(EX - 1), ROWS, w_ref, b_ref)
    energy_planes(lhs, w_ref, b_ref, s_ref, e_ref, 0, EX - 2, ROWS, range(1, EY - 1, 2), 0)


def average(flag, low, high, own):
    return jnp.where(flag, 0.5 * low + 0.5 * high, own)


def has_lower(axis):
    return lax.axis_index(axis) > 0


def has_upper(axis):
    return lax.axis_index(axis) < lax.axis_size(axis) - 1


def message_dofs(message_ref):
    row = message_ref[12, EY : EY + 1, :]
    lane = iota((1, EZ), 1)
    return lambda k: jnp.sum(jnp.where(lane == k, row, 0.0)).astype(jnp.int32)


def top_interp(corners, c, rows):
    rx = iota((rows, EZ), 0).astype(F32) * (1.0 / EX)
    ry = iota((rows, EZ), 1).astype(F32) * (1.0 / EY)
    low = (1.0 - ry) * corners[c][1] + ry * corners[c][3]
    high = (1.0 - ry) * corners[c][5] + ry * corners[c][7]
    return (1.0 - rx) * low + rx * high


TOP_AT = 368
Y_MESSAGE = 392


def x_kernel(shared, own_ref, top_ref, dens_ref, low_ref, high_ref, coarse_ref, dofs_ref,
             xl_ref, xh_ref, tx_ref, up_ref, down_ref, t_ref):
    corners = corner_scalars(coarse_ref, lambda k: dofs_ref[k], shared)
    corners_low = corner_scalars(coarse_ref, message_dofs(low_ref), shared)
    corners_high = corner_scalars(coarse_ref, message_dofs(high_ref), shared)
    lower, upper = has_lower("gx"), has_upper("gx")
    for c in range(3):
        for j in range(4):
            value = low_ref[c * 4 + j] + plane_interp(corners_low, c, EX - RADIUS + j, ROWS)
            if j == 3:
                mine = own_ref[c * NX]
                value = average(lower, value, mine, mine)
            xl_ref[c * 4 + j] = value
            value = high_ref[c * 4 + j] + plane_interp(corners_high, c, j, ROWS)
            if j == 0:
                mine = own_ref[c * NX + EX]
                value = average(upper, mine, value, mine)
            xh_ref[c * 4 + j] = value

    t_ref[...] = jnp.zeros(t_ref.shape, F32)
    for c in range(3):
        mine = top_ref[c] + top_interp(corners, c, NX)[:, 0:NY]
        t_ref[0, 0:NX, 0:NY] = mine
        for j in range(4):
            t_ref[1, j : j + 1, 0:NY] = low_ref[c * 4 + j, NY : NY + 1, 0:NY]
            t_ref[2, j : j + 1, 0:NY] = high_ref[c * 4 + j, NY : NY + 1, 0:NY]
        t_low = t_ref[1, 0:8, :] + pltpu.roll(top_interp(corners_low, c, 24), 24 - (EX - RADIUS), 0)[0:8]
        t_high = t_ref[2, 0:8, :] + top_interp(corners_high, c, 8)
        first = average(lower, t_low[3:4], t_ref[0, 0:1, :], t_ref[0, 0:1, :])
        last = average(upper, t_ref[0, EX : EX + 1, :], t_high[0:1], t_ref[0, EX : EX + 1, :])
        t_ref[3, 0:3, :] = t_low[0:3]
        t_ref[3, 3:4, :] = first
        t_ref[3, 4:19, :] = t_ref[0, 1:EX, :]
        t_ref[3, 19:20, :] = last
        t_ref[3, 20:23, :] = t_high[1:4]
        lane = iota((XR, EZ), 1)
        tx_ref[c] = jnp.where(lane < NY + 8, pltpu.roll(t_ref[3], 8, 1), 0.0)

    def plane(c, p):
        if p < 4:
            return xl_ref[c * 4 + p]
        if p < 19:
            return own_ref[c * NX + p - 3]
        return xh_ref[c * 4 + p - 19]

    def density(x):
        if x < 3:
            return low_ref[12 + x, 0:EY, :]
        if x < 19:
            return dens_ref[pl.ds(x - 3, EY, stride=EX), :]
        return high_ref[12 + x - 19, 0:EY, :]

    for out_ref, node, elem, lane_at in ((up_ref, EY - RADIUS, EY - RADIUS, EY - RADIUS + 8), (down_ref, 0, 0, 8)):
        for c in range(3):
            for p in range(XN):
                at = (c * XN + p) * 4
                out_ref[at : at + 4, :] = plane(c, p)[node : node + 4]
        for x in range(XE):
            at = 3 * XN * 4 + x * 4
            out_ref[at : at + 3, :] = density(x)[elem : elem + 3]
            out_ref[at + 3 : at + 4, :] = jnp.zeros((1, EZ), F32)
        out_ref[364:TOP_AT, :] = jnp.zeros((TOP_AT - 364, EZ), F32)
        lane = iota((XR, EZ), 1)
        total = jnp.zeros((XR, EZ), F32)
        for c in range(3):
            moved = pltpu.roll(tx_ref[c], (4 * c - lane_at) % EZ, 1)
            total = jnp.where((lane >= 4 * c) & (lane < 4 * c + 4), moved, total)
        out_ref[TOP_AT:Y_MESSAGE, :] = total


def side_kernel(own_ref, xl_ref, xh_ref, lhs_ref, e_ref, w_ref, b_ref, s_ref):
    s_ref[...] = jnp.zeros(s_ref.shape, F32)

    def plane(c, p):
        if p < 4:
            return xl_ref[c * 4 + p]
        if p == 4:
            return own_ref[c * NX + 1]
        if p == 5:
            return own_ref[c * NX + EX - 1]
        return xh_ref[c * 4 + p - 6]

    build_nodes(plane, range(10), ROWS, w_ref, b_ref)
    lhs = lhs_ref[0]
    for first, out_first in ((0, 0), (5, 4)):
        energy_planes(lhs, w_ref, b_ref, s_ref, e_ref, first, 4, ROWS, range(1, EY - 1, 2), out_first)


Z_MESSAGE = 192


def y_kernel(own_ref, xl_ref, xh_ref, tx_ref, dens_ref, lowx_ref, highx_ref, low_ref, high_ref,
             first_ref, last_ref, dext_ref, oa_ref, ob_ref, od_ref, up_ref, down_ref, z_ref, d_ref):
    lower, upper = has_lower("gy"), has_upper("gy")

    def plane(c, p):
        if p < 4:
            return xl_ref[c * 4 + p]
        if p < 19:
            return own_ref[c * NX + p - 3]
        return xh_ref[c * 4 + p - 19]

    def keep_planes(dest, at, step, block):
        turned = block.T
        dest[pl.ds(at, 8, stride=step), 0:64] = jnp.concatenate([turned[0:4], turned[EZ - 4 : EZ]], axis=0)

    pad = jnp.zeros((64 - QROWS, EZ), F32)
    z_ref[...] = jnp.zeros(z_ref.shape, F32)
    d_ref[...] = jnp.zeros(d_ref.shape, F32)
    for c in range(3):
        for p in range(XN):
            i = c * XN + p
            mine = plane(c, p)
            first_ref[i, 0:5, :] = jnp.zeros((5, EZ), F32)
            first_ref[i, 5:8, :] = low_ref[i * 4 : i * 4 + 3, :]
            first_ref[i, 8:16, :] = mine[0:8]
            first_ref[i, 8:9, :] = average(lower, low_ref[i * 4 + 3 : i * 4 + 4, :], mine[0:1], mine[0:1])
            last_ref[i, 0:4, :] = mine[40:44]
            last_ref[i, 4:5, :] = average(upper, mine[44:45], high_ref[i * 4 : i * 4 + 1, :], mine[44:45])
            last_ref[i, 5:8, :] = high_ref[i * 4 + 1 : i * 4 + 4, :]
            keep_planes(z_ref, c * XR + p, 3 * XR, jnp.concatenate([first_ref[i], mine[8:40], last_ref[i], pad], axis=0))

    dext_ref[...] = jnp.zeros(dext_ref.shape, F32)
    for x in range(XE):
        at = 3 * XN * 4 + x * 4
        if x < 3:
            mine = lowx_ref[12 + x, 0:EY, :]
        elif x < 19:
            mine = dens_ref[pl.ds(x - 3, EY, stride=EX), :]
        else:
            mine = highx_ref[12 + x - 19, 0:EY, :]
        dext_ref[x, 8 : 8 + EY, :] = mine
        dext_ref[x, 5:8, :] = low_ref[at : at + 3, :]
        dext_ref[x, 52:55, :] = high_ref[at : at + 3, :]
        keep_planes(d_ref, x, XR, jnp.concatenate([dext_ref[x], pad], axis=0))

    lane = iota((XR, EZ), 1)
    tops = []
    for c in range(3):
        mine = tx_ref[c]
        low = pltpu.roll(low_ref[TOP_AT:Y_MESSAGE, :], (5 - 4 * c) % EZ, 1)
        high = pltpu.roll(high_ref[TOP_AT:Y_MESSAGE, :], (52 - 4 * c) % EZ, 1)
        value = jnp.where((lane >= 5) & (lane < 8), low, mine)
        value = jnp.where(lane == 8, average(lower, low, mine, mine), value)
        value = jnp.where(lane == 52, average(upper, mine, high, mine), value)
        tops.append(jnp.where((lane > 52) & (lane < 56), high, value))
    top = jnp.concatenate(tops, axis=0)

    def nodes(k):
        return z_ref[k * 3 * XR : (k + 1) * 3 * XR, :]

    def dens(k):
        return d_ref[k * XR : (k + 1) * XR, :]

    def pack(low, high):
        return low + pltpu.roll(high, 64, 1)

    oa_ref[...] = pack(nodes(0), top)
    ob_ref[...] = pack(nodes(1), nodes(7))
    od_ref[...] = pack(dens(0), dens(7))
    up_ref[0:72, :] = pack(nodes(5), nodes(6))
    up_ref[72:144, :] = pack(nodes(7), top)
    up_ref[144:168, :] = pack(dens(5), dens(6))
    up_ref[168:192, :] = dens(7)
    down_ref[0:72, :] = pack(nodes(0), nodes(1))
    down_ref[72:144, :] = pack(nodes(2), nodes(3))
    down_ref[144:168, :] = pack(dens(0), dens(1))
    down_ref[168:192, :] = dens(2)


def edge_kernel(own_ref, xl_ref, xh_ref, first_ref, last_ref, lhs_ref, el_ref, eh_ref, w_ref, b_ref, s_ref):
    s_ref[...] = jnp.zeros(s_ref.shape, F32)
    lhs = lhs_ref[0]
    build_nodes(lambda c, p: first_ref[c * XN + p], range(XN), 16, w_ref, b_ref)
    energy_planes(lhs, w_ref, b_ref, s_ref, el_ref, 0, XE, 16, (5, 7), 0)
    build_nodes(lambda c, p: last_ref[c * XN + p], range(XN), 8, w_ref, b_ref)
    energy_planes(lhs, w_ref, b_ref, s_ref, eh_ref, 0, XE, 8, (3, 5), 0)


def triangle(value, axis):
    size = value.shape[axis]
    value = value + pltpu.roll(value, size - 1, axis)
    value = value + pltpu.roll(value, size - 2, axis)
    value = value + pltpu.roll(value, 1, axis)
    return value + pltpu.roll(value, 2, axis)


def weights(distance):
    return jnp.maximum(4 - jnp.abs(distance), 0).astype(F32)


def three_parts(value):
    high = value.astype(BF16)
    rest = value - high.astype(F32)
    middle = rest.astype(BF16)
    return high, middle, (rest - middle.astype(F32)).astype(BF16)


def exact_dot(value, right):
    parts = [jnp.dot(part, right, preferred_element_type=F32) for part in three_parts(value)]
    return parts[0] + parts[1] + parts[2]


def edge_total(count, position, parts):
    total = None
    for offset in range(-RADIUS, RADIUS + 1):
        place = position + offset
        term = float(RADIUS + 1 - abs(offset)) * one_hot((place >= 0) & (place < count * parts))
        total = term if total is None else total + term
    return total


def last_kernel(ea_ref, eb_ref, el_ref, eh_ref, dext_ref, oa_ref, ob_ref, od_ref, zl_ref, zh_ref, lhs_ref,
                sens_ref, smooth_ref, w_ref, b_ref, s_ref, ez_ref, f_ref, g_ref, c_ref):
    lower, upper = has_lower("gz"), has_upper("gz")

    def swap(value):
        return pltpu.roll(value, 64, 1)

    is_low = iota((3 * XR, EZ), 1) < 64
    oa, ob = oa_ref[...], ob_ref[...]
    zl0, zl1 = zl_ref[0:72, :], zl_ref[72:144, :]
    zh0, zh1 = zh_ref[0:72, :], zh_ref[72:144, :]
    nodes = (
        jnp.where(is_low, zl0, ob),
        jnp.where(is_low, swap(zl0), average(upper, oa, swap(zh0), oa)),
        jnp.where(is_low, zl1, zh0),
        jnp.where(is_low, average(lower, swap(zl1), oa, oa), swap(zh1)),
        jnp.where(is_low, ob, zh1),
    )
    build_nodes(lambda c, k: nodes[k][c * XR : (c + 1) * XR], range(5), XR, w_ref, b_ref)
    s_ref[...] = jnp.zeros(s_ref.shape, F32)
    energy_planes(lhs_ref[1], w_ref, b_ref, s_ref, ez_ref, 0, 4, XR, range(0, XE, 2), 0)

    lane = iota((XR, EZ), 1)
    low_side = lane < 64
    od = od_ref[...]
    dl0, dl1 = zl_ref[144:168, :], zl_ref[168:192, :]
    dh0, dh1 = zh_ref[144:168, :], zh_ref[168:192, :]
    dens = (
        jnp.where(low_side, dl0, od),
        jnp.where(low_side, swap(dl0), swap(dh0)),
        jnp.where(low_side, dl1, dh0),
        jnp.where(low_side, od, swap(dh1)),
    )
    inside = (lane % 64 >= 5) & (lane % 64 < 55) & (iota((XR, EZ), 0) < XE)
    for j in range(4):
        d = dens[j]
        for f, value in ((0, (SCALE * d) * d * d * ez_ref[j]), (1, d)):
            value = triangle_forward(jnp.where(inside, value, 0.0))
            c_ref[f, j * EX : (j + 1) * EX, :] = value[0:EX]
    row, col = iota((EZ, EZ), 0), iota((EZ, EZ), 1)
    along_y = jnp.where(row // 64 == col // 64, weights(row - col), 0.0).astype(BF16)

    rows = iota((QROWS, EZ), 0)
    lanes = iota((QROWS, EZ), 1)
    ok = (rows >= 5) & (rows < 55) & (lanes > 0) & (lanes < EZ - 1)
    for x in range(XE):
        if x < 4:
            middle = eb_ref[x]
        elif x < 18:
            middle = ea_ref[x - 4]
        else:
            middle = eb_ref[x - 14]
        start = jnp.where(rows[0:8] < 1, el_ref[x, 8:16, :], middle[0:8])
        end = jnp.where(rows[0:8] < 3, middle[40:48], eh_ref[x])
        energy = jnp.concatenate([el_ref[x, 0:8, :], start, middle[8:40], end], axis=0)
        d = dext_ref[x]
        f_ref[0, x] = jnp.where(ok, (SCALE * d) * d * d * energy, 0.0)
        f_ref[1, x] = jnp.where(ok, d, 0.0)

    for f in range(2):
        for t in range(QROWS // 8):
            at = slice(t * 8, t * 8 + 8)
            line = [f_ref[f, x, at, :] for x in range(XE)]
            for step in (1, 2, 1, 2):
                line = [line[i] + line[i + step] for i in range(len(line) - step)]
            for x in range(EX):
                g_ref[f, x, at, :] = line[x]

    k = iota((EZ, EZ), 0)
    j = (k % 64) // EX
    place = jnp.where(k < 64, j - 3, EZ - 1 + j)
    z = iota((EZ, EZ), 1)
    right = jnp.concatenate([weights(k - z), weights(place - z)], axis=0).astype(BF16)

    ends = []
    for f in range(2):
        turned = exact_dot(c_ref[f], along_y)
        turned = jnp.concatenate([turned, jnp.zeros((EZ - 4 * EX, EZ), F32)], axis=0).T
        ends.append(turned[8:56] + pltpu.roll(turned[72:120], 64, 1))

    base_x, base_y, base_z = lax.axis_index("gx") * EX, lax.axis_index("gy") * EY, lax.axis_index("gz") * EZ
    norm_y = edge_total(EY, base_y + iota((ROWS, EZ), 0), lax.axis_size("gy"))
    norm_z = edge_total(EZ, base_z + iota((ROWS, EZ), 1), lax.axis_size("gz"))
    norm_yz = norm_y * norm_z
    lanes = iota((ROWS, EZ), 1)
    for x in range(EX):
        sums = []
        for f in range(2):
            body = triangle(g_ref[f, x], 0)[8:QROWS]
            tail = jnp.where(lanes % EX == x, ends[f], 0.0)
            sums.append(exact_dot(jnp.concatenate([body, tail], axis=1), right))
        norm = norm_yz * edge_total(EX, base_x + x, lax.axis_size("gx"))
        d = dext_ref[x + 3, 8:QROWS, :]
        d = jnp.where(rows[0:ROWS] < EY, d, 1.0)
        sens_ref[pl.ds(x, EY, stride=EX), :] = (sums[0] / (d * norm))[0:EY]
        smooth_ref[pl.ds(x, EY, stride=EX), :] = (sums[1] / norm)[0:EY]


def triangle_forward(value):
    size = value.shape[0]
    for step in (1, 2, 1, 2):
        value = value + pltpu.roll(value, size - step, 0)
    return value


def call(kernel, outs, spaces, scratch=(), limit=32, flops=0, moved=0):
    return pl.pallas_call(
        kernel,
        out_shape=[jax.ShapeDtypeStruct(shape, dtype) for shape, dtype in outs],
        in_specs=[pl.BlockSpec(memory_space=space) for space in spaces],
        out_specs=[pl.BlockSpec(memory_space=VM)] * len(outs),
        scratch_shapes=[pltpu.VMEM(shape, dtype) for shape, dtype in scratch],
        compiler_params=pltpu.CompilerParams(vmem_limit_bytes=limit * 2**20),
        cost_estimate=pl.CostEstimate(flops=flops, bytes_accessed=moved, transcendentals=0),
    )


def both_ways(up, down, axis):
    count = lax.axis_size(axis)
    ups = [(i, i + 1) for i in range(count - 1)]
    downs = [(j, i) for i, j in ups]
    return lax.ppermute(up, axis, ups), lax.ppermute(down, axis, downs)


def local(local_solution, top_nodes, coarse_solution, corner_dofs, density, element_stiffness):
    top = top_nodes.reshape(3, NX, NY)
    dens = jnp.transpose(density, (1, 0, 2)).reshape(EY * EX, EZ)
    dofs = corner_dofs.reshape(8)
    shared = lax.axis_size("gz") == 2
    if shared:
        other = lax.ppermute(coarse_solution, "gz", [(0, 1), (1, 0)])
        coarse = jnp.stack([coarse_solution, other])
    else:
        coarse = lax.all_gather(coarse_solution, "gz")

    up, down = call(pack_kernel, [((15, ROWS, EZ), F32)] * 2, [VM] * 4)(local_solution, top, dens, dofs.reshape(1, 8))
    low_x, high_x = both_ways(up, down, "gx")

    def nodes(count):
        return [((count * 8, EZ), F32), ((count * 16, EZ), BF16)]

    own, ea, lhs = call(
        functools.partial(own_kernel, shared),
        [((3 * NX, ROWS, EZ), F32), ((EX - 2, ROWS, EZ), F32), ((2, 64, 64), BF16)],
        [VM, VM, SM, SM],
        nodes((EX - 1) * ROWS) + [((ROWS * 8, EZ), F32)],
    )(local_solution, element_stiffness, coarse, dofs)

    xl, xh, tx, up, down = call(
        functools.partial(x_kernel, shared),
        [((12, ROWS, EZ), F32), ((12, ROWS, EZ), F32), ((3, XR, EZ), F32), ((Y_MESSAGE, EZ), F32), ((Y_MESSAGE, EZ), F32)],
        [VM, VM, VM, VM, VM, SM, SM],
        [((4, XR, EZ), F32)],
    )(own, top, dens, low_x, high_x, coarse, dofs)
    low_y, high_y = both_ways(up, down, "gy")

    (eb,) = call(side_kernel, [((8, ROWS, EZ), F32)], [VM] * 4, nodes(10 * ROWS) + [((ROWS * 8, EZ), F32)])(own, xl, xh, lhs)

    first, last, dext, oa, ob, od, up, down = call(
        y_kernel,
        [((3 * XN, 16, EZ), F32), ((3 * XN, 8, EZ), F32), ((XE, QROWS, EZ), F32), ((72, EZ), F32), ((72, EZ), F32),
         ((XR, EZ), F32), ((Z_MESSAGE, EZ), F32), ((Z_MESSAGE, EZ), F32)],
        [VM] * 9,
        [((8 * 3 * XR, EZ), F32), ((8 * XR, EZ), F32)],
    )(own, xl, xh, tx, dens, low_x, high_x, low_y, high_y)
    if shared:
        is_first = lax.axis_index("gz") == 0
        other = lax.ppermute(jnp.where(is_first, up, down), "gz", [(0, 1), (1, 0)])
        low_z = jnp.where(is_first, 0.0, other)
        high_z = jnp.where(is_first, other, 0.0)
    else:
        low_z, high_z = both_ways(up, down, "gz")

    el, eh = call(
        edge_kernel,
        [((XE, 16, EZ), F32), ((XE, 8, EZ), F32)],
        [VM] * 6,
        nodes(XN * 16) + [((16 * 8, EZ), F32)],
    )(own, xl, xh, first, last, lhs)

    sens, smooth = call(
        last_kernel,
        [((EY * EX, EZ), F32)] * 2,
        [VM] * 11,
        nodes(5 * XR) + [((XR * 8, EZ), F32), ((4, XR, EZ), F32), ((2, XE, QROWS, EZ), F32), ((2, EX, QROWS, EZ), F32),
                         ((2, 4 * EX, EZ), F32)],
    )(ea, eb, el, eh, dext, oa, ob, od, low_z, high_z, lhs)

    def grid(value):
        return jnp.transpose(value.reshape(EY, EX, EZ), (1, 0, 2))

    return grid(sens), grid(smooth)


def solution(mesh):
    in_specs = (
        P(None, "gx", "gy", "gz"),
        P(None, "gx", "gy", "gz"),
        P(None, "gz"),
        P("gx", "gy", "gz", None),
        P("gx", "gy", "gz"),
        P(),
    )
    out_specs = (P("gx", "gy", "gz"), P("gx", "gy", "gz"))
    return jax.shard_map(local, mesh=mesh, in_specs=in_specs, out_specs=out_specs, check_vma=False)
```

time: 130 us -> 55.8 us (0.43)
  Pallas kernels: 0 us -> 29 us
  starting transfers between devices: 41.5 us -> 14.9 us
  local copies, waits for them, and re-layouts: 25.9 us -> 3.7 us
  matrix products: 17.4 us -> 0 us
  other arithmetic: 13.8 us -> 0.04 us
  waiting for transfers between devices: 17.5 us -> 6.98 us
  loops' own time: 8.02 us -> 0 us
  blocking collectives: 3.43 us -> 0 us
    pallas_call x0 -> x7, Pallas kernels: none -> 29 us  [the longest x1 8.59 us: local(): call(edge_kernel, [((XE, 16, EZ), F32), ((XE, 8, EZ), F32)], [VM] * 6, no...]
    ppermute x16 -> x6, starting transfers between devices: 41.5 us -> 14.9 us  [the longest x4 12.3 us: both_ways(): return (lax.ppermute(up, axis, ups), lax.ppermute(down, axis, downs))]
    dot_general x4 -> x0, matrix products: 17.4 us -> none  [rows_energy(): jnp.einsum('ij,jabc->iabc', stiffness, vectors, precision=lax.Precision.H...]
    ppermute x16 -> x6, waiting for transfers between devices: 17.5 us -> 6.98 us  [the longest x4 5.42 us: both_ways(): return (lax.ppermute(up, axis, ups), lax.ppermute(down, axis, downs))]
    another operation x1 -> x0, loops' own time: 8.02 us -> none  [element_energy(): energies = lax.map(rows_energy, starts)]
    add x12 -> x0, other arithmetic: 5.34 us -> none  [the longest x3 2.83 us: smooth(): summed = term_value if summed is None else summed + term_value]
    dynamic_slice x4 -> x0, local copies, waits for them, and re-layouts: 5.1 us -> none  [element_energy(): energies = lax.map(rows_energy, starts)]
    slice x16 -> x0, local copies, waits for them, and re-layouts: 4.57 us -> none  [the longest x5 2.45 us: with_halo(): last = lax.slice_in_dim(shard, length - width, length, axis=dim)]
  transfers between devices with their start and end apart: 16 -> 6, of which waited for: 7 -> 3; matrix products, arithmetic and copies ran while one was open for 6% -> 0% of each run, Pallas kernels for 0% -> 36%
where the time goes in v1:
time: 55.8 us; the launch traced here: 55.4 us
  Pallas kernels  29 us (52%)
  starting transfers between devices  14.9 us (27%)
  waiting for transfers between devices  6.98 us (13%)
  local copies, waits for them, and re-layouts  3.7 us (7%)
  between operations  0.78 us (1%)
    ppermute x4, starting transfers between devices, both_ways(): return (lax.ppermute(up, axis, ups), lax.ppermute(down, axis, downs))  12.3 us
    pallas_call x1, Pallas kernels, local(): call(edge_kernel, [((XE, 16, EZ), F32), ((XE, 8, EZ), F32)], [VM] * 6, no...  8.59 us
    pallas_call x1, Pallas kernels, local(): call(functools.partial(own_kernel, shared), [((3 * NX, ROWS, EZ), F32), (...  7.39 us
    ppermute x4, waiting for transfers between devices, both_ways(): return (lax.ppermute(up, axis, ups), lax.ppermute(down, axis, downs))  5.42 us
    pallas_call x1, Pallas kernels, local(): call(last_kernel, [((EY * EX, EZ), F32)] * 2, [VM] * 11, nodes(5 * XR) +...  4.23 us
    pallas_call x1, Pallas kernels, local(): call(side_kernel, [((8, ROWS, EZ), F32)], [VM] * 4, nodes(10 * ROWS) + [(...  3.72 us
    unnamed x13, local copies, waits for them, and re-layouts  3.7 us
    pallas_call x1, Pallas kernels, local(): call(y_kernel, [((3 * XN, 16, EZ), F32), ((3 * XN, 8, EZ), F32), ((XE, QR...  2.76 us
  transfers between devices with their start and end apart: 6, of which 3 were waited for; matrix products, arithmetic and copies ran while one was open for 0% of the time, Pallas kernels for 36%

profile of v1, /device:TPU:9, one launch (start us, length us, event | category | flops | bytes accessed | tf_op | source)
XLA Modules:
  0.0 55.4 jit_solution(2808313684917413974)
XLA Ops:
  0.6 0.0 copy-start.5
  0.6 0.0 copy-start.3
  0.7 0.8 %copy.10 = f32[3,17,45,1]{2,1,3,0:T(8,128)S(1)} copy(f32[3,17,45,1]{2,3,1,0:T(1,128)} %param.7) | data formatting | bytes 18360
  1.4 0.0 copy-start
  1.4 1.3 %copy-done = f32[3,17,45,128]{3,2,1,0:T(8,128)S(1)} copy-done((f32[3,17,45,128]{3,2,1,0:T(8,128)S(1)}, f32[3,17,45,128]{3,2,1,0:T(8,128)}, u32[]{:S(2)}) %copy-start) | copy-done | bytes 1175064
  2.7 0.0 copy-start.1
  2.7 1.0 %copy-done.1 = f32[16,44,128]{2,0,1:T(8,128)S(1)} copy-done((f32[16,44,128]{2,0,1:T(8,128)S(1)}, f32[16,44,128]{2,0,1:T(8,128)}, u32[]{:S(2)}) %copy-start.1) | copy-done | bytes 360472
  3.7 0.0 copy-start.4
  3.7 0.7 %copy-done.4 = s32[1,1,1,8]{3,2,1,0:T(1,128)S(1)} copy-done((s32[1,1,1,8]{3,2,1,0:T(1,128)S(1)}, s32[1,1,1,8]{3,2,1,0:T(1,128)}, u32[]{:S(2)}) %copy-start.4) | copy-done | bytes 56
  4.3 0.0 copy-start.2
  4.3 0.1 shard_map.78
  4.4 3.2 %collective-permute-start.1 = (f32[15,48,128]{2,1,0:T(8,128)S(1)}, f32[15,48,128]{2,1,0:T(8,128)S(1)}, u32[]{:S(2)}, u32[]{:S(2)}) collective-permute-start(f32[15,48,128]{2,1,0:T(8,128)S(1)} %get-tuple-element.26), channel_id=1, source_target_pairs={{0,8},{8,16},{16,24},{1,9},{9,17},{17,25},{2,10},{10,18},{18,26},{... | collective-permute-start | bytes 1105928 | tf_op jit(solution)/shard_map/ppermute | solution.py:528
  7.7 2.1 %collective-permute-start.2 = (f32[15,48,128]{2,1,0:T(8,128)S(1)}, f32[15,48,128]{2,1,0:T(8,128)S(1)}, u32[]{:S(2)}, u32[]{:S(2)}) collective-permute-start(f32[15,48,128]{2,1,0:T(8,128)S(1)} %get-tuple-element.27), channel_id=1, source_target_pairs={{8,0},{16,8},{24,16},{9,1},{17,9},{25,17},{10,2},{18,10},{26,18},{... | collective-permute-start | bytes 1105928 | tf_op jit(solution)/shard_map/ppermute | solution.py:528
  9.8 0.0 copy-done.5
  9.8 1.3 %collective-permute-start = (f32[3,512]{1,0:T(4,128)S(1)}, f32[3,512]{1,0:T(4,128)S(1)}, u32[]{:S(2)}, u32[]{:S(2)}) collective-permute-start(f32[3,512]{1,0:T(4,128)S(1)} %copy-done.5), channel_id=1, source_target_pairs={{0,1},{1,0},{2,3},{3,2},{4,5},{5,4},{6,7},{7,6},{8,9},{9,8},{10,11... | collective-permute-start | bytes 18440 | tf_op jit(solution)/shard_map/ppermute | solution.py:537
  11.1 1.6 %collective-permute-done = f32[3,512]{1,0:T(4,128)S(1)} collective-permute-done((f32[3,512]{1,0:T(4,128)S(1)}, f32[3,512]{1,0:T(4,128)S(1)}, u32[]{:S(2)}, u32[]{:S(2)}) %collective-permute-start) | collective-permute-done | bytes 6176 | tf_op jit(solution)/shard_map/ppermute | solution.py:537
  12.6 0.0 copy-done.3
  12.6 7.4 %shard_map.77 = (f32[51,48,128]{2,1,0:T(8,128)S(1)}, f32[14,48,128]{2,1,0:T(8,128)S(1)}, bf16[2,64,64]{2,1,0:T(8,128)(2,1)S(1)}) custom-call(f32[3,17,45,128]{3,2,1,0:T(8,128)S(1)} %copy-done, f32[24,24]{1,0:T(8,128)S(1)} %copy-done.3, f32[2,3,512]{2,1,0:T(4,128)S(1)} %pad_maximum_fusion.coarse_ref, s32[8]{0:T(128)S(1)} %bitcast.22), custom_call_target="tpu_custom_call" | custom-call | tf_op jit(solution)/shard_map/pallas_call | solution.py:548
  20.0 0.0 collective-permute-done.1.low_ref.lowx_ref
  20.0 0.0 collective-permute-done.2.high_ref.highx_ref
  20.1 0.0 copy-done.2
  20.1 2.2 %shard_map.79 = (f32[12,48,128]{2,1,0:T(8,128)S(1)}, f32[12,48,128]{2,1,0:T(8,128)S(1)}, f32[3,24,128]{2,1,0:T(8,128)S(1)}, f32[392,128]{1,0:T(8,128)}, f32[392,128]{1,0:T(8,128)}) custom-call(f32[51,48,128]{2,1,0:T(8,128)S(1)} %get-tuple-element.25.own_ref, f32[3,17,45]{2,1,0:T(8,128)S(1)} %bitcast.20, f32[704,128]{1,0:T(8,128)S(1)} %bitcast.17, ...), custom_call_target="tpu_custom_call" | custom-call | tf_op jit(solution)/shard_map/pallas_call | solution.py:555
  22.3 5.1 %collective-permute-start.3 = (f32[392,128]{1,0:T(8,128)}, f32[392,128]{1,0:T(8,128)S(1)}, u32[]{:S(2)}, u32[]{:S(2)}) collective-permute-start(f32[392,128]{1,0:T(8,128)} %get-tuple-element.32), channel_id=1, source_target_pairs={{0,2},{2,4},{4,6},{1,3},{3,5},{5,7},{8,10},{10,12},{12,14},{9,11},... | collective-permute-start | bytes 602120 | tf_op jit(solution)/shard_map/ppermute | solution.py:528
  27.4 1.9 %collective-permute-start.4 = (f32[392,128]{1,0:T(8,128)}, f32[392,128]{1,0:T(8,128)}, u32[]{:S(2)}, u32[]{:S(2)}) collective-permute-start(f32[392,128]{1,0:T(8,128)} %get-tuple-element.33), channel_id=1, source_target_pairs={{2,0},{4,2},{6,4},{3,1},{5,3},{7,5},{10,8},{12,10},{14,12},{11,9},... | collective-permute-start | bytes 602120 | tf_op jit(solution)/shard_map/ppermute | solution.py:528
  29.3 1.0 %collective-permute-done.3.low_ref = f32[392,128]{1,0:T(8,128)S(1)} collective-permute-done((f32[392,128]{1,0:T(8,128)}, f32[392,128]{1,0:T(8,128)S(1)}, u32[]{:S(2)}, u32[]{:S(2)}) %collective-permute-start.3) | collective-permute-done | bytes 200736 | tf_op jit(solution)/shard_map/ppermute | solution.py:528
  30.3 4.4 %collective-permute-done.4.high_ref = f32[392,128]{1,0:T(8,128)} collective-permute-done((f32[392,128]{1,0:T(8,128)}, f32[392,128]{1,0:T(8,128)}, u32[]{:S(2)}, u32[]{:S(2)}) %collective-permute-start.4) | collective-permute-done | bytes 200736 | tf_op jit(solution)/shard_map/ppermute | solution.py:528
  34.7 2.8 %shard_map.81 = (f32[69,16,128]{2,1,0:T(8,128)S(1)}, f32[69,8,128]{2,1,0:T(8,128)S(1)}, f32[22,56,128]{2,1,0:T(8,128)S(1)}, f32[72,128]{1,0:T(8,128)S(1)}, f32[7...) custom-call(f32[51,48,128]{2,1,0:T(8,128)S(1)} %get-tuple-element.25.own_ref, ...), custom_call_target="tpu_custom_call" | custom-call | tf_op jit(solution)/shard_map/pallas_call | solution.py:565
  37.5 1.3 %collective-permute-start.5 = (f32[192,128]{1,0:T(8,128)S(1)}, f32[192,128]{1,0:T(8,128)S(1)}, u32[]{:S(2)}, u32[]{:S(2)}) collective-permute-start(f32[192,128]{1,0:T(8,128)S(1)} %broadcast_select_fusion.2), channel_id=1, source_target_pairs={{0,1},{1,0},{2,3},{3,2},{4,5},{5,4},{6,7},{7,6},{8,9},{9,8},{10,11... | collective-permute-start | bytes 294920 | tf_op jit(solution)/shard_map/ppermute | solution.py:574
  38.8 3.7 %shard_map.80.eb_ref = f32[8,48,128]{2,1,0:T(8,128)S(1)} custom-call(f32[51,48,128]{2,1,0:T(8,128)S(1)} %get-tuple-element.25.own_ref, f32[12,48,128]{2,1,0:T(8,128)S(1)} %get-tuple-element.28.xl_ref, f32[12,48,128]{2,1,0:T(8,128)S(1)} %get-tuple-element.29.xh_ref, bf16[2,64,64]{2,1,0:T(8,128)(2,1)S(1)} %get-tuple-element.30.lhs_ref), custom_call_target="tpu_custom_call" | custom-call | tf_op jit(solution)/shard_map/pallas_call | solution.py:563
  42.5 8.6 %shard_map.82 = (f32[22,16,128]{2,1,0:T(8,128)S(1)}, f32[22,8,128]{2,1,0:T(8,128)S(1)}) custom-call(f32[51,48,128]{2,1,0:T(8,128)S(1)} %get-tuple-element.25.own_ref, f32[12,48,128]{2,1,0:T(8,128)S(1)} %get-tuple-element.28.xl_ref, f32[12,48,128]{2,1,0:T(8,128)S(1)} %get-tuple-element.29.xh_ref, f32[69,16,128]{2,1,0:T(8,128)S(1)} %get-tuple-element.34.first_ref, ...), custom_call_target="tpu_custom_call" | custom-call | tf_op jit(solution)/shard_map/pallas_call | solution.py:580
  51.1 0.0 collective-permute-done.5
  51.2 4.2 %shard_map.83 = (f32[704,128]{1,0:T(8,128)}, f32[704,128]{1,0:T(8,128)}) custom-call(f32[14,48,128]{2,1,0:T(8,128)S(1)} %get-tuple-element.24.ea_ref, f32[8,48,128]{2,1,0:T(8,128)S(1)} %shard_map.80.eb_ref, f32[22,16,128]{2,1,0:T(8,128)S(1)} %get-tuple-element.36.el_ref, f32[22,8,128]{2,1,0:T(8,128)S(1)} %get-tuple-element.37.eh_ref, ...), custom_call_target="tpu_custom_call" | custom-call | tf_op jit(solution)/shard_map/pallas_call | solution.py:587
  (3 shorter events, 0.0 us)
Async XLA Ops:
  0.6 9.1 %copy-start.5 = (f32[3,512]{1,0:T(4,128)S(1)}, f32[3,512]{1,0:T(4,128)}, u32[]{:S(2)}) copy-start(f32[3,512]{1,0:T(4,128)} %param.8) | copy-start | bytes 18436
  0.6 12.0 %copy-start.3 = (f32[24,24]{1,0:T(8,128)S(1)}, f32[24,24]{1,0:T(8,128)}, u32[]{:S(2)}) copy-start(f32[24,24]{1,0:T(8,128)} %stiff_ref.1) | copy-start | bytes 6916
  1.4 1.3 %copy-start = (f32[3,17,45,128]{3,2,1,0:T(8,128)S(1)}, f32[3,17,45,128]{3,2,1,0:T(8,128)}, u32[]{:S(2)}) copy-start(f32[3,17,45,128]{3,2,1,0:T(8,128)} %local_ref.3) | copy-start | bytes 3525124
  2.7 1.0 %copy-start.1 = (f32[16,44,128]{2,0,1:T(8,128)S(1)}, f32[16,44,128]{2,0,1:T(8,128)}, u32[]{:S(2)}) copy-start(f32[16,44,128]{2,0,1:T(8,128)} %param.10) | copy-start | bytes 1081348
  3.7 0.7 %copy-start.4 = (s32[1,1,1,8]{3,2,1,0:T(1,128)S(1)}, s32[1,1,1,8]{3,2,1,0:T(1,128)}, u32[]{:S(2)}) copy-start(s32[1,1,1,8]{3,2,1,0:T(1,128)} %param.9) | copy-start | bytes 100
  4.3 15.7 %copy-start.2 = (f32[16,44,128]{2,0,1:T(8,128)S(1)}, f32[16,44,128]{2,0,1:T(8,128)}, u32[]{:S(2)}) copy-start(f32[16,44,128]{2,0,1:T(8,128)} %param.10) | copy-start | bytes 1081348
  4.4 15.6 %collective-permute-start.1 = (f32[15,48,128]{2,1,0:T(8,128)S(1)}, f32[15,48,128]{2,1,0:T(8,128)S(1)}, u32[]{:S(2)}, u32[]{:S(2)}) collective-permute-start(f32[15,48,128]{2,1,0:T(8,128)S(1)} %get-tuple-element.26), channel_id=1, source_target_pairs={{0,8},{8,16},{16,24},{1,9},{9,17},{17,25},{2,10},{10,18},{18,26},{... | collective-permute-start | bytes 1105928 | tf_op jit(solution)/shard_map/ppermute | solution.py:528
  7.7 12.4 %collective-permute-start.2 = (f32[15,48,128]{2,1,0:T(8,128)S(1)}, f32[15,48,128]{2,1,0:T(8,128)S(1)}, u32[]{:S(2)}, u32[]{:S(2)}) collective-permute-start(f32[15,48,128]{2,1,0:T(8,128)S(1)} %get-tuple-element.27), channel_id=1, source_target_pairs={{8,0},{16,8},{24,16},{9,1},{17,9},{25,17},{10,2},{18,10},{26,18},{... | collective-permute-start | bytes 1105928 | tf_op jit(solution)/shard_map/ppermute | solution.py:528
  9.8 2.9 %collective-permute-start = (f32[3,512]{1,0:T(4,128)S(1)}, f32[3,512]{1,0:T(4,128)S(1)}, u32[]{:S(2)}, u32[]{:S(2)}) collective-permute-start(f32[3,512]{1,0:T(4,128)S(1)} %copy-done.5), channel_id=1, source_target_pairs={{0,1},{1,0},{2,3},{3,2},{4,5},{5,4},{6,7},{7,6},{8,9},{9,8},{10,11... | collective-permute-start | bytes 18440 | tf_op jit(solution)/shard_map/ppermute | solution.py:537
  22.3 8.0 %collective-permute-start.3 = (f32[392,128]{1,0:T(8,128)}, f32[392,128]{1,0:T(8,128)S(1)}, u32[]{:S(2)}, u32[]{:S(2)}) collective-permute-start(f32[392,128]{1,0:T(8,128)} %get-tuple-element.32), channel_id=1, source_target_pairs={{0,2},{2,4},{4,6},{1,3},{3,5},{5,7},{8,10},{10,12},{12,14},{9,11},... | collective-permute-start | bytes 602120 | tf_op jit(solution)/shard_map/ppermute | solution.py:528
  27.4 7.3 %collective-permute-start.4 = (f32[392,128]{1,0:T(8,128)}, f32[392,128]{1,0:T(8,128)}, u32[]{:S(2)}, u32[]{:S(2)}) collective-permute-start(f32[392,128]{1,0:T(8,128)} %get-tuple-element.33), channel_id=1, source_target_pairs={{2,0},{4,2},{6,4},{3,1},{5,3},{7,5},{10,8},{12,10},{14,12},{11,9},... | collective-permute-start | bytes 602120 | tf_op jit(solution)/shard_map/ppermute | solution.py:528
  37.5 13.6 %collective-permute-start.5 = (f32[192,128]{1,0:T(8,128)S(1)}, f32[192,128]{1,0:T(8,128)S(1)}, u32[]{:S(2)}, u32[]{:S(2)}) collective-permute-start(f32[192,128]{1,0:T(8,128)S(1)} %broadcast_select_fusion.2), channel_id=1, source_target_pairs={{0,1},{1,0},{2,3},{3,2},{4,5},{5,4},{6,7},{7,6},{8,9},{9,8},{10,11... | collective-permute-start | bytes 294920 | tf_op jit(solution)/shard_map/ppermute | solution.py:574

commit v2 on v1

--- a/solution.py
+++ b/solution.py
@@ -106,45 +106,78 @@
     lax.fori_loop(0, count, split, 0)
 
 
-def energy_planes(lhs, w_ref, b_ref, s_ref, e_ref, first, count, rows, starts, out_first):
+def energy_planes(lhs, w_ref, b_ref, s_ref, e_ref, first, count, rows, starts, out_first, group):
     def step(i, _):
-        base = (first + i) * rows
-        for r in starts:
-            right = []
-            for t in (0, 1):
-                here = pl.multiple_of((base + r + t) * 16, 16)
-                there = pl.multiple_of((base + rows + r + t) * 16, 16)
-                right.append(jnp.concatenate([b_ref[pl.ds(here, 32), :], b_ref[pl.ds(there, 32), :]], axis=0))
-            product = jnp.dot(lhs, jnp.concatenate(right, axis=1), preferred_element_type=F32)
-            product = product[0:32] + product[32:64]
-            for t in (0, 1):
-                here = pl.multiple_of((base + r + t) * 8, 8)
-                there = pl.multiple_of((base + rows + r + t) * 8, 8)
-                part = product[:, t * EZ : (t + 1) * EZ]
-                low = w_ref[pl.ds(here, 16), :] * part[0:16]
-                high = w_ref[pl.ds(there, 16), :] * part[16:32]
-                both = low + high
-                s_ref[pl.ds(pl.multiple_of((r + t) * 8, 8), 8), :] = both[0:8] + both[8:16]
-        total = None
-        for s in (0, 1, 2, 4, 5, 6):
-            term = s_ref[pl.ds(s, rows, stride=8), :]
-            total = term if total is None else total + term
-        e_ref[out_first + i] = total
+        for g in range(group):
+            base = (first + i * group + g) * rows
+            for r in starts:
+                right = []
+                for t in (0, 1):
+                    here = pl.multiple_of((base + r + t) * 16, 16)
+                    there = pl.multiple_of((base + rows + r + t) * 16, 16)
+                    right.append(jnp.concatenate([b_ref[pl.ds(here, 32), :], b_ref[pl.ds(there, 32), :]], axis=0))
+                product = jnp.dot(lhs, jnp.concatenate(right, axis=1), preferred_element_type=F32)
+                product = product[0:32] + product[32:64]
+                for t in (0, 1):
+                    here = pl.multiple_of((base + r + t) * 8, 8)
+                    there = pl.multiple_of((base + rows + r + t) * 8, 8)
+                    part = product[:, t * EZ : (t + 1) * EZ]
+                    low = w_ref[pl.ds(here, 16), :] * part[0:16]
+                    high = w_ref[pl.ds(there, 16), :] * part[16:32]
+                    both = low + high
+                    s_ref[pl.ds((g * rows + r + t) * 8, 8), :] = both[0:8] + both[8:16]
+            total = None
+            for s in (0, 1, 2, 4, 5, 6):
+                term = s_ref[pl.ds(g * rows * 8 + s, rows, stride=8), :]
+                total = term if total is None else total + term
+            e_ref[out_first + i * group + g] = total
         return 0
 
-    lax.fori_loop(0, count, step, 0)
-
-
-def pack_kernel(local_ref, top_ref, dens_ref, dofs_ref, up_ref, down_ref):
-    for out_ref, node, elem in ((up_ref, EX - RADIUS, EX - RADIUS), (down_ref, 0, 0)):
-        out_ref[...] = jnp.zeros(out_ref.shape, F32)
+    if count == group:
+        step(0, 0)
+    else:
+        lax.fori_loop(0, count // group, step, 0)
+
+
+def odd_place(axis):
+    return lax.axis_index(axis) % 2 == 1
+
+
+def pack_kernel(local_ref, top_ref, dens_ref, dofs_ref, even_ref, odd_ref, tops_ref, l_ref, t_ref, d_ref, c_ref, sem):
+    copies = [pltpu.make_async_copy(top_ref, t_ref, sem.at[0]), pltpu.make_async_copy(dens_ref, d_ref, sem.at[1]),
+              pltpu.make_async_copy(dofs_ref, c_ref, sem.at[2])]
+    for side, node in ((0, EX - RADIUS), (1, 0)):
+        for c in range(3):
+            copies.append(pltpu.make_async_copy(local_ref.at[c, node : node + 4], l_ref.at[side, c], sem.at[len(copies)]))
+    for copy in copies:
+        copy.start()
+    even_ref[...] = jnp.zeros(even_ref.shape, F32)
+    odd_ref[...] = jnp.zeros(odd_ref.shape, F32)
+    tops_ref[...] = jnp.zeros(tops_ref.shape, F32)
+    for copy in copies:
+        copy.wait()
+    for c in range(3):
+        for i in range(NX):
+            tops_ref[c, i : i + 1, 0:NY] = t_ref[c, i]
+    odd = odd_place("gx")
+    for out_ref, flip in ((even_ref, odd), (odd_ref, jnp.logical_not(odd))):
+        side = flip.astype(jnp.int32)
         for c in range(3):
             for j in range(4):
-                out_ref[c * 4 + j, 0:NY, :] = local_ref[c, node + j]
-                out_ref[c * 4 + j, NY : NY + 1, 0:NY] = top_ref[c, node + j : node + j + 1, :]
+                out_ref[c * 4 + j, 0:NY, :] = l_ref[side, c, j]
+                out_ref[c * 4 + j, NY : NY + 1, :] = jnp.where(
+                    flip, tops_ref[c, j : j + 1, :], tops_ref[c, EX - RADIUS + j : EX - RADIUS + j + 1, :])
         for j in range(3):
-            out_ref[12 + j, 0:EY, :] = dens_ref[pl.ds(elem + j, EY, stride=EX), :]
-        out_ref[12, EY : EY + 1, 0:8] = dofs_ref[...].astype(F32)
+            out_ref[12 + j, 0:EY, :] = jnp.where(
+                flip, d_ref[pl.ds(j, EY, stride=EX), :], d_ref[pl.ds(EX - RADIUS + j, EY, stride=EX), :])
+        out_ref[12, EY : EY + 1, 0:8] = c_ref[...].astype(F32)
+
+
+def sort_sides(axis, even_ref, odd_ref, low_ref, high_ref):
+    odd = odd_place(axis)
+    even, other = even_ref[...], odd_ref[...]
+    low_ref[...] = jnp.where(odd, even, other)
+    high_ref[...] = jnp.where(odd, other, even)
 
 
 def own_kernel(shared, local_ref, stiff_ref, coarse_ref, dofs_ref, own_ref, e_ref, lhs_ref, w_ref, b_ref, s_ref):
@@ -159,7 +192,7 @@
     lhs_ref[1] = stiffness_rows(stiff, True)
     s_ref[...] = jnp.zeros(s_ref.shape, F32)
     build_nodes(lambda c, p: own_ref[c * NX + p + 1], range(EX - 1), ROWS, w_ref, b_ref)
-    energy_planes(lhs, w_ref, b_ref, s_ref, e_ref, 0, EX - 2, ROWS, range(1, EY - 1, 2), 0)
+    energy_planes(lhs, w_ref, b_ref, s_ref, e_ref, 0, EX - 2, ROWS, range(1, EY - 1, 2), 0, EX - 2)
 
 
 def average(flag, low, high, own):
@@ -192,8 +225,9 @@
 Y_MESSAGE = 392
 
 
-def x_kernel(shared, own_ref, top_ref, dens_ref, low_ref, high_ref, coarse_ref, dofs_ref,
-             xl_ref, xh_ref, tx_ref, up_ref, down_ref, t_ref):
+def x_kernel(shared, own_ref, top_ref, dens_ref, even_ref, odd_ref, coarse_ref, dofs_ref,
+             xl_ref, xh_ref, tx_ref, yeven_ref, yodd_ref, low_ref, high_ref, up_ref, down_ref, t_ref):
+    sort_sides("gx", even_ref, odd_ref, low_ref, high_ref)
     corners = corner_scalars(coarse_ref, lambda k: dofs_ref[k], shared)
     corners_low = corner_scalars(coarse_ref, message_dofs(low_ref), shared)
     corners_high = corner_scalars(coarse_ref, message_dofs(high_ref), shared)
@@ -213,8 +247,7 @@
 
     t_ref[...] = jnp.zeros(t_ref.shape, F32)
     for c in range(3):
-        mine = top_ref[c] + top_interp(corners, c, NX)[:, 0:NY]
-        t_ref[0, 0:NX, 0:NY] = mine
+        t_ref[0] = top_ref[c] + top_interp(corners, c, XR)
         for j in range(4):
             t_ref[1, j : j + 1, 0:NY] = low_ref[c * 4 + j, NY : NY + 1, 0:NY]
             t_ref[2, j : j + 1, 0:NY] = high_ref[c * 4 + j, NY : NY + 1, 0:NY]
@@ -260,6 +293,7 @@
             moved = pltpu.roll(tx_ref[c], (4 * c - lane_at) % EZ, 1)
             total = jnp.where((lane >= 4 * c) & (lane < 4 * c + 4), moved, total)
         out_ref[TOP_AT:Y_MESSAGE, :] = total
+    sort_sides("gy", up_ref, down_ref, yodd_ref, yeven_ref)
 
 
 def side_kernel(own_ref, xl_ref, xh_ref, lhs_ref, e_ref, w_ref, b_ref, s_ref):
@@ -277,14 +311,16 @@
     build_nodes(plane, range(10), ROWS, w_ref, b_ref)
     lhs = lhs_ref[0]
     for first, out_first in ((0, 0), (5, 4)):
-        energy_planes(lhs, w_ref, b_ref, s_ref, e_ref, first, 4, ROWS, range(1, EY - 1, 2), out_first)
+        energy_planes(lhs, w_ref, b_ref, s_ref, e_ref, first, 4, ROWS, range(1, EY - 1, 2), out_first, 4)
 
 
 Z_MESSAGE = 192
 
 
-def y_kernel(own_ref, xl_ref, xh_ref, tx_ref, dens_ref, lowx_ref, highx_ref, low_ref, high_ref,
-             first_ref, last_ref, dext_ref, oa_ref, ob_ref, od_ref, up_ref, down_ref, z_ref, d_ref):
+def y_kernel(own_ref, xl_ref, xh_ref, tx_ref, dens_ref, lowx_ref, highx_ref, even_ref, odd_ref,
+             first_ref, last_ref, dext_ref, oa_ref, ob_ref, od_ref, zeven_ref, zodd_ref,
+             z_ref, d_ref, low_ref, high_ref, up_ref, down_ref):
+    sort_sides("gy", even_ref, odd_ref, low_ref, high_ref)
     lower, upper = has_lower("gy"), has_upper("gy")
 
     def plane(c, p):
@@ -360,15 +396,16 @@
     down_ref[72:144, :] = pack(nodes(2), nodes(3))
     down_ref[144:168, :] = pack(dens(0), dens(1))
     down_ref[168:192, :] = dens(2)
+    sort_sides("gz", up_ref, down_ref, zodd_ref, zeven_ref)
 
 
 def edge_kernel(own_ref, xl_ref, xh_ref, first_ref, last_ref, lhs_ref, el_ref, eh_ref, w_ref, b_ref, s_ref):
     s_ref[...] = jnp.zeros(s_ref.shape, F32)
     lhs = lhs_ref[0]
     build_nodes(lambda c, p: first_ref[c * XN + p], range(XN), 16, w_ref, b_ref)
-    energy_planes(lhs, w_ref, b_ref, s_ref, el_ref, 0, XE, 16, (5, 7), 0)
+    energy_planes(lhs, w_ref, b_ref, s_ref, el_ref, 0, XE, 16, (5, 7), 0, XE)
     build_nodes(lambda c, p: last_ref[c * XN + p], range(XN), 8, w_ref, b_ref)
-    energy_planes(lhs, w_ref, b_ref, s_ref, eh_ref, 0, XE, 8, (3, 5), 0)
+    energy_planes(lhs, w_ref, b_ref, s_ref, eh_ref, 0, XE, 8, (3, 5), 0, XE)
 
 
 def triangle(value, axis):
@@ -404,8 +441,9 @@
     return total
 
 
-def last_kernel(ea_ref, eb_ref, el_ref, eh_ref, dext_ref, oa_ref, ob_ref, od_ref, zl_ref, zh_ref, lhs_ref,
-                sens_ref, smooth_ref, w_ref, b_ref, s_ref, ez_ref, f_ref, g_ref, c_ref):
+def last_kernel(ea_ref, eb_ref, el_ref, eh_ref, dext_ref, oa_ref, ob_ref, od_ref, even_ref, odd_ref, lhs_ref,
+                sens_ref, smooth_ref, w_ref, b_ref, s_ref, ez_ref, f_ref, g_ref, c_ref, zl_ref, zh_ref):
+    sort_sides("gz", even_ref, odd_ref, zl_ref, zh_ref)
     lower, upper = has_lower("gz"), has_upper("gz")
 
     def swap(value):
@@ -424,7 +462,7 @@
     )
     build_nodes(lambda c, k: nodes[k][c * XR : (c + 1) * XR], range(5), XR, w_ref, b_ref)
     s_ref[...] = jnp.zeros(s_ref.shape, F32)
-    energy_planes(lhs_ref[1], w_ref, b_ref, s_ref, ez_ref, 0, 4, XR, range(0, XE, 2), 0)
+    energy_planes(lhs_ref[1], w_ref, b_ref, s_ref, ez_ref, 0, 4, XR, range(0, XE, 2), 0, 4)
 
     lane = iota((XR, EZ), 1)
     low_side = lane < 64
@@ -509,27 +547,31 @@
     return value
 
 
-def call(kernel, outs, spaces, scratch=(), limit=32, flops=0, moved=0):
+def call(kernel, outs, ins, scratch=(), limit=16, micros=1.0):
     return pl.pallas_call(
         kernel,
         out_shape=[jax.ShapeDtypeStruct(shape, dtype) for shape, dtype in outs],
-        in_specs=[pl.BlockSpec(memory_space=space) for space in spaces],
+        in_specs=[pl.BlockSpec(memory_space=space) for space in ins],
         out_specs=[pl.BlockSpec(memory_space=VM)] * len(outs),
-        scratch_shapes=[pltpu.VMEM(shape, dtype) for shape, dtype in scratch],
+        scratch_shapes=[pltpu.VMEM(item[0], item[1]) if isinstance(item, tuple) else item for item in scratch],
         compiler_params=pltpu.CompilerParams(vmem_limit_bytes=limit * 2**20),
-        cost_estimate=pl.CostEstimate(flops=flops, bytes_accessed=moved, transcendentals=0),
+        cost_estimate=pl.CostEstimate(flops=0, bytes_accessed=int(micros * 3.6e6), transcendentals=0),
     )
 
 
-def both_ways(up, down, axis):
+def exchange(even, odd, axis):
     count = lax.axis_size(axis)
-    ups = [(i, i + 1) for i in range(count - 1)]
-    downs = [(j, i) for i, j in ups]
-    return lax.ppermute(up, axis, ups), lax.ppermute(down, axis, downs)
+    results = []
+    for value, first in ((even, 0), (odd, 1)):
+        pairs = [(i, i + 1) for i in range(first, count - 1, 2)]
+        if pairs:
+            results.append(lax.ppermute(value, axis, pairs + [(j, i) for i, j in pairs]))
+        else:
+            results.append(jnp.zeros_like(value))
+    return results
 
 
 def local(local_solution, top_nodes, coarse_solution, corner_dofs, density, element_stiffness):
-    top = top_nodes.reshape(3, NX, NY)
     dens = jnp.transpose(density, (1, 0, 2)).reshape(EY * EX, EZ)
     dofs = corner_dofs.reshape(8)
     shared = lax.axis_size("gz") == 2
@@ -539,8 +581,14 @@
     else:
         coarse = lax.all_gather(coarse_solution, "gz")
 
-    up, down = call(pack_kernel, [((15, ROWS, EZ), F32)] * 2, [VM] * 4)(local_solution, top, dens, dofs.reshape(1, 8))
-    low_x, high_x = both_ways(up, down, "gx")
+    message = ((15, ROWS, EZ), F32)
+    even, odd, tops = call(
+        pack_kernel,
+        [message, message, ((3, XR, EZ), F32)],
+        [pltpu.HBM] * 4,
+        [((2, 3, 4, NY, EZ), F32), ((3, NX, 1, NY), F32), ((EY * EX, EZ), F32), ((1, 8), jnp.int32), pltpu.SemaphoreType.DMA((9,))],
+    )(local_solution, jnp.transpose(top_nodes, (0, 1, 3, 2)), dens, dofs.reshape(1, 8))
+    even_x, odd_x = exchange(even, odd, "gx")
 
     def nodes(count):
         return [((count * 8, EZ), F32), ((count * 16, EZ), BF16)]
@@ -549,48 +597,52 @@
         functools.partial(own_kernel, shared),
         [((3 * NX, ROWS, EZ), F32), ((EX - 2, ROWS, EZ), F32), ((2, 64, 64), BF16)],
         [VM, VM, SM, SM],
-        nodes((EX - 1) * ROWS) + [((ROWS * 8, EZ), F32)],
+        nodes((EX - 1) * ROWS) + [(((EX - 2) * ROWS * 8, EZ), F32)],
+        micros=6.0,
     )(local_solution, element_stiffness, coarse, dofs)
 
-    xl, xh, tx, up, down = call(
+    face = ((12, ROWS, EZ), F32)
+    y_message = ((Y_MESSAGE, EZ), F32)
+    xl, xh, tx, even, odd, low_x, high_x = call(
         functools.partial(x_kernel, shared),
-        [((12, ROWS, EZ), F32), ((12, ROWS, EZ), F32), ((3, XR, EZ), F32), ((Y_MESSAGE, EZ), F32), ((Y_MESSAGE, EZ), F32)],
+        [face, face, ((3, XR, EZ), F32), y_message, y_message, message, message],
         [VM, VM, VM, VM, VM, SM, SM],
-        [((4, XR, EZ), F32)],
-    )(own, top, dens, low_x, high_x, coarse, dofs)
-    low_y, high_y = both_ways(up, down, "gy")
-
-    (eb,) = call(side_kernel, [((8, ROWS, EZ), F32)], [VM] * 4, nodes(10 * ROWS) + [((ROWS * 8, EZ), F32)])(own, xl, xh, lhs)
-
-    first, last, dext, oa, ob, od, up, down = call(
+        [y_message, y_message, ((4, XR, EZ), F32)],
+        micros=2.0,
+    )(own, tops, dens, even_x, odd_x, coarse, dofs)
+    even_y, odd_y = exchange(even, odd, "gy")
+
+    (eb,) = call(
+        side_kernel, [((8, ROWS, EZ), F32)], [VM] * 4, nodes(10 * ROWS) + [((4 * ROWS * 8, EZ), F32)], micros=3.5
+    )(own, xl, xh, lhs)
+
+    z_message = ((Z_MESSAGE, EZ), F32)
+    first, last, dext, oa, ob, od, even, odd = call(
         y_kernel,
         [((3 * XN, 16, EZ), F32), ((3 * XN, 8, EZ), F32), ((XE, QROWS, EZ), F32), ((72, EZ), F32), ((72, EZ), F32),
-         ((XR, EZ), F32), ((Z_MESSAGE, EZ), F32), ((Z_MESSAGE, EZ), F32)],
+         ((XR, EZ), F32), z_message, z_message],
         [VM] * 9,
-        [((8 * 3 * XR, EZ), F32), ((8 * XR, EZ), F32)],
-    )(own, xl, xh, tx, dens, low_x, high_x, low_y, high_y)
-    if shared:
-        is_first = lax.axis_index("gz") == 0
-        other = lax.ppermute(jnp.where(is_first, up, down), "gz", [(0, 1), (1, 0)])
-        low_z = jnp.where(is_first, 0.0, other)
-        high_z = jnp.where(is_first, other, 0.0)
-    else:
-        low_z, high_z = both_ways(up, down, "gz")
+        [((8 * 3 * XR, EZ), F32), ((8 * XR, EZ), F32), y_message, y_message, z_message, z_message],
+        micros=2.7,
+    )(own, xl, xh, tx, dens, low_x, high_x, even_y, odd_y)
+    even_z, odd_z = exchange(even, odd, "gz")
 
     el, eh = call(
         edge_kernel,
         [((XE, 16, EZ), F32), ((XE, 8, EZ), F32)],
         [VM] * 6,
-        nodes(XN * 16) + [((16 * 8, EZ), F32)],
+        nodes(XN * 16) + [((XE * 16 * 8, EZ), F32)],
+        micros=3.0,
     )(own, xl, xh, first, last, lhs)
 
     sens, smooth = call(
         last_kernel,
         [((EY * EX, EZ), F32)] * 2,
         [VM] * 11,
-        nodes(5 * XR) + [((XR * 8, EZ), F32), ((4, XR, EZ), F32), ((2, XE, QROWS, EZ), F32), ((2, EX, QROWS, EZ), F32),
-                         ((2, 4 * EX, EZ), F32)],
-    )(ea, eb, el, eh, dext, oa, ob, od, low_z, high_z, lhs)
+        nodes(5 * XR) + [((4 * XR * 8, EZ), F32), ((4, XR, EZ), F32), ((2, XE, QROWS, EZ), F32), ((2, EX, QROWS, EZ), F32),
+                         ((2, 4 * EX, EZ), F32), z_message, z_message],
+        micros=4.3,
+    )(ea, eb, el, eh, dext, oa, ob, od, even_z, odd_z, lhs)
 
     def grid(value):
         return jnp.transpose(value.reshape(EY, EX, EZ), (1, 0, 2))

time: 55.8 us -> 41.5 us (0.74)
  Pallas kernels: 29 us -> 18.7 us
  starting transfers between devices: 14.9 us -> 12.3 us
  waiting for transfers between devices: 6.98 us -> 5.85 us
    pallas_call x1, Pallas kernels: 8.59 us -> 2.31 us  [local(): call(edge_kernel, [((XE, 16, EZ), F32), ((XE, 8, EZ), F32)], [VM] * 6, no...]
    ppermute x5, starting transfers between devices: 13.6 us -> 10.9 us  [exchange(): lax.ppermute(value, axis, pairs + [(j, i) for i, j in pairs])]
    pallas_call x1, Pallas kernels: 7.39 us -> 5.45 us  [local(): call(functools.partial(own_kernel, shared), [((3 * NX, ROWS, EZ), F32), (...]
    ppermute x5, waiting for transfers between devices: 5.42 us -> 4.29 us  [exchange(): lax.ppermute(value, axis, pairs + [(j, i) for i, j in pairs])]
    pallas_call x1, Pallas kernels: 3.72 us -> 2.62 us  [local(): call(side_kernel, [((8, ROWS, EZ), F32)], [VM] * 4, nodes(10 * ROWS) + [(...]
    pallas_call x1, Pallas kernels: 4.23 us -> 3.6 us  [local(): call(last_kernel, [((EY * EX, EZ), F32)] * 2, [VM] * 11, nodes(5 * XR) +...]
    unnamed x13 -> x14, local copies, waits for them, and re-layouts: 3.7 us -> 3.68 us
  transfers between devices with their start and end apart: 6 -> 6, of which waited for: 3 -> 2; matrix products, arithmetic and copies ran while one was open for 0% -> 0% of each run, Pallas kernels for 36% -> 25%
where the time goes in v2:
time: 41.5 us; the launch traced here: 41.2 us
  Pallas kernels  18.7 us (45%)
  starting transfers between devices  12.3 us (30%)
  waiting for transfers between devices  5.85 us (14%)
  local copies, waits for them, and re-layouts  3.69 us (9%)
  between operations  0.75 us (2%)
    ppermute x5, starting transfers between devices, exchange(): lax.ppermute(value, axis, pairs + [(j, i) for i, j in pairs])  10.9 us
    pallas_call x1, Pallas kernels, local(): call(functools.partial(own_kernel, shared), [((3 * NX, ROWS, EZ), F32), (...  5.45 us
    ppermute x5, waiting for transfers between devices, exchange(): lax.ppermute(value, axis, pairs + [(j, i) for i, j in pairs])  4.29 us
    unnamed x14, local copies, waits for them, and re-layouts  3.68 us
    pallas_call x1, Pallas kernels, local(): call(last_kernel, [((EY * EX, EZ), F32)] * 2, [VM] * 11, nodes(5 * XR) +...  3.6 us
    pallas_call x1, Pallas kernels, local(): call(y_kernel, [((3 * XN, 16, EZ), F32), ((3 * XN, 8, EZ), F32), ((XE, QR...  2.64 us
    pallas_call x1, Pallas kernels, local(): call(side_kernel, [((8, ROWS, EZ), F32)], [VM] * 4, nodes(10 * ROWS) + [(...  2.62 us
    pallas_call x1, Pallas kernels, local(): call(edge_kernel, [((XE, 16, EZ), F32), ((XE, 8, EZ), F32)], [VM] * 6, no...  2.31 us
  transfers between devices with their start and end apart: 6, of which 2 were waited for; matrix products, arithmetic and copies ran while one was open for 0% of the time, Pallas kernels for 25%

profile of v2, /device:TPU:9, one launch (start us, length us, event | category | flops | bytes accessed | tf_op | source)
XLA Modules:
  0.0 41.2 jit_solution(4760637369229251309)
XLA Ops:
  0.6 0.0 copy-start
  0.6 1.3 %copy-done = f32[3,17,45,128]{3,2,1,0:T(8,128)S(1)} copy-done((f32[3,17,45,128]{3,2,1,0:T(8,128)S(1)}, f32[3,17,45,128]{3,2,1,0:T(8,128)}, u32[]{:S(2)}) %copy-start) | copy-done | bytes 1175064
  1.9 0.0 copy-start.1
  1.9 1.0 %copy-done.1 = f32[16,44,128]{2,0,1:T(8,128)S(1)} copy-done((f32[16,44,128]{2,0,1:T(8,128)S(1)}, f32[16,44,128]{2,0,1:T(8,128)}, u32[]{:S(2)}) %copy-start.1) | copy-done | bytes 360472
  2.9 0.0 copy-start.3
  2.9 0.7 %copy-done.3 = f32[3,17,45,1]{2,3,1,0:T(1,128)S(1)} copy-done((f32[3,17,45,1]{2,3,1,0:T(1,128)S(1)}, f32[3,17,45,1]{2,3,1,0:T(1,128)}, u32[]{:S(2)}) %copy-start.3) | copy-done | bytes 9204
  3.7 0.0 copy-start.5
  3.7 0.7 %copy-done.5 = s32[1,1,1,8]{3,2,1,0:T(1,128)S(1)} copy-done((s32[1,1,1,8]{3,2,1,0:T(1,128)S(1)}, s32[1,1,1,8]{3,2,1,0:T(1,128)}, u32[]{:S(2)}) %copy-start.5) | copy-done | bytes 56
  4.3 0.0 copy-start.6
  4.3 0.0 copy-start.4
  4.3 0.6 %shard_map.78 = (f32[15,48,128]{2,1,0:T(8,128)S(1)}, f32[15,48,128]{2,1,0:T(8,128)S(1)}, f32[3,24,128]{2,1,0:T(8,128)S(1)}) custom-call(f32[3,17,45,128]{3,2,1,0:T(8,128)S(1)} %copy-done, f32[3,17,1,45]{3,2,1,0:T(1,128)S(1)} %bitcast.17, f32[704,128]{1,0:T(8,128)S(1)} %bitcast.14, s32[1,8]{1,0:T(1,128)S(1)} %bitcast.18), custom_call_target="tpu_custom_call" | custom-call | bytes 3600000 | tf_op jit(solution)/shard_map/pallas_call | solution.py:585
  4.9 0.1 collective-permute-start.1
  5.0 4.5 %collective-permute-start.2 = (f32[15,48,128]{2,1,0:T(8,128)S(1)}, f32[15,48,128]{2,1,0:T(8,128)S(1)}, u32[]{:S(2)}, u32[]{:S(2)}) collective-permute-start(f32[15,48,128]{2,1,0:T(8,128)S(1)} %get-tuple-element.30), channel_id=1, source_target_pairs={{8,16},{16,8},{9,17},{17,9},{10,18},{18,10},{11,19},{19,11},{12,20... | collective-permute-start | bytes 1105928 | tf_op jit(solution)/shard_map/ppermute | solution.py:568
  9.5 0.0 copy-done.6
  9.5 1.3 %collective-permute-start = (f32[3,512]{1,0:T(4,128)S(1)}, f32[3,512]{1,0:T(4,128)S(1)}, u32[]{:S(2)}, u32[]{:S(2)}) collective-permute-start(f32[3,512]{1,0:T(4,128)S(1)} %copy-done.6), channel_id=1, source_target_pairs={{0,1},{1,0},{2,3},{3,2},{4,5},{5,4},{6,7},{7,6},{8,9},{9,8},{10,11... | collective-permute-start | bytes 18440 | tf_op jit(solution)/shard_map/ppermute | solution.py:579
  10.8 1.6 %collective-permute-done = f32[3,512]{1,0:T(4,128)S(1)} collective-permute-done((f32[3,512]{1,0:T(4,128)S(1)}, f32[3,512]{1,0:T(4,128)S(1)}, u32[]{:S(2)}, u32[]{:S(2)}) %collective-permute-start) | collective-permute-done | bytes 6176 | tf_op jit(solution)/shard_map/ppermute | solution.py:579
  12.3 0.0 copy-done.4
  12.4 5.5 %shard_map.77 = (f32[51,48,128]{2,1,0:T(8,128)S(1)}, f32[14,48,128]{2,1,0:T(8,128)S(1)}, bf16[2,64,64]{2,1,0:T(8,128)(2,1)S(1)}) custom-call(f32[3,17,45,128]{3,2,1,0:T(8,128)S(1)} %copy-done, f32[24,24]{1,0:T(8,128)S(1)} %copy-done.4, f32[2,3,512]{2,1,0:T(4,128)S(1)} %pad_maximum_fusion.coarse_ref, s32[8]{0:T(128)S(1)} %bitcast.19), custom_call_target="tpu_custom_call" | custom-call | bytes 21600000 | tf_op jit(solution)/shard_map/pallas_call | solution.py:596
  17.8 0.0 collective-permute-done.1.even_ref
  17.8 0.0 collective-permute-done.2.odd_ref
  17.8 0.0 copy-done.2
  17.8 1.5 %shard_map.79 = (f32[12,48,128]{2,1,0:T(8,128)S(1)}, f32[12,48,128]{2,1,0:T(8,128)S(1)}, f32[3,24,128]{2,1,0:T(8,128)S(1)}, f32[392,128]{1,0:T(8,128)S(1)}, f32[...) custom-call(f32[51,48,128]{2,1,0:T(8,128)S(1)} %get-tuple-element.27.own_ref, ...), custom_call_target="tpu_custom_call" | custom-call | bytes 7200000 | tf_op jit(solution)/shard_map/pallas_call | solution.py:606
  19.3 2.1 %collective-permute-start.3 = (f32[392,128]{1,0:T(8,128)S(1)}, f32[392,128]{1,0:T(8,128)S(1)}, u32[]{:S(2)}, u32[]{:S(2)}) collective-permute-start(f32[392,128]{1,0:T(8,128)S(1)} %get-tuple-element.37), channel_id=1, source_target_pairs={{0,2},{4,6},{2,0},{6,4},{1,3},{5,7},{3,1},{7,5},{8,10},{12,14},{10... | collective-permute-start | bytes 602120 | tf_op jit(solution)/shard_map/ppermute | solution.py:568
  21.5 3.0 %collective-permute-start.4 = (f32[392,128]{1,0:T(8,128)S(1)}, f32[392,128]{1,0:T(8,128)S(1)}, u32[]{:S(2)}, u32[]{:S(2)}) collective-permute-start(f32[392,128]{1,0:T(8,128)S(1)} %get-tuple-element.38), channel_id=1, source_target_pairs={{2,4},{4,2},{3,5},{5,3},{10,12},{12,10},{11,13},{13,11},{18,20},{2... | collective-permute-start | bytes 602120 | tf_op jit(solution)/shard_map/ppermute | solution.py:568
  24.5 0.0 collective-permute-done.3.even_ref
  24.5 4.3 %collective-permute-done.4.odd_ref = f32[392,128]{1,0:T(8,128)S(1)} collective-permute-done((f32[392,128]{1,0:T(8,128)S(1)}, f32[392,128]{1,0:T(8,128)S(1)}, u32[]{:S(2)}, u32[]{:S(2)}) %collective-permute-start.4) | collective-permute-done | bytes 200736 | tf_op jit(solution)/shard_map/ppermute | solution.py:568
  28.8 2.6 %shard_map.81 = (f32[69,16,128]{2,1,0:T(8,128)S(1)}, f32[69,8,128]{2,1,0:T(8,128)S(1)}, f32[22,56,128]{2,1,0:T(8,128)S(1)}, f32[72,128]{1,0:T(8,128)S(1)}, f32[7...) custom-call(f32[51,48,128]{2,1,0:T(8,128)S(1)} %get-tuple-element.27.own_ref, ...), custom_call_target="tpu_custom_call" | custom-call | bytes 9720000 | tf_op jit(solution)/shard_map/pallas_call | solution.py:620
  31.4 1.2 %collective-permute-start.5 = (f32[192,128]{1,0:T(8,128)S(1)}, f32[192,128]{1,0:T(8,128)S(1)}, u32[]{:S(2)}, u32[]{:S(2)}) collective-permute-start(f32[192,128]{1,0:T(8,128)S(1)} %get-tuple-element.47), channel_id=1, source_target_pairs={{0,1},{1,0},{2,3},{3,2},{4,5},{5,4},{6,7},{7,6},{8,9},{9,8},{10,11... | collective-permute-start | bytes 294920 | tf_op jit(solution)/shard_map/ppermute | solution.py:568
  32.7 2.6 %shard_map.80.eb_ref = f32[8,48,128]{2,1,0:T(8,128)S(1)} custom-call(f32[51,48,128]{2,1,0:T(8,128)S(1)} %get-tuple-element.27.own_ref, f32[12,48,128]{2,1,0:T(8,128)S(1)} %get-tuple-element.31.xl_ref, f32[12,48,128]{2,1,0:T(8,128)S(1)} %get-tuple-element.32.xh_ref, bf16[2,64,64]{2,1,0:T(8,128)(2,1)S(1)} %get-tuple-element.33.lhs_ref), custom_call_target="tpu_custom_call" | custom-call | bytes 12600000 | tf_op jit(solution)/shard_map/pallas_call | solution.py:615
  35.3 2.3 %shard_map.82 = (f32[22,16,128]{2,1,0:T(8,128)S(1)}, f32[22,8,128]{2,1,0:T(8,128)S(1)}) custom-call(f32[51,48,128]{2,1,0:T(8,128)S(1)} %get-tuple-element.27.own_ref, f32[12,48,128]{2,1,0:T(8,128)S(1)} %get-tuple-element.31.xl_ref, f32[12,48,128]{2,1,0:T(8,128)S(1)} %get-tuple-element.32.xh_ref, f32[69,16,128]{2,1,0:T(8,128)S(1)} %get-tuple-element.39.first_ref, ...), custom_call_target="tpu_custom_call" | custom-call | bytes 10800000 | tf_op jit(solution)/shard_map/pallas_call | solution.py:630
  37.6 0.0 collective-permute-done.5.even_ref
  37.6 3.6 %shard_map.83 = (f32[704,128]{1,0:T(8,128)}, f32[704,128]{1,0:T(8,128)}) custom-call(f32[14,48,128]{2,1,0:T(8,128)S(1)} %get-tuple-element.26.ea_ref, f32[8,48,128]{2,1,0:T(8,128)S(1)} %shard_map.80.eb_ref, f32[22,16,128]{2,1,0:T(8,128)S(1)} %get-tuple-element.41.el_ref, f32[22,8,128]{2,1,0:T(8,128)S(1)} %get-tuple-element.42.eh_ref, ...), custom_call_target="tpu_custom_call" | custom-call | bytes 15480000 | tf_op jit(solution)/shard_map/pallas_call | solution.py:638
  (3 shorter events, 0.0 us)
Async XLA Ops:
  0.6 1.3 %copy-start = (f32[3,17,45,128]{3,2,1,0:T(8,128)S(1)}, f32[3,17,45,128]{3,2,1,0:T(8,128)}, u32[]{:S(2)}) copy-start(f32[3,17,45,128]{3,2,1,0:T(8,128)} %local_ref.3) | copy-start | bytes 3525124
  1.9 1.0 %copy-start.1 = (f32[16,44,128]{2,0,1:T(8,128)S(1)}, f32[16,44,128]{2,0,1:T(8,128)}, u32[]{:S(2)}) copy-start(f32[16,44,128]{2,0,1:T(8,128)} %param.10) | copy-start | bytes 1081348
  2.9 0.7 %copy-start.3 = (f32[3,17,45,1]{2,3,1,0:T(1,128)S(1)}, f32[3,17,45,1]{2,3,1,0:T(1,128)}, u32[]{:S(2)}) copy-start(f32[3,17,45,1]{2,3,1,0:T(1,128)} %param.7) | copy-start | bytes 27544
  3.7 0.7 %copy-start.5 = (s32[1,1,1,8]{3,2,1,0:T(1,128)S(1)}, s32[1,1,1,8]{3,2,1,0:T(1,128)}, u32[]{:S(2)}) copy-start(s32[1,1,1,8]{3,2,1,0:T(1,128)} %param.9) | copy-start | bytes 100
  4.3 5.2 %copy-start.6 = (f32[3,512]{1,0:T(4,128)S(1)}, f32[3,512]{1,0:T(4,128)}, u32[]{:S(2)}) copy-start(f32[3,512]{1,0:T(4,128)} %param.8) | copy-start | bytes 18436
  4.3 8.0 %copy-start.4 = (f32[24,24]{1,0:T(8,128)S(1)}, f32[24,24]{1,0:T(8,128)}, u32[]{:S(2)}) copy-start(f32[24,24]{1,0:T(8,128)} %stiff_ref.1) | copy-start | bytes 6916
  4.3 13.5 %copy-start.2 = (f32[16,44,128]{2,0,1:T(8,128)S(1)}, f32[16,44,128]{2,0,1:T(8,128)}, u32[]{:S(2)}) copy-start(f32[16,44,128]{2,0,1:T(8,128)} %param.10) | copy-start | bytes 1081348
  4.9 12.9 %collective-permute-start.1 = (f32[15,48,128]{2,1,0:T(8,128)S(1)}, f32[15,48,128]{2,1,0:T(8,128)S(1)}, u32[]{:S(2)}, u32[]{:S(2)}) collective-permute-start(f32[15,48,128]{2,1,0:T(8,128)S(1)} %get-tuple-element.29), channel_id=1, source_target_pairs={{0,8},{16,24},{8,0},{24,16},{1,9},{17,25},{9,1},{25,17},{2,10},{18... | collective-permute-start | bytes 1105928 | tf_op jit(solution)/shard_map/ppermute | solution.py:568
  5.0 12.8 %collective-permute-start.2 = (f32[15,48,128]{2,1,0:T(8,128)S(1)}, f32[15,48,128]{2,1,0:T(8,128)S(1)}, u32[]{:S(2)}, u32[]{:S(2)}) collective-permute-start(f32[15,48,128]{2,1,0:T(8,128)S(1)} %get-tuple-element.30), channel_id=1, source_target_pairs={{8,16},{16,8},{9,17},{17,9},{10,18},{18,10},{11,19},{19,11},{12,20... | collective-permute-start | bytes 1105928 | tf_op jit(solution)/shard_map/ppermute | solution.py:568
  9.5 2.9 %collective-permute-start = (f32[3,512]{1,0:T(4,128)S(1)}, f32[3,512]{1,0:T(4,128)S(1)}, u32[]{:S(2)}, u32[]{:S(2)}) collective-permute-start(f32[3,512]{1,0:T(4,128)S(1)} %copy-done.6), channel_id=1, source_target_pairs={{0,1},{1,0},{2,3},{3,2},{4,5},{5,4},{6,7},{7,6},{8,9},{9,8},{10,11... | collective-permute-start | bytes 18440 | tf_op jit(solution)/shard_map/ppermute | solution.py:579
  19.3 5.2 %collective-permute-start.3 = (f32[392,128]{1,0:T(8,128)S(1)}, f32[392,128]{1,0:T(8,128)S(1)}, u32[]{:S(2)}, u32[]{:S(2)}) collective-permute-start(f32[392,128]{1,0:T(8,128)S(1)} %get-tuple-element.37), channel_id=1, source_target_pairs={{0,2},{4,6},{2,0},{6,4},{1,3},{5,7},{3,1},{7,5},{8,10},{12,14},{10... | collective-permute-start | bytes 602120 | tf_op jit(solution)/shard_map/ppermute | solution.py:568
  21.5 7.3 %collective-permute-start.4 = (f32[392,128]{1,0:T(8,128)S(1)}, f32[392,128]{1,0:T(8,128)S(1)}, u32[]{:S(2)}, u32[]{:S(2)}) collective-permute-start(f32[392,128]{1,0:T(8,128)S(1)} %get-tuple-element.38), channel_id=1, source_target_pairs={{2,4},{4,2},{3,5},{5,3},{10,12},{12,10},{11,13},{13,11},{18,20},{2... | collective-permute-start | bytes 602120 | tf_op jit(solution)/shard_map/ppermute | solution.py:568
  31.4 6.2 %collective-permute-start.5 = (f32[192,128]{1,0:T(8,128)S(1)}, f32[192,128]{1,0:T(8,128)S(1)}, u32[]{:S(2)}, u32[]{:S(2)}) collective-permute-start(f32[192,128]{1,0:T(8,128)S(1)} %get-tuple-element.47), channel_id=1, source_target_pairs={{0,1},{1,0},{2,3},{3,2},{4,5},{5,4},{6,7},{7,6},{8,9},{9,8},{10,11... | collective-permute-start | bytes 294920 | tf_op jit(solution)/shard_map/ppermute | solution.py:568

commit v3 on v2

--- a/solution.py
+++ b/solution.py
@@ -263,28 +263,14 @@
         lane = iota((XR, EZ), 1)
         tx_ref[c] = jnp.where(lane < NY + 8, pltpu.roll(t_ref[3], 8, 1), 0.0)
 
-    def plane(c, p):
-        if p < 4:
-            return xl_ref[c * 4 + p]
-        if p < 19:
-            return own_ref[c * NX + p - 3]
-        return xh_ref[c * 4 + p - 19]
-
-    def density(x):
-        if x < 3:
-            return low_ref[12 + x, 0:EY, :]
-        if x < 19:
-            return dens_ref[pl.ds(x - 3, EY, stride=EX), :]
-        return high_ref[12 + x - 19, 0:EY, :]
-
     for out_ref, node, elem, lane_at in ((up_ref, EY - RADIUS, EY - RADIUS, EY - RADIUS + 8), (down_ref, 0, 0, 8)):
         for c in range(3):
             for p in range(XN):
                 at = (c * XN + p) * 4
-                out_ref[at : at + 4, :] = plane(c, p)[node : node + 4]
+                out_ref[at : at + 4, :] = x_plane(own_ref, xl_ref, xh_ref, c, p)[node : node + 4]
         for x in range(XE):
             at = 3 * XN * 4 + x * 4
-            out_ref[at : at + 3, :] = density(x)[elem : elem + 3]
+            out_ref[at : at + 3, :] = x_density(dens_ref, low_ref, high_ref, x)[elem : elem + 3]
             out_ref[at + 3 : at + 4, :] = jnp.zeros((1, EZ), F32)
         out_ref[364:TOP_AT, :] = jnp.zeros((TOP_AT - 364, EZ), F32)
         lane = iota((XR, EZ), 1)
@@ -315,54 +301,79 @@
 
 
 Z_MESSAGE = 192
-
-
-def y_kernel(own_ref, xl_ref, xh_ref, tx_ref, dens_ref, lowx_ref, highx_ref, even_ref, odd_ref,
-             first_ref, last_ref, dext_ref, oa_ref, ob_ref, od_ref, zeven_ref, zodd_ref,
-             z_ref, d_ref, low_ref, high_ref, up_ref, down_ref):
+TILES = 3 * XN + XE
+
+
+def x_plane(own_ref, xl_ref, xh_ref, c, p):
+    if p < 4:
+        return xl_ref[c * 4 + p]
+    if p < 19:
+        return own_ref[c * NX + p - 3]
+    return xh_ref[c * 4 + p - 19]
+
+
+def x_density(dens_ref, low_ref, high_ref, x):
+    if x < 3:
+        return low_ref[12 + x, 0:EY, :]
+    if x < 19:
+        return dens_ref[pl.ds(x - 3, EY, stride=EX), :]
+    return high_ref[12 + x - 19, 0:EY, :]
+
+
+def end_planes(turned):
+    return jnp.concatenate([turned[0:4], turned[EZ - 4 : EZ]], axis=0)
+
+
+def turn_kernel(own_ref, xl_ref, xh_ref, dens_ref, lowx_ref, highx_ref, z_ref):
+    head = jnp.zeros((8, EZ), F32)
+    tail = jnp.zeros((8, EZ), F32)
+    for i in range(TILES):
+        if i < 3 * XN:
+            value = x_plane(own_ref, xl_ref, xh_ref, i // XN, i % XN)
+        else:
+            value = x_density(dens_ref, lowx_ref, highx_ref, i - 3 * XN)
+            value = jnp.concatenate([value, jnp.zeros((ROWS - EY, EZ), F32)], axis=0)
+        z_ref[i, :, 0:64] = end_planes(jnp.concatenate([head, value, tail], axis=0).T)
+        z_ref[i, :, 64:EZ] = jnp.zeros((8, 64), F32)
+
+
+def y_kernel(own_ref, xl_ref, xh_ref, tx_ref, zo_ref, eb_ref, even_ref, odd_ref,
+             edge_ref, low_ref, high_ref, oa_ref, ob_ref, od_ref, zeven_ref, zodd_ref,
+             z_ref, d_ref, up_ref, down_ref):
+    del eb_ref
     sort_sides("gy", even_ref, odd_ref, low_ref, high_ref)
     lower, upper = has_lower("gy"), has_upper("gy")
-
-    def plane(c, p):
-        if p < 4:
-            return xl_ref[c * 4 + p]
-        if p < 19:
-            return own_ref[c * NX + p - 3]
-        return xh_ref[c * 4 + p - 19]
-
-    def keep_planes(dest, at, step, block):
-        turned = block.T
-        dest[pl.ds(at, 8, stride=step), 0:64] = jnp.concatenate([turned[0:4], turned[EZ - 4 : EZ]], axis=0)
-
-    pad = jnp.zeros((64 - QROWS, EZ), F32)
+    for i in range(TILES):
+        edge_ref[i, 0:4, :] = low_ref[i * 4 : i * 4 + 4, :]
+        edge_ref[i, 4:8, :] = high_ref[i * 4 : i * 4 + 4, :]
+        if i < 3 * XN:
+            c, p = i // XN, i % XN
+            mine = x_plane(own_ref, xl_ref, xh_ref, c, p)
+            edge_ref[i, 3:4, :] = average(lower, low_ref[i * 4 + 3 : i * 4 + 4, :], mine[0:1], mine[0:1])
+            edge_ref[i, 4:5, :] = average(upper, mine[EY:NY], high_ref[i * 4 : i * 4 + 1, :], mine[EY:NY])
+
     z_ref[...] = jnp.zeros(z_ref.shape, F32)
     d_ref[...] = jnp.zeros(d_ref.shape, F32)
-    for c in range(3):
-        for p in range(XN):
-            i = c * XN + p
-            mine = plane(c, p)
-            first_ref[i, 0:5, :] = jnp.zeros((5, EZ), F32)
-            first_ref[i, 5:8, :] = low_ref[i * 4 : i * 4 + 3, :]
-            first_ref[i, 8:16, :] = mine[0:8]
-            first_ref[i, 8:9, :] = average(lower, low_ref[i * 4 + 3 : i * 4 + 4, :], mine[0:1], mine[0:1])
-            last_ref[i, 0:4, :] = mine[40:44]
-            last_ref[i, 4:5, :] = average(upper, mine[44:45], high_ref[i * 4 : i * 4 + 1, :], mine[44:45])
-            last_ref[i, 5:8, :] = high_ref[i * 4 + 1 : i * 4 + 4, :]
-            keep_planes(z_ref, c * XR + p, 3 * XR, jnp.concatenate([first_ref[i], mine[8:40], last_ref[i], pad], axis=0))
-
-    dext_ref[...] = jnp.zeros(dext_ref.shape, F32)
-    for x in range(XE):
-        at = 3 * XN * 4 + x * 4
-        if x < 3:
-            mine = lowx_ref[12 + x, 0:EY, :]
-        elif x < 19:
-            mine = dens_ref[pl.ds(x - 3, EY, stride=EX), :]
-        else:
-            mine = highx_ref[12 + x - 19, 0:EY, :]
-        dext_ref[x, 8 : 8 + EY, :] = mine
-        dext_ref[x, 5:8, :] = low_ref[at : at + 3, :]
-        dext_ref[x, 52:55, :] = high_ref[at : at + 3, :]
-        keep_planes(d_ref, x, XR, jnp.concatenate([dext_ref[x], pad], axis=0))
+    lane = iota((8, EZ), 1)
+    for first in range(0, TILES, 16):
+        count = min(16, TILES - first)
+        block = edge_ref[first : first + count].reshape(count * 8, EZ)
+        if count < 16:
+            block = jnp.concatenate([block, jnp.zeros(((16 - count) * 8, EZ), F32)], axis=0)
+        turned = end_planes(block.T)
+        for t in range(count):
+            i = first + t
+            low = pltpu.roll(turned, (5 - 8 * t) % EZ, 1)
+            high = pltpu.roll(turned, (52 - 8 * t - 4) % EZ, 1)
+            width = 4 if i < 3 * XN else 3
+            value = jnp.where((lane >= 5) & (lane < 5 + width), low, zo_ref[i])
+            value = jnp.where((lane >= 52) & (lane < 52 + width), high, value)
+            if i < 3 * XN:
+                at = (i // XN) * XR + i % XN
+                z_ref[at * 8 : at * 8 + 8, :] = value
+            else:
+                at = i - 3 * XN
+                d_ref[at * 8 : at * 8 + 8, :] = value
 
     lane = iota((XR, EZ), 1)
     tops = []
@@ -377,10 +388,10 @@
     top = jnp.concatenate(tops, axis=0)
 
     def nodes(k):
-        return z_ref[k * 3 * XR : (k + 1) * 3 * XR, :]
+        return z_ref[pl.ds(k, 3 * XR, stride=8), :]
 
     def dens(k):
-        return d_ref[k * XR : (k + 1) * XR, :]
+        return d_ref[pl.ds(k, XR, stride=8), :]
 
     def pack(low, high):
         return low + pltpu.roll(high, 64, 1)
@@ -399,13 +410,22 @@
     sort_sides("gz", up_ref, down_ref, zodd_ref, zeven_ref)
 
 
-def edge_kernel(own_ref, xl_ref, xh_ref, first_ref, last_ref, lhs_ref, el_ref, eh_ref, w_ref, b_ref, s_ref):
+def edge_kernel(own_ref, xl_ref, xh_ref, edge_ref, lhs_ref, el_ref, eh_ref, w_ref, b_ref, s_ref):
     s_ref[...] = jnp.zeros(s_ref.shape, F32)
     lhs = lhs_ref[0]
-    build_nodes(lambda c, p: first_ref[c * XN + p], range(XN), 16, w_ref, b_ref)
-    energy_planes(lhs, w_ref, b_ref, s_ref, el_ref, 0, XE, 16, (5, 7), 0, XE)
-    build_nodes(lambda c, p: last_ref[c * XN + p], range(XN), 8, w_ref, b_ref)
-    energy_planes(lhs, w_ref, b_ref, s_ref, eh_ref, 0, XE, 8, (3, 5), 0, XE)
+    pad = jnp.zeros((3, EZ), F32)
+
+    def low(c, p):
+        mine = x_plane(own_ref, xl_ref, xh_ref, c, p)
+        return jnp.concatenate([edge_ref[c * XN + p, 0:4, :], mine[1:2], pad], axis=0)
+
+    def high(c, p):
+        mine = x_plane(own_ref, xl_ref, xh_ref, c, p)
+        return jnp.concatenate([mine[EY - 1 : EY], edge_ref[c * XN + p, 4:8, :], pad], axis=0)
+
+    for side, e_ref in ((low, el_ref), (high, eh_ref)):
+        build_nodes(side, range(XN), 8, w_ref, b_ref)
+        energy_planes(lhs, w_ref, b_ref, s_ref, e_ref, 0, XE, 8, (0, 2), 0, XE)
 
 
 def triangle(value, axis):
@@ -441,8 +461,45 @@
     return total
 
 
-def last_kernel(ea_ref, eb_ref, el_ref, eh_ref, dext_ref, oa_ref, ob_ref, od_ref, even_ref, odd_ref, lhs_ref,
-                sens_ref, smooth_ref, w_ref, b_ref, s_ref, ez_ref, f_ref, g_ref, c_ref, zl_ref, zh_ref):
+def field_kernel(ea_ref, eb_ref, el_ref, eh_ref, dens_ref, lowx_ref, highx_ref, lowy_ref, highy_ref, g_ref, f_ref):
+    rows = iota((QROWS, EZ), 0)
+    lanes = iota((QROWS, EZ), 1)
+    ok = (rows >= 5) & (rows < 55) & (lanes > 0) & (lanes < EZ - 1)
+    row = iota((8, EZ), 0)
+    for x in range(XE):
+        if x < 4:
+            middle = eb_ref[x]
+        elif x < 18:
+            middle = ea_ref[x - 4]
+        else:
+            middle = eb_ref[x - 14]
+        low = pltpu.roll(el_ref[x], 5, 0)
+        high = pltpu.roll(eh_ref[x], 3, 0)
+        start = jnp.where(row < 1, low, middle[0:8])
+        end = jnp.where(row < 3, middle[40:48], high)
+        energy = jnp.concatenate([low, start, middle[8:40], end], axis=0)
+        at = 3 * XN * 4 + x * 4
+        pad = jnp.zeros((5, EZ), F32)
+        d = jnp.concatenate(
+            [pad, lowy_ref[at : at + 3, :], x_density(dens_ref, lowx_ref, highx_ref, x), highy_ref[at : at + 3, :], pad[0:1]], axis=0)
+        f_ref[0, x] = jnp.where(ok, (SCALE * d) * d * d * energy, 0.0)
+        f_ref[1, x] = jnp.where(ok, d, 0.0)
+
+    for f in range(2):
+        for t in range(QROWS // 8):
+            at = slice(t * 8, t * 8 + 8)
+            line = [f_ref[f, x, at, :] for x in range(XE)]
+            for step in (1, 2, 1, 2):
+                line = [line[i] + line[i + step] for i in range(len(line) - step)]
+            for x in range(EX):
+                f_ref[f, x, at, :] = line[x]
+    for f in range(2):
+        for x in range(EX):
+            g_ref[f, x] = triangle(f_ref[f, x], 0)[8:QROWS]
+
+
+def last_kernel(g_ref, dens_ref, oa_ref, ob_ref, od_ref, even_ref, odd_ref, lhs_ref,
+                sens_ref, smooth_ref, w_ref, b_ref, s_ref, ez_ref, c_ref, zl_ref, zh_ref):
     sort_sides("gz", even_ref, odd_ref, zl_ref, zh_ref)
     lower, upper = has_lower("gz"), has_upper("gz")
 
@@ -484,32 +541,6 @@
     row, col = iota((EZ, EZ), 0), iota((EZ, EZ), 1)
     along_y = jnp.where(row // 64 == col // 64, weights(row - col), 0.0).astype(BF16)
 
-    rows = iota((QROWS, EZ), 0)
-    lanes = iota((QROWS, EZ), 1)
-    ok = (rows >= 5) & (rows < 55) & (lanes > 0) & (lanes < EZ - 1)
-    for x in range(XE):
-        if x < 4:
-            middle = eb_ref[x]
-        elif x < 18:
-            middle = ea_ref[x - 4]
-        else:
-            middle = eb_ref[x - 14]
-        start = jnp.where(rows[0:8] < 1, el_ref[x, 8:16, :], middle[0:8])
-        end = jnp.where(rows[0:8] < 3, middle[40:48], eh_ref[x])
-        energy = jnp.concatenate([el_ref[x, 0:8, :], start, middle[8:40], end], axis=0)
-        d = dext_ref[x]
-        f_ref[0, x] = jnp.where(ok, (SCALE * d) * d * d * energy, 0.0)
-        f_ref[1, x] = jnp.where(ok, d, 0.0)
-
-    for f in range(2):
-        for t in range(QROWS // 8):
-            at = slice(t * 8, t * 8 + 8)
-            line = [f_ref[f, x, at, :] for x in range(XE)]
-            for step in (1, 2, 1, 2):
-                line = [line[i] + line[i + step] for i in range(len(line) - step)]
-            for x in range(EX):
-                g_ref[f, x, at, :] = line[x]
-
     k = iota((EZ, EZ), 0)
     j = (k % 64) // EX
     place = jnp.where(k < 64, j - 3, EZ - 1 + j)
@@ -530,14 +561,12 @@
     for x in range(EX):
         sums = []
         for f in range(2):
-            body = triangle(g_ref[f, x], 0)[8:QROWS]
             tail = jnp.where(lanes % EX == x, ends[f], 0.0)
-            sums.append(exact_dot(jnp.concatenate([body, tail], axis=1), right))
-        norm = norm_yz * edge_total(EX, base_x + x, lax.axis_size("gx"))
-        d = dext_ref[x + 3, 8:QROWS, :]
-        d = jnp.where(rows[0:ROWS] < EY, d, 1.0)
-        sens_ref[pl.ds(x, EY, stride=EX), :] = (sums[0] / (d * norm))[0:EY]
-        smooth_ref[pl.ds(x, EY, stride=EX), :] = (sums[1] / norm)[0:EY]
+            sums.append(exact_dot(jnp.concatenate([g_ref[f, x], tail], axis=1), right)[0:EY])
+        norm = (norm_yz * edge_total(EX, base_x + x, lax.axis_size("gx")))[0:EY]
+        d = dens_ref[pl.ds(x, EY, stride=EX), :]
+        sens_ref[pl.ds(x, EY, stride=EX), :] = sums[0] / (d * norm)
+        smooth_ref[pl.ds(x, EY, stride=EX), :] = sums[1] / norm
 
 
 def triangle_forward(value):
@@ -587,7 +616,10 @@
         [message, message, ((3, XR, EZ), F32)],
         [pltpu.HBM] * 4,
         [((2, 3, 4, NY, EZ), F32), ((3, NX, 1, NY), F32), ((EY * EX, EZ), F32), ((1, 8), jnp.int32), pltpu.SemaphoreType.DMA((9,))],
-    )(local_solution, jnp.transpose(top_nodes, (0, 1, 3, 2)), dens, dofs.reshape(1, 8))
+    )(*[
+        pltpu.with_memory_space_constraint(value, pltpu.HBM)
+        for value in (local_solution, jnp.transpose(top_nodes, (0, 1, 3, 2)), dens, dofs.reshape(1, 8))
+    ])
     even_x, odd_x = exchange(even, odd, "gx")
 
     def nodes(count):
@@ -613,36 +645,40 @@
     even_y, odd_y = exchange(even, odd, "gy")
 
     (eb,) = call(
-        side_kernel, [((8, ROWS, EZ), F32)], [VM] * 4, nodes(10 * ROWS) + [((4 * ROWS * 8, EZ), F32)], micros=3.5
+        side_kernel, [((8, ROWS, EZ), F32)], [VM] * 4, nodes(10 * ROWS) + [((4 * ROWS * 8, EZ), F32)], micros=2.6
     )(own, xl, xh, lhs)
 
+    (zo,) = call(turn_kernel, [((TILES, 8, EZ), F32)], [VM] * 6, micros=1.5)(own, xl, xh, dens, low_x, high_x)
+
     z_message = ((Z_MESSAGE, EZ), F32)
-    first, last, dext, oa, ob, od, even, odd = call(
+    edge, low_y, high_y, oa, ob, od, even, odd = call(
         y_kernel,
-        [((3 * XN, 16, EZ), F32), ((3 * XN, 8, EZ), F32), ((XE, QROWS, EZ), F32), ((72, EZ), F32), ((72, EZ), F32),
-         ((XR, EZ), F32), z_message, z_message],
-        [VM] * 9,
-        [((8 * 3 * XR, EZ), F32), ((8 * XR, EZ), F32), y_message, y_message, z_message, z_message],
-        micros=2.7,
-    )(own, xl, xh, tx, dens, low_x, high_x, even_y, odd_y)
+        [((TILES, 8, EZ), F32), y_message, y_message, ((72, EZ), F32), ((72, EZ), F32), ((XR, EZ), F32), z_message, z_message],
+        [VM] * 8,
+        [((8 * 3 * XR, EZ), F32), ((8 * XR, EZ), F32), z_message, z_message],
+        micros=1.0,
+    )(own, xl, xh, tx, zo, eb, even_y, odd_y)
     even_z, odd_z = exchange(even, odd, "gz")
 
     el, eh = call(
         edge_kernel,
-        [((XE, 16, EZ), F32), ((XE, 8, EZ), F32)],
-        [VM] * 6,
-        nodes(XN * 16) + [((XE * 16 * 8, EZ), F32)],
-        micros=3.0,
-    )(own, xl, xh, first, last, lhs)
+        [((XE, 8, EZ), F32)] * 2,
+        [VM] * 5,
+        nodes(XN * 8) + [((XE * 8 * 8, EZ), F32)],
+        micros=2.3,
+    )(own, xl, xh, edge, lhs)
+
+    (filtered,) = call(
+        field_kernel, [((2, EX, ROWS, EZ), F32)], [VM] * 9, [((2, XE, QROWS, EZ), F32)], micros=1.5
+    )(ea, eb, el, eh, dens, low_x, high_x, low_y, high_y)
 
     sens, smooth = call(
         last_kernel,
         [((EY * EX, EZ), F32)] * 2,
-        [VM] * 11,
-        nodes(5 * XR) + [((4 * XR * 8, EZ), F32), ((4, XR, EZ), F32), ((2, XE, QROWS, EZ), F32), ((2, EX, QROWS, EZ), F32),
-                         ((2, 4 * EX, EZ), F32), z_message, z_message],
-        micros=4.3,
-    )(ea, eb, el, eh, dext, oa, ob, od, even_z, odd_z, lhs)
+        [VM] * 8,
+        nodes(5 * XR) + [((4 * XR * 8, EZ), F32), ((4, XR, EZ), F32), ((2, 4 * EX, EZ), F32), z_message, z_message],
+        micros=2.5,
+    )(filtered, dens, oa, ob, od, even_z, odd_z, lhs)
 
     def grid(value):
         return jnp.transpose(value.reshape(EY, EX, EZ), (1, 0, 2))

time: 41.5 us -> 34.7 us (0.84)
  waiting for transfers between devices: 5.85 us -> 1.57 us
  local copies, waits for them, and re-layouts: 3.69 us -> 0.03 us
  Pallas kernels: 18.7 us -> 19.9 us
    ppermute x5, waiting for transfers between devices: 4.29 us -> 0.02 us  [exchange(): lax.ppermute(value, axis, pairs + [(j, i) for i, j in pairs])]
    unnamed x14 -> x10, local copies, waits for them, and re-layouts: 3.68 us -> 0.02 us
    pallas_call x1, Pallas kernels: 0.58 us -> 1.5 us  [local(): call(pack_kernel, [message, message, ((3, XR, EZ), F32)], [pltpu.HBM] * 4...]
    pallas_call x3 -> x5, Pallas kernels: 8.55 us -> 8.76 us  [the longest x1 3.1 us: local(): call(last_kernel, [((EY * EX, EZ), F32)] * 2, [VM] * 8, nodes(5 * XR) + [...]
  transfers between devices with their start and end apart: 6 -> 6, of which waited for: 2 -> 1; matrix products, arithmetic and copies ran while one was open for 0% -> 0% of each run, Pallas kernels for 25% -> 36%
where the time goes in v3:
time: 34.7 us; the launch traced here: 34.5 us
  Pallas kernels  19.9 us (57%)
  starting transfers between devices  12.3 us (35%)
  waiting for transfers between devices  1.57 us (5%)
  between operations  0.81 us (2%)
    ppermute x5, starting transfers between devices, exchange(): lax.ppermute(value, axis, pairs + [(j, i) for i, j in pairs])  11 us
    pallas_call x1, Pallas kernels, local(): call(functools.partial(own_kernel, shared), [((3 * NX, ROWS, EZ), F32), (...  5.45 us
    pallas_call x1, Pallas kernels, local(): call(last_kernel, [((EY * EX, EZ), F32)] * 2, [VM] * 8, nodes(5 * XR) + [...  3.1 us
    pallas_call x1, Pallas kernels, local(): call(side_kernel, [((8, ROWS, EZ), F32)], [VM] * 4, nodes(10 * ROWS) + [(...  2.62 us
    pallas_call x1, Pallas kernels, local(): call(edge_kernel, [((XE, 8, EZ), F32)] * 2, [VM] * 5, nodes(XN * 8) + [((...  1.98 us
    pallas_call x1, Pallas kernels, local(): call(turn_kernel, [((TILES, 8, EZ), F32)], [VM] * 6, micros=1.5)  1.6 us
    ppermute x1, waiting for transfers between devices, local(): other = lax.ppermute(coarse_solution, 'gz', [(0, 1), (1, 0)])  1.56 us
    pallas_call x1, Pallas kernels, local(): call(functools.partial(x_kernel, shared), [face, face, ((3, XR, EZ), F32)...  1.51 us
  transfers between devices with their start and end apart: 6, of which 1 were waited for; matrix products, arithmetic and copies ran while one was open for 0% of the time, Pallas kernels for 36%

profile of v3, /device:TPU:9, one launch (start us, length us, event | category | flops | bytes accessed | tf_op | source)
XLA Modules:
  0.0 34.5 jit_solution(10603074339042322889)
XLA Ops:
  0.6 0.0 copy-start.1
  0.6 0.0 copy-start.3
  0.7 0.0 copy-start.4
  0.7 0.0 copy-start.2
  0.7 0.0 copy-start
  0.7 1.5 %shard_map.78 = (f32[15,48,128]{2,1,0:T(8,128)S(1)}, f32[15,48,128]{2,1,0:T(8,128)S(1)}, f32[3,24,128]{2,1,0:T(8,128)S(1)}) custom-call(f32[3,17,45,128]{3,2,1,0:T(8,128)} %local_ref.3, f32[3,17,1,45]{3,2,1,0:T(1,128)} %bitcast.22, f32[704,128]{1,0:T(8,128)} %bitcast.14, s32[1,8]{1,0:T(1,128)} %bitcast.19), custom_call_target="tpu_custom_call" | custom-call | bytes 3600000 | tf_op jit(solution)/shard_map/pallas_call | solution.py:614
  2.2 0.1 collective-permute-start.1
  2.3 4.5 %collective-permute-start.2 = (f32[15,48,128]{2,1,0:T(8,128)S(1)}, f32[15,48,128]{2,1,0:T(8,128)S(1)}, u32[]{:S(2)}, u32[]{:S(2)}) collective-permute-start(f32[15,48,128]{2,1,0:T(8,128)S(1)} %get-tuple-element.30), channel_id=1, source_target_pairs={{8,16},{16,8},{9,17},{17,9},{10,18},{18,10},{11,19},{19,11},{12,20... | collective-permute-start | bytes 1105928 | tf_op jit(solution)/shard_map/ppermute | solution.py:597
  6.8 0.0 copy-done.4
  6.8 1.3 %collective-permute-start = (f32[3,512]{1,0:T(4,128)S(1)}, f32[3,512]{1,0:T(4,128)S(1)}, u32[]{:S(2)}, u32[]{:S(2)}) collective-permute-start(f32[3,512]{1,0:T(4,128)S(1)} %copy-done.4), channel_id=1, source_target_pairs={{0,1},{1,0},{2,3},{3,2},{4,5},{5,4},{6,7},{7,6},{8,9},{9,8},{10,11... | collective-permute-start | bytes 18440 | tf_op jit(solution)/shard_map/ppermute | solution.py:608
  8.1 1.6 %collective-permute-done = f32[3,512]{1,0:T(4,128)S(1)} collective-permute-done((f32[3,512]{1,0:T(4,128)S(1)}, f32[3,512]{1,0:T(4,128)S(1)}, u32[]{:S(2)}, u32[]{:S(2)}) %collective-permute-start) | collective-permute-done | bytes 6176 | tf_op jit(solution)/shard_map/ppermute | solution.py:608
  9.6 0.0 copy-done.1
  9.6 0.0 copy-done.3
  9.7 0.0 copy-done.2
  9.7 5.5 %shard_map.77 = (f32[51,48,128]{2,1,0:T(8,128)S(1)}, f32[14,48,128]{2,1,0:T(8,128)S(1)}, bf16[2,64,64]{2,1,0:T(8,128)(2,1)S(1)}) custom-call(f32[3,17,45,128]{3,2,1,0:T(8,128)S(1)} %copy-done.1, f32[24,24]{1,0:T(8,128)S(1)} %copy-done.2, f32[2,3,512]{2,1,0:T(4,128)S(1)} %pad_maximum_fusion.coarse_ref, s32[8]{0:T(128)S(1)} %bitcast.20), custom_call_target="tpu_custom_call" | custom-call | bytes 21600000 | tf_op jit(solution)/shard_map/pallas_call | solution.py:628
  15.1 0.0 collective-permute-done.1.even_ref
  15.1 0.0 collective-permute-done.2.odd_ref
  15.1 0.0 copy-done
  15.1 1.5 %shard_map.79 = (f32[12,48,128]{2,1,0:T(8,128)S(1)}, f32[12,48,128]{2,1,0:T(8,128)S(1)}, f32[3,24,128]{2,1,0:T(8,128)S(1)}, f32[392,128]{1,0:T(8,128)S(1)}, f32[...) custom-call(f32[51,48,128]{2,1,0:T(8,128)S(1)} %get-tuple-element.27.own_ref, ...), custom_call_target="tpu_custom_call" | custom-call | bytes 7200000 | tf_op jit(solution)/shard_map/pallas_call | solution.py:638
  16.7 2.1 %collective-permute-start.3 = (f32[392,128]{1,0:T(8,128)S(1)}, f32[392,128]{1,0:T(8,128)S(1)}, u32[]{:S(2)}, u32[]{:S(2)}) collective-permute-start(f32[392,128]{1,0:T(8,128)S(1)} %get-tuple-element.37), channel_id=1, source_target_pairs={{0,2},{4,6},{2,0},{6,4},{1,3},{5,7},{3,1},{7,5},{8,10},{12,14},{10... | collective-permute-start | bytes 602120 | tf_op jit(solution)/shard_map/ppermute | solution.py:597
  18.8 3.0 %collective-permute-start.4 = (f32[392,128]{1,0:T(8,128)S(1)}, f32[392,128]{1,0:T(8,128)S(1)}, u32[]{:S(2)}, u32[]{:S(2)}) collective-permute-start(f32[392,128]{1,0:T(8,128)S(1)} %get-tuple-element.38), channel_id=1, source_target_pairs={{2,4},{4,2},{3,5},{5,3},{10,12},{12,10},{11,13},{13,11},{18,20},{2... | collective-permute-start | bytes 602120 | tf_op jit(solution)/shard_map/ppermute | solution.py:597
  21.8 2.6 %shard_map.80.eb_ref = f32[8,48,128]{2,1,0:T(8,128)S(1)} custom-call(f32[51,48,128]{2,1,0:T(8,128)S(1)} %get-tuple-element.27.own_ref, f32[12,48,128]{2,1,0:T(8,128)S(1)} %get-tuple-element.31.xl_ref, f32[12,48,128]{2,1,0:T(8,128)S(1)} %get-tuple-element.32.xh_ref, bf16[2,64,64]{2,1,0:T(8,128)(2,1)S(1)} %get-tuple-element.33.lhs_ref), custom_call_target="tpu_custom_call" | custom-call | bytes 9360000 | tf_op jit(solution)/shard_map/pallas_call | solution.py:647
  24.5 1.6 %shard_map.81.zo_ref = f32[91,8,128]{2,1,0:T(8,128)S(1)} custom-call(f32[51,48,128]{2,1,0:T(8,128)S(1)} %get-tuple-element.27.own_ref, f32[12,48,128]{2,1,0:T(8,128)S(1)} %get-tuple-element.31.xl_ref, f32[12,48,128]{2,1,0:T(8,128)S(1)} %get-tuple-element.32.xh_ref, f32[704,128]{1,0:T(8,128)S(1)} %bitcast.16, f32[15,48,128]{2,1,0:T(8,128)S(1)} %get-tuple-element.35.lowx_ref, ...), custom_call_target="tpu_custom_call" | custom-call | bytes 5400000 | tf_op jit(solution)/shard_map/pallas_call | solution.py:651
  26.1 0.0 collective-permute-done.3.even_ref
  26.1 0.0 collective-permute-done.4.odd_ref
  26.1 1.3 %shard_map.82 = (f32[91,8,128]{2,1,0:T(8,128)S(1)}, f32[392,128]{1,0:T(8,128)S(1)}, f32[392,128]{1,0:T(8,128)S(1)}, f32[72,128]{1,0:T(8,128)S(1)}, f32[72,128]{1...) custom-call(f32[51,48,128]{2,1,0:T(8,128)S(1)} %get-tuple-element.27.own_ref, ...), custom_call_target="tpu_custom_call" | custom-call | bytes 3600000 | tf_op jit(solution)/shard_map/pallas_call | solution.py:654
  27.4 1.2 %collective-permute-start.5 = (f32[192,128]{1,0:T(8,128)S(1)}, f32[192,128]{1,0:T(8,128)S(1)}, u32[]{:S(2)}, u32[]{:S(2)}) collective-permute-start(f32[192,128]{1,0:T(8,128)S(1)} %get-tuple-element.47), channel_id=1, source_target_pairs={{0,1},{1,0},{2,3},{3,2},{4,5},{5,4},{6,7},{7,6},{8,9},{9,8},{10,11... | collective-permute-start | bytes 294920 | tf_op jit(solution)/shard_map/ppermute | solution.py:597
  28.7 2.0 %shard_map.83 = (f32[22,8,128]{2,1,0:T(8,128)S(1)}, f32[22,8,128]{2,1,0:T(8,128)S(1)}) custom-call(f32[51,48,128]{2,1,0:T(8,128)S(1)} %get-tuple-element.27.own_ref, f32[12,48,128]{2,1,0:T(8,128)S(1)} %get-tuple-element.31.xl_ref, f32[12,48,128]{2,1,0:T(8,128)S(1)} %get-tuple-element.32.xh_ref, f32[91,8,128]{2,1,0:T(8,128)S(1)} %get-tuple-element.39.edge_ref, ...), custom_call_target="tpu_custom_call" | custom-call | bytes 8279999 | tf_op jit(solution)/shard_map/pallas_call | solution.py:663
  30.6 0.8 %shard_map.84.g_ref = f32[2,16,48,128]{3,2,1,0:T(8,128)S(1)} custom-call(f32[14,48,128]{2,1,0:T(8,128)S(1)} %get-tuple-element.26.ea_ref, f32[8,48,128]{2,1,0:T(8,128)S(1)} %shard_map.80.eb_ref, f32[22,8,128]{2,1,0:T(8,128)S(1)} %get-tuple-element.40.el_ref, f32[22,8,128]{2,1,0:T(8,128)S(1)} %get-tuple-element.41.eh_ref, f32[704,128]{1,0:T(8,128)S(1)} %bitcast.17, ...), custom_call_target="tpu_custom_call" | custom-call | bytes 5400000 | tf_op jit(solution)/shard_map/pallas_call | solution.py:671
  31.4 0.0 collective-permute-done.5.even_ref
  31.4 3.1 %shard_map.85 = (f32[704,128]{1,0:T(8,128)}, f32[704,128]{1,0:T(8,128)}) custom-call(f32[2,16,48,128]{3,2,1,0:T(8,128)S(1)} %shard_map.84.g_ref, f32[704,128]{1,0:T(8,128)S(1)} %bitcast.18, f32[72,128]{1,0:T(8,128)S(1)} %get-tuple-element.44.oa_ref, f32[72,128]{1,0:T(8,128)S(1)} %get-tuple-element.45.ob_ref, f32[24,128]{1,0:T(8,128)S(1)} %get-tuple-element.46.od_ref, ...), custom_call_target="tpu_custom_call" | custom-call | bytes 9000000 | tf_op jit(solution)/shard_map/pallas_call | solution.py:675
  (2 shorter events, 0.0 us)
Async XLA Ops:
  0.6 9.0 %copy-start.1 = (f32[3,17,45,128]{3,2,1,0:T(8,128)S(1)}, f32[3,17,45,128]{3,2,1,0:T(8,128)}, u32[]{:S(2)}) copy-start(f32[3,17,45,128]{3,2,1,0:T(8,128)} %local_ref.3) | copy-start | bytes 3525124
  0.6 9.0 %copy-start.3 = (s32[1,1,1,8]{3,2,1,0:T(1,128)S(1)}, s32[1,1,1,8]{3,2,1,0:T(1,128)}, u32[]{:S(2)}) copy-start(s32[1,1,1,8]{3,2,1,0:T(1,128)} %param.9) | copy-start | bytes 100
  0.7 6.1 %copy-start.4 = (f32[3,512]{1,0:T(4,128)S(1)}, f32[3,512]{1,0:T(4,128)}, u32[]{:S(2)}) copy-start(f32[3,512]{1,0:T(4,128)} %param.8) | copy-start | bytes 18436
  0.7 9.0 %copy-start.2 = (f32[24,24]{1,0:T(8,128)S(1)}, f32[24,24]{1,0:T(8,128)}, u32[]{:S(2)}) copy-start(f32[24,24]{1,0:T(8,128)} %stiff_ref.1) | copy-start | bytes 6916
  0.7 14.5 %copy-start = (f32[16,44,128]{2,0,1:T(8,128)S(1)}, f32[16,44,128]{2,0,1:T(8,128)}, u32[]{:S(2)}) copy-start(f32[16,44,128]{2,0,1:T(8,128)} %param.10) | copy-start | bytes 1081348
  2.2 12.9 %collective-permute-start.1 = (f32[15,48,128]{2,1,0:T(8,128)S(1)}, f32[15,48,128]{2,1,0:T(8,128)S(1)}, u32[]{:S(2)}, u32[]{:S(2)}) collective-permute-start(f32[15,48,128]{2,1,0:T(8,128)S(1)} %get-tuple-element.29), channel_id=1, source_target_pairs={{0,8},{16,24},{8,0},{24,16},{1,9},{17,25},{9,1},{25,17},{2,10},{18... | collective-permute-start | bytes 1105928 | tf_op jit(solution)/shard_map/ppermute | solution.py:597
  2.3 12.9 %collective-permute-start.2 = (f32[15,48,128]{2,1,0:T(8,128)S(1)}, f32[15,48,128]{2,1,0:T(8,128)S(1)}, u32[]{:S(2)}, u32[]{:S(2)}) collective-permute-start(f32[15,48,128]{2,1,0:T(8,128)S(1)} %get-tuple-element.30), channel_id=1, source_target_pairs={{8,16},{16,8},{9,17},{17,9},{10,18},{18,10},{11,19},{19,11},{12,20... | collective-permute-start | bytes 1105928 | tf_op jit(solution)/shard_map/ppermute | solution.py:597
  6.8 2.9 %collective-permute-start = (f32[3,512]{1,0:T(4,128)S(1)}, f32[3,512]{1,0:T(4,128)S(1)}, u32[]{:S(2)}, u32[]{:S(2)}) collective-permute-start(f32[3,512]{1,0:T(4,128)S(1)} %copy-done.4), channel_id=1, source_target_pairs={{0,1},{1,0},{2,3},{3,2},{4,5},{5,4},{6,7},{7,6},{8,9},{9,8},{10,11... | collective-permute-start | bytes 18440 | tf_op jit(solution)/shard_map/ppermute | solution.py:608
  16.7 9.4 %collective-permute-start.3 = (f32[392,128]{1,0:T(8,128)S(1)}, f32[392,128]{1,0:T(8,128)S(1)}, u32[]{:S(2)}, u32[]{:S(2)}) collective-permute-start(f32[392,128]{1,0:T(8,128)S(1)} %get-tuple-element.37), channel_id=1, source_target_pairs={{0,2},{4,6},{2,0},{6,4},{1,3},{5,7},{3,1},{7,5},{8,10},{12,14},{10... | collective-permute-start | bytes 602120 | tf_op jit(solution)/shard_map/ppermute | solution.py:597
  18.8 7.3 %collective-permute-start.4 = (f32[392,128]{1,0:T(8,128)S(1)}, f32[392,128]{1,0:T(8,128)S(1)}, u32[]{:S(2)}, u32[]{:S(2)}) collective-permute-start(f32[392,128]{1,0:T(8,128)S(1)} %get-tuple-element.38), channel_id=1, source_target_pairs={{2,4},{4,2},{3,5},{5,3},{10,12},{12,10},{11,13},{13,11},{18,20},{2... | collective-permute-start | bytes 602120 | tf_op jit(solution)/shard_map/ppermute | solution.py:597
  27.4 4.0 %collective-permute-start.5 = (f32[192,128]{1,0:T(8,128)S(1)}, f32[192,128]{1,0:T(8,128)S(1)}, u32[]{:S(2)}, u32[]{:S(2)}) collective-permute-start(f32[192,128]{1,0:T(8,128)S(1)} %get-tuple-element.47), channel_id=1, source_target_pairs={{0,1},{1,0},{2,3},{3,2},{4,5},{5,4},{6,7},{7,6},{8,9},{9,8},{10,11... | collective-permute-start | bytes 294920 | tf_op jit(solution)/shard_map/ppermute | solution.py:597

commit v4 on v3

v4 whole, which is shorter than its diff:
```python
import functools

import jax
import jax.numpy as jnp
from jax import lax
from jax.experimental import pallas as pl
from jax.experimental.pallas import tpu as pltpu
from jax.sharding import PartitionSpec as P

RADIUS = 3
F32 = jnp.float32
BF16 = jnp.bfloat16
SCALE = -3.0 / 96.0
HIGHEST = lax.Precision.HIGHEST
VM = pltpu.VMEM
SM = pltpu.SMEM

EX, EY, EZ = 16, 44, 128
NX, NY = EX + 1, EY + 1
XN, XE = NX + 2 * RADIUS, EX + 2 * RADIUS
ROWS = 48
QROWS = 56
XR = 24


def iota(shape, dim):
    return lax.broadcasted_iota(jnp.int32, shape, dim)


def one_hot(mask):
    return jnp.where(mask, 1.0, 0.0).astype(F32)


def halves(value):
    high = value.astype(BF16)
    return high, (value - high.astype(F32)).astype(BF16)


def corner_scalars(coarse_ref, dof_of, shared):
    width = coarse_ref.shape[2]
    own = lax.axis_index("gz")
    out = [[None] * 8 for _ in range(3)]
    for k in range(8):
        dof = dof_of(k)
        part = dof // width
        place = dof - part * width
        if shared:
            part = jnp.where(part == own, 0, 1)
        for c in range(3):
            out[c][k] = coarse_ref[part, c, place]
    return out


def corner_rows(corners, c):
    rz = iota((8, EZ), 1).astype(F32) * (1.0 / EZ)
    other = 1.0 - rz
    return [[corners[c][4 * kx + 2 * ky] * other + corners[c][4 * kx + 2 * ky + 1] * rz for ky in (0, 1)] for kx in (0, 1)]


def plane_interp(edges, i, rows):
    wx = i / EX
    first, second = [((1.0 - wx) * edges[0][ky] + wx * edges[1][ky])[0:1] for ky in (0, 1)]
    ry = iota((rows, EZ), 0).astype(F32) * (1.0 / EY)
    return (1.0 - ry) * first + ry * second


def block_rows(block):
    nodes = block + 1
    return 2 * (16 * nodes + 16 * ((nodes + 1) // 2))


def stiffness_rows(stiff, block, in_lanes):
    def target(h, t, r):
        s, c = r // 4, r % 4
        place = 4 * t + 2 * s + h if in_lanes else 4 * h + 2 * t + s
        return jnp.where(c < 3, 8 * c + place, -1)

    row = iota((32, 24), 0)
    left = one_hot(iota((32, 24), 1) == target(row // 16, row // 8 % 2, row % 8))
    full = jnp.dot(left, stiff, precision=HIGHEST, preferred_element_type=F32)
    nodes, width = block + 1, block_rows(block)
    split = 32 * nodes
    half = (width - split) // 2
    col = iota((24, width), 1)
    again = col >= split
    h = jnp.where(again, (col - split) // half, col // (16 * nodes))
    node = jnp.where(again, (col - split) % half // 8, col % (16 * nodes) // 16)
    wide = iota((32, width), 1) >= split
    rows = []
    for e in range(block):
        t = node - e
        right = one_hot((iota((24, width), 0) == target(h, t, col % 8)) & (t >= 0) & (t < 2))
        part = jnp.dot(full, right, precision=HIGHEST, preferred_element_type=F32)
        high = part.astype(BF16).astype(F32)
        rows.append(jnp.where(wide, part - high, high))
    return jnp.concatenate(rows, axis=0).astype(BF16)


def build_nodes(plane_of, planes, rows, refs, first=0):
    w_ref, b_ref, h_ref, _ = refs
    for p in planes:
        base = (first + p) * rows * 8
        zero = jnp.zeros((rows, EZ), F32)
        for c in range(3):
            value = plane_of(c, p)
            w_ref[pl.ds(base + c, rows, stride=8), :] = value
            w_ref[pl.ds(base + 4 + c, rows, stride=8), :] = pltpu.roll(value, EZ - 1, 1)
        w_ref[pl.ds(base + 3, rows, stride=8), :] = zero
        w_ref[pl.ds(base + 7, rows, stride=8), :] = zero

    def split(p, _):
        base = (first + p) * rows
        last = None
        for r in range(rows):
            value = w_ref[pl.ds(pl.multiple_of((base + r) * 8, 8), 8), :]
            high = value.astype(BF16).astype(F32)
            at = pl.ds(pl.multiple_of((base + r) * 16, 16), 16)
            b_ref[at, :] = jnp.concatenate([high, value - high], axis=0).astype(BF16)
            if last is not None:
                h_ref[pl.ds(pl.multiple_of((base + r - 1) * 16, 16), 16), :] = jnp.concatenate([last, high], axis=0).astype(BF16)
            last = high
        h_ref[at, :] = jnp.concatenate([last, last], axis=0).astype(BF16)
        return 0

    lax.fori_loop(0, len(planes), split, 0)


def energy_planes(lhs, block, refs, e_ref, first, count, rows, blocks, out_first):
    w_ref, b_ref, h_ref, s_ref = refs
    nodes = block + 1
    for i in range(0, len(blocks), 2):
        pair = [((first + p) * rows + r, p * rows + r) for p, r in blocks[i : i + 2]]
        right = []
        for at, _ in pair:
            parts = [b_ref[(at + far) * 16 : (at + far + nodes) * 16, :] for far in (0, rows)]
            for far in (0, rows):
                parts += [h_ref[(at + far + t) * 16 : (at + far + t + 1) * 16, :] for t in range(0, nodes, 2)]
            right.append(jnp.concatenate(parts, axis=0))
        product = jnp.dot(lhs, jnp.concatenate(right, axis=1), preferred_element_type=F32)
        for u, (at, out) in enumerate(pair):
            for e in range(block):
                part = product[32 * e : 32 * e + 32, u * EZ : (u + 1) * EZ]
                low = w_ref[(at + e) * 8 : (at + e + 2) * 8, :] * part[0:16]
                high = w_ref[(at + rows + e) * 8 : (at + rows + e + 2) * 8, :] * part[16:32]
                both = low + high
                s_ref[(out + e) * 8 : (out + e + 1) * 8, :] = both[0:8] + both[8:16]
    for p in range(count):
        total = None
        for s in (0, 1, 2, 4, 5, 6):
            term = s_ref[pl.ds(p * rows * 8 + s, rows, stride=8), :]
            total = term if total is None else total + term
        e_ref[out_first + p] = total


def node_buffers(count, energies):
    return [((count * 8, EZ), F32), ((count * 16, EZ), BF16), ((count * 16, EZ), BF16), ((energies * 8, EZ), F32)]


def odd_place(axis):
    return lax.axis_index(axis) % 2 == 1


def pack_kernel(local_ref, top_ref, dens_ref, dofs_ref, even_ref, odd_ref, tops_ref, l_ref, t_ref, d_ref, c_ref, sem):
    copies = [pltpu.make_async_copy(top_ref, t_ref, sem.at[0]), pltpu.make_async_copy(dens_ref, d_ref, sem.at[1]),
              pltpu.make_async_copy(dofs_ref, c_ref, sem.at[2])]
    for side, node in ((0, EX - RADIUS), (1, 0)):
        for c in range(3):
            copies.append(pltpu.make_async_copy(local_ref.at[c, node : node + 4], l_ref.at[side, c], sem.at[len(copies)]))
    for copy in copies:
        copy.start()
    even_ref[...] = jnp.zeros(even_ref.shape, F32)
    odd_ref[...] = jnp.zeros(odd_ref.shape, F32)
    tops_ref[...] = jnp.zeros(tops_ref.shape, F32)
    for copy in copies:
        copy.wait()
    for c in range(3):
        for i in range(NX):
            tops_ref[c, i : i + 1, 0:NY] = t_ref[c, i]
    odd = odd_place("gx")
    for out_ref, flip in ((even_ref, odd), (odd_ref, jnp.logical_not(odd))):
        side = flip.astype(jnp.int32)
        for c in range(3):
            for j in range(4):
                out_ref[c * 4 + j, 0:NY, :] = l_ref[side, c, j]
                out_ref[c * 4 + j, NY : NY + 1, :] = jnp.where(
                    flip, tops_ref[c, j : j + 1, :], tops_ref[c, EX - RADIUS + j : EX - RADIUS + j + 1, :])
        for j in range(3):
            out_ref[12 + j, 0:EY, :] = jnp.where(
                flip, d_ref[pl.ds(j, EY, stride=EX), :], d_ref[pl.ds(EX - RADIUS + j, EY, stride=EX), :])
        out_ref[12, EY : EY + 1, 0:8] = c_ref[...].astype(F32)


def sort_sides(axis, even_ref, odd_ref, low_ref, high_ref):
    odd = odd_place(axis)
    even, other = even_ref[...], odd_ref[...]
    low_ref[...] = jnp.where(odd, even, other)
    high_ref[...] = jnp.where(odd, other, even)


def prepare_kernel(stiff_ref, dens_ref, lhs_ref, lhs_edge_ref, lhs_z_ref, od_ref, rs_ref, rd_ref):
    stiff = stiff_ref[...]
    lhs_ref[...] = stiffness_rows(stiff, 3, False)
    lhs_edge_ref[...] = stiffness_rows(stiff, 4, False)
    lhs_z_ref[...] = stiffness_rows(stiff, 4, True)
    base_x, base_y, base_z = lax.axis_index("gx") * EX, lax.axis_index("gy") * EY, lax.axis_index("gz") * EZ
    inside = iota((ROWS, EZ), 0) < EY
    norm_y = edge_total(EY, base_y + iota((ROWS, EZ), 0), lax.axis_size("gy"))
    norm_z = edge_total(EZ, base_z + iota((ROWS, EZ), 1), lax.axis_size("gz"))
    inverse = 1.0 / jnp.where(inside, norm_y * norm_z, 1.0)
    place = base_x + iota((8, EZ), 0)
    inverse_x = [1.0 / edge_total(EX, place + t, lax.axis_size("gx")) for t in (0, 8)]
    for x in range(EX):
        d = dens_ref[pl.ds(x, EY, stride=EX), :]
        od_ref[x, 0:EY, :] = d
        od_ref[x, EY:ROWS, :] = jnp.ones((ROWS - EY, EZ), F32)
        both = inverse * inverse_x[x // 8][x % 8 : x % 8 + 1, :]
        rd_ref[x] = both
        rs_ref[x] = both / od_ref[x]


def own_kernel(shared, local_ref, lhs_ref, coarse_ref, dofs_ref, own_ref, e_ref, *refs):
    corners = corner_scalars(coarse_ref, lambda k: dofs_ref[k], shared)
    for c in range(3):
        edges = corner_rows(corners, c)
        for i in range(NX):
            own_ref[c * NX + i, 0:NY, :] = local_ref[c, i] + plane_interp(edges, i, NY)
            own_ref[c * NX + i, NY:ROWS, :] = jnp.zeros((ROWS - NY, EZ), F32)
    clear(refs[3])
    build_nodes(lambda c, p: own_ref[c * NX + p + 1], range(EX - 1), ROWS, refs)
    blocks = [(p, r) for p in range(EX - 2) for r in range(1, EY - 1, 3)]
    energy_planes(lhs_ref[...], 3, refs, e_ref, 0, EX - 2, ROWS, blocks, 0)


def clear(ref):
    ref[...] = jnp.zeros(ref.shape, ref.dtype)


def average(flag, low, high, own):
    return jnp.where(flag, 0.5 * low + 0.5 * high, own)


def has_lower(axis):
    return lax.axis_index(axis) > 0


def has_upper(axis):
    return lax.axis_index(axis) < lax.axis_size(axis) - 1


def message_dofs(message_ref):
    row = message_ref[12, EY : EY + 1, :]
    lane = iota((1, EZ), 1)
    return lambda k: jnp.sum(jnp.where(lane == k, row, 0.0)).astype(jnp.int32)


def top_interp(corners, c, rows):
    rx = iota((rows, EZ), 0).astype(F32) * (1.0 / EX)
    ry = iota((rows, EZ), 1).astype(F32) * (1.0 / EY)
    low = (1.0 - ry) * corners[c][1] + ry * corners[c][3]
    high = (1.0 - ry) * corners[c][5] + ry * corners[c][7]
    return (1.0 - rx) * low + rx * high


TOP_AT = 368
Y_MESSAGE = 392


def x_kernel(shared, own_ref, top_ref, dens_ref, even_ref, odd_ref, coarse_ref, dofs_ref,
             xl_ref, xh_ref, tx_ref, yeven_ref, yodd_ref, low_ref, high_ref, up_ref, down_ref, t_ref):
    sort_sides("gx", even_ref, odd_ref, low_ref, high_ref)
    corners = corner_scalars(coarse_ref, lambda k: dofs_ref[k], shared)
    corners_low = corner_scalars(coarse_ref, message_dofs(low_ref), shared)
    corners_high = corner_scalars(coarse_ref, message_dofs(high_ref), shared)
    lower, upper = has_lower("gx"), has_upper("gx")
    for c in range(3):
        edges_low, edges_high = corner_rows(corners_low, c), corner_rows(corners_high, c)
        for j in range(4):
            value = low_ref[c * 4 + j] + plane_interp(edges_low, EX - RADIUS + j, ROWS)
            if j == 3:
                mine = own_ref[c * NX]
                value = average(lower, value, mine, mine)
            xl_ref[c * 4 + j] = value
            value = high_ref[c * 4 + j] + plane_interp(edges_high, j, ROWS)
            if j == 0:
                mine = own_ref[c * NX + EX]
                value = average(upper, mine, value, mine)
            xh_ref[c * 4 + j] = value

    t_ref[...] = jnp.zeros(t_ref.shape, F32)
    for c in range(3):
        t_ref[0] = top_ref[c] + top_interp(corners, c, XR)
        for j in range(4):
            t_ref[1, j : j + 1, 0:NY] = low_ref[c * 4 + j, NY : NY + 1, 0:NY]
            t_ref[2, j : j + 1, 0:NY] = high_ref[c * 4 + j, NY : NY + 1, 0:NY]
        t_low = t_ref[1, 0:8, :] + pltpu.roll(top_interp(corners_low, c, 24), 24 - (EX - RADIUS), 0)[0:8]
        t_high = t_ref[2, 0:8, :] + top_interp(corners_high, c, 8)
        first = average(lower, t_low[3:4], t_ref[0, 0:1, :], t_ref[0, 0:1, :])
        last = average(upper, t_ref[0, EX : EX + 1, :], t_high[0:1], t_ref[0, EX : EX + 1, :])
        t_ref[3, 0:3, :] = t_low[0:3]
        t_ref[3, 3:4, :] = first
        t_ref[3, 4:19, :] = t_ref[0, 1:EX, :]
        t_ref[3, 19:20, :] = last
        t_ref[3, 20:23, :] = t_high[1:4]
        lane = iota((XR, EZ), 1)
        tx_ref[c] = jnp.where(lane < NY + 8, pltpu.roll(t_ref[3], 8, 1), 0.0)

    for out_ref, node, elem, lane_at in ((up_ref, EY - RADIUS, EY - RADIUS, EY - RADIUS + 8), (down_ref, 0, 0, 8)):
        for c in range(3):
            for p in range(XN):
                at = (c * XN + p) * 4
                out_ref[at : at + 4, :] = x_plane(own_ref, xl_ref, xh_ref, c, p)[node : node + 4]
        for x in range(XE):
            at = 3 * XN * 4 + x * 4
            out_ref[at : at + 3, :] = x_density(dens_ref, low_ref, high_ref, x)[elem : elem + 3]
            out_ref[at + 3 : at + 4, :] = jnp.zeros((1, EZ), F32)
        out_ref[364:TOP_AT, :] = jnp.zeros((TOP_AT - 364, EZ), F32)
        lane = iota((XR, EZ), 1)
        total = jnp.zeros((XR, EZ), F32)
        for c in range(3):
            moved = pltpu.roll(tx_ref[c], (4 * c - lane_at) % EZ, 1)
            total = jnp.where((lane >= 4 * c) & (lane < 4 * c + 4), moved, total)
        out_ref[TOP_AT:Y_MESSAGE, :] = total
    sort_sides("gy", up_ref, down_ref, yodd_ref, yeven_ref)


def side_kernel(own_ref, xl_ref, xh_ref, lhs_ref, e_ref, *refs):
    clear(refs[3])

    def plane(c, p):
        if p < 4:
            return xl_ref[c * 4 + p]
        if p == 4:
            return own_ref[c * NX + 1]
        if p == 5:
            return own_ref[c * NX + EX - 1]
        return xh_ref[c * 4 + p - 6]

    build_nodes(plane, range(10), ROWS, refs)
    blocks = [(p, r) for p in range(4) for r in range(1, EY - 1, 3)]
    for first, out_first in ((0, 0), (5, 4)):
        energy_planes(lhs_ref[...], 3, refs, e_ref, first, 4, ROWS, blocks, out_first)


Z_MESSAGE = 192
TILES = 3 * XN + XE


def x_plane(own_ref, xl_ref, xh_ref, c, p):
    if p < 4:
        return xl_ref[c * 4 + p]
    if p < 19:
        return own_ref[c * NX + p - 3]
    return xh_ref[c * 4 + p - 19]


def x_density(dens_ref, low_ref, high_ref, x, rows=EY):
    if x < 3:
        return low_ref[12 + x, 0:rows, :]
    if x < 19:
        return dens_ref[x - 3, 0:rows, :]
    return high_ref[12 + x - 19, 0:rows, :]


def end_planes(turned):
    return jnp.concatenate([turned[0:4], turned[EZ - 4 : EZ]], axis=0)


def turn_kernel(own_ref, xl_ref, xh_ref, dens_ref, lowx_ref, highx_ref, z_ref):
    head = jnp.zeros((8, EZ), F32)

    def padded(i):
        if i < 3 * XN:
            return [head, x_plane(own_ref, xl_ref, xh_ref, i // XN, i % XN), head]
        return [head, x_density(dens_ref, lowx_ref, highx_ref, i - 3 * XN, ROWS), head]

    lane = iota((8, EZ), 1)
    for i in range(0, TILES, 2):
        both = end_planes(jnp.concatenate(padded(i) + padded(min(i + 1, TILES - 1)), axis=0).T)
        z_ref[i] = jnp.where(lane < 64, both, 0.0)
        if i + 1 < TILES:
            z_ref[i + 1] = jnp.where(lane < 64, pltpu.roll(both, 64, 1), 0.0)


def y_kernel(tx_ref, zo_ref, eb_ref, even_ref, odd_ref,
             low_ref, high_ref, oa_ref, ob_ref, od_ref, *refs):
    del eb_ref
    z_ref, d_ref, up_ref, down_ref = refs[-4:]
    sort_sides("gy", even_ref, odd_ref, low_ref, high_ref)
    lower, upper = has_lower("gy"), has_upper("gy")
    clear(z_ref)
    clear(d_ref)
    lane = iota((8, EZ), 1)
    for first in range(0, TILES, 32):
        count = min(32, TILES - first)
        turned = []
        for ref in (low_ref, high_ref):
            block = ref[first * 4 : (first + count) * 4, :]
            if count < 32:
                block = jnp.concatenate([block, jnp.zeros(((32 - count) * 4, EZ), F32)], axis=0)
            turned.append(end_planes(block.T))
        for t in range(count):
            i = first + t
            low = pltpu.roll(turned[0], (5 - 4 * t) % EZ, 1)
            high = pltpu.roll(turned[1], (52 - 4 * t) % EZ, 1)
            mine = zo_ref[i]
            if i < 3 * XN:
                at = (i // XN) * XR + i % XN
                value = jnp.where((lane >= 5) & (lane < 8), low, mine)
                value = jnp.where((lane == 8) & lower, 0.5 * low + 0.5 * mine, value)
                value = jnp.where((lane == 52) & upper, 0.5 * mine + 0.5 * high, value)
                z_ref[at * 8 : at * 8 + 8, :] = jnp.where((lane > 52) & (lane < 56), high, value)
            else:
                at = i - 3 * XN
                value = jnp.where((lane >= 5) & (lane < 8), low, mine)
                d_ref[at * 8 : at * 8 + 8, :] = jnp.where((lane >= 52) & (lane < 55), high, value)

    lane = iota((XR, EZ), 1)
    tops = []
    for c in range(3):
        mine = tx_ref[c]
        low = pltpu.roll(low_ref[TOP_AT:Y_MESSAGE, :], (5 - 4 * c) % EZ, 1)
        high = pltpu.roll(high_ref[TOP_AT:Y_MESSAGE, :], (52 - 4 * c) % EZ, 1)
        value = jnp.where((lane >= 5) & (lane < 8), low, mine)
        value = jnp.where(lane == 8, average(lower, low, mine, mine), value)
        value = jnp.where(lane == 52, average(upper, mine, high, mine), value)
        tops.append(jnp.where((lane > 52) & (lane < 56), high, value))
    top = jnp.concatenate(tops, axis=0)

    def nodes(k):
        return z_ref[pl.ds(k, 3 * XR, stride=8), :]

    def dens(k):
        return d_ref[pl.ds(k, XR, stride=8), :]

    def pack(low, high):
        return low + pltpu.roll(high, 64, 1)

    oa_ref[...] = pack(nodes(0), top)
    ob_ref[...] = pack(nodes(1), nodes(7))
    od_ref[...] = pack(dens(0), dens(7))
    up_ref[0:72, :] = pack(nodes(5), nodes(6))
    up_ref[72:144, :] = pack(nodes(7), top)
    up_ref[144:168, :] = pack(dens(5), dens(6))
    up_ref[168:192, :] = dens(7)
    down_ref[0:72, :] = pack(nodes(0), nodes(1))
    down_ref[72:144, :] = pack(nodes(2), nodes(3))
    down_ref[144:168, :] = pack(dens(0), dens(1))
    down_ref[168:192, :] = dens(2)
    odd = odd_place("gz")
    refs[0][...] = jnp.where(odd, down_ref[...], up_ref[...])
    if len(refs) > 5:
        refs[1][...] = jnp.where(odd, up_ref[...], down_ref[...])


def edge_kernel(own_ref, xl_ref, xh_ref, lowy_ref, highy_ref, lhs_ref, el_ref, eh_ref, *refs):
    clear(refs[3])
    lower, upper = has_lower("gy"), has_upper("gy")
    row = iota((8, EZ), 0)

    def low(c, p):
        mine = pltpu.roll(x_plane(own_ref, xl_ref, xh_ref, c, p)[0:8], 3, 0)
        other = lowy_ref[(c * XN + p) * 4 : (c * XN + p) * 4 + 4, :]
        other = jnp.concatenate([other, other], axis=0)
        value = jnp.where(row == 3, average(lower, other, mine, mine), jnp.where(row < 3, other, mine))
        return jnp.where(row < 5, value, 0.0)

    def high(c, p):
        mine = pltpu.roll(x_plane(own_ref, xl_ref, xh_ref, c, p)[EY - 4 : EY + 4], 5, 0)
        other = highy_ref[(c * XN + p) * 4 : (c * XN + p) * 4 + 4, :]
        other = pltpu.roll(jnp.concatenate([other, other], axis=0), 1, 0)
        value = jnp.where(row == 1, average(upper, mine, other, mine), jnp.where(row < 1, mine, other))
        return jnp.where(row < 5, value, 0.0)

    for side, e_ref in ((low, el_ref), (high, eh_ref)):
        build_nodes(side, range(XN), 8, refs)
        energy_planes(lhs_ref[...], 4, refs, e_ref, 0, XE, 8, [(p, 0) for p in range(XE)], 0)


def triangle(value, axis):
    size = value.shape[axis]
    value = value + pltpu.roll(value, size - 1, axis)
    value = value + pltpu.roll(value, size - 2, axis)
    value = value + pltpu.roll(value, 1, axis)
    return value + pltpu.roll(value, 2, axis)


def weights(distance):
    return jnp.maximum(4 - jnp.abs(distance), 0).astype(F32)


def split_dot(value, right):
    rows = value.shape[0]
    product = jnp.dot(jnp.concatenate(halves(value), axis=0), right, preferred_element_type=F32)
    return product[0:rows] + product[rows:]


def edge_total(count, position, parts):
    total = None
    for offset in range(-RADIUS, RADIUS + 1):
        place = position + offset
        term = float(RADIUS + 1 - abs(offset)) * one_hot((place >= 0) & (place < count * parts))
        total = term if total is None else total + term
    return total


def field_kernel(ea_ref, eb_ref, el_ref, eh_ref, dens_ref, lowx_ref, highx_ref, lowy_ref, highy_ref,
                 g_ref, along_ref, right_ref, f_ref):
    rows = iota((QROWS, EZ), 0)
    lanes = iota((QROWS, EZ), 1)
    ok = (rows >= 5) & (rows < 55) & (lanes > 0) & (lanes < EZ - 1)
    row = iota((8, EZ), 0)
    for x in range(XE):
        if x < 4:
            middle = eb_ref[x]
        elif x < 18:
            middle = ea_ref[x - 4]
        else:
            middle = eb_ref[x - 14]
        low = pltpu.roll(el_ref[x], 5, 0)
        high = pltpu.roll(eh_ref[x], 3, 0)
        start = jnp.where(row < 1, low, middle[0:8])
        end = jnp.where(row < 3, middle[40:48], high)
        energy = jnp.concatenate([low, start, middle[8:40], end], axis=0)
        at = 3 * XN * 4 + x * 4
        pad = jnp.zeros((5, EZ), F32)
        d = jnp.concatenate(
            [pad, lowy_ref[at : at + 3, :], x_density(dens_ref, lowx_ref, highx_ref, x), highy_ref[at : at + 3, :], pad[0:1]], axis=0)
        f_ref[0, x] = jnp.where(ok, (SCALE * d) * d * d * energy, 0.0)
        f_ref[1, x] = jnp.where(ok, d, 0.0)

    for f in range(2):
        for t in range(QROWS // 8):
            at = slice(t * 8, t * 8 + 8)
            line = [f_ref[f, x, at, :] for x in range(XE)]
            for step in (1, 2, 1, 2):
                line = [line[i] + line[i + step] for i in range(len(line) - step)]
            for x in range(EX):
                f_ref[f, x, at, :] = line[x]
    k, col = iota((EZ, EZ), 0), iota((EZ, EZ), 1)
    along_ref[...] = jnp.where(k // 64 == col // 64, weights(k - col), 0.0).astype(BF16)
    j = (k % 64) // EX
    place = jnp.where(k < 64, j - 3, EZ - 1 + j)
    z = jnp.where(col % 8 < 4, EZ - 4 + col % 8, col % 8 - 4)
    right_ref[...] = jnp.where(k % EX == col // 8, weights(place - z), 0.0).astype(BF16)
    right = weights(k - col).astype(BF16)
    for f in range(2):
        for x in range(EX):
            g_ref[f, x] = split_dot(triangle(f_ref[f, x], 0)[8:QROWS], right)


def last_kernel(g_ref, along_ref, right_ref, rs_ref, rd_ref, oa_ref, ob_ref, od_ref, lhs_ref, *refs):
    messages, refs = refs[:-12], refs[-12:]
    outs, (ez_ref, c_ref, zl_ref, zh_ref, o_ref, sem), refs = refs[:2], refs[2:8], refs[8:]
    if len(messages) > 1:
        sort_sides("gz", *messages, zl_ref, zh_ref)
    else:
        odd = odd_place("gz")
        zl_ref[...] = jnp.where(odd, messages[0][...], 0.0)
        zh_ref[...] = jnp.where(odd, 0.0, messages[0][...])
    lower, upper = has_lower("gz"), has_upper("gz")

    def swap(value):
        return pltpu.roll(value, 64, 1)

    is_low = iota((3 * XR, EZ), 1) < 64
    oa, ob = oa_ref[...], ob_ref[...]
    zl0, zl1 = zl_ref[0:72, :], zl_ref[72:144, :]
    zh0, zh1 = zh_ref[0:72, :], zh_ref[72:144, :]
    nodes = (
        jnp.where(is_low, zl0, ob),
        jnp.where(is_low, swap(zl0), average(upper, oa, swap(zh0), oa)),
        jnp.where(is_low, zl1, zh0),
        jnp.where(is_low, average(lower, swap(zl1), oa, oa), swap(zh1)),
        jnp.where(is_low, ob, zh1),
    )
    build_nodes(lambda c, k: nodes[k][c * XR : (c + 1) * XR], range(5), XR, refs)
    for ref, step in zip(refs[:3], (8, 16, 16)):
        ref[5 * XR * step : (5 * XR + 8) * step, :] = jnp.zeros((8 * step, EZ), ref.dtype)

    lane = iota((XR, EZ), 1)
    low_side = lane < 64
    od = od_ref[...]
    dl0, dl1 = zl_ref[144:168, :], zl_ref[168:192, :]
    dh0, dh1 = zh_ref[144:168, :], zh_ref[168:192, :]
    dens = (
        jnp.where(low_side, dl0, od),
        jnp.where(low_side, swap(dl0), swap(dh0)),
        jnp.where(low_side, dl1, dh0),
        jnp.where(low_side, od, swap(dh1)),
    )
    inside = (lane % 64 >= 5) & (lane % 64 < 55) & (iota((XR, EZ), 0) < XE)
    lanes = iota((8, EZ), 1)
    at_end = (lanes < 4) | (lanes >= EZ - 4)
    copies = []
    for f in (1, 0):
        if f == 0:
            energy_planes(lhs_ref[...], 4, refs, ez_ref, 0, 4, XR, [(j, x) for j in range(4) for x in range(0, XR, 4)], 0)
        for j in range(4):
            d = dens[j]
            value = d if f == 1 else (SCALE * d) * d * d * ez_ref[j]
            c_ref[f, j * EX : (j + 1) * EX, :] = triangle_forward(jnp.where(inside, value, 0.0))[0:EX]
        turned = split_dot(c_ref[f], along_ref[...])
        turned = jnp.concatenate([turned, jnp.zeros((EZ - 4 * EX, EZ), F32)], axis=0).T
        ends = split_dot(turned[8:56] + pltpu.roll(turned[72:120], 64, 1), right_ref[...])
        inverse_ref = rs_ref if f == 0 else rd_ref
        for y in range(0, EY, 8):
            count = min(8, EY - y)
            for x in range(EX):
                end = jnp.where(at_end, pltpu.roll(ends[y : y + 8], (EZ - 4 - 8 * x) % EZ, 1), 0.0)
                value = (g_ref[f, x, y : y + 8, :] + end) * inverse_ref[x, y : y + 8, :]
                o_ref[f, pl.ds(y * EX + x, count, stride=EX), :] = value[0:count]
            block = pl.ds(y * EX, count * EX)
            copies.append(pltpu.make_async_copy(o_ref.at[f, block], outs[f].at[block], sem.at[len(copies)]))
            copies[-1].start()
    for copy in copies:
        copy.wait()


def triangle_forward(value):
    size = value.shape[0]
    for step in (1, 2, 1, 2):
        value = value + pltpu.roll(value, size - step, 0)
    return value


def call(kernel, outs, ins, scratch=(), limit=16, micros=1.0, space=VM):
    return pl.pallas_call(
        kernel,
        out_shape=[jax.ShapeDtypeStruct(shape, dtype) for shape, dtype in outs],
        in_specs=[pl.BlockSpec(memory_space=space) for space in ins],
        out_specs=[pl.BlockSpec(memory_space=space)] * len(outs),
        scratch_shapes=[pltpu.VMEM(item[0], item[1]) if isinstance(item, tuple) else item for item in scratch],
        compiler_params=pltpu.CompilerParams(vmem_limit_bytes=limit * 2**20),
        cost_estimate=pl.CostEstimate(flops=0, bytes_accessed=int(micros * 3.6e6), transcendentals=0),
    )


def exchange(axis, *values):
    count = lax.axis_size(axis)
    results = []
    for first, value in enumerate(values):
        pairs = [(i, i + 1) for i in range(first, count - 1, 2)]
        results.append(lax.ppermute(value, axis, pairs + [(j, i) for i, j in pairs]))
    return results


def local(local_solution, top_nodes, coarse_solution, corner_dofs, density, element_stiffness):
    dens = jnp.transpose(density, (1, 0, 2)).reshape(EY * EX, EZ)
    dofs = corner_dofs.reshape(8)
    shared = lax.axis_size("gz") == 2
    if shared:
        other = lax.ppermute(coarse_solution, "gz", [(0, 1), (1, 0)])
        coarse = jnp.stack([coarse_solution, other])
    else:
        coarse = lax.all_gather(coarse_solution, "gz")

    message = ((15, ROWS, EZ), F32)
    even, odd, tops = call(
        pack_kernel,
        [message, message, ((3, XR, EZ), F32)],
        [pltpu.HBM] * 4,
        [((2, 3, 4, NY, EZ), F32), ((3, NX, 1, NY), F32), ((EY * EX, EZ), F32), ((1, 8), jnp.int32), pltpu.SemaphoreType.DMA((9,))],
    )(*[
        pltpu.with_memory_space_constraint(value, pltpu.HBM)
        for value in (local_solution, jnp.transpose(top_nodes, (0, 1, 3, 2)), dens, dofs.reshape(1, 8))
    ])
    even_x, odd_x = exchange("gx", even, odd)

    own_planes = ((EX, ROWS, EZ), F32)
    rows3, rows4 = ((96, block_rows(3)), BF16), ((128, block_rows(4)), BF16)
    lhs, lhs_edge, lhs_z, dens, inverse_sens, inverse_smooth = call(
        prepare_kernel, [rows3, rows4, rows4, own_planes, own_planes, own_planes], [VM, VM], micros=1.0
    )(element_stiffness, dens)

    own, ea = call(
        functools.partial(own_kernel, shared),
        [((3 * NX, ROWS, EZ), F32), ((EX - 2, ROWS, EZ), F32)],
        [VM, VM, SM, SM],
        node_buffers((EX - 1) * ROWS, (EX - 2) * ROWS),
        micros=6.0,
    )(local_solution, lhs, coarse, dofs)

    face = ((12, ROWS, EZ), F32)
    y_message = ((Y_MESSAGE, EZ), F32)
    xl, xh, tx, even, odd, low_x, high_x = call(
        functools.partial(x_kernel, shared),
        [face, face, ((3, XR, EZ), F32), y_message, y_message, message, message],
        [VM, VM, VM, VM, VM, SM, SM],
        [y_message, y_message, ((4, XR, EZ), F32)],
        micros=2.0,
    )(own, tops, dens, even_x, odd_x, coarse, dofs)
    even_y, odd_y = exchange("gy", even, odd)

    (eb,) = call(
        side_kernel, [((8, ROWS, EZ), F32)], [VM] * 4, node_buffers(10 * ROWS, 4 * ROWS), micros=2.6
    )(own, xl, xh, lhs)

    (zo,) = call(turn_kernel, [((TILES, 8, EZ), F32)], [VM] * 6, micros=1.5)(own, xl, xh, dens, low_x, high_x)

    z_message = ((Z_MESSAGE, EZ), F32)
    low_y, high_y, oa, ob, od, *messages = call(
        y_kernel,
        [y_message, y_message, ((72, EZ), F32), ((72, EZ), F32), ((XR, EZ), F32)] + [z_message] * (1 if shared else 2),
        [VM] * 5,
        [((8 * 3 * XR, EZ), F32), ((8 * XR, EZ), F32), z_message, z_message],
        micros=1.0,
    )(tx, zo, eb, even_y, odd_y)
    received_z = exchange("gz", *messages)

    el, eh = call(
        edge_kernel,
        [((XE, 8, EZ), F32)] * 2,
        [VM] * 6,
        node_buffers(XN * 8, XE * 8),
        micros=2.3,
    )(own, xl, xh, low_y, high_y, lhs_edge)

    square = ((EZ, EZ), BF16)
    filtered, along_y, ends = call(
        field_kernel, [((2, EX, ROWS, EZ), F32), square, square], [VM] * 9, [((2, XE, QROWS, EZ), F32)], micros=1.5
    )(ea, eb, el, eh, dens, low_x, high_x, low_y, high_y)

    sens, smooth = call(
        last_kernel,
        [((EY * EX, EZ), F32)] * 2,
        [VM] * (9 + len(received_z)),
        [((4, XR, EZ), F32), ((2, 4 * EX, EZ), F32), z_message, z_message, ((2, EY * EX, EZ), F32),
         pltpu.SemaphoreType.DMA((12,))] + node_buffers(5 * XR + 8, 4 * XR),
        space=pltpu.HBM,
        micros=2.5,
    )(filtered, along_y, ends, inverse_sens, inverse_smooth, oa, ob, od, lhs_z, *received_z)

    def grid(value):
        return jnp.transpose(value.reshape(EY, EX, EZ), (1, 0, 2))

    return grid(sens), grid(smooth)


def solution(mesh):
    in_specs = (
        P(None, "gx", "gy", "gz"),
        P(None, "gx", "gy", "gz"),
        P(None, "gz"),
        P("gx", "gy", "gz", None),
        P("gx", "gy", "gz"),
        P(),
    )
    out_specs = (P("gx", "gy", "gz"), P("gx", "gy", "gz"))
    return jax.shard_map(local, mesh=mesh, in_specs=in_specs, out_specs=out_specs, check_vma=False)
```

time: 34.7 us -> 32.6 us (0.939)
  Pallas kernels: 19.9 us -> 17.8 us
    ppermute x5, waiting for transfers between devices: 0.02 us -> 1.11 us  [exchange(): lax.ppermute(value, axis, pairs + [(j, i) for i, j in pairs])]
    ppermute x1, waiting for transfers between devices: 1.56 us -> 0.69 us  [local(): other = lax.ppermute(coarse_solution, 'gz', [(0, 1), (1, 0)])]
    pallas_call x1, Pallas kernels: 1.6 us -> 0.91 us  [local(): call(turn_kernel, [((TILES, 8, EZ), F32)], [VM] * 6, micros=1.5)]
    pallas_call x1, Pallas kernels: 5.45 us -> 4.77 us  [local(): call(functools.partial(own_kernel, shared), [((3 * NX, ROWS, EZ), F32), (...]
    pallas_call x5 -> x6, Pallas kernels: 9.79 us -> 9.14 us  [the longest x1 2.47 us: local(): call(last_kernel, [((EY * EX, EZ), F32)] * 2, [VM] * (9 + len(received_z)...]
  transfers between devices with their start and end apart: 6 -> 6, of which waited for: 1 -> 3; matrix products, arithmetic and copies ran while one was open for 0% -> 0% of each run, Pallas kernels for 36% -> 36%
where the time goes in v4:
time: 32.6 us; the launch traced here: 32.4 us
  Pallas kernels  17.8 us (55%)
  starting transfers between devices  12 us (37%)
  waiting for transfers between devices  1.8 us (6%)
  between operations  0.81 us (2%)
    ppermute x5, starting transfers between devices, exchange(): lax.ppermute(value, axis, pairs + [(j, i) for i, j in pairs])  10.7 us
    pallas_call x1, Pallas kernels, local(): call(functools.partial(own_kernel, shared), [((3 * NX, ROWS, EZ), F32), (...  4.77 us
    pallas_call x1, Pallas kernels, local(): call(last_kernel, [((EY * EX, EZ), F32)] * 2, [VM] * (9 + len(received_z)...  2.47 us
    pallas_call x1, Pallas kernels, local(): call(side_kernel, [((8, ROWS, EZ), F32)], [VM] * 4, node_buffers(10 * ROW...  2.28 us
    pallas_call x1, Pallas kernels, local(): call(edge_kernel, [((XE, 8, EZ), F32)] * 2, [VM] * 6, node_buffers(XN * 8...  1.84 us
    pallas_call x1, Pallas kernels, local(): call(pack_kernel, [message, message, ((3, XR, EZ), F32)], [pltpu.HBM] * 4...  1.5 us
    pallas_call x1, Pallas kernels, local(): call(functools.partial(x_kernel, shared), [face, face, ((3, XR, EZ), F32)...  1.46 us
    ppermute x1, starting transfers between devices, local(): other = lax.ppermute(coarse_solution, 'gz', [(0, 1), (1, 0)])  1.3 us
  transfers between devices with their start and end apart: 6, of which 3 were waited for; matrix products, arithmetic and copies ran while one was open for 0% of the time, Pallas kernels for 36%

profile of v4, /device:TPU:9, one launch (start us, length us, event | category | flops | bytes accessed | tf_op | source)
XLA Modules:
  0.0 32.4 jit_solution(7258532911054147759)
XLA Ops:
  0.6 0.0 copy-start
  0.6 0.0 copy-start.3
  0.7 0.0 copy-start.1
  0.7 0.0 copy-start.4
  0.7 0.0 copy-start.2
  0.7 1.5 %shard_map.79 = (f32[15,48,128]{2,1,0:T(8,128)S(1)}, f32[15,48,128]{2,1,0:T(8,128)S(1)}, f32[3,24,128]{2,1,0:T(8,128)S(1)}) custom-call(f32[3,17,45,128]{3,2,1,0:T(8,128)} %local_ref.3, f32[3,17,1,45]{3,2,1,0:T(1,128)} %bitcast.19, f32[704,128]{1,0:T(8,128)} %bitcast.14, s32[1,8]{1,0:T(1,128)} %bitcast.16), custom_call_target="tpu_custom_call" | custom-call | bytes 3600000 | tf_op jit(solution)/shard_map/pallas_call | solution.py:658
  2.2 0.1 collective-permute-start.1
  2.3 4.5 %collective-permute-start.2 = (f32[15,48,128]{2,1,0:T(8,128)S(1)}, f32[15,48,128]{2,1,0:T(8,128)S(1)}, u32[]{:S(2)}, u32[]{:S(2)}) collective-permute-start(f32[15,48,128]{2,1,0:T(8,128)S(1)} %get-tuple-element.39), channel_id=1, source_target_pairs={{8,16},{16,8},{9,17},{17,9},{10,18},{18,10},{11,19},{19,11},{12,20... | collective-permute-start | bytes 1105928 | tf_op jit(solution)/shard_map/ppermute | solution.py:643
  6.8 0.0 copy-done.4
  6.8 1.3 %collective-permute-start = (f32[3,512]{1,0:T(4,128)S(1)}, f32[3,512]{1,0:T(4,128)S(1)}, u32[]{:S(2)}, u32[]{:S(2)}) collective-permute-start(f32[3,512]{1,0:T(4,128)S(1)} %copy-done.4), channel_id=1, source_target_pairs={{0,1},{1,0},{2,3},{3,2},{4,5},{5,4},{6,7},{7,6},{8,9},{9,8},{10,11... | collective-permute-start | bytes 18440 | tf_op jit(solution)/shard_map/ppermute | solution.py:652
  8.1 0.0 copy-done.1
  8.1 0.0 copy-done.2
  8.1 0.8 %shard_map.77 = (bf16[96,192]{1,0:T(8,128)(2,1)S(1)}, bf16[128,256]{1,0:T(8,128)(2,1)S(1)}, bf16[128,256]{1,0:T(8,128)(2,1)S(1)}, f32[16,48,128]{2,1,0:T(8,128)S...) custom-call(f32[24,24]{1,0:T(8,128)S(1)} %copy-done.2, f32[704,128]{1,0:T(8,128)S(1)} %bitcast.15), custom_call_target="tpu_custom_call" | custom-call | bytes 3600000 | tf_op jit(solution)/shard_map/pallas_call | solution.py:671
  8.9 0.7 %collective-permute-done = f32[3,512]{1,0:T(4,128)S(1)} collective-permute-done((f32[3,512]{1,0:T(4,128)S(1)}, f32[3,512]{1,0:T(4,128)S(1)}, u32[]{:S(2)}, u32[]{:S(2)}) %collective-permute-start) | collective-permute-done | bytes 6176 | tf_op jit(solution)/shard_map/ppermute | solution.py:652
  9.6 0.0 copy-done
  9.6 0.0 copy-done.3
  9.7 4.8 %shard_map.78 = (f32[51,48,128]{2,1,0:T(8,128)S(1)}, f32[14,48,128]{2,1,0:T(8,128)S(1)}) custom-call(f32[3,17,45,128]{3,2,1,0:T(8,128)S(1)} %copy-done, bf16[96,192]{1,0:T(8,128)(2,1)S(1)} %get-tuple-element.33.lhs_ref, f32[2,3,512]{2,1,0:T(4,128)S(1)} %pad_maximum_fusion.coarse_ref, s32[8]{0:T(128)S(1)} %bitcast.17), custom_call_target="tpu_custom_call" | custom-call | bytes 21600000 | tf_op jit(solution)/shard_map/pallas_call | solution.py:675
  14.4 0.0 collective-permute-done.1.even_ref
  14.4 0.3 collective-permute-done.2.odd_ref
  14.7 1.5 %shard_map.80 = (f32[12,48,128]{2,1,0:T(8,128)S(1)}, f32[12,48,128]{2,1,0:T(8,128)S(1)}, f32[3,24,128]{2,1,0:T(8,128)S(1)}, f32[392,128]{1,0:T(8,128)S(1)}, f32[...) custom-call(f32[51,48,128]{2,1,0:T(8,128)S(1)} %get-tuple-element.35.own_ref, ...), custom_call_target="tpu_custom_call" | custom-call | bytes 7200000 | tf_op jit(solution)/shard_map/pallas_call | solution.py:685
  16.2 1.9 %collective-permute-start.3 = (f32[392,128]{1,0:T(8,128)S(1)}, f32[392,128]{1,0:T(8,128)S(1)}, u32[]{:S(2)}, u32[]{:S(2)}) collective-permute-start(f32[392,128]{1,0:T(8,128)S(1)} %get-tuple-element.45), channel_id=1, source_target_pairs={{0,2},{4,6},{2,0},{6,4},{1,3},{5,7},{3,1},{7,5},{8,10},{12,14},{10... | collective-permute-start | bytes 602120 | tf_op jit(solution)/shard_map/ppermute | solution.py:643
  18.1 3.0 %collective-permute-start.4 = (f32[392,128]{1,0:T(8,128)S(1)}, f32[392,128]{1,0:T(8,128)S(1)}, u32[]{:S(2)}, u32[]{:S(2)}) collective-permute-start(f32[392,128]{1,0:T(8,128)S(1)} %get-tuple-element.46), channel_id=1, source_target_pairs={{2,4},{4,2},{3,5},{5,3},{10,12},{12,10},{11,13},{13,11},{18,20},{2... | collective-permute-start | bytes 602120 | tf_op jit(solution)/shard_map/ppermute | solution.py:643
  21.1 2.3 %shard_map.81.eb_ref = f32[8,48,128]{2,1,0:T(8,128)S(1)} custom-call(f32[51,48,128]{2,1,0:T(8,128)S(1)} %get-tuple-element.35.own_ref, f32[12,48,128]{2,1,0:T(8,128)S(1)} %get-tuple-element.40.xl_ref, f32[12,48,128]{2,1,0:T(8,128)S(1)} %get-tuple-element.41.xh_ref, bf16[96,192]{1,0:T(8,128)(2,1)S(1)} %get-tuple-element.33.lhs_ref), custom_call_target="tpu_custom_call" | custom-call | bytes 9360000 | tf_op jit(solution)/shard_map/pallas_call | solution.py:694
  23.3 0.9 %shard_map.82.zo_ref = f32[91,8,128]{2,1,0:T(8,128)S(1)} custom-call(f32[51,48,128]{2,1,0:T(8,128)S(1)} %get-tuple-element.35.own_ref, f32[12,48,128]{2,1,0:T(8,128)S(1)} %get-tuple-element.40.xl_ref, f32[12,48,128]{2,1,0:T(8,128)S(1)} %get-tuple-element.41.xh_ref, f32[16,48,128]{2,1,0:T(8,128)S(1)} %get-tuple-element.37.dens_ref, ...), custom_call_target="tpu_custom_call" | custom-call | bytes 5400000 | tf_op jit(solution)/shard_map/pallas_call | solution.py:698
  24.3 0.0 collective-permute-done.3.even_ref
  24.3 0.8 %collective-permute-done.4.odd_ref = f32[392,128]{1,0:T(8,128)S(1)} collective-permute-done((f32[392,128]{1,0:T(8,128)S(1)}, f32[392,128]{1,0:T(8,128)S(1)}, u32[]{:S(2)}, u32[]{:S(2)}) %collective-permute-start.4) | collective-permute-done | bytes 200736 | tf_op jit(solution)/shard_map/ppermute | solution.py:643
  25.1 0.5 %shard_map.83 = (f32[392,128]{1,0:T(8,128)S(1)}, f32[392,128]{1,0:T(8,128)S(1)}, f32[72,128]{1,0:T(8,128)S(1)}, f32[72,128]{1,0:T(8,128)S(1)}, f32[24,128]{1,0:T(8,128)S(1)}, /*index=5*/f32[192,128]{1,0:T(8,128)S(1)}) custom-call(f32[3,24,128]{2,1,0:T(8,128)S(1)} %get-tuple-element.42.tx_ref, f32[91,8,128]{2,1,0:T(8,128)S(1)} %shard_map.82.zo_ref, ...), custom_call_target="tpu_custom_call" | custom-call | bytes 3600000 | tf_op jit(solution)/shard_map/pallas_call | solution.py:701
  25.6 1.3 %collective-permute-start.5 = (f32[192,128]{1,0:T(8,128)S(1)}, f32[192,128]{1,0:T(8,128)S(1)}, u32[]{:S(2)}, u32[]{:S(2)}) collective-permute-start(f32[192,128]{1,0:T(8,128)S(1)} %get-tuple-element.61), channel_id=1, source_target_pairs={{0,1},{1,0},{2,3},{3,2},{4,5},{5,4},{6,7},{7,6},{8,9},{9,8},{10,11... | collective-permute-start | bytes 294920 | tf_op jit(solution)/shard_map/ppermute | solution.py:643
  26.9 1.8 %shard_map.84 = (f32[22,8,128]{2,1,0:T(8,128)S(1)}, f32[22,8,128]{2,1,0:T(8,128)S(1)}) custom-call(f32[51,48,128]{2,1,0:T(8,128)S(1)} %get-tuple-element.35.own_ref, f32[12,48,128]{2,1,0:T(8,128)S(1)} %get-tuple-element.40.xl_ref, f32[12,48,128]{2,1,0:T(8,128)S(1)} %get-tuple-element.41.xh_ref, f32[392,128]{1,0:T(8,128)S(1)} %get-tuple-element.47.lowy_ref, ...), custom_call_target="tpu_custom_call" | custom-call | bytes 8279999 | tf_op jit(solution)/shard_map/pallas_call | solution.py:710
  28.7 1.2 %shard_map.85 = (f32[2,16,48,128]{3,2,1,0:T(8,128)S(1)}, bf16[128,128]{1,0:T(8,128)(2,1)S(1)}, bf16[128,128]{1,0:T(8,128)(2,1)S(1)}) custom-call(f32[14,48,128]{2,1,0:T(8,128)S(1)} %get-tuple-element.34.ea_ref, f32[8,48,128]{2,1,0:T(8,128)S(1)} %shard_map.81.eb_ref, f32[22,8,128]{2,1,0:T(8,128)S(1)} %get-tuple-element.50.el_ref, ...), custom_call_target="tpu_custom_call" | custom-call | bytes 5400000 | tf_op jit(solution)/shard_map/pallas_call | solution.py:719
  29.9 0.0 collective-permute-done.5.refs_0_
  29.9 2.5 %shard_map.86 = (f32[704,128]{1,0:T(8,128)}, f32[704,128]{1,0:T(8,128)}) custom-call(f32[2,16,48,128]{3,2,1,0:T(8,128)S(1)} %get-tuple-element.52.g_ref, bf16[128,128]{1,0:T(8,128)(2,1)S(1)} %get-tuple-element.53.along_ref, bf16[128,128]{1,0:T(8,128)(2,1)S(1)} %get-tuple-element.54.right_ref, f32[16,48,128]{2,1,0:T(8,128)S(1)} %get-tuple-element.55.rs_ref, ...), custom_call_target="tpu_custom_call" | custom-call | bytes 9000000 | tf_op jit(solution)/shard_map/pallas_call | solution.py:723
  (1 shorter events, 0.0 us)
Async XLA Ops:
  0.6 9.0 %copy-start = (f32[3,17,45,128]{3,2,1,0:T(8,128)S(1)}, f32[3,17,45,128]{3,2,1,0:T(8,128)}, u32[]{:S(2)}) copy-start(f32[3,17,45,128]{3,2,1,0:T(8,128)} %local_ref.3) | copy-start | bytes 3525124
  0.6 9.0 %copy-start.3 = (s32[1,1,1,8]{3,2,1,0:T(1,128)S(1)}, s32[1,1,1,8]{3,2,1,0:T(1,128)}, u32[]{:S(2)}) copy-start(s32[1,1,1,8]{3,2,1,0:T(1,128)} %param.9) | copy-start | bytes 100
  0.7 7.4 %copy-start.1 = (f32[16,44,128]{2,0,1:T(8,128)S(1)}, f32[16,44,128]{2,0,1:T(8,128)}, u32[]{:S(2)}) copy-start(f32[16,44,128]{2,0,1:T(8,128)} %param.10) | copy-start | bytes 1081348
  0.7 6.1 %copy-start.4 = (f32[3,512]{1,0:T(4,128)S(1)}, f32[3,512]{1,0:T(4,128)}, u32[]{:S(2)}) copy-start(f32[3,512]{1,0:T(4,128)} %param.8) | copy-start | bytes 18436
  0.7 7.4 %copy-start.2 = (f32[24,24]{1,0:T(8,128)S(1)}, f32[24,24]{1,0:T(8,128)}, u32[]{:S(2)}) copy-start(f32[24,24]{1,0:T(8,128)} %stiff_ref.1) | copy-start | bytes 6916
  2.2 12.2 %collective-permute-start.1 = (f32[15,48,128]{2,1,0:T(8,128)S(1)}, f32[15,48,128]{2,1,0:T(8,128)S(1)}, u32[]{:S(2)}, u32[]{:S(2)}) collective-permute-start(f32[15,48,128]{2,1,0:T(8,128)S(1)} %get-tuple-element.38), channel_id=1, source_target_pairs={{0,8},{16,24},{8,0},{24,16},{1,9},{17,25},{9,1},{25,17},{2,10},{18... | collective-permute-start | bytes 1105928 | tf_op jit(solution)/shard_map/ppermute | solution.py:643
  2.3 12.5 %collective-permute-start.2 = (f32[15,48,128]{2,1,0:T(8,128)S(1)}, f32[15,48,128]{2,1,0:T(8,128)S(1)}, u32[]{:S(2)}, u32[]{:S(2)}) collective-permute-start(f32[15,48,128]{2,1,0:T(8,128)S(1)} %get-tuple-element.39), channel_id=1, source_target_pairs={{8,16},{16,8},{9,17},{17,9},{10,18},{18,10},{11,19},{19,11},{12,20... | collective-permute-start | bytes 1105928 | tf_op jit(solution)/shard_map/ppermute | solution.py:643
  6.8 2.9 %collective-permute-start = (f32[3,512]{1,0:T(4,128)S(1)}, f32[3,512]{1,0:T(4,128)S(1)}, u32[]{:S(2)}, u32[]{:S(2)}) collective-permute-start(f32[3,512]{1,0:T(4,128)S(1)} %copy-done.4), channel_id=1, source_target_pairs={{0,1},{1,0},{2,3},{3,2},{4,5},{5,4},{6,7},{7,6},{8,9},{9,8},{10,11... | collective-permute-start | bytes 18440 | tf_op jit(solution)/shard_map/ppermute | solution.py:652
  16.2 8.1 %collective-permute-start.3 = (f32[392,128]{1,0:T(8,128)S(1)}, f32[392,128]{1,0:T(8,128)S(1)}, u32[]{:S(2)}, u32[]{:S(2)}) collective-permute-start(f32[392,128]{1,0:T(8,128)S(1)} %get-tuple-element.45), channel_id=1, source_target_pairs={{0,2},{4,6},{2,0},{6,4},{1,3},{5,7},{3,1},{7,5},{8,10},{12,14},{10... | collective-permute-start | bytes 602120 | tf_op jit(solution)/shard_map/ppermute | solution.py:643
  18.1 7.0 %collective-permute-start.4 = (f32[392,128]{1,0:T(8,128)S(1)}, f32[392,128]{1,0:T(8,128)S(1)}, u32[]{:S(2)}, u32[]{:S(2)}) collective-permute-start(f32[392,128]{1,0:T(8,128)S(1)} %get-tuple-element.46), channel_id=1, source_target_pairs={{2,4},{4,2},{3,5},{5,3},{10,12},{12,10},{11,13},{13,11},{18,20},{2... | collective-permute-start | bytes 602120 | tf_op jit(solution)/shard_map/ppermute | solution.py:643
  25.6 4.3 %collective-permute-start.5 = (f32[192,128]{1,0:T(8,128)S(1)}, f32[192,128]{1,0:T(8,128)S(1)}, u32[]{:S(2)}, u32[]{:S(2)}) collective-permute-start(f32[192,128]{1,0:T(8,128)S(1)} %get-tuple-element.61), channel_id=1, source_target_pairs={{0,1},{1,0},{2,3},{3,2},{4,5},{5,4},{6,7},{7,6},{8,9},{9,8},{10,11... | collective-permute-start | bytes 294920 | tf_op jit(solution)/shard_map/ppermute | solution.py:643

commit v5 on v4

--- a/solution.py
+++ b/solution.py
@@ -20,6 +20,7 @@
 XN, XE = NX + 2 * RADIUS, EX + 2 * RADIUS
 ROWS = 48
 QROWS = 56
+OWN = 12
 XR = 24
 
 
@@ -160,41 +161,60 @@
     return lax.axis_index(axis) % 2 == 1
 
 
+X_MESSAGE = 688
+X_DENSITY, X_TOP, X_DOFS = 576, 672, 684
+
+
+def third_rows():
+    spare = [(48 * i + NY, 3 * i, 3) for i in range(12)]
+    return spare + [(X_DENSITY + EY, 36, 4), (X_DENSITY + ROWS + EY, 40, 4)]
+
+
 def pack_kernel(local_ref, top_ref, dens_ref, dofs_ref, even_ref, odd_ref, tops_ref, l_ref, t_ref, d_ref, c_ref, sem):
-    copies = [pltpu.make_async_copy(top_ref, t_ref, sem.at[0]), pltpu.make_async_copy(dens_ref, d_ref, sem.at[1]),
-              pltpu.make_async_copy(dofs_ref, c_ref, sem.at[2])]
+    copies = []
     for side, node in ((0, EX - RADIUS), (1, 0)):
         for c in range(3):
             copies.append(pltpu.make_async_copy(local_ref.at[c, node : node + 4], l_ref.at[side, c], sem.at[len(copies)]))
+    for source, dest in ((top_ref, t_ref), (dofs_ref, c_ref), (dens_ref, d_ref)):
+        copies.append(pltpu.make_async_copy(source, dest, sem.at[len(copies)]))
     for copy in copies:
         copy.start()
-    even_ref[...] = jnp.zeros(even_ref.shape, F32)
-    odd_ref[...] = jnp.zeros(odd_ref.shape, F32)
-    tops_ref[...] = jnp.zeros(tops_ref.shape, F32)
-    for copy in copies:
+    for out_ref in (even_ref, odd_ref):
+        out_ref[X_TOP:X_MESSAGE, :] = jnp.zeros((X_MESSAGE - X_TOP, EZ), F32)
+    clear(tops_ref)
+    odd = odd_place("gx")
+    outs = ((even_ref, odd), (odd_ref, jnp.logical_not(odd)))
+    for copy in copies[:6]:
+        copy.wait()
+    for out_ref, flip in outs:
+        side = flip.astype(jnp.int32)
+        for c in range(3):
+            for j in range(4):
+                out_ref[(c * 4 + j) * ROWS : (c * 4 + j) * ROWS + NY, :] = l_ref[side, c, j]
+    for copy in copies[6:]:
         copy.wait()
     for c in range(3):
         for i in range(NX):
             tops_ref[c, i : i + 1, 0:NY] = t_ref[c, i]
-    odd = odd_place("gx")
-    for out_ref, flip in ((even_ref, odd), (odd_ref, jnp.logical_not(odd))):
-        side = flip.astype(jnp.int32)
+    for out_ref, flip in outs:
         for c in range(3):
-            for j in range(4):
-                out_ref[c * 4 + j, 0:NY, :] = l_ref[side, c, j]
-                out_ref[c * 4 + j, NY : NY + 1, :] = jnp.where(
-                    flip, tops_ref[c, j : j + 1, :], tops_ref[c, EX - RADIUS + j : EX - RADIUS + j + 1, :])
+            out_ref[X_TOP + 4 * c : X_TOP + 4 * c + 4, :] = jnp.where(
+                flip, tops_ref[c, 0:4, :], tops_ref[c, EX - RADIUS : EX - RADIUS + 4, :])
         for j in range(3):
-            out_ref[12 + j, 0:EY, :] = jnp.where(
-                flip, d_ref[pl.ds(j, EY, stride=EX), :], d_ref[pl.ds(EX - RADIUS + j, EY, stride=EX), :])
-        out_ref[12, EY : EY + 1, 0:8] = c_ref[...].astype(F32)
+            value = jnp.where(flip, d_ref[pl.ds(j, EY, stride=EX), :], d_ref[pl.ds(EX - RADIUS + j, EY, stride=EX), :])
+            if j < 2:
+                out_ref[X_DENSITY + j * ROWS : X_DENSITY + j * ROWS + EY, :] = value
+            else:
+                for at, first, count in third_rows():
+                    out_ref[at : at + count, :] = value[first : first + count]
+        out_ref[X_DOFS : X_DOFS + 1, 0:8] = c_ref[...].astype(F32)
 
 
 def sort_sides(axis, even_ref, odd_ref, low_ref, high_ref):
     odd = odd_place(axis)
     even, other = even_ref[...], odd_ref[...]
-    low_ref[...] = jnp.where(odd, even, other)
-    high_ref[...] = jnp.where(odd, other, even)
+    low_ref[...] = jnp.where(has_lower(axis), jnp.where(odd, even, other), 0.0)
+    high_ref[...] = jnp.where(has_upper(axis), jnp.where(odd, other, even), 0.0)
 
 
 def prepare_kernel(stiff_ref, dens_ref, lhs_ref, lhs_edge_ref, lhs_z_ref, od_ref, rs_ref, rd_ref):
@@ -226,9 +246,9 @@
             own_ref[c * NX + i, 0:NY, :] = local_ref[c, i] + plane_interp(edges, i, NY)
             own_ref[c * NX + i, NY:ROWS, :] = jnp.zeros((ROWS - NY, EZ), F32)
     clear(refs[3])
-    build_nodes(lambda c, p: own_ref[c * NX + p + 1], range(EX - 1), ROWS, refs)
-    blocks = [(p, r) for p in range(EX - 2) for r in range(1, EY - 1, 3)]
-    energy_planes(lhs_ref[...], 3, refs, e_ref, 0, EX - 2, ROWS, blocks, 0)
+    build_nodes(lambda c, p: own_ref[c * NX + p + 1], range(OWN + 1), ROWS, refs)
+    blocks = [(p, r) for p in range(OWN) for r in range(1, EY - 1, 3)]
+    energy_planes(lhs_ref[...], 3, refs, e_ref, 0, OWN, ROWS, blocks, 0)
 
 
 def clear(ref):
@@ -247,8 +267,7 @@
     return lax.axis_index(axis) < lax.axis_size(axis) - 1
 
 
-def message_dofs(message_ref):
-    row = message_ref[12, EY : EY + 1, :]
+def message_dofs(row):
     lane = iota((1, EZ), 1)
     return lambda k: jnp.sum(jnp.where(lane == k, row, 0.0)).astype(jnp.int32)
 
@@ -266,21 +285,34 @@
 
 
 def x_kernel(shared, own_ref, top_ref, dens_ref, even_ref, odd_ref, coarse_ref, dofs_ref,
-             xl_ref, xh_ref, tx_ref, yeven_ref, yodd_ref, low_ref, high_ref, up_ref, down_ref, t_ref):
-    sort_sides("gx", even_ref, odd_ref, low_ref, high_ref)
+             xl_ref, xh_ref, tx_ref, yeven_ref, yodd_ref, hd_ref, up_ref, down_ref, t_ref):
+    odd = odd_place("gx")
+
+    def low_rows(at, count):
+        return jnp.where(odd, even_ref[at : at + count, :], odd_ref[at : at + count, :])
+
+    def high_rows(at, count):
+        return jnp.where(odd, odd_ref[at : at + count, :], even_ref[at : at + count, :])
+
     corners = corner_scalars(coarse_ref, lambda k: dofs_ref[k], shared)
-    corners_low = corner_scalars(coarse_ref, message_dofs(low_ref), shared)
-    corners_high = corner_scalars(coarse_ref, message_dofs(high_ref), shared)
+    corners_low = corner_scalars(coarse_ref, message_dofs(low_rows(X_DOFS, 1)), shared)
+    corners_high = corner_scalars(coarse_ref, message_dofs(high_rows(X_DOFS, 1)), shared)
     lower, upper = has_lower("gx"), has_upper("gx")
+    for side, side_rows, there in ((0, low_rows, lower), (3, high_rows, upper)):
+        for j in range(2):
+            hd_ref[side + j] = jnp.where(there, side_rows(X_DENSITY + j * ROWS, ROWS), 0.0)
+        hd_ref[side + 2, EY:ROWS, :] = jnp.zeros((ROWS - EY, EZ), F32)
+        for at, first, count in third_rows():
+            hd_ref[side + 2, first : first + count, :] = jnp.where(there, side_rows(at, count), 0.0)
     for c in range(3):
         edges_low, edges_high = corner_rows(corners_low, c), corner_rows(corners_high, c)
         for j in range(4):
-            value = low_ref[c * 4 + j] + plane_interp(edges_low, EX - RADIUS + j, ROWS)
+            value = low_rows((c * 4 + j) * ROWS, ROWS) + plane_interp(edges_low, EX - RADIUS + j, ROWS)
             if j == 3:
                 mine = own_ref[c * NX]
                 value = average(lower, value, mine, mine)
             xl_ref[c * 4 + j] = value
-            value = high_ref[c * 4 + j] + plane_interp(edges_high, j, ROWS)
+            value = high_rows((c * 4 + j) * ROWS, ROWS) + plane_interp(edges_high, j, ROWS)
             if j == 0:
                 mine = own_ref[c * NX + EX]
                 value = average(upper, mine, value, mine)
@@ -289,9 +321,8 @@
     t_ref[...] = jnp.zeros(t_ref.shape, F32)
     for c in range(3):
         t_ref[0] = top_ref[c] + top_interp(corners, c, XR)
-        for j in range(4):
-            t_ref[1, j : j + 1, 0:NY] = low_ref[c * 4 + j, NY : NY + 1, 0:NY]
-            t_ref[2, j : j + 1, 0:NY] = high_ref[c * 4 + j, NY : NY + 1, 0:NY]
+        t_ref[1, 0:4, :] = low_rows(X_TOP + 4 * c, 4)
+        t_ref[2, 0:4, :] = high_rows(X_TOP + 4 * c, 4)
         t_low = t_ref[1, 0:8, :] + pltpu.roll(top_interp(corners_low, c, 24), 24 - (EX - RADIUS), 0)[0:8]
         t_high = t_ref[2, 0:8, :] + top_interp(corners_high, c, 8)
         first = average(lower, t_low[3:4], t_ref[0, 0:1, :], t_ref[0, 0:1, :])
@@ -311,7 +342,7 @@
                 out_ref[at : at + 4, :] = x_plane(own_ref, xl_ref, xh_ref, c, p)[node : node + 4]
         for x in range(XE):
             at = 3 * XN * 4 + x * 4
-            out_ref[at : at + 3, :] = x_density(dens_ref, low_ref, high_ref, x)[elem : elem + 3]
+            out_ref[at : at + 3, :] = x_density(dens_ref, hd_ref, x)[elem : elem + 3]
             out_ref[at + 3 : at + 4, :] = jnp.zeros((1, EZ), F32)
         out_ref[364:TOP_AT, :] = jnp.zeros((TOP_AT - 364, EZ), F32)
         lane = iota((XR, EZ), 1)
@@ -320,25 +351,25 @@
             moved = pltpu.roll(tx_ref[c], (4 * c - lane_at) % EZ, 1)
             total = jnp.where((lane >= 4 * c) & (lane < 4 * c + 4), moved, total)
         out_ref[TOP_AT:Y_MESSAGE, :] = total
-    sort_sides("gy", up_ref, down_ref, yodd_ref, yeven_ref)
+    odd = odd_place("gy")
+    up, down = up_ref[...], down_ref[...]
+    yeven_ref[...] = jnp.where(odd, down, up)
+    yodd_ref[...] = jnp.where(odd, up, down)
 
 
 def side_kernel(own_ref, xl_ref, xh_ref, lhs_ref, e_ref, *refs):
     clear(refs[3])
+    high = XE - 4 - OWN
 
     def plane(c, p):
-        if p < 4:
-            return xl_ref[c * 4 + p]
-        if p == 4:
-            return own_ref[c * NX + 1]
-        if p == 5:
-            return own_ref[c * NX + EX - 1]
-        return xh_ref[c * 4 + p - 6]
-
-    build_nodes(plane, range(10), ROWS, refs)
-    blocks = [(p, r) for p in range(4) for r in range(1, EY - 1, 3)]
-    for first, out_first in ((0, 0), (5, 4)):
-        energy_planes(lhs_ref[...], 3, refs, e_ref, first, 4, ROWS, blocks, out_first)
+        if p < 5:
+            return x_plane(own_ref, xl_ref, xh_ref, c, p)
+        return x_plane(own_ref, xl_ref, xh_ref, c, p - 5 + 4 + OWN)
+
+    build_nodes(plane, range(5 + high + 1), ROWS, refs)
+    for first, count, out_first in ((0, 4, 0), (5, high, 4)):
+        blocks = [(p, r) for p in range(count) for r in range(1, EY - 1, 3)]
+        energy_planes(lhs_ref[...], 3, refs, e_ref, first, count, ROWS, blocks, out_first)
 
 
 Z_MESSAGE = 192
@@ -353,25 +384,25 @@
     return xh_ref[c * 4 + p - 19]
 
 
-def x_density(dens_ref, low_ref, high_ref, x, rows=EY):
+def x_density(dens_ref, hd_ref, x, rows=EY):
     if x < 3:
-        return low_ref[12 + x, 0:rows, :]
+        return hd_ref[x, 0:rows, :]
     if x < 19:
         return dens_ref[x - 3, 0:rows, :]
-    return high_ref[12 + x - 19, 0:rows, :]
+    return hd_ref[x - 16, 0:rows, :]
 
 
 def end_planes(turned):
     return jnp.concatenate([turned[0:4], turned[EZ - 4 : EZ]], axis=0)
 
 
-def turn_kernel(own_ref, xl_ref, xh_ref, dens_ref, lowx_ref, highx_ref, z_ref):
+def turn_kernel(own_ref, xl_ref, xh_ref, dens_ref, hd_ref, z_ref):
     head = jnp.zeros((8, EZ), F32)
 
     def padded(i):
         if i < 3 * XN:
             return [head, x_plane(own_ref, xl_ref, xh_ref, i // XN, i % XN), head]
-        return [head, x_density(dens_ref, lowx_ref, highx_ref, i - 3 * XN, ROWS), head]
+        return [head, x_density(dens_ref, hd_ref, i - 3 * XN, ROWS), head]
 
     lane = iota((8, EZ), 1)
     for i in range(0, TILES, 2):
@@ -503,7 +534,7 @@
     return total
 
 
-def field_kernel(ea_ref, eb_ref, el_ref, eh_ref, dens_ref, lowx_ref, highx_ref, lowy_ref, highy_ref,
+def field_kernel(ea_ref, eb_ref, el_ref, eh_ref, dens_ref, hd_ref, lowy_ref, highy_ref,
                  g_ref, along_ref, right_ref, f_ref):
     rows = iota((QROWS, EZ), 0)
     lanes = iota((QROWS, EZ), 1)
@@ -512,10 +543,10 @@
     for x in range(XE):
         if x < 4:
             middle = eb_ref[x]
-        elif x < 18:
+        elif x < 4 + OWN:
             middle = ea_ref[x - 4]
         else:
-            middle = eb_ref[x - 14]
+            middle = eb_ref[x - OWN]
         low = pltpu.roll(el_ref[x], 5, 0)
         high = pltpu.roll(eh_ref[x], 3, 0)
         start = jnp.where(row < 1, low, middle[0:8])
@@ -524,7 +555,7 @@
         at = 3 * XN * 4 + x * 4
         pad = jnp.zeros((5, EZ), F32)
         d = jnp.concatenate(
-            [pad, lowy_ref[at : at + 3, :], x_density(dens_ref, lowx_ref, highx_ref, x), highy_ref[at : at + 3, :], pad[0:1]], axis=0)
+            [pad, lowy_ref[at : at + 3, :], x_density(dens_ref, hd_ref, x), highy_ref[at : at + 3, :], pad[0:1]], axis=0)
         f_ref[0, x] = jnp.where(ok, (SCALE * d) * d * d * energy, 0.0)
         f_ref[1, x] = jnp.where(ok, d, 0.0)
 
@@ -589,25 +620,25 @@
         jnp.where(low_side, od, swap(dh1)),
     )
     inside = (lane % 64 >= 5) & (lane % 64 < 55) & (iota((XR, EZ), 0) < XE)
-    lanes = iota((8, EZ), 1)
+    lanes = iota((16, EZ), 1)
     at_end = (lanes < 4) | (lanes >= EZ - 4)
-    copies = []
-    for f in (1, 0):
-        if f == 0:
-            energy_planes(lhs_ref[...], 4, refs, ez_ref, 0, 4, XR, [(j, x) for j in range(4) for x in range(0, XR, 4)], 0)
+    energy_planes(lhs_ref[...], 4, refs, ez_ref, 0, 4, XR, [(j, x) for j in range(4) for x in range(0, XR, 4)], 0)
+    ends = []
+    for f in range(2):
         for j in range(4):
             d = dens[j]
             value = d if f == 1 else (SCALE * d) * d * d * ez_ref[j]
             c_ref[f, j * EX : (j + 1) * EX, :] = triangle_forward(jnp.where(inside, value, 0.0))[0:EX]
         turned = split_dot(c_ref[f], along_ref[...])
         turned = jnp.concatenate([turned, jnp.zeros((EZ - 4 * EX, EZ), F32)], axis=0).T
-        ends = split_dot(turned[8:56] + pltpu.roll(turned[72:120], 64, 1), right_ref[...])
-        inverse_ref = rs_ref if f == 0 else rd_ref
-        for y in range(0, EY, 8):
-            count = min(8, EY - y)
+        ends.append(split_dot(turned[8:56] + pltpu.roll(turned[72:120], 64, 1), right_ref[...]))
+    copies = []
+    for y in (0, 16, 32):
+        count = min(16, EY - y)
+        for f, inverse_ref in ((0, rs_ref), (1, rd_ref)):
             for x in range(EX):
-                end = jnp.where(at_end, pltpu.roll(ends[y : y + 8], (EZ - 4 - 8 * x) % EZ, 1), 0.0)
-                value = (g_ref[f, x, y : y + 8, :] + end) * inverse_ref[x, y : y + 8, :]
+                end = jnp.where(at_end, pltpu.roll(ends[f][y : y + 16], (EZ - 4 - 8 * x) % EZ, 1), 0.0)
+                value = (g_ref[f, x, y : y + 16, :] + end) * inverse_ref[x, y : y + 16, :]
                 o_ref[f, pl.ds(y * EX + x, count, stride=EX), :] = value[0:count]
             block = pl.ds(y * EX, count * EX)
             copies.append(pltpu.make_async_copy(o_ref.at[f, block], outs[f].at[block], sem.at[len(copies)]))
@@ -635,12 +666,19 @@
     )
 
 
-def exchange(axis, *values):
-    count = lax.axis_size(axis)
+def exchange(axis, spare, *values):
+    count, others = lax.axis_size(axis), lax.axis_size(spare)
+    names = tuple(sorted((axis, spare)))
+    step, spare_step = (others, 1) if names[0] == axis else (1, count)
     results = []
     for first, value in enumerate(values):
-        pairs = [(i, i + 1) for i in range(first, count - 1, 2)]
-        results.append(lax.ppermute(value, axis, pairs + [(j, i) for i, j in pairs]))
+        moves = []
+        for i in range(count):
+            j = i + 1 if i % 2 == first else i - 1
+            for o in range(others):
+                target = (j, o) if 0 <= j < count else (i, o ^ 1)
+                moves.append((i * step + o * spare_step, target[0] * step + target[1] * spare_step))
+        results.append(lax.ppermute(value, names, moves))
     return results
 
 
@@ -654,7 +692,7 @@
     else:
         coarse = lax.all_gather(coarse_solution, "gz")
 
-    message = ((15, ROWS, EZ), F32)
+    message = ((X_MESSAGE, EZ), F32)
     even, odd, tops = call(
         pack_kernel,
         [message, message, ((3, XR, EZ), F32)],
@@ -664,7 +702,7 @@
         pltpu.with_memory_space_constraint(value, pltpu.HBM)
         for value in (local_solution, jnp.transpose(top_nodes, (0, 1, 3, 2)), dens, dofs.reshape(1, 8))
     ])
-    even_x, odd_x = exchange("gx", even, odd)
+    even_x, odd_x = exchange("gx", "gy", even, odd)
 
     own_planes = ((EX, ROWS, EZ), F32)
     rows3, rows4 = ((96, block_rows(3)), BF16), ((128, block_rows(4)), BF16)
@@ -674,28 +712,28 @@
 
     own, ea = call(
         functools.partial(own_kernel, shared),
-        [((3 * NX, ROWS, EZ), F32), ((EX - 2, ROWS, EZ), F32)],
+        [((3 * NX, ROWS, EZ), F32), ((OWN, ROWS, EZ), F32)],
         [VM, VM, SM, SM],
-        node_buffers((EX - 1) * ROWS, (EX - 2) * ROWS),
+        node_buffers((OWN + 1) * ROWS, OWN * ROWS),
         micros=6.0,
     )(local_solution, lhs, coarse, dofs)
 
     face = ((12, ROWS, EZ), F32)
     y_message = ((Y_MESSAGE, EZ), F32)
-    xl, xh, tx, even, odd, low_x, high_x = call(
+    xl, xh, tx, even, odd, halo_dens = call(
         functools.partial(x_kernel, shared),
-        [face, face, ((3, XR, EZ), F32), y_message, y_message, message, message],
+        [face, face, ((3, XR, EZ), F32), y_message, y_message, ((6, ROWS, EZ), F32)],
         [VM, VM, VM, VM, VM, SM, SM],
         [y_message, y_message, ((4, XR, EZ), F32)],
         micros=2.0,
     )(own, tops, dens, even_x, odd_x, coarse, dofs)
-    even_y, odd_y = exchange("gy", even, odd)
+    even_y, odd_y = exchange("gy", "gz", even, odd)
 
     (eb,) = call(
-        side_kernel, [((8, ROWS, EZ), F32)], [VM] * 4, node_buffers(10 * ROWS, 4 * ROWS), micros=2.6
+        side_kernel, [((XE - OWN, ROWS, EZ), F32)], [VM] * 4, node_buffers((XE - OWN + 2) * ROWS, (XE - 4 - OWN) * ROWS), micros=2.6
     )(own, xl, xh, lhs)
 
-    (zo,) = call(turn_kernel, [((TILES, 8, EZ), F32)], [VM] * 6, micros=1.5)(own, xl, xh, dens, low_x, high_x)
+    (zo,) = call(turn_kernel, [((TILES, 8, EZ), F32)], [VM] * 5, micros=1.5)(own, xl, xh, dens, halo_dens)
 
     z_message = ((Z_MESSAGE, EZ), F32)
     low_y, high_y, oa, ob, od, *messages = call(
@@ -705,7 +743,7 @@
         [((8 * 3 * XR, EZ), F32), ((8 * XR, EZ), F32), z_message, z_message],
         micros=1.0,
     )(tx, zo, eb, even_y, odd_y)
-    received_z = exchange("gz", *messages)
+    received_z = exchange("gz", "gy", *messages)
 
     el, eh = call(
         edge_kernel,
@@ -717,15 +755,15 @@
 
     square = ((EZ, EZ), BF16)
     filtered, along_y, ends = call(
-        field_kernel, [((2, EX, ROWS, EZ), F32), square, square], [VM] * 9, [((2, XE, QROWS, EZ), F32)], micros=1.5
-    )(ea, eb, el, eh, dens, low_x, high_x, low_y, high_y)
+        field_kernel, [((2, EX, ROWS, EZ), F32), square, square], [VM] * 8, [((2, XE, QROWS, EZ), F32)], micros=1.5
+    )(ea, eb, el, eh, dens, halo_dens, low_y, high_y)
 
     sens, smooth = call(
         last_kernel,
         [((EY * EX, EZ), F32)] * 2,
         [VM] * (9 + len(received_z)),
         [((4, XR, EZ), F32), ((2, 4 * EX, EZ), F32), z_message, z_message, ((2, EY * EX, EZ), F32),
-         pltpu.SemaphoreType.DMA((12,))] + node_buffers(5 * XR + 8, 4 * XR),
+         pltpu.SemaphoreType.DMA((6,))] + node_buffers(5 * XR + 8, 4 * XR),
         space=pltpu.HBM,
         micros=2.5,
     )(filtered, along_y, ends, inverse_sens, inverse_smooth, oa, ob, od, lhs_z, *received_z)

time: 32.6 us -> 28.8 us (0.88); the launches traced: 32.4 us -> 28.2 us
  starting transfers between devices: 12 us -> 7.99 us
    ppermute x5, starting transfers between devices: 10.7 us -> 6.75 us  [exchange(): results.append(lax.ppermute(value, names, moves))]
    pallas_call x1, Pallas kernels: 4.77 us -> 4.25 us  [local(): call(functools.partial(own_kernel, shared), [((3 * NX, ROWS, EZ), F32), (...]
    pallas_call x3, Pallas kernels: 4.37 us -> 4.82 us  [the longest x1 2.73 us: local(): call(side_kernel, [((XE - OWN, ROWS, EZ), F32)], [VM] * 4, node_buffers((...]
  transfers between devices with their start and end apart: 6 -> 6, of which waited for: 3 -> 3; matrix products, arithmetic and copies ran while one was open for 0% -> 0% of each run, Pallas kernels for 36% -> 42%
where the time goes in v5:
time: 28.8 us; the launch traced here: 28.2 us
  Pallas kernels  17.6 us (61%)
  starting transfers between devices  7.99 us (28%)
  waiting for transfers between devices  1.79 us (6%)
  between operations  0.78 us (3%)
    ppermute x5, starting transfers between devices, exchange(): results.append(lax.ppermute(value, names, moves))  6.75 us
    pallas_call x1, Pallas kernels, local(): call(functools.partial(own_kernel, shared), [((3 * NX, ROWS, EZ), F32), (...  4.25 us
    pallas_call x1, Pallas kernels, local(): call(side_kernel, [((XE - OWN, ROWS, EZ), F32)], [VM] * 4, node_buffers((...  2.73 us
    pallas_call x1, Pallas kernels, local(): call(last_kernel, [((EY * EX, EZ), F32)] * 2, [VM] * (9 + len(received_z)...  2.31 us
    pallas_call x1, Pallas kernels, local(): call(edge_kernel, [((XE, 8, EZ), F32)] * 2, [VM] * 6, node_buffers(XN * 8...  1.82 us
    pallas_call x1, Pallas kernels, local(): call(pack_kernel, [message, message, ((3, XR, EZ), F32)], [pltpu.HBM] * 4...  1.52 us
    pallas_call x1, Pallas kernels, local(): call(functools.partial(x_kernel, shared), [face, face, ((3, XR, EZ), F32)...  1.51 us
    ppermute x1, starting transfers between devices, local(): other = lax.ppermute(coarse_solution, 'gz', [(0, 1), (1, 0)])  1.24 us
  transfers between devices with their start and end apart: 6, of which 3 were waited for; matrix products, arithmetic and copies ran while one was open for 0% of the time, Pallas kernels for 42%

profile of v5, /device:TPU:9, one launch (start us, length us, event | category | flops | bytes accessed | tf_op | source)
XLA Modules:
  0.0 28.2 jit_solution(15649329711306235998)
XLA Ops:
  0.6 0.0 copy-start
  0.6 0.0 copy-start.3
  0.7 0.0 copy-start.1
  0.7 0.0 copy-start.4
  0.7 0.0 copy-start.2
  0.7 1.5 %shard_map.79 = (f32[688,128]{1,0:T(8,128)S(1)}, f32[688,128]{1,0:T(8,128)S(1)}, f32[3,24,128]{2,1,0:T(8,128)S(1)}) custom-call(f32[3,17,45,128]{3,2,1,0:T(8,128)} %local_ref.3, f32[3,17,1,45]{3,2,1,0:T(1,128)} %bitcast.19, f32[704,128]{1,0:T(8,128)} %bitcast.14, s32[1,8]{1,0:T(1,128)} %bitcast.16), custom_call_target="tpu_custom_call" | custom-call | bytes 3600000 | tf_op jit(solution)/shard_map/pallas_call | solution.py:696
  2.2 0.1 collective-permute-start.1
  2.3 2.6 %collective-permute-start.2 = (f32[688,128]{1,0:T(8,128)S(1)}, f32[688,128]{1,0:T(8,128)S(1)}, u32[]{:S(2)}, u32[]{:S(2)}) collective-permute-start(f32[688,128]{1,0:T(8,128)S(1)} %get-tuple-element.38), channel_id=1, source_target_pairs={{0,2},{2,0},{4,6},{6,4},{8,16},{10,18},{12,20},{14,22},{16,8},{18,... | collective-permute-start | bytes 1056776 | tf_op jit(solution)/shard_map/ppermute | solution.py:681
  4.9 0.0 copy-done.4
  4.9 1.2 %collective-permute-start = (f32[3,512]{1,0:T(4,128)S(1)}, f32[3,512]{1,0:T(4,128)S(1)}, u32[]{:S(2)}, u32[]{:S(2)}) collective-permute-start(f32[3,512]{1,0:T(4,128)S(1)} %copy-done.4), channel_id=1, source_target_pairs={{0,1},{1,0},{2,3},{3,2},{4,5},{5,4},{6,7},{7,6},{8,9},{9,8},{10,11... | collective-permute-start | bytes 18440 | tf_op jit(solution)/shard_map/ppermute | solution.py:690
  6.1 0.0 copy-done.1
  6.1 0.0 copy-done.2
  6.1 0.8 %shard_map.77 = (bf16[96,192]{1,0:T(8,128)(2,1)S(1)}, bf16[128,256]{1,0:T(8,128)(2,1)S(1)}, bf16[128,256]{1,0:T(8,128)(2,1)S(1)}, f32[16,48,128]{2,1,0:T(8,128)S...) custom-call(f32[24,24]{1,0:T(8,128)S(1)} %copy-done.2, f32[704,128]{1,0:T(8,128)S(1)} %bitcast.15), custom_call_target="tpu_custom_call" | custom-call | bytes 3600000 | tf_op jit(solution)/shard_map/pallas_call | solution.py:709
  7.0 0.7 %collective-permute-done = f32[3,512]{1,0:T(4,128)S(1)} collective-permute-done((f32[3,512]{1,0:T(4,128)S(1)}, f32[3,512]{1,0:T(4,128)S(1)}, u32[]{:S(2)}, u32[]{:S(2)}) %collective-permute-start) | collective-permute-done | bytes 6176 | tf_op jit(solution)/shard_map/ppermute | solution.py:690
  7.7 0.0 copy-done
  7.7 0.0 copy-done.3
  7.7 4.2 %shard_map.78 = (f32[51,48,128]{2,1,0:T(8,128)S(1)}, f32[12,48,128]{2,1,0:T(8,128)S(1)}) custom-call(f32[3,17,45,128]{3,2,1,0:T(8,128)S(1)} %copy-done, bf16[96,192]{1,0:T(8,128)(2,1)S(1)} %get-tuple-element.32.lhs_ref, f32[2,3,512]{2,1,0:T(4,128)S(1)} %pad_maximum_fusion.coarse_ref, s32[8]{0:T(128)S(1)} %bitcast.17), custom_call_target="tpu_custom_call" | custom-call | bytes 21600000 | tf_op jit(solution)/shard_map/pallas_call | solution.py:713
  11.9 0.0 collective-permute-done.1.even_ref
  12.0 0.6 %collective-permute-done.2.odd_ref = f32[688,128]{1,0:T(8,128)S(1)} collective-permute-done((f32[688,128]{1,0:T(8,128)S(1)}, f32[688,128]{1,0:T(8,128)S(1)}, u32[]{:S(2)}, u32[]{:S(2)}) %collective-permute-start.2) | collective-permute-done | bytes 352288 | tf_op jit(solution)/shard_map/ppermute | solution.py:681
  12.5 1.5 %shard_map.80 = (f32[12,48,128]{2,1,0:T(8,128)S(1)}, f32[12,48,128]{2,1,0:T(8,128)S(1)}, f32[3,24,128]{2,1,0:T(8,128)S(1)}, f32[392,128]{1,0:T(8,128)S(1)}, f32[...) custom-call(f32[51,48,128]{2,1,0:T(8,128)S(1)} %get-tuple-element.34.own_ref, f32[3,24,128]{2,1,0:T(8,128)S(1)} %get-tuple-element.35.top_ref, ...), custom_call_target="tpu_custom_call" | custom-call | bytes 7200000 | tf_op jit(solution)/shard_map/pallas_call | solution.py:723
  14.0 1.6 %collective-permute-start.3 = (f32[392,128]{1,0:T(8,128)S(1)}, f32[392,128]{1,0:T(8,128)S(1)}, u32[]{:S(2)}, u32[]{:S(2)}) collective-permute-start(f32[392,128]{1,0:T(8,128)S(1)} %get-tuple-element.43), channel_id=1, source_target_pairs={{0,2},{1,3},{2,0},{3,1},{4,6},{5,7},{6,4},{7,5},{8,10},{9,11},{10,... | collective-permute-start | bytes 602120 | tf_op jit(solution)/shard_map/ppermute | solution.py:681
  15.6 1.2 %collective-permute-start.4 = (f32[392,128]{1,0:T(8,128)S(1)}, f32[392,128]{1,0:T(8,128)S(1)}, u32[]{:S(2)}, u32[]{:S(2)}) collective-permute-start(f32[392,128]{1,0:T(8,128)S(1)} %get-tuple-element.44), channel_id=1, source_target_pairs={{0,1},{1,0},{2,4},{3,5},{4,2},{5,3},{6,7},{7,6},{8,9},{9,8},{10,12... | collective-permute-start | bytes 602120 | tf_op jit(solution)/shard_map/ppermute | solution.py:681
  16.8 2.7 %shard_map.81.eb_ref = f32[10,48,128]{2,1,0:T(8,128)S(1)} custom-call(f32[51,48,128]{2,1,0:T(8,128)S(1)} %get-tuple-element.34.own_ref, f32[12,48,128]{2,1,0:T(8,128)S(1)} %get-tuple-element.39.xl_ref, f32[12,48,128]{2,1,0:T(8,128)S(1)} %get-tuple-element.40.xh_ref, bf16[96,192]{1,0:T(8,128)(2,1)S(1)} %get-tuple-element.32.lhs_ref), custom_call_target="tpu_custom_call" | custom-call | bytes 9360000 | tf_op jit(solution)/shard_map/pallas_call | solution.py:732
  19.5 0.9 %shard_map.82.zo_ref = f32[91,8,128]{2,1,0:T(8,128)S(1)} custom-call(f32[51,48,128]{2,1,0:T(8,128)S(1)} %get-tuple-element.34.own_ref, f32[12,48,128]{2,1,0:T(8,128)S(1)} %get-tuple-element.39.xl_ref, f32[12,48,128]{2,1,0:T(8,128)S(1)} %get-tuple-element.40.xh_ref, f32[16,48,128]{2,1,0:T(8,128)S(1)} %get-tuple-element.36.dens_ref, ...), custom_call_target="tpu_custom_call" | custom-call | bytes 5400000 | tf_op jit(solution)/shard_map/pallas_call | solution.py:736
  20.5 0.0 collective-permute-done.3.even_ref
  20.5 0.5 %collective-permute-done.4.odd_ref = f32[392,128]{1,0:T(8,128)S(1)} collective-permute-done((f32[392,128]{1,0:T(8,128)S(1)}, f32[392,128]{1,0:T(8,128)S(1)}, u32[]{:S(2)}, u32[]{:S(2)}) %collective-permute-start.4) | collective-permute-done | bytes 200736 | tf_op jit(solution)/shard_map/ppermute | solution.py:681
  21.0 0.5 %shard_map.83 = (f32[392,128]{1,0:T(8,128)S(1)}, f32[392,128]{1,0:T(8,128)S(1)}, f32[72,128]{1,0:T(8,128)S(1)}, f32[72,128]{1,0:T(8,128)S(1)}, f32[24,128]{1,0:T(8,128)S(1)}, /*index=5*/f32[192,128]{1,0:T(8,128)S(1)}) custom-call(f32[3,24,128]{2,1,0:T(8,128)S(1)} %get-tuple-element.41.tx_ref, f32[91,8,128]{2,1,0:T(8,128)S(1)} %shard_map.82.zo_ref, ...), custom_call_target="tpu_custom_call" | custom-call | bytes 3600000 | tf_op jit(solution)/shard_map/pallas_call | solution.py:739
  21.5 1.3 %collective-permute-start.5 = (f32[192,128]{1,0:T(8,128)S(1)}, f32[192,128]{1,0:T(8,128)S(1)}, u32[]{:S(2)}, u32[]{:S(2)}) collective-permute-start(f32[192,128]{1,0:T(8,128)S(1)} %get-tuple-element.59), channel_id=1, source_target_pairs={{0,1},{2,3},{4,5},{6,7},{1,0},{3,2},{5,4},{7,6},{8,9},{10,11},{12,... | collective-permute-start | bytes 294920 | tf_op jit(solution)/shard_map/ppermute | solution.py:681
  22.9 1.8 %shard_map.84 = (f32[22,8,128]{2,1,0:T(8,128)S(1)}, f32[22,8,128]{2,1,0:T(8,128)S(1)}) custom-call(f32[51,48,128]{2,1,0:T(8,128)S(1)} %get-tuple-element.34.own_ref, f32[12,48,128]{2,1,0:T(8,128)S(1)} %get-tuple-element.39.xl_ref, f32[12,48,128]{2,1,0:T(8,128)S(1)} %get-tuple-element.40.xh_ref, f32[392,128]{1,0:T(8,128)S(1)} %get-tuple-element.45.lowy_ref, ...), custom_call_target="tpu_custom_call" | custom-call | bytes 8279999 | tf_op jit(solution)/shard_map/pallas_call | solution.py:748
  24.7 1.2 %shard_map.85 = (f32[2,16,48,128]{3,2,1,0:T(8,128)S(1)}, bf16[128,128]{1,0:T(8,128)(2,1)S(1)}, bf16[128,128]{1,0:T(8,128)(2,1)S(1)}) custom-call(f32[12,48,128]{2,1,0:T(8,128)S(1)} %get-tuple-element.33.ea_ref, f32[10,48,128]{2,1,0:T(8,128)S(1)} %shard_map.81.eb_ref, f32[22,8,128]{2,1,0:T(8,128)S(1)} %get-tuple-element.48.el_ref, ...), custom_call_target="tpu_custom_call" | custom-call | bytes 5400000 | tf_op jit(solution)/shard_map/pallas_call | solution.py:757
  25.9 0.0 collective-permute-done.5.refs_0_
  25.9 2.3 %shard_map.86 = (f32[704,128]{1,0:T(8,128)}, f32[704,128]{1,0:T(8,128)}) custom-call(f32[2,16,48,128]{3,2,1,0:T(8,128)S(1)} %get-tuple-element.50.g_ref, bf16[128,128]{1,0:T(8,128)(2,1)S(1)} %get-tuple-element.51.along_ref, bf16[128,128]{1,0:T(8,128)(2,1)S(1)} %get-tuple-element.52.right_ref, f32[16,48,128]{2,1,0:T(8,128)S(1)} %get-tuple-element.53.rs_ref, ...), custom_call_target="tpu_custom_call" | custom-call | bytes 9000000 | tf_op jit(solution)/shard_map/pallas_call | solution.py:761
  (1 shorter events, 0.0 us)
Async XLA Ops:
  0.6 7.0 %copy-start = (f32[3,17,45,128]{3,2,1,0:T(8,128)S(1)}, f32[3,17,45,128]{3,2,1,0:T(8,128)}, u32[]{:S(2)}) copy-start(f32[3,17,45,128]{3,2,1,0:T(8,128)} %local_ref.3) | copy-start | bytes 3525124
  0.6 7.0 %copy-start.3 = (s32[1,1,1,8]{3,2,1,0:T(1,128)S(1)}, s32[1,1,1,8]{3,2,1,0:T(1,128)}, u32[]{:S(2)}) copy-start(s32[1,1,1,8]{3,2,1,0:T(1,128)} %param.9) | copy-start | bytes 100
  0.7 5.5 %copy-start.1 = (f32[16,44,128]{2,0,1:T(8,128)S(1)}, f32[16,44,128]{2,0,1:T(8,128)}, u32[]{:S(2)}) copy-start(f32[16,44,128]{2,0,1:T(8,128)} %param.10) | copy-start | bytes 1081348
  0.7 4.2 %copy-start.4 = (f32[3,512]{1,0:T(4,128)S(1)}, f32[3,512]{1,0:T(4,128)}, u32[]{:S(2)}) copy-start(f32[3,512]{1,0:T(4,128)} %param.8) | copy-start | bytes 18436
  0.7 5.4 %copy-start.2 = (f32[24,24]{1,0:T(8,128)S(1)}, f32[24,24]{1,0:T(8,128)}, u32[]{:S(2)}) copy-start(f32[24,24]{1,0:T(8,128)} %stiff_ref.1) | copy-start | bytes 6916
  2.2 9.7 %collective-permute-start.1 = (f32[688,128]{1,0:T(8,128)S(1)}, f32[688,128]{1,0:T(8,128)S(1)}, u32[]{:S(2)}, u32[]{:S(2)}) collective-permute-start(f32[688,128]{1,0:T(8,128)S(1)} %get-tuple-element.37), channel_id=1, source_target_pairs={{0,8},{2,10},{4,12},{6,14},{8,0},{10,2},{12,4},{14,6},{16,24},{18,... | collective-permute-start | bytes 1056776 | tf_op jit(solution)/shard_map/ppermute | solution.py:681
  2.3 10.2 %collective-permute-start.2 = (f32[688,128]{1,0:T(8,128)S(1)}, f32[688,128]{1,0:T(8,128)S(1)}, u32[]{:S(2)}, u32[]{:S(2)}) collective-permute-start(f32[688,128]{1,0:T(8,128)S(1)} %get-tuple-element.38), channel_id=1, source_target_pairs={{0,2},{2,0},{4,6},{6,4},{8,16},{10,18},{12,20},{14,22},{16,8},{18,... | collective-permute-start | bytes 1056776 | tf_op jit(solution)/shard_map/ppermute | solution.py:681
  4.9 2.8 %collective-permute-start = (f32[3,512]{1,0:T(4,128)S(1)}, f32[3,512]{1,0:T(4,128)S(1)}, u32[]{:S(2)}, u32[]{:S(2)}) collective-permute-start(f32[3,512]{1,0:T(4,128)S(1)} %copy-done.4), channel_id=1, source_target_pairs={{0,1},{1,0},{2,3},{3,2},{4,5},{5,4},{6,7},{7,6},{8,9},{9,8},{10,11... | collective-permute-start | bytes 18440 | tf_op jit(solution)/shard_map/ppermute | solution.py:690
  14.0 6.4 %collective-permute-start.3 = (f32[392,128]{1,0:T(8,128)S(1)}, f32[392,128]{1,0:T(8,128)S(1)}, u32[]{:S(2)}, u32[]{:S(2)}) collective-permute-start(f32[392,128]{1,0:T(8,128)S(1)} %get-tuple-element.43), channel_id=1, source_target_pairs={{0,2},{1,3},{2,0},{3,1},{4,6},{5,7},{6,4},{7,5},{8,10},{9,11},{10,... | collective-permute-start | bytes 602120 | tf_op jit(solution)/shard_map/ppermute | solution.py:681
  15.6 5.4 %collective-permute-start.4 = (f32[392,128]{1,0:T(8,128)S(1)}, f32[392,128]{1,0:T(8,128)S(1)}, u32[]{:S(2)}, u32[]{:S(2)}) collective-permute-start(f32[392,128]{1,0:T(8,128)S(1)} %get-tuple-element.44), channel_id=1, source_target_pairs={{0,1},{1,0},{2,4},{3,5},{4,2},{5,3},{6,7},{7,6},{8,9},{9,8},{10,12... | collective-permute-start | bytes 602120 | tf_op jit(solution)/shard_map/ppermute | solution.py:681
  21.5 4.3 %collective-permute-start.5 = (f32[192,128]{1,0:T(8,128)S(1)}, f32[192,128]{1,0:T(8,128)S(1)}, u32[]{:S(2)}, u32[]{:S(2)}) collective-permute-start(f32[192,128]{1,0:T(8,128)S(1)} %get-tuple-element.59), channel_id=1, source_target_pairs={{0,1},{2,3},{4,5},{6,7},{1,0},{3,2},{5,4},{7,6},{8,9},{10,11},{12,... | collective-permute-start | bytes 294920 | tf_op jit(solution)/shard_map/ppermute | solution.py:681

commit v6 on v5

--- a/solution.py
+++ b/solution.py
@@ -13,7 +13,6 @@
 SCALE = -3.0 / 96.0
 HIGHEST = lax.Precision.HIGHEST
 VM = pltpu.VMEM
-SM = pltpu.SMEM
 
 EX, EY, EZ = 16, 44, 128
 NX, NY = EX + 1, EY + 1
@@ -37,31 +36,36 @@
     return high, (value - high.astype(F32)).astype(BF16)
 
 
-def corner_scalars(coarse_ref, dof_of, shared):
-    width = coarse_ref.shape[2]
+def as_column(row):
+    lane, sub = iota((8, EZ), 1), iota((8, EZ), 0)
+    return jnp.sum(jnp.where(lane == sub, row, 0.0), axis=1, keepdims=True)
+
+
+def corner_values(coarse_ref, dofs, shared):
+    parts, _, width = coarse_ref.shape
+    dofs = dofs.astype(jnp.int32)
     own = lax.axis_index("gz")
-    out = [[None] * 8 for _ in range(3)]
-    for k in range(8):
-        dof = dof_of(k)
-        part = dof // width
-        place = dof - part * width
-        if shared:
-            part = jnp.where(part == own, 0, 1)
+    lane = iota((8, width), 1)
+    totals = [0.0] * 3
+    for part in range(parts):
+        place = part if not shared else own if part == 0 else 1 - own
+        found = lane + place * width == dofs
         for c in range(3):
-            out[c][k] = coarse_ref[part, c, place]
-    return out
+            totals[c] = totals[c] + jnp.where(found, coarse_ref[part, c : c + 1, :], 0.0)
+    return [jnp.broadcast_to(jnp.sum(total, axis=1, keepdims=True), (8, EZ)) for total in totals]
 
 
 def corner_rows(corners, c):
     rz = iota((8, EZ), 1).astype(F32) * (1.0 / EZ)
     other = 1.0 - rz
-    return [[corners[c][4 * kx + 2 * ky] * other + corners[c][4 * kx + 2 * ky + 1] * rz for ky in (0, 1)] for kx in (0, 1)]
-
-
-def plane_interp(edges, i, rows):
+    value = [corners[c][k : k + 1] for k in range(8)]
+    return [[value[4 * kx + 2 * ky] * other + value[4 * kx + 2 * ky + 1] * rz for ky in (0, 1)] for kx in (0, 1)]
+
+
+def plane_interp(edges, i, rows, start=0):
     wx = i / EX
     first, second = [((1.0 - wx) * edges[0][ky] + wx * edges[1][ky])[0:1] for ky in (0, 1)]
-    ry = iota((rows, EZ), 0).astype(F32) * (1.0 / EY)
+    ry = (start + iota((rows, EZ), 0)).astype(F32) * (1.0 / EY)
     return (1.0 - ry) * first + ry * second
 
 
@@ -98,7 +102,7 @@
 
 
 def build_nodes(plane_of, planes, rows, refs, first=0):
-    w_ref, b_ref, h_ref, _ = refs
+    w_ref, b_ref, h_ref = refs
     for p in planes:
         base = (first + p) * rows * 8
         zero = jnp.zeros((rows, EZ), F32)
@@ -126,35 +130,53 @@
     lax.fori_loop(0, len(planes), split, 0)
 
 
+def sum_rows(values):
+    row = iota((8, EZ), 0)
+    for step in (1, 2, 4):
+        first = row % (2 * step) < step
+        values = [
+            jnp.where(first, a, b) + pltpu.roll(jnp.where(first, b, a), step, 0)
+            for a, b in zip(values[::2], values[1::2])
+        ]
+    return values[0]
+
+
 def energy_planes(lhs, block, refs, e_ref, first, count, rows, blocks, out_first):
-    w_ref, b_ref, h_ref, s_ref = refs
+    w_ref, b_ref, h_ref = refs
     nodes = block + 1
+    zero = jnp.zeros((8, EZ), F32)
+    found, left = {}, {(p, t) for p in range(count) for t in range(0, rows, 8)}
+
+    def store(before):
+        for p, t in sorted(left):
+            if (p, t + 7) < before:
+                values = [found.pop((p, t + i), zero) for i in range(8)]
+                e_ref[out_first + p, t : t + 8, :] = zero if all(v is zero for v in values) else sum_rows(values)
+                left.remove((p, t))
+
     for i in range(0, len(blocks), 2):
-        pair = [((first + p) * rows + r, p * rows + r) for p, r in blocks[i : i + 2]]
+        pair = blocks[i : i + 2]
         right = []
-        for at, _ in pair:
+        for p, r in pair:
+            at = (first + p) * rows + r
             parts = [b_ref[(at + far) * 16 : (at + far + nodes) * 16, :] for far in (0, rows)]
             for far in (0, rows):
                 parts += [h_ref[(at + far + t) * 16 : (at + far + t + 1) * 16, :] for t in range(0, nodes, 2)]
             right.append(jnp.concatenate(parts, axis=0))
         product = jnp.dot(lhs, jnp.concatenate(right, axis=1), preferred_element_type=F32)
-        for u, (at, out) in enumerate(pair):
-            for e in range(block):
+        for u, (p, r) in enumerate(pair):
+            at = (first + p) * rows + r
+            for e in range(min(block, rows - r)):
                 part = product[32 * e : 32 * e + 32, u * EZ : (u + 1) * EZ]
                 low = w_ref[(at + e) * 8 : (at + e + 2) * 8, :] * part[0:16]
                 high = w_ref[(at + rows + e) * 8 : (at + rows + e + 2) * 8, :] * part[16:32]
                 both = low + high
-                s_ref[(out + e) * 8 : (out + e + 1) * 8, :] = both[0:8] + both[8:16]
-    for p in range(count):
-        total = None
-        for s in (0, 1, 2, 4, 5, 6):
-            term = s_ref[pl.ds(p * rows * 8 + s, rows, stride=8), :]
-            total = term if total is None else total + term
-        e_ref[out_first + p] = total
-
-
-def node_buffers(count, energies):
-    return [((count * 8, EZ), F32), ((count * 16, EZ), BF16), ((count * 16, EZ), BF16), ((energies * 8, EZ), F32)]
+                found[p, r + e] = both[0:8] + both[8:16]
+        store(blocks[i + 2] if i + 2 < len(blocks) else (count, 0))
+
+
+def node_buffers(count):
+    return [((count * 8, EZ), F32), ((count * 16, EZ), BF16), ((count * 16, EZ), BF16)]
 
 
 def odd_place(axis):
@@ -170,7 +192,7 @@
     return spare + [(X_DENSITY + EY, 36, 4), (X_DENSITY + ROWS + EY, 40, 4)]
 
 
-def pack_kernel(local_ref, top_ref, dens_ref, dofs_ref, even_ref, odd_ref, tops_ref, l_ref, t_ref, d_ref, c_ref, sem):
+def pack_kernel(local_ref, top_ref, dens_ref, dofs_ref, even_ref, odd_ref, tops_ref, dofs_out_ref, l_ref, t_ref, d_ref, c_ref, sem):
     copies = []
     for side, node in ((0, EX - RADIUS), (1, 0)):
         for c in range(3):
@@ -208,6 +230,7 @@
                 for at, first, count in third_rows():
                     out_ref[at : at + count, :] = value[first : first + count]
         out_ref[X_DOFS : X_DOFS + 1, 0:8] = c_ref[...].astype(F32)
+    dofs_out_ref[...] = jnp.broadcast_to(as_column(even_ref[X_DOFS : X_DOFS + 1, :]), (8, EZ))
 
 
 def sort_sides(axis, even_ref, odd_ref, low_ref, high_ref):
@@ -238,14 +261,22 @@
         rs_ref[x] = both / od_ref[x]
 
 
-def own_kernel(shared, local_ref, lhs_ref, coarse_ref, dofs_ref, own_ref, e_ref, *refs):
-    corners = corner_scalars(coarse_ref, lambda k: dofs_ref[k], shared)
+def own_kernel(shared, local_ref, lhs_ref, dens_ref, coarse_ref, dofs_ref, own_ref, e_ref, up_ref, down_ref, *refs):
+    corners = corner_values(coarse_ref, dofs_ref[:, 0:1], shared)
     for c in range(3):
         edges = corner_rows(corners, c)
         for i in range(NX):
             own_ref[c * NX + i, 0:NY, :] = local_ref[c, i] + plane_interp(edges, i, NY)
             own_ref[c * NX + i, NY:ROWS, :] = jnp.zeros((ROWS - NY, EZ), F32)
-    clear(refs[3])
+    for out_ref, first in ((up_ref, EY - RADIUS), (down_ref, 0)):
+        out_ref[61 * 4 : OWN_SLOTS * 4, :] = jnp.zeros((4, EZ), F32)
+        for slot in range(61):
+            kind, c, p = SLOTS[slot]
+            if kind == "node":
+                out_ref[slot * 4 : slot * 4 + 4, :] = own_ref[c * NX + p - 3, first : first + 4, :]
+            else:
+                out_ref[slot * 4 : slot * 4 + 3, :] = dens_ref[c - 3, first : first + 3, :]
+                out_ref[slot * 4 + 3 : slot * 4 + 4, :] = jnp.zeros((1, EZ), F32)
     build_nodes(lambda c, p: own_ref[c * NX + p + 1], range(OWN + 1), ROWS, refs)
     blocks = [(p, r) for p in range(OWN) for r in range(1, EY - 1, 3)]
     energy_planes(lhs_ref[...], 3, refs, e_ref, 0, OWN, ROWS, blocks, 0)
@@ -259,64 +290,118 @@
     return jnp.where(flag, 0.5 * low + 0.5 * high, own)
 
 
+OWN_SLOTS = 62
+
+
+def node_slot(c, p):
+    if 4 <= p < 19:
+        return c * 15 + p - 4
+    return OWN_SLOTS + c * 8 + (p if p < 4 else p - 15)
+
+
+def dens_slot(x):
+    if 3 <= x < 19:
+        return 45 + x - 3
+    return OWN_SLOTS + 24 + (x if x < 3 else x - 16)
+
+
+SLOTS = [None] * (OWN_SLOTS + 30)
+for _x in range(XE):
+    SLOTS[dens_slot(_x)] = ("density", _x, 0)
+for _p in range(XN):
+    for _c in range(3):
+        SLOTS[node_slot(_c, _p)] = ("node", _c, _p)
+TOP_AT = 4 * len(SLOTS)
+Y_MESSAGE = TOP_AT + XR
+
+
 def has_lower(axis):
     return lax.axis_index(axis) > 0
 
 
 def has_upper(axis):
     return lax.axis_index(axis) < lax.axis_size(axis) - 1
-
-
-def message_dofs(row):
-    lane = iota((1, EZ), 1)
-    return lambda k: jnp.sum(jnp.where(lane == k, row, 0.0)).astype(jnp.int32)
 
 
 def top_interp(corners, c, rows):
     rx = iota((rows, EZ), 0).astype(F32) * (1.0 / EX)
     ry = iota((rows, EZ), 1).astype(F32) * (1.0 / EY)
-    low = (1.0 - ry) * corners[c][1] + ry * corners[c][3]
-    high = (1.0 - ry) * corners[c][5] + ry * corners[c][7]
+    value = [corners[c][k : k + 1] for k in range(8)]
+    low = (1.0 - ry) * value[1] + ry * value[3]
+    high = (1.0 - ry) * value[5] + ry * value[7]
     return (1.0 - rx) * low + rx * high
 
 
-TOP_AT = 368
-Y_MESSAGE = 392
-
-
-def x_kernel(shared, own_ref, top_ref, dens_ref, even_ref, odd_ref, coarse_ref, dofs_ref,
-             xl_ref, xh_ref, tx_ref, yeven_ref, yodd_ref, hd_ref, up_ref, down_ref, t_ref):
+def x_sides(even_ref, odd_ref):
     odd = odd_place("gx")
 
-    def low_rows(at, count):
+    def low(at, count):
         return jnp.where(odd, even_ref[at : at + count, :], odd_ref[at : at + count, :])
 
-    def high_rows(at, count):
+    def high(at, count):
         return jnp.where(odd, odd_ref[at : at + count, :], even_ref[at : at + count, :])
 
-    corners = corner_scalars(coarse_ref, lambda k: dofs_ref[k], shared)
-    corners_low = corner_scalars(coarse_ref, message_dofs(low_rows(X_DOFS, 1)), shared)
-    corners_high = corner_scalars(coarse_ref, message_dofs(high_rows(X_DOFS, 1)), shared)
+    return low, high
+
+
+def side_corners(shared, coarse_ref, sides):
+    return [corner_values(coarse_ref, as_column(side(X_DOFS, 1)), shared) for side in sides]
+
+
+def x_faces(own_ref, sides, corners, start, rows):
     lower, upper = has_lower("gx"), has_upper("gx")
-    for side, side_rows, there in ((0, low_rows, lower), (3, high_rows, upper)):
+    for c in range(3):
+        edges = [corner_rows(corner, c) for corner in corners]
+        for j in range(4):
+            low, high = [
+                side((c * 4 + j) * ROWS + start, rows) + plane_interp(edge, i, rows, start)
+                for side, edge, i in zip(sides, edges, (EX - RADIUS + j, j))
+            ]
+            if j == 3:
+                mine = own_ref[c * NX, start : start + rows, :]
+                low = average(lower, low, mine, mine)
+            if j == 0:
+                mine = own_ref[c * NX + EX, start : start + rows, :]
+                high = average(upper, mine, high, mine)
+            yield c, j, low
+            yield c, 19 + j, high
+
+
+def halo_kernel(shared, own_ref, even_ref, odd_ref, coarse_ref, xl_ref, xh_ref, hd_ref):
+    sides = x_sides(even_ref, odd_ref)
+    for c, p, value in x_faces(own_ref, sides, side_corners(shared, coarse_ref, sides), 0, ROWS):
+        if p < 4:
+            xl_ref[c * 4 + p] = value
+        else:
+            xh_ref[c * 4 + p - 19] = value
+    for first, side, there in zip((0, 3), sides, (has_lower("gx"), has_upper("gx"))):
         for j in range(2):
-            hd_ref[side + j] = jnp.where(there, side_rows(X_DENSITY + j * ROWS, ROWS), 0.0)
-        hd_ref[side + 2, EY:ROWS, :] = jnp.zeros((ROWS - EY, EZ), F32)
-        for at, first, count in third_rows():
-            hd_ref[side + 2, first : first + count, :] = jnp.where(there, side_rows(at, count), 0.0)
-    for c in range(3):
-        edges_low, edges_high = corner_rows(corners_low, c), corner_rows(corners_high, c)
-        for j in range(4):
-            value = low_rows((c * 4 + j) * ROWS, ROWS) + plane_interp(edges_low, EX - RADIUS + j, ROWS)
-            if j == 3:
-                mine = own_ref[c * NX]
-                value = average(lower, value, mine, mine)
-            xl_ref[c * 4 + j] = value
-            value = high_rows((c * 4 + j) * ROWS, ROWS) + plane_interp(edges_high, j, ROWS)
-            if j == 0:
-                mine = own_ref[c * NX + EX]
-                value = average(upper, mine, value, mine)
-            xh_ref[c * 4 + j] = value
+            hd_ref[first + j] = jnp.where(there, side(X_DENSITY + j * ROWS, ROWS), 0.0)
+        hd_ref[first + 2, EY:ROWS, :] = jnp.zeros((ROWS - EY, EZ), F32)
+        for at, row, count in third_rows():
+            hd_ref[first + 2, row : row + count, :] = jnp.where(there, side(at, count), 0.0)
+
+
+def x_kernel(shared, own_ref, up_own_ref, down_own_ref, top_ref, even_ref, odd_ref, coarse_ref, dofs_ref,
+             tx_ref, yeven_ref, yodd_ref, up_ref, down_ref, t_ref):
+    sides = low_rows, high_rows = x_sides(even_ref, odd_ref)
+    corners = corner_values(coarse_ref, dofs_ref[:, 0:1], shared)
+    corners_low, corners_high = side_corners(shared, coarse_ref, sides)
+    lower, upper = has_lower("gx"), has_upper("gx")
+    for out_ref, start, skip in ((up_ref, EY - 4, 1), (down_ref, 0, 0)):
+        for c, p, value in x_faces(own_ref, sides, (corners_low, corners_high), start, 8):
+            at = (node_slot(c, p) - OWN_SLOTS) * 4
+            out_ref[at : at + 4, :] = value[skip : skip + 4]
+        for x in (0, 1, 2, 19, 20, 21):
+            j, side, there = (x, low_rows, lower) if x < 3 else (x - 19, high_rows, upper)
+            row = start + skip
+            if j < 2:
+                value = side(X_DENSITY + j * ROWS + row, 3)
+            else:
+                value = side(NY if row == 0 else X_DENSITY + ROWS + EY + 1, 3)
+            at = (dens_slot(x) - OWN_SLOTS) * 4
+            out_ref[at : at + 3, :] = jnp.where(there, value, 0.0)
+            out_ref[at + 3 : at + 4, :] = jnp.zeros((1, EZ), F32)
 
     t_ref[...] = jnp.zeros(t_ref.shape, F32)
     for c in range(3):
@@ -335,30 +420,21 @@
         lane = iota((XR, EZ), 1)
         tx_ref[c] = jnp.where(lane < NY + 8, pltpu.roll(t_ref[3], 8, 1), 0.0)
 
-    for out_ref, node, elem, lane_at in ((up_ref, EY - RADIUS, EY - RADIUS, EY - RADIUS + 8), (down_ref, 0, 0, 8)):
-        for c in range(3):
-            for p in range(XN):
-                at = (c * XN + p) * 4
-                out_ref[at : at + 4, :] = x_plane(own_ref, xl_ref, xh_ref, c, p)[node : node + 4]
-        for x in range(XE):
-            at = 3 * XN * 4 + x * 4
-            out_ref[at : at + 3, :] = x_density(dens_ref, hd_ref, x)[elem : elem + 3]
-            out_ref[at + 3 : at + 4, :] = jnp.zeros((1, EZ), F32)
-        out_ref[364:TOP_AT, :] = jnp.zeros((TOP_AT - 364, EZ), F32)
-        lane = iota((XR, EZ), 1)
+    lane = iota((XR, EZ), 1)
+    for out_ref, lane_at in ((up_ref, EY - RADIUS + 8), (down_ref, 8)):
         total = jnp.zeros((XR, EZ), F32)
         for c in range(3):
             moved = pltpu.roll(tx_ref[c], (4 * c - lane_at) % EZ, 1)
             total = jnp.where((lane >= 4 * c) & (lane < 4 * c + 4), moved, total)
-        out_ref[TOP_AT:Y_MESSAGE, :] = total
+        out_ref[TOP_AT - OWN_SLOTS * 4 :, :] = total
     odd = odd_place("gy")
-    up, down = up_ref[...], down_ref[...]
-    yeven_ref[...] = jnp.where(odd, down, up)
-    yodd_ref[...] = jnp.where(odd, up, down)
+    for mine, other, out_ref in ((up_own_ref, down_own_ref, yeven_ref), (down_own_ref, up_own_ref, yodd_ref)):
+        out_ref[0 : OWN_SLOTS * 4, :] = jnp.where(odd, other[...], mine[...])
+    for mine, other, out_ref in ((up_ref, down_ref, yeven_ref), (down_ref, up_ref, yodd_ref)):
+        out_ref[OWN_SLOTS * 4 :, :] = jnp.where(odd, other[...], mine[...])
 
 
 def side_kernel(own_ref, xl_ref, xh_ref, lhs_ref, e_ref, *refs):
-    clear(refs[3])
     high = XE - 4 - OWN
 
     def plane(c, p):
@@ -373,7 +449,6 @@
 
 
 Z_MESSAGE = 192
-TILES = 3 * XN + XE
 
 
 def x_plane(own_ref, xl_ref, xh_ref, c, p):
@@ -399,17 +474,17 @@
 def turn_kernel(own_ref, xl_ref, xh_ref, dens_ref, hd_ref, z_ref):
     head = jnp.zeros((8, EZ), F32)
 
-    def padded(i):
-        if i < 3 * XN:
-            return [head, x_plane(own_ref, xl_ref, xh_ref, i // XN, i % XN), head]
-        return [head, x_density(dens_ref, hd_ref, i - 3 * XN, ROWS), head]
+    def padded(slot):
+        kind, c, p = SLOTS[slot] or SLOTS[0]
+        if kind == "node":
+            return [head, x_plane(own_ref, xl_ref, xh_ref, c, p), head]
+        return [head, x_density(dens_ref, hd_ref, c, ROWS), head]
 
     lane = iota((8, EZ), 1)
-    for i in range(0, TILES, 2):
-        both = end_planes(jnp.concatenate(padded(i) + padded(min(i + 1, TILES - 1)), axis=0).T)
-        z_ref[i] = jnp.where(lane < 64, both, 0.0)
-        if i + 1 < TILES:
-            z_ref[i + 1] = jnp.where(lane < 64, pltpu.roll(both, 64, 1), 0.0)
+    for slot in range(0, len(SLOTS), 2):
+        both = end_planes(jnp.concatenate(padded(slot) + padded(slot + 1), axis=0).T)
+        z_ref[slot] = jnp.where(lane < 64, both, 0.0)
+        z_ref[slot + 1] = jnp.where(lane < 64, pltpu.roll(both, 64, 1), 0.0)
 
 
 def y_kernel(tx_ref, zo_ref, eb_ref, even_ref, odd_ref,
@@ -421,8 +496,8 @@
     clear(z_ref)
     clear(d_ref)
     lane = iota((8, EZ), 1)
-    for first in range(0, TILES, 32):
-        count = min(32, TILES - first)
+    for first in range(0, len(SLOTS), 32):
+        count = min(32, len(SLOTS) - first)
         turned = []
         for ref in (low_ref, high_ref):
             block = ref[first * 4 : (first + count) * 4, :]
@@ -430,20 +505,20 @@
                 block = jnp.concatenate([block, jnp.zeros(((32 - count) * 4, EZ), F32)], axis=0)
             turned.append(end_planes(block.T))
         for t in range(count):
-            i = first + t
+            if SLOTS[first + t] is None:
+                continue
+            kind, c, p = SLOTS[first + t]
             low = pltpu.roll(turned[0], (5 - 4 * t) % EZ, 1)
             high = pltpu.roll(turned[1], (52 - 4 * t) % EZ, 1)
-            mine = zo_ref[i]
-            if i < 3 * XN:
-                at = (i // XN) * XR + i % XN
-                value = jnp.where((lane >= 5) & (lane < 8), low, mine)
+            mine = zo_ref[first + t]
+            value = jnp.where((lane >= 5) & (lane < 8), low, mine)
+            if kind == "node":
+                at = c * XR + p
                 value = jnp.where((lane == 8) & lower, 0.5 * low + 0.5 * mine, value)
                 value = jnp.where((lane == 52) & upper, 0.5 * mine + 0.5 * high, value)
                 z_ref[at * 8 : at * 8 + 8, :] = jnp.where((lane > 52) & (lane < 56), high, value)
             else:
-                at = i - 3 * XN
-                value = jnp.where((lane >= 5) & (lane < 8), low, mine)
-                d_ref[at * 8 : at * 8 + 8, :] = jnp.where((lane >= 52) & (lane < 55), high, value)
+                d_ref[c * 8 : c * 8 + 8, :] = jnp.where((lane >= 52) & (lane < 55), high, value)
 
     lane = iota((XR, EZ), 1)
     tops = []
@@ -484,20 +559,19 @@
 
 
 def edge_kernel(own_ref, xl_ref, xh_ref, lowy_ref, highy_ref, lhs_ref, el_ref, eh_ref, *refs):
-    clear(refs[3])
     lower, upper = has_lower("gy"), has_upper("gy")
     row = iota((8, EZ), 0)
 
     def low(c, p):
         mine = pltpu.roll(x_plane(own_ref, xl_ref, xh_ref, c, p)[0:8], 3, 0)
-        other = lowy_ref[(c * XN + p) * 4 : (c * XN + p) * 4 + 4, :]
+        other = lowy_ref[node_slot(c, p) * 4 : node_slot(c, p) * 4 + 4, :]
         other = jnp.concatenate([other, other], axis=0)
         value = jnp.where(row == 3, average(lower, other, mine, mine), jnp.where(row < 3, other, mine))
         return jnp.where(row < 5, value, 0.0)
 
     def high(c, p):
         mine = pltpu.roll(x_plane(own_ref, xl_ref, xh_ref, c, p)[EY - 4 : EY + 4], 5, 0)
-        other = highy_ref[(c * XN + p) * 4 : (c * XN + p) * 4 + 4, :]
+        other = highy_ref[node_slot(c, p) * 4 : node_slot(c, p) * 4 + 4, :]
         other = pltpu.roll(jnp.concatenate([other, other], axis=0), 1, 0)
         value = jnp.where(row == 1, average(upper, mine, other, mine), jnp.where(row < 1, mine, other))
         return jnp.where(row < 5, value, 0.0)
@@ -552,7 +626,7 @@
         start = jnp.where(row < 1, low, middle[0:8])
         end = jnp.where(row < 3, middle[40:48], high)
         energy = jnp.concatenate([low, start, middle[8:40], end], axis=0)
-        at = 3 * XN * 4 + x * 4
+        at = dens_slot(x) * 4
         pad = jnp.zeros((5, EZ), F32)
         d = jnp.concatenate(
             [pad, lowy_ref[at : at + 3, :], x_density(dens_ref, hd_ref, x), highy_ref[at : at + 3, :], pad[0:1]], axis=0)
@@ -580,7 +654,7 @@
 
 
 def last_kernel(g_ref, along_ref, right_ref, rs_ref, rd_ref, oa_ref, ob_ref, od_ref, lhs_ref, *refs):
-    messages, refs = refs[:-12], refs[-12:]
+    messages, refs = refs[:-11], refs[-11:]
     outs, (ez_ref, c_ref, zl_ref, zh_ref, o_ref, sem), refs = refs[:2], refs[2:8], refs[8:]
     if len(messages) > 1:
         sort_sides("gz", *messages, zl_ref, zh_ref)
@@ -605,7 +679,7 @@
         jnp.where(is_low, ob, zh1),
     )
     build_nodes(lambda c, k: nodes[k][c * XR : (c + 1) * XR], range(5), XR, refs)
-    for ref, step in zip(refs[:3], (8, 16, 16)):
+    for ref, step in zip(refs, (8, 16, 16)):
         ref[5 * XR * step : (5 * XR + 8) * step, :] = jnp.zeros((8 * step, EZ), ref.dtype)
 
     lane = iota((XR, EZ), 1)
@@ -684,7 +758,6 @@
 
 def local(local_solution, top_nodes, coarse_solution, corner_dofs, density, element_stiffness):
     dens = jnp.transpose(density, (1, 0, 2)).reshape(EY * EX, EZ)
-    dofs = corner_dofs.reshape(8)
     shared = lax.axis_size("gz") == 2
     if shared:
         other = lax.ppermute(coarse_solution, "gz", [(0, 1), (1, 0)])
@@ -693,14 +766,14 @@
         coarse = lax.all_gather(coarse_solution, "gz")
 
     message = ((X_MESSAGE, EZ), F32)
-    even, odd, tops = call(
+    even, odd, tops, dofs = call(
         pack_kernel,
-        [message, message, ((3, XR, EZ), F32)],
+        [message, message, ((3, XR, EZ), F32), ((8, EZ), F32)],
         [pltpu.HBM] * 4,
         [((2, 3, 4, NY, EZ), F32), ((3, NX, 1, NY), F32), ((EY * EX, EZ), F32), ((1, 8), jnp.int32), pltpu.SemaphoreType.DMA((9,))],
     )(*[
         pltpu.with_memory_space_constraint(value, pltpu.HBM)
-        for value in (local_solution, jnp.transpose(top_nodes, (0, 1, 3, 2)), dens, dofs.reshape(1, 8))
+        for value in (local_solution, jnp.transpose(top_nodes, (0, 1, 3, 2)), dens, corner_dofs.reshape(1, 8))
     ])
     even_x, odd_x = exchange("gx", "gy", even, odd)
 
@@ -710,30 +783,35 @@
         prepare_kernel, [rows3, rows4, rows4, own_planes, own_planes, own_planes], [VM, VM], micros=1.0
     )(element_stiffness, dens)
 
-    own, ea = call(
+    own_part = ((OWN_SLOTS * 4, EZ), F32)
+    own, ea, up_own, down_own = call(
         functools.partial(own_kernel, shared),
-        [((3 * NX, ROWS, EZ), F32), ((OWN, ROWS, EZ), F32)],
-        [VM, VM, SM, SM],
-        node_buffers((OWN + 1) * ROWS, OWN * ROWS),
+        [((3 * NX, ROWS, EZ), F32), ((OWN, ROWS, EZ), F32), own_part, own_part],
+        [VM] * 5,
+        node_buffers((OWN + 1) * ROWS),
         micros=6.0,
-    )(local_solution, lhs, coarse, dofs)
+    )(local_solution, lhs, dens, coarse, dofs)
 
     face = ((12, ROWS, EZ), F32)
     y_message = ((Y_MESSAGE, EZ), F32)
-    xl, xh, tx, even, odd, halo_dens = call(
+    halo_part = ((Y_MESSAGE - OWN_SLOTS * 4, EZ), F32)
+    tx, even, odd = call(
         functools.partial(x_kernel, shared),
-        [face, face, ((3, XR, EZ), F32), y_message, y_message, ((6, ROWS, EZ), F32)],
-        [VM, VM, VM, VM, VM, SM, SM],
-        [y_message, y_message, ((4, XR, EZ), F32)],
-        micros=2.0,
-    )(own, tops, dens, even_x, odd_x, coarse, dofs)
+        [((3, XR, EZ), F32), y_message, y_message],
+        [VM] * 8,
+        [halo_part, halo_part, ((4, XR, EZ), F32)],
+        micros=1.0,
+    )(own, up_own, down_own, tops, even_x, odd_x, coarse, dofs)
     even_y, odd_y = exchange("gy", "gz", even, odd)
 
+    xl, xh, halo_dens = call(
+        functools.partial(halo_kernel, shared), [face, face, ((6, ROWS, EZ), F32)], [VM] * 4, micros=0.7
+    )(own, even_x, odd_x, coarse)
     (eb,) = call(
-        side_kernel, [((XE - OWN, ROWS, EZ), F32)], [VM] * 4, node_buffers((XE - OWN + 2) * ROWS, (XE - 4 - OWN) * ROWS), micros=2.6
+        side_kernel, [((XE - OWN, ROWS, EZ), F32)], [VM] * 4, node_buffers((XE - OWN + 2) * ROWS), micros=2.6
     )(own, xl, xh, lhs)
 
-    (zo,) = call(turn_kernel, [((TILES, 8, EZ), F32)], [VM] * 5, micros=1.5)(own, xl, xh, dens, halo_dens)
+    (zo,) = call(turn_kernel, [((len(SLOTS), 8, EZ), F32)], [VM] * 5, micros=1.5)(own, xl, xh, dens, halo_dens)
 
     z_message = ((Z_MESSAGE, EZ), F32)
     low_y, high_y, oa, ob, od, *messages = call(
@@ -749,7 +827,7 @@
         edge_kernel,
         [((XE, 8, EZ), F32)] * 2,
         [VM] * 6,
-        node_buffers(XN * 8, XE * 8),
+        node_buffers(XN * 8),
         micros=2.3,
     )(own, xl, xh, low_y, high_y, lhs_edge)
 
@@ -763,7 +841,7 @@
         [((EY * EX, EZ), F32)] * 2,
         [VM] * (9 + len(received_z)),
         [((4, XR, EZ), F32), ((2, 4 * EX, EZ), F32), z_message, z_message, ((2, EY * EX, EZ), F32),
-         pltpu.SemaphoreType.DMA((6,))] + node_buffers(5 * XR + 8, 4 * XR),
+         pltpu.SemaphoreType.DMA((6,))] + node_buffers(5 * XR + 8),
         space=pltpu.HBM,
         micros=2.5,
     )(filtered, along_y, ends, inverse_sens, inverse_smooth, oa, ob, od, lhs_z, *received_z)

time: 28.8 us -> 27.8 us (0.965)
  the two profiles are of different devices: /device:TPU:9 before, /device:TPU:16 now
where the time goes in v6:
time: 27.8 us; the launch traced here: 27.6 us
  Pallas kernels  15.3 us (55%)
  starting transfers between devices  6.4 us (23%)
  waiting for transfers between devices  5.13 us (18%)
  between operations  0.77 us (3%)
    ppermute x5, starting transfers between devices, exchange(): results.append(lax.ppermute(value, names, moves))  4.88 us
    ppermute x5, waiting for transfers between devices, exchange(): results.append(lax.ppermute(value, names, moves))  3.86 us
    pallas_call x1, Pallas kernels, local(): call(functools.partial(own_kernel, shared), [((3 * NX, ROWS, EZ), F32), (...  3.02 us
    pallas_call x1, Pallas kernels, local(): call(side_kernel, [((XE - OWN, ROWS, EZ), F32)], [VM] * 4, node_buffers((...  2.4 us
    pallas_call x1, Pallas kernels, local(): call(last_kernel, [((EY * EX, EZ), F32)] * 2, [VM] * (9 + len(received_z)...  2.27 us
    pallas_call x1, Pallas kernels, local(): call(edge_kernel, [((XE, 8, EZ), F32)] * 2, [VM] * 6, node_buffers(XN * 8...  1.74 us
    pallas_call x1, Pallas kernels, local(): call(pack_kernel, [message, message, ((3, XR, EZ), F32), ((8, EZ), F32)],...  1.6 us
    ppermute x1, starting transfers between devices, local(): other = lax.ppermute(coarse_solution, 'gz', [(0, 1), (1, 0)])  1.52 us
  transfers between devices with their start and end apart: 6, of which 5 were waited for; matrix products, arithmetic and copies ran while one was open for 0% of the time, Pallas kernels for 38%

profile of v6, /device:TPU:16, one launch (start us, length us, event | category | flops | bytes accessed | tf_op | source)
XLA Modules:
  0.0 27.6 jit_solution(1618201798986919204)
XLA Ops:
  0.6 0.0 copy-start
  0.6 0.0 copy-start.1
  0.7 0.0 copy-start.3
  0.7 0.0 copy-start.2
  0.7 1.6 %shard_map.78 = (f32[688,128]{1,0:T(8,128)S(1)}, f32[688,128]{1,0:T(8,128)S(1)}, f32[3,24,128]{2,1,0:T(8,128)S(1)}, f32[8,128]{1,0:T(8,128)S(1)}) custom-call(f32[3,17,45,128]{3,2,1,0:T(8,128)} %local_ref.3, f32[3,17,1,45]{3,2,1,0:T(1,128)} %bitcast.15, f32[704,128]{1,0:T(8,128)} %bitcast.13, s32[1,8]{1,0:T(1,128)} %bitcast.18), custom_call_target="tpu_custom_call" | custom-call | bytes 3600000 | tf_op jit(solution)/shard_map/pallas_call | solution.py:769
  2.3 1.6 %collective-permute-start.1 = (f32[688,128]{1,0:T(8,128)S(1)}, f32[688,128]{1,0:T(8,128)S(1)}, u32[]{:S(2)}, u32[]{:S(2)}) collective-permute-start(f32[688,128]{1,0:T(8,128)S(1)} %get-tuple-element.40), channel_id=1, source_target_pairs={{0,8},{2,10},{4,12},{6,14},{8,0},{10,2},{12,4},{14,6},{16,24},{18,... | collective-permute-start | bytes 1056776 | tf_op jit(solution)/shard_map/ppermute | solution.py:755
  3.9 0.0 collective-permute-start.2
  3.9 0.0 copy-done.3
  3.9 1.5 %collective-permute-start = (f32[3,512]{1,0:T(4,128)S(1)}, f32[3,512]{1,0:T(4,128)S(1)}, u32[]{:S(2)}, u32[]{:S(2)}) collective-permute-start(f32[3,512]{1,0:T(4,128)S(1)} %copy-done.3), channel_id=1, source_target_pairs={{0,1},{1,0},{2,3},{3,2},{4,5},{5,4},{6,7},{7,6},{8,9},{9,8},{10,11... | collective-permute-start | bytes 18440 | tf_op jit(solution)/shard_map/ppermute | solution.py:763
  5.4 0.0 copy-done.1
  5.5 0.0 copy-done.2
  5.5 0.8 %shard_map.77 = (bf16[96,192]{1,0:T(8,128)(2,1)S(1)}, bf16[128,256]{1,0:T(8,128)(2,1)S(1)}, bf16[128,256]{1,0:T(8,128)(2,1)S(1)}, f32[16,48,128]{2,1,0:T(8,128)S...) custom-call(f32[24,24]{1,0:T(8,128)S(1)} %copy-done.2, f32[704,128]{1,0:T(8,128)S(1)} %bitcast.14), custom_call_target="tpu_custom_call" | custom-call | bytes 3600000 | tf_op jit(solution)/shard_map/pallas_call | solution.py:782
  6.3 1.3 %collective-permute-done = f32[3,512]{1,0:T(4,128)S(1)} collective-permute-done((f32[3,512]{1,0:T(4,128)S(1)}, f32[3,512]{1,0:T(4,128)S(1)}, u32[]{:S(2)}, u32[]{:S(2)}) %collective-permute-start) | collective-permute-done | bytes 6176 | tf_op jit(solution)/shard_map/ppermute | solution.py:763
  7.6 0.0 copy-done
  7.6 3.0 %shard_map.79 = (f32[51,48,128]{2,1,0:T(8,128)S(1)}, f32[12,48,128]{2,1,0:T(8,128)S(1)}, f32[248,128]{1,0:T(8,128)S(1)}, f32[248,128]{1,0:T(8,128)S(1)}) custom-call(f32[3,17,45,128]{3,2,1,0:T(8,128)S(1)} %copy-done, bf16[96,192]{1,0:T(8,128)(2,1)S(1)} %get-tuple-element.35.lhs_ref, f32[16,48,128]{2,1,0:T(8,128)S(1)} %get-tuple-element.36.dens_ref, ...), custom_call_target="tpu_custom_call" | custom-call | bytes 21600000 | tf_op jit(solution)/shard_map/pallas_call | solution.py:787
  10.6 1.7 %collective-permute-done.1.even_ref = f32[688,128]{1,0:T(8,128)S(1)} collective-permute-done((f32[688,128]{1,0:T(8,128)S(1)}, f32[688,128]{1,0:T(8,128)S(1)}, u32[]{:S(2)}, u32[]{:S(2)}) %collective-permute-start.1) | collective-permute-done | bytes 352288 | tf_op jit(solution)/shard_map/ppermute | solution.py:755
  12.3 1.3 %collective-permute-done.2.odd_ref = f32[688,128]{1,0:T(8,128)S(1)} collective-permute-done((f32[688,128]{1,0:T(8,128)S(1)}, f32[688,128]{1,0:T(8,128)S(1)}, u32[]{:S(2)}, u32[]{:S(2)}) %collective-permute-start.2) | collective-permute-done | bytes 352288 | tf_op jit(solution)/shard_map/ppermute | solution.py:755
  13.6 0.4 %shard_map.82 = (f32[3,24,128]{2,1,0:T(8,128)S(1)}, f32[392,128]{1,0:T(8,128)S(1)}, f32[392,128]{1,0:T(8,128)S(1)}) custom-call(f32[51,48,128]{2,1,0:T(8,128)S(1)} %get-tuple-element.39.own_ref, f32[248,128]{1,0:T(8,128)S(1)} %get-tuple-element.44.up_own_ref, f32[248,128]{1,0:T(8,128)S(1)} %get-tuple-element.45.down_own_ref, ...), custom_call_target="tpu_custom_call" | custom-call | bytes 3600000 | tf_op jit(solution)/shard_map/pallas_call | solution.py:798
  14.1 0.1 collective-permute-start.3
  14.1 1.6 %collective-permute-start.4 = (f32[392,128]{1,0:T(8,128)S(1)}, f32[392,128]{1,0:T(8,128)S(1)}, u32[]{:S(2)}, u32[]{:S(2)}) collective-permute-start(f32[392,128]{1,0:T(8,128)S(1)} %get-tuple-element.50), channel_id=1, source_target_pairs={{0,1},{1,0},{2,4},{3,5},{4,2},{5,3},{6,7},{7,6},{8,9},{9,8},{10,12... | collective-permute-start | bytes 602120 | tf_op jit(solution)/shard_map/ppermute | solution.py:755
  15.7 0.4 %shard_map.80 = (f32[12,48,128]{2,1,0:T(8,128)S(1)}, f32[12,48,128]{2,1,0:T(8,128)S(1)}, f32[6,48,128]{2,1,0:T(8,128)S(1)}) custom-call(f32[51,48,128]{2,1,0:T(8,128)S(1)} %get-tuple-element.39.own_ref, f32[688,128]{1,0:T(8,128)S(1)} %collective-permute-done.1.even_ref, f32[688,128]{1,0:T(8,128)S(1)} %collective-permute-done.2.odd_ref, ...), custom_call_target="tpu_custom_call" | custom-call | bytes 2520000 | tf_op jit(solution)/shard_map/pallas_call | solution.py:807
  16.1 2.4 %shard_map.81.eb_ref = f32[10,48,128]{2,1,0:T(8,128)S(1)} custom-call(f32[51,48,128]{2,1,0:T(8,128)S(1)} %get-tuple-element.39.own_ref, f32[12,48,128]{2,1,0:T(8,128)S(1)} %get-tuple-element.42.xl_ref, f32[12,48,128]{2,1,0:T(8,128)S(1)} %get-tuple-element.43.xh_ref, bf16[96,192]{1,0:T(8,128)(2,1)S(1)} %get-tuple-element.35.lhs_ref), custom_call_target="tpu_custom_call" | custom-call | bytes 9360000 | tf_op jit(solution)/shard_map/pallas_call | solution.py:810
  18.5 0.9 %shard_map.83.zo_ref = f32[92,8,128]{2,1,0:T(8,128)S(1)} custom-call(f32[51,48,128]{2,1,0:T(8,128)S(1)} %get-tuple-element.39.own_ref, f32[12,48,128]{2,1,0:T(8,128)S(1)} %get-tuple-element.42.xl_ref, f32[12,48,128]{2,1,0:T(8,128)S(1)} %get-tuple-element.43.xh_ref, f32[16,48,128]{2,1,0:T(8,128)S(1)} %get-tuple-element.36.dens_ref, ...), custom_call_target="tpu_custom_call" | custom-call | bytes 5400000 | tf_op jit(solution)/shard_map/pallas_call | solution.py:814
  19.4 0.0 collective-permute-done.3.even_ref
  19.4 0.5 %collective-permute-done.4.odd_ref = f32[392,128]{1,0:T(8,128)S(1)} collective-permute-done((f32[392,128]{1,0:T(8,128)S(1)}, f32[392,128]{1,0:T(8,128)S(1)}, u32[]{:S(2)}, u32[]{:S(2)}) %collective-permute-start.4) | collective-permute-done | bytes 200736 | tf_op jit(solution)/shard_map/ppermute | solution.py:755
  19.9 0.5 %shard_map.84 = (f32[392,128]{1,0:T(8,128)S(1)}, f32[392,128]{1,0:T(8,128)S(1)}, f32[72,128]{1,0:T(8,128)S(1)}, f32[72,128]{1,0:T(8,128)S(1)}, f32[24,128]{1,0:T(8,128)S(1)}, /*index=5*/f32[192,128]{1,0:T(8,128)S(1)}) custom-call(f32[3,24,128]{2,1,0:T(8,128)S(1)} %get-tuple-element.47.tx_ref, f32[92,8,128]{2,1,0:T(8,128)S(1)} %shard_map.83.zo_ref, ...), custom_call_target="tpu_custom_call" | custom-call | bytes 3600000 | tf_op jit(solution)/shard_map/pallas_call | solution.py:817
  20.5 1.6 %collective-permute-start.5 = (f32[192,128]{1,0:T(8,128)S(1)}, f32[192,128]{1,0:T(8,128)S(1)}, u32[]{:S(2)}, u32[]{:S(2)}) collective-permute-start(f32[192,128]{1,0:T(8,128)S(1)} %get-tuple-element.65), channel_id=1, source_target_pairs={{0,1},{2,3},{4,5},{6,7},{1,0},{3,2},{5,4},{7,6},{8,9},{10,11},{12,... | collective-permute-start | bytes 294920 | tf_op jit(solution)/shard_map/ppermute | solution.py:755
  22.0 1.7 %shard_map.85 = (f32[22,8,128]{2,1,0:T(8,128)S(1)}, f32[22,8,128]{2,1,0:T(8,128)S(1)}) custom-call(f32[51,48,128]{2,1,0:T(8,128)S(1)} %get-tuple-element.39.own_ref, f32[12,48,128]{2,1,0:T(8,128)S(1)} %get-tuple-element.42.xl_ref, f32[12,48,128]{2,1,0:T(8,128)S(1)} %get-tuple-element.43.xh_ref, f32[392,128]{1,0:T(8,128)S(1)} %get-tuple-element.51.lowy_ref, ...), custom_call_target="tpu_custom_call" | custom-call | bytes 8279999 | tf_op jit(solution)/shard_map/pallas_call | solution.py:826
  23.8 1.2 %shard_map.86 = (f32[2,16,48,128]{3,2,1,0:T(8,128)S(1)}, bf16[128,128]{1,0:T(8,128)(2,1)S(1)}, bf16[128,128]{1,0:T(8,128)(2,1)S(1)}) custom-call(f32[12,48,128]{2,1,0:T(8,128)S(1)} %get-tuple-element.38.ea_ref, f32[10,48,128]{2,1,0:T(8,128)S(1)} %shard_map.81.eb_ref, f32[22,8,128]{2,1,0:T(8,128)S(1)} %get-tuple-element.54.el_ref, ...), custom_call_target="tpu_custom_call" | custom-call | bytes 5400000 | tf_op jit(solution)/shard_map/pallas_call | solution.py:835
  25.0 0.4 %collective-permute-done.5.refs_0_ = f32[192,128]{1,0:T(8,128)S(1)} collective-permute-done((f32[192,128]{1,0:T(8,128)S(1)}, f32[192,128]{1,0:T(8,128)S(1)}, u32[]{:S(2)}, u32[]{:S(2)}) %collective-permute-start.5) | collective-permute-done | bytes 98336 | tf_op jit(solution)/shard_map/ppermute | solution.py:755
  25.3 2.3 %shard_map.87 = (f32[704,128]{1,0:T(8,128)}, f32[704,128]{1,0:T(8,128)}) custom-call(f32[2,16,48,128]{3,2,1,0:T(8,128)S(1)} %get-tuple-element.56.g_ref, bf16[128,128]{1,0:T(8,128)(2,1)S(1)} %get-tuple-element.57.along_ref, bf16[128,128]{1,0:T(8,128)(2,1)S(1)} %get-tuple-element.58.right_ref, f32[16,48,128]{2,1,0:T(8,128)S(1)} %get-tuple-element.59.rs_ref, ...), custom_call_target="tpu_custom_call" | custom-call | bytes 9000000 | tf_op jit(solution)/shard_map/pallas_call | solution.py:839
  (1 shorter events, 0.0 us)
Async XLA Ops:
  0.6 7.0 %copy-start = (f32[3,17,45,128]{3,2,1,0:T(8,128)S(1)}, f32[3,17,45,128]{3,2,1,0:T(8,128)}, u32[]{:S(2)}) copy-start(f32[3,17,45,128]{3,2,1,0:T(8,128)} %local_ref.3) | copy-start | bytes 3525124
  0.6 4.8 %copy-start.1 = (f32[16,44,128]{2,0,1:T(8,128)S(1)}, f32[16,44,128]{2,0,1:T(8,128)}, u32[]{:S(2)}) copy-start(f32[16,44,128]{2,0,1:T(8,128)} %param.10) | copy-start | bytes 1081348
  0.7 3.3 %copy-start.3 = (f32[3,512]{1,0:T(4,128)S(1)}, f32[3,512]{1,0:T(4,128)}, u32[]{:S(2)}) copy-start(f32[3,512]{1,0:T(4,128)} %param.8) | copy-start | bytes 18436
  0.7 4.8 %copy-start.2 = (f32[24,24]{1,0:T(8,128)S(1)}, f32[24,24]{1,0:T(8,128)}, u32[]{:S(2)}) copy-start(f32[24,24]{1,0:T(8,128)} %stiff_ref.1) | copy-start | bytes 6916
  2.3 10.0 %collective-permute-start.1 = (f32[688,128]{1,0:T(8,128)S(1)}, f32[688,128]{1,0:T(8,128)S(1)}, u32[]{:S(2)}, u32[]{:S(2)}) collective-permute-start(f32[688,128]{1,0:T(8,128)S(1)} %get-tuple-element.40), channel_id=1, source_target_pairs={{0,8},{2,10},{4,12},{6,14},{8,0},{10,2},{12,4},{14,6},{16,24},{18,... | collective-permute-start | bytes 1056776 | tf_op jit(solution)/shard_map/ppermute | solution.py:755
  3.9 9.7 %collective-permute-start.2 = (f32[688,128]{1,0:T(8,128)S(1)}, f32[688,128]{1,0:T(8,128)S(1)}, u32[]{:S(2)}, u32[]{:S(2)}) collective-permute-start(f32[688,128]{1,0:T(8,128)S(1)} %get-tuple-element.41), channel_id=1, source_target_pairs={{0,2},{2,0},{4,6},{6,4},{8,16},{10,18},{12,20},{14,22},{16,8},{18,... | collective-permute-start | bytes 1056776 | tf_op jit(solution)/shard_map/ppermute | solution.py:755
  3.9 3.7 %collective-permute-start = (f32[3,512]{1,0:T(4,128)S(1)}, f32[3,512]{1,0:T(4,128)S(1)}, u32[]{:S(2)}, u32[]{:S(2)}) collective-permute-start(f32[3,512]{1,0:T(4,128)S(1)} %copy-done.3), channel_id=1, source_target_pairs={{0,1},{1,0},{2,3},{3,2},{4,5},{5,4},{6,7},{7,6},{8,9},{9,8},{10,11... | collective-permute-start | bytes 18440 | tf_op jit(solution)/shard_map/ppermute | solution.py:763
  14.1 5.4 %collective-permute-start.3 = (f32[392,128]{1,0:T(8,128)S(1)}, f32[392,128]{1,0:T(8,128)S(1)}, u32[]{:S(2)}, u32[]{:S(2)}) collective-permute-start(f32[392,128]{1,0:T(8,128)S(1)} %get-tuple-element.49), channel_id=1, source_target_pairs={{0,2},{1,3},{2,0},{3,1},{4,6},{5,7},{6,4},{7,5},{8,10},{9,11},{10,... | collective-permute-start | bytes 602120 | tf_op jit(solution)/shard_map/ppermute | solution.py:755
  14.1 5.8 %collective-permute-start.4 = (f32[392,128]{1,0:T(8,128)S(1)}, f32[392,128]{1,0:T(8,128)S(1)}, u32[]{:S(2)}, u32[]{:S(2)}) collective-permute-start(f32[392,128]{1,0:T(8,128)S(1)} %get-tuple-element.50), channel_id=1, source_target_pairs={{0,1},{1,0},{2,4},{3,5},{4,2},{5,3},{6,7},{7,6},{8,9},{9,8},{10,12... | collective-permute-start | bytes 602120 | tf_op jit(solution)/shard_map/ppermute | solution.py:755
  20.5 4.9 %collective-permute-start.5 = (f32[192,128]{1,0:T(8,128)S(1)}, f32[192,128]{1,0:T(8,128)S(1)}, u32[]{:S(2)}, u32[]{:S(2)}) collective-permute-start(f32[192,128]{1,0:T(8,128)S(1)} %get-tuple-element.65), channel_id=1, source_target_pairs={{0,1},{2,3},{4,5},{6,7},{1,0},{3,2},{5,4},{7,6},{8,9},{10,11},{12,... | collective-permute-start | bytes 294920 | tf_op jit(solution)/shard_map/ppermute | solution.py:755

commit v7 on v6

--- a/solution.py
+++ b/solution.py
@@ -192,28 +192,21 @@
     return spare + [(X_DENSITY + EY, 36, 4), (X_DENSITY + ROWS + EY, 40, 4)]
 
 
-def pack_kernel(local_ref, top_ref, dens_ref, dofs_ref, even_ref, odd_ref, tops_ref, dofs_out_ref, l_ref, t_ref, d_ref, c_ref, sem):
+def pack_kernel(local_ref, top_ref, dens_ref, dofs_ref, even_ref, odd_ref, tops_ref, l_ref, t_ref, d_ref, c_ref, sem):
     copies = []
-    for side, node in ((0, EX - RADIUS), (1, 0)):
-        for c in range(3):
-            copies.append(pltpu.make_async_copy(local_ref.at[c, node : node + 4], l_ref.at[side, c], sem.at[len(copies)]))
     for source, dest in ((top_ref, t_ref), (dofs_ref, c_ref), (dens_ref, d_ref)):
         copies.append(pltpu.make_async_copy(source, dest, sem.at[len(copies)]))
+    for c in range(3):
+        for side, node in ((0, EX - RADIUS), (1, 0)):
+            copies.append(pltpu.make_async_copy(local_ref.at[c, node : node + 4], l_ref.at[side, c], sem.at[len(copies)]))
     for copy in copies:
         copy.start()
     for out_ref in (even_ref, odd_ref):
         out_ref[X_TOP:X_MESSAGE, :] = jnp.zeros((X_MESSAGE - X_TOP, EZ), F32)
     clear(tops_ref)
-    odd = odd_place("gx")
-    outs = ((even_ref, odd), (odd_ref, jnp.logical_not(odd)))
-    for copy in copies[:6]:
-        copy.wait()
-    for out_ref, flip in outs:
-        side = flip.astype(jnp.int32)
-        for c in range(3):
-            for j in range(4):
-                out_ref[(c * 4 + j) * ROWS : (c * 4 + j) * ROWS + NY, :] = l_ref[side, c, j]
-    for copy in copies[6:]:
+    flip = odd_place("gx")
+    outs = ((even_ref, flip), (odd_ref, jnp.logical_not(flip)))
+    for copy in copies[:3]:
         copy.wait()
     for c in range(3):
         for i in range(NX):
@@ -230,7 +223,13 @@
                 for at, first, count in third_rows():
                     out_ref[at : at + count, :] = value[first : first + count]
         out_ref[X_DOFS : X_DOFS + 1, 0:8] = c_ref[...].astype(F32)
-    dofs_out_ref[...] = jnp.broadcast_to(as_column(even_ref[X_DOFS : X_DOFS + 1, :]), (8, EZ))
+    for c in range(3):
+        for copy in copies[3 + 2 * c : 5 + 2 * c]:
+            copy.wait()
+        for out_ref, flip in outs:
+            side = flip.astype(jnp.int32)
+            for j in range(4):
+                out_ref[(c * 4 + j) * ROWS : (c * 4 + j) * ROWS + NY, :] = l_ref[side, c, j]
 
 
 def sort_sides(axis, even_ref, odd_ref, low_ref, high_ref):
@@ -240,8 +239,20 @@
     high_ref[...] = jnp.where(has_upper(axis), jnp.where(odd, other, even), 0.0)
 
 
-def prepare_kernel(stiff_ref, dens_ref, lhs_ref, lhs_edge_ref, lhs_z_ref, od_ref, rs_ref, rd_ref):
+def prepare_kernel(stiff_ref, dens_ref, dofs_in_ref, lhs_ref, lhs_edge_ref, lhs_z_ref, od_ref, rs_ref, rd_ref,
+                   dofs_ref, along_ref, right_ref, row_ref):
     stiff = stiff_ref[...]
+    clear(row_ref)
+    row_ref[0:1, 0:8] = dofs_in_ref[...].astype(F32)
+    dofs_ref[...] = jnp.broadcast_to(as_column(row_ref[0:1, :]), (8, EZ))
+    k, col = iota((EZ, EZ), 0), iota((EZ, EZ), 1)
+    along_ref[...] = jnp.where(k // 64 == col // 64, weights(k - col), 0.0).astype(BF16)
+    j = (k % 64) // EX
+    weight = weights(jnp.where(k < 64, j - 3, EZ - 1 + j) - col)
+    for x in range(EX):
+        part = jnp.where(k % EX == x, weight, 0.0).astype(BF16)
+        right_ref[0:EZ, x * EZ : (x + 1) * EZ] = part
+        right_ref[EZ : 2 * EZ, x * EZ : (x + 1) * EZ] = part
     lhs_ref[...] = stiffness_rows(stiff, 3, False)
     lhs_edge_ref[...] = stiffness_rows(stiff, 4, False)
     lhs_z_ref[...] = stiffness_rows(stiff, 4, True)
@@ -269,14 +280,13 @@
             own_ref[c * NX + i, 0:NY, :] = local_ref[c, i] + plane_interp(edges, i, NY)
             own_ref[c * NX + i, NY:ROWS, :] = jnp.zeros((ROWS - NY, EZ), F32)
     for out_ref, first in ((up_ref, EY - RADIUS), (down_ref, 0)):
-        out_ref[61 * 4 : OWN_SLOTS * 4, :] = jnp.zeros((4, EZ), F32)
-        for slot in range(61):
-            kind, c, p = SLOTS[slot]
-            if kind == "node":
-                out_ref[slot * 4 : slot * 4 + 4, :] = own_ref[c * NX + p - 3, first : first + 4, :]
-            else:
-                out_ref[slot * 4 : slot * 4 + 3, :] = dens_ref[c - 3, first : first + 3, :]
-                out_ref[slot * 4 + 3 : slot * 4 + 4, :] = jnp.zeros((1, EZ), F32)
+        out_ref[OWN_ROWS - 4 : OWN_ROWS, :] = jnp.zeros((4, EZ), F32)
+        for p in range(4, 19):
+            for c in range(3):
+                at = node_row(c, p)
+                out_ref[at : at + 4, :] = own_ref[c * NX + p - 3, first : first + 4, :]
+        for x in range(3, 19):
+            out_ref[dens_row(x) : dens_row(x) + 3, :] = dens_ref[x - 3, first : first + 3, :]
     build_nodes(lambda c, p: own_ref[c * NX + p + 1], range(OWN + 1), ROWS, refs)
     blocks = [(p, r) for p in range(OWN) for r in range(1, EY - 1, 3)]
     energy_planes(lhs_ref[...], 3, refs, e_ref, 0, OWN, ROWS, blocks, 0)
@@ -290,29 +300,27 @@
     return jnp.where(flag, 0.5 * low + 0.5 * high, own)
 
 
-OWN_SLOTS = 62
-
-
-def node_slot(c, p):
+OWN_ROWS = 232
+TOP_AT = 352
+Y_MESSAGE = TOP_AT + 8
+
+
+def node_row(c, p):
     if 4 <= p < 19:
-        return c * 15 + p - 4
-    return OWN_SLOTS + c * 8 + (p if p < 4 else p - 15)
-
-
-def dens_slot(x):
+        return 4 * (c * 15 + p - 4)
+    return OWN_ROWS + 4 * (c * 8 + (p if p < 4 else p - 15))
+
+
+def dens_row(x):
     if 3 <= x < 19:
-        return 45 + x - 3
-    return OWN_SLOTS + 24 + (x if x < 3 else x - 16)
-
-
-SLOTS = [None] * (OWN_SLOTS + 30)
-for _x in range(XE):
-    SLOTS[dens_slot(_x)] = ("density", _x, 0)
-for _p in range(XN):
-    for _c in range(3):
-        SLOTS[node_slot(_c, _p)] = ("node", _c, _p)
-TOP_AT = 4 * len(SLOTS)
-Y_MESSAGE = TOP_AT + XR
+        return 180 + 3 * (x - 3)
+    return OWN_ROWS + 96 + 3 * (x if x < 3 else x - 16)
+
+
+SLOTS = sorted(
+    [("node", c, p) for c in range(3) for p in range(XN)] + [("density", x, x) for x in range(XE)],
+    key=lambda slot: node_row(*slot[1:]) if slot[0] == "node" else dens_row(slot[1]),
+)
 
 
 def has_lower(axis):
@@ -333,13 +341,13 @@
 
 
 def x_sides(even_ref, odd_ref):
-    odd = odd_place("gx")
+    flip = odd_place("gx")
 
     def low(at, count):
-        return jnp.where(odd, even_ref[at : at + count, :], odd_ref[at : at + count, :])
+        return jnp.where(flip, even_ref[at : at + count, :], odd_ref[at : at + count, :])
 
     def high(at, count):
-        return jnp.where(odd, odd_ref[at : at + count, :], even_ref[at : at + count, :])
+        return jnp.where(flip, odd_ref[at : at + count, :], even_ref[at : at + count, :])
 
     return low, high
 
@@ -390,7 +398,7 @@
     lower, upper = has_lower("gx"), has_upper("gx")
     for out_ref, start, skip in ((up_ref, EY - 4, 1), (down_ref, 0, 0)):
         for c, p, value in x_faces(own_ref, sides, (corners_low, corners_high), start, 8):
-            at = (node_slot(c, p) - OWN_SLOTS) * 4
+            at = node_row(c, p) - OWN_ROWS
             out_ref[at : at + 4, :] = value[skip : skip + 4]
         for x in (0, 1, 2, 19, 20, 21):
             j, side, there = (x, low_rows, lower) if x < 3 else (x - 19, high_rows, upper)
@@ -399,9 +407,9 @@
                 value = side(X_DENSITY + j * ROWS + row, 3)
             else:
                 value = side(NY if row == 0 else X_DENSITY + ROWS + EY + 1, 3)
-            at = (dens_slot(x) - OWN_SLOTS) * 4
+            at = dens_row(x) - OWN_ROWS
             out_ref[at : at + 3, :] = jnp.where(there, value, 0.0)
-            out_ref[at + 3 : at + 4, :] = jnp.zeros((1, EZ), F32)
+        out_ref[TOP_AT - 6 - OWN_ROWS : TOP_AT - OWN_ROWS, :] = jnp.zeros((6, EZ), F32)
 
     t_ref[...] = jnp.zeros(t_ref.shape, F32)
     for c in range(3):
@@ -426,12 +434,12 @@
         for c in range(3):
             moved = pltpu.roll(tx_ref[c], (4 * c - lane_at) % EZ, 1)
             total = jnp.where((lane >= 4 * c) & (lane < 4 * c + 4), moved, total)
-        out_ref[TOP_AT - OWN_SLOTS * 4 :, :] = total
+        out_ref[TOP_AT - OWN_ROWS :, :] = total[0:8] + pltpu.roll(total[8:16], 16, 1) + pltpu.roll(total[16:24], 32, 1)
     odd = odd_place("gy")
     for mine, other, out_ref in ((up_own_ref, down_own_ref, yeven_ref), (down_own_ref, up_own_ref, yodd_ref)):
-        out_ref[0 : OWN_SLOTS * 4, :] = jnp.where(odd, other[...], mine[...])
+        out_ref[0:OWN_ROWS, :] = jnp.where(odd, other[...], mine[...])
     for mine, other, out_ref in ((up_ref, down_ref, yeven_ref), (down_ref, up_ref, yodd_ref)):
-        out_ref[OWN_SLOTS * 4 :, :] = jnp.where(odd, other[...], mine[...])
+        out_ref[OWN_ROWS:, :] = jnp.where(odd, other[...], mine[...])
 
 
 def side_kernel(own_ref, xl_ref, xh_ref, lhs_ref, e_ref, *refs):
@@ -448,7 +456,7 @@
         energy_planes(lhs_ref[...], 3, refs, e_ref, first, count, ROWS, blocks, out_first)
 
 
-Z_MESSAGE = 192
+Z_MESSAGE = 184
 
 
 def x_plane(own_ref, xl_ref, xh_ref, c, p):
@@ -475,7 +483,7 @@
     head = jnp.zeros((8, EZ), F32)
 
     def padded(slot):
-        kind, c, p = SLOTS[slot] or SLOTS[0]
+        kind, c, p = SLOTS[min(slot, len(SLOTS) - 1)]
         if kind == "node":
             return [head, x_plane(own_ref, xl_ref, xh_ref, c, p), head]
         return [head, x_density(dens_ref, hd_ref, c, ROWS), head]
@@ -484,7 +492,8 @@
     for slot in range(0, len(SLOTS), 2):
         both = end_planes(jnp.concatenate(padded(slot) + padded(slot + 1), axis=0).T)
         z_ref[slot] = jnp.where(lane < 64, both, 0.0)
-        z_ref[slot + 1] = jnp.where(lane < 64, pltpu.roll(both, 64, 1), 0.0)
+        if slot + 1 < len(SLOTS):
+            z_ref[slot + 1] = jnp.where(lane < 64, pltpu.roll(both, 64, 1), 0.0)
 
 
 def y_kernel(tx_ref, zo_ref, eb_ref, even_ref, odd_ref,
@@ -496,36 +505,36 @@
     clear(z_ref)
     clear(d_ref)
     lane = iota((8, EZ), 1)
-    for first in range(0, len(SLOTS), 32):
-        count = min(32, len(SLOTS) - first)
-        turned = []
+    turned = []
+    for first in range(0, TOP_AT, EZ):
+        turned.append([])
         for ref in (low_ref, high_ref):
-            block = ref[first * 4 : (first + count) * 4, :]
-            if count < 32:
-                block = jnp.concatenate([block, jnp.zeros(((32 - count) * 4, EZ), F32)], axis=0)
-            turned.append(end_planes(block.T))
-        for t in range(count):
-            if SLOTS[first + t] is None:
-                continue
-            kind, c, p = SLOTS[first + t]
-            low = pltpu.roll(turned[0], (5 - 4 * t) % EZ, 1)
-            high = pltpu.roll(turned[1], (52 - 4 * t) % EZ, 1)
-            mine = zo_ref[first + t]
-            value = jnp.where((lane >= 5) & (lane < 8), low, mine)
-            if kind == "node":
-                at = c * XR + p
-                value = jnp.where((lane == 8) & lower, 0.5 * low + 0.5 * mine, value)
-                value = jnp.where((lane == 52) & upper, 0.5 * mine + 0.5 * high, value)
-                z_ref[at * 8 : at * 8 + 8, :] = jnp.where((lane > 52) & (lane < 56), high, value)
-            else:
-                d_ref[c * 8 : c * 8 + 8, :] = jnp.where((lane >= 52) & (lane < 55), high, value)
+            block = ref[first : min(first + EZ, TOP_AT), :]
+            if block.shape[0] < EZ:
+                block = jnp.concatenate([block, jnp.zeros((EZ - block.shape[0], EZ), F32)], axis=0)
+            turned[-1].append(end_planes(block.T))
+    for slot, (kind, c, p) in enumerate(SLOTS):
+        at = node_row(c, p) if kind == "node" else dens_row(c)
+        low = pltpu.roll(turned[at // EZ][0], (5 - at) % EZ, 1)
+        high = pltpu.roll(turned[at // EZ][1], (52 - at) % EZ, 1)
+        mine = zo_ref[slot]
+        value = jnp.where((lane >= 5) & (lane < 8), low, mine)
+        if kind == "node":
+            at = c * XR + p
+            value = jnp.where((lane == 8) & lower, 0.5 * low + 0.5 * mine, value)
+            value = jnp.where((lane == 52) & upper, 0.5 * mine + 0.5 * high, value)
+            z_ref[at * 8 : at * 8 + 8, :] = jnp.where((lane > 52) & (lane < 56), high, value)
+        else:
+            d_ref[c * 8 : c * 8 + 8, :] = jnp.where((lane >= 52) & (lane < 55), high, value)
 
     lane = iota((XR, EZ), 1)
     tops = []
     for c in range(3):
         mine = tx_ref[c]
-        low = pltpu.roll(low_ref[TOP_AT:Y_MESSAGE, :], (5 - 4 * c) % EZ, 1)
-        high = pltpu.roll(high_ref[TOP_AT:Y_MESSAGE, :], (52 - 4 * c) % EZ, 1)
+        low, high = [
+            jnp.concatenate([pltpu.roll(ref[TOP_AT:Y_MESSAGE, :], (to - 4 * c - 16 * g) % EZ, 1) for g in range(3)], axis=0)
+            for ref, to in ((low_ref, 5), (high_ref, 52))
+        ]
         value = jnp.where((lane >= 5) & (lane < 8), low, mine)
         value = jnp.where(lane == 8, average(lower, low, mine, mine), value)
         value = jnp.where(lane == 52, average(upper, mine, high, mine), value)
@@ -540,6 +549,9 @@
 
     def pack(low, high):
         return low + pltpu.roll(high, 64, 1)
+
+    def fold(value):
+        return jnp.concatenate([pack(value[0:8], value[8:16]), value[16:24]], axis=0)
 
     oa_ref[...] = pack(nodes(0), top)
     ob_ref[...] = pack(nodes(1), nodes(7))
@@ -547,11 +559,11 @@
     up_ref[0:72, :] = pack(nodes(5), nodes(6))
     up_ref[72:144, :] = pack(nodes(7), top)
     up_ref[144:168, :] = pack(dens(5), dens(6))
-    up_ref[168:192, :] = dens(7)
+    up_ref[168:184, :] = fold(dens(7))
     down_ref[0:72, :] = pack(nodes(0), nodes(1))
     down_ref[72:144, :] = pack(nodes(2), nodes(3))
     down_ref[144:168, :] = pack(dens(0), dens(1))
-    down_ref[168:192, :] = dens(2)
+    down_ref[168:184, :] = fold(dens(2))
     odd = odd_place("gz")
     refs[0][...] = jnp.where(odd, down_ref[...], up_ref[...])
     if len(refs) > 5:
@@ -564,14 +576,14 @@
 
     def low(c, p):
         mine = pltpu.roll(x_plane(own_ref, xl_ref, xh_ref, c, p)[0:8], 3, 0)
-        other = lowy_ref[node_slot(c, p) * 4 : node_slot(c, p) * 4 + 4, :]
+        other = lowy_ref[node_row(c, p) : node_row(c, p) + 4, :]
         other = jnp.concatenate([other, other], axis=0)
         value = jnp.where(row == 3, average(lower, other, mine, mine), jnp.where(row < 3, other, mine))
         return jnp.where(row < 5, value, 0.0)
 
     def high(c, p):
         mine = pltpu.roll(x_plane(own_ref, xl_ref, xh_ref, c, p)[EY - 4 : EY + 4], 5, 0)
-        other = highy_ref[node_slot(c, p) * 4 : node_slot(c, p) * 4 + 4, :]
+        other = highy_ref[node_row(c, p) : node_row(c, p) + 4, :]
         other = pltpu.roll(jnp.concatenate([other, other], axis=0), 1, 0)
         value = jnp.where(row == 1, average(upper, mine, other, mine), jnp.where(row < 1, mine, other))
         return jnp.where(row < 5, value, 0.0)
@@ -608,8 +620,7 @@
     return total
 
 
-def field_kernel(ea_ref, eb_ref, el_ref, eh_ref, dens_ref, hd_ref, lowy_ref, highy_ref,
-                 g_ref, along_ref, right_ref, f_ref):
+def field_kernel(ea_ref, eb_ref, el_ref, eh_ref, dens_ref, hd_ref, lowy_ref, highy_ref, g_ref, f_ref):
     rows = iota((QROWS, EZ), 0)
     lanes = iota((QROWS, EZ), 1)
     ok = (rows >= 5) & (rows < 55) & (lanes > 0) & (lanes < EZ - 1)
@@ -626,7 +637,7 @@
         start = jnp.where(row < 1, low, middle[0:8])
         end = jnp.where(row < 3, middle[40:48], high)
         energy = jnp.concatenate([low, start, middle[8:40], end], axis=0)
-        at = dens_slot(x) * 4
+        at = dens_row(x)
         pad = jnp.zeros((5, EZ), F32)
         d = jnp.concatenate(
             [pad, lowy_ref[at : at + 3, :], x_density(dens_ref, hd_ref, x), highy_ref[at : at + 3, :], pad[0:1]], axis=0)
@@ -642,11 +653,6 @@
             for x in range(EX):
                 f_ref[f, x, at, :] = line[x]
     k, col = iota((EZ, EZ), 0), iota((EZ, EZ), 1)
-    along_ref[...] = jnp.where(k // 64 == col // 64, weights(k - col), 0.0).astype(BF16)
-    j = (k % 64) // EX
-    place = jnp.where(k < 64, j - 3, EZ - 1 + j)
-    z = jnp.where(col % 8 < 4, EZ - 4 + col % 8, col % 8 - 4)
-    right_ref[...] = jnp.where(k % EX == col // 8, weights(place - z), 0.0).astype(BF16)
     right = weights(k - col).astype(BF16)
     for f in range(2):
         for x in range(EX):
@@ -654,8 +660,8 @@
 
 
 def last_kernel(g_ref, along_ref, right_ref, rs_ref, rd_ref, oa_ref, ob_ref, od_ref, lhs_ref, *refs):
-    messages, refs = refs[:-11], refs[-11:]
-    outs, (ez_ref, c_ref, zl_ref, zh_ref, o_ref, sem), refs = refs[:2], refs[2:8], refs[8:]
+    messages, refs = refs[:-12], refs[-12:]
+    outs, (ez_ref, c_ref, zl_ref, zh_ref, e_ref, o_ref, sem), refs = refs[:2], refs[2:9], refs[9:]
     if len(messages) > 1:
         sort_sides("gz", *messages, zl_ref, zh_ref)
     else:
@@ -685,8 +691,10 @@
     lane = iota((XR, EZ), 1)
     low_side = lane < 64
     od = od_ref[...]
-    dl0, dl1 = zl_ref[144:168, :], zl_ref[168:192, :]
-    dh0, dh1 = zh_ref[144:168, :], zh_ref[168:192, :]
+    dl0, dh0 = zl_ref[144:168, :], zh_ref[144:168, :]
+    dl1, dh1 = [
+        jnp.concatenate([ref[168:176, :], swap(ref[168:176, :]), ref[176:184, :]], axis=0) for ref in (zl_ref, zh_ref)
+    ]
     dens = (
         jnp.where(low_side, dl0, od),
         jnp.where(low_side, swap(dl0), swap(dh0)),
@@ -694,10 +702,8 @@
         jnp.where(low_side, od, swap(dh1)),
     )
     inside = (lane % 64 >= 5) & (lane % 64 < 55) & (iota((XR, EZ), 0) < XE)
-    lanes = iota((16, EZ), 1)
-    at_end = (lanes < 4) | (lanes >= EZ - 4)
     energy_planes(lhs_ref[...], 4, refs, ez_ref, 0, 4, XR, [(j, x) for j in range(4) for x in range(0, XR, 4)], 0)
-    ends = []
+    parts = []
     for f in range(2):
         for j in range(4):
             d = dens[j]
@@ -705,13 +711,16 @@
             c_ref[f, j * EX : (j + 1) * EX, :] = triangle_forward(jnp.where(inside, value, 0.0))[0:EX]
         turned = split_dot(c_ref[f], along_ref[...])
         turned = jnp.concatenate([turned, jnp.zeros((EZ - 4 * EX, EZ), F32)], axis=0).T
-        ends.append(split_dot(turned[8:56] + pltpu.roll(turned[72:120], 64, 1), right_ref[...]))
+        parts.append(jnp.concatenate(halves(turned[8:56] + pltpu.roll(turned[72:120], 64, 1)), axis=1))
+    both = jnp.concatenate(parts, axis=0)
+    for x in range(0, EX, 2):
+        e_ref[:, x * EZ : (x + 2) * EZ] = jnp.dot(both, right_ref[:, x * EZ : (x + 2) * EZ], preferred_element_type=F32)
     copies = []
     for y in (0, 16, 32):
         count = min(16, EY - y)
         for f, inverse_ref in ((0, rs_ref), (1, rd_ref)):
             for x in range(EX):
-                end = jnp.where(at_end, pltpu.roll(ends[f][y : y + 16], (EZ - 4 - 8 * x) % EZ, 1), 0.0)
+                end = e_ref[f * ROWS + y : f * ROWS + y + 16, x * EZ : (x + 1) * EZ]
                 value = (g_ref[f, x, y : y + 16, :] + end) * inverse_ref[x, y : y + 16, :]
                 o_ref[f, pl.ds(y * EX + x, count, stride=EX), :] = value[0:count]
             block = pl.ds(y * EX, count * EX)
@@ -766,9 +775,9 @@
         coarse = lax.all_gather(coarse_solution, "gz")
 
     message = ((X_MESSAGE, EZ), F32)
-    even, odd, tops, dofs = call(
+    even, odd, tops = call(
         pack_kernel,
-        [message, message, ((3, XR, EZ), F32), ((8, EZ), F32)],
+        [message, message, ((3, XR, EZ), F32)],
         [pltpu.HBM] * 4,
         [((2, 3, 4, NY, EZ), F32), ((3, NX, 1, NY), F32), ((EY * EX, EZ), F32), ((1, 8), jnp.int32), pltpu.SemaphoreType.DMA((9,))],
     )(*[
@@ -779,11 +788,15 @@
 
     own_planes = ((EX, ROWS, EZ), F32)
     rows3, rows4 = ((96, block_rows(3)), BF16), ((128, block_rows(4)), BF16)
-    lhs, lhs_edge, lhs_z, dens, inverse_sens, inverse_smooth = call(
-        prepare_kernel, [rows3, rows4, rows4, own_planes, own_planes, own_planes], [VM, VM], micros=1.0
-    )(element_stiffness, dens)
-
-    own_part = ((OWN_SLOTS * 4, EZ), F32)
+    lhs, lhs_edge, lhs_z, dens, inverse_sens, inverse_smooth, dofs, along_y, ends = call(
+        prepare_kernel,
+        [rows3, rows4, rows4, own_planes, own_planes, own_planes, ((8, EZ), F32), ((EZ, EZ), BF16), ((2 * EZ, EX * EZ), BF16)],
+        [VM] * 3,
+        [((8, EZ), F32)],
+        micros=1.0,
+    )(element_stiffness, dens, corner_dofs.reshape(1, 8))
+
+    own_part = ((OWN_ROWS, EZ), F32)
     own, ea, up_own, down_own = call(
         functools.partial(own_kernel, shared),
         [((3 * NX, ROWS, EZ), F32), ((OWN, ROWS, EZ), F32), own_part, own_part],
@@ -794,7 +807,7 @@
 
     face = ((12, ROWS, EZ), F32)
     y_message = ((Y_MESSAGE, EZ), F32)
-    halo_part = ((Y_MESSAGE - OWN_SLOTS * 4, EZ), F32)
+    halo_part = ((Y_MESSAGE - OWN_ROWS, EZ), F32)
     tx, even, odd = call(
         functools.partial(x_kernel, shared),
         [((3, XR, EZ), F32), y_message, y_message],
@@ -831,16 +844,15 @@
         micros=2.3,
     )(own, xl, xh, low_y, high_y, lhs_edge)
 
-    square = ((EZ, EZ), BF16)
-    filtered, along_y, ends = call(
-        field_kernel, [((2, EX, ROWS, EZ), F32), square, square], [VM] * 8, [((2, XE, QROWS, EZ), F32)], micros=1.5
+    (filtered,) = call(
+        field_kernel, [((2, EX, ROWS, EZ), F32)], [VM] * 8, [((2, XE, QROWS, EZ), F32)], micros=1.5
     )(ea, eb, el, eh, dens, halo_dens, low_y, high_y)
 
     sens, smooth = call(
         last_kernel,
         [((EY * EX, EZ), F32)] * 2,
         [VM] * (9 + len(received_z)),
-        [((4, XR, EZ), F32), ((2, 4 * EX, EZ), F32), z_message, z_message, ((2, EY * EX, EZ), F32),
+        [((4, XR, EZ), F32), ((2, 4 * EX, EZ), F32), z_message, z_message, ((2 * ROWS, EX * EZ), F32), ((2, EY * EX, EZ), F32),
          pltpu.SemaphoreType.DMA((6,))] + node_buffers(5 * XR + 8),
         space=pltpu.HBM,
         micros=2.5,

time: 27.8 us -> 27.3 us (0.982)
  the two profiles are of different devices: /device:TPU:16 before, /device:TPU:20 now
where the time goes in v7:
time: 27.3 us; the launch traced here: 27.2 us
  Pallas kernels  15.4 us (56%)
  waiting for transfers between devices  7.66 us (28%)
  starting transfers between devices  3.31 us (12%)
  between operations  0.77 us (3%)
    ppermute x5, waiting for transfers between devices, exchange(): results.append(lax.ppermute(value, names, moves))  5.71 us
    pallas_call x1, Pallas kernels, local(): call(functools.partial(own_kernel, shared), [((3 * NX, ROWS, EZ), F32), (...  2.98 us
    ppermute x5, starting transfers between devices, exchange(): results.append(lax.ppermute(value, names, moves))  2.81 us
    pallas_call x1, Pallas kernels, local(): call(side_kernel, [((XE - OWN, ROWS, EZ), F32)], [VM] * 4, node_buffers((...  2.37 us
    pallas_call x1, Pallas kernels, local(): call(last_kernel, [((EY * EX, EZ), F32)] * 2, [VM] * (9 + len(received_z)...  2.25 us
    ppermute x1, waiting for transfers between devices, local(): other = lax.ppermute(coarse_solution, 'gz', [(0, 1), (1, 0)])  1.95 us
    pallas_call x1, Pallas kernels, local(): call(edge_kernel, [((XE, 8, EZ), F32)] * 2, [VM] * 6, node_buffers(XN * 8...  1.76 us
    pallas_call x1, Pallas kernels, local(): call(pack_kernel, [message, message, ((3, XR, EZ), F32)], [pltpu.HBM] * 4...  1.41 us
  transfers between devices with their start and end apart: 6, of which 5 were waited for; matrix products, arithmetic and copies ran while one was open for 0% of the time, Pallas kernels for 39%

profile of v7, /device:TPU:20, one launch (start us, length us, event | category | flops | bytes accessed | tf_op | source)
XLA Modules:
  0.0 27.2 jit_solution(6429588667922285177)
XLA Ops:
  0.6 0.0 copy-start
  0.6 0.0 copy-start.1
  0.7 0.0 copy-start.3
  0.7 0.0 copy-start.4
  0.7 0.0 copy-start.2
  0.7 1.4 %shard_map.79 = (f32[688,128]{1,0:T(8,128)S(1)}, f32[688,128]{1,0:T(8,128)S(1)}, f32[3,24,128]{2,1,0:T(8,128)S(1)}) custom-call(f32[3,17,45,128]{3,2,1,0:T(8,128)} %local_ref.3, f32[3,17,1,45]{3,2,1,0:T(1,128)} %bitcast.17, f32[704,128]{1,0:T(8,128)} %bitcast.13, s32[1,8]{1,0:T(1,128)} %bitcast.15), custom_call_target="tpu_custom_call" | custom-call | bytes 3600000 | tf_op jit(solution)/shard_map/pallas_call | solution.py:778
  2.1 1.6 %collective-permute-start.1 = (f32[688,128]{1,0:T(8,128)S(1)}, f32[688,128]{1,0:T(8,128)S(1)}, u32[]{:S(2)}, u32[]{:S(2)}) collective-permute-start(f32[688,128]{1,0:T(8,128)S(1)} %get-tuple-element.39), channel_id=1, source_target_pairs={{0,8},{2,10},{4,12},{6,14},{8,0},{10,2},{12,4},{14,6},{16,24},{18,... | collective-permute-start | bytes 1056776 | tf_op jit(solution)/shard_map/ppermute | solution.py:764
  3.7 0.0 collective-permute-start.2
  3.7 0.0 copy-done.4
  3.7 0.5 %collective-permute-start = (f32[3,512]{1,0:T(4,128)S(1)}, f32[3,512]{1,0:T(4,128)S(1)}, u32[]{:S(2)}, u32[]{:S(2)}) collective-permute-start(f32[3,512]{1,0:T(4,128)S(1)} %copy-done.4), channel_id=1, source_target_pairs={{0,1},{1,0},{2,3},{3,2},{4,5},{5,4},{6,7},{7,6},{8,9},{9,8},{10,11... | collective-permute-start | bytes 18440 | tf_op jit(solution)/shard_map/ppermute | solution.py:772
  4.3 0.0 copy-done.1
  4.3 0.0 copy-done.3
  4.3 0.0 copy-done.2
  4.3 1.2 %shard_map.77 = (bf16[96,192]{1,0:T(8,128)(2,1)S(1)}, bf16[128,256]{1,0:T(8,128)(2,1)S(1)}, bf16[128,256]{1,0:T(8,128)(2,1)S(1)}, f32[16,48,128]{2,1,0:T(8,128)S...) custom-call(f32[24,24]{1,0:T(8,128)S(1)} %copy-done.2, ...), custom_call_target="tpu_custom_call" | custom-call | bytes 3600000 | tf_op jit(solution)/shard_map/pallas_call | solution.py:791
  5.4 1.9 %collective-permute-done = f32[3,512]{1,0:T(4,128)S(1)} collective-permute-done((f32[3,512]{1,0:T(4,128)S(1)}, f32[3,512]{1,0:T(4,128)S(1)}, u32[]{:S(2)}, u32[]{:S(2)}) %collective-permute-start) | collective-permute-done | bytes 6176 | tf_op jit(solution)/shard_map/ppermute | solution.py:772
  7.4 3.0 %shard_map.78 = (f32[51,48,128]{2,1,0:T(8,128)S(1)}, f32[12,48,128]{2,1,0:T(8,128)S(1)}, f32[232,128]{1,0:T(8,128)S(1)}, f32[232,128]{1,0:T(8,128)S(1)}) custom-call(f32[3,17,45,128]{3,2,1,0:T(8,128)S(1)} %copy-done, bf16[96,192]{1,0:T(8,128)(2,1)S(1)} %get-tuple-element.34.lhs_ref, f32[16,48,128]{2,1,0:T(8,128)S(1)} %get-tuple-element.35.dens_ref, ...), custom_call_target="tpu_custom_call" | custom-call | bytes 21600000 | tf_op jit(solution)/shard_map/pallas_call | solution.py:800
  10.4 1.7 %collective-permute-done.1.even_ref = f32[688,128]{1,0:T(8,128)S(1)} collective-permute-done((f32[688,128]{1,0:T(8,128)S(1)}, f32[688,128]{1,0:T(8,128)S(1)}, u32[]{:S(2)}, u32[]{:S(2)}) %collective-permute-start.1) | collective-permute-done | bytes 352288 | tf_op jit(solution)/shard_map/ppermute | solution.py:764
  12.1 1.3 %collective-permute-done.2.odd_ref = f32[688,128]{1,0:T(8,128)S(1)} collective-permute-done((f32[688,128]{1,0:T(8,128)S(1)}, f32[688,128]{1,0:T(8,128)S(1)}, u32[]{:S(2)}, u32[]{:S(2)}) %collective-permute-start.2) | collective-permute-done | bytes 352288 | tf_op jit(solution)/shard_map/ppermute | solution.py:764
  13.4 0.5 %shard_map.82 = (f32[3,24,128]{2,1,0:T(8,128)S(1)}, f32[360,128]{1,0:T(8,128)S(1)}, f32[360,128]{1,0:T(8,128)S(1)}) custom-call(f32[51,48,128]{2,1,0:T(8,128)S(1)} %get-tuple-element.38.own_ref, f32[232,128]{1,0:T(8,128)S(1)} %get-tuple-element.43.up_own_ref, f32[232,128]{1,0:T(8,128)S(1)} %get-tuple-element.44.down_own_ref, ...), custom_call_target="tpu_custom_call" | custom-call | bytes 3600000 | tf_op jit(solution)/shard_map/pallas_call | solution.py:811
  14.0 0.0 collective-permute-start.3
  14.0 0.6 %collective-permute-start.4 = (f32[360,128]{1,0:T(8,128)S(1)}, f32[360,128]{1,0:T(8,128)S(1)}, u32[]{:S(2)}, u32[]{:S(2)}) collective-permute-start(f32[360,128]{1,0:T(8,128)S(1)} %get-tuple-element.49), channel_id=1, source_target_pairs={{0,1},{1,0},{2,4},{3,5},{4,2},{5,3},{6,7},{7,6},{8,9},{9,8},{10,12... | collective-permute-start | bytes 552968 | tf_op jit(solution)/shard_map/ppermute | solution.py:764
  14.6 0.4 %shard_map.80 = (f32[12,48,128]{2,1,0:T(8,128)S(1)}, f32[12,48,128]{2,1,0:T(8,128)S(1)}, f32[6,48,128]{2,1,0:T(8,128)S(1)}) custom-call(f32[51,48,128]{2,1,0:T(8,128)S(1)} %get-tuple-element.38.own_ref, f32[688,128]{1,0:T(8,128)S(1)} %collective-permute-done.1.even_ref, f32[688,128]{1,0:T(8,128)S(1)} %collective-permute-done.2.odd_ref, ...), custom_call_target="tpu_custom_call" | custom-call | bytes 2520000 | tf_op jit(solution)/shard_map/pallas_call | solution.py:820
  14.9 2.4 %shard_map.81.eb_ref = f32[10,48,128]{2,1,0:T(8,128)S(1)} custom-call(f32[51,48,128]{2,1,0:T(8,128)S(1)} %get-tuple-element.38.own_ref, f32[12,48,128]{2,1,0:T(8,128)S(1)} %get-tuple-element.41.xl_ref, f32[12,48,128]{2,1,0:T(8,128)S(1)} %get-tuple-element.42.xh_ref, bf16[96,192]{1,0:T(8,128)(2,1)S(1)} %get-tuple-element.34.lhs_ref), custom_call_target="tpu_custom_call" | custom-call | bytes 9360000 | tf_op jit(solution)/shard_map/pallas_call | solution.py:823
  17.3 0.9 %shard_map.83.zo_ref = f32[91,8,128]{2,1,0:T(8,128)S(1)} custom-call(f32[51,48,128]{2,1,0:T(8,128)S(1)} %get-tuple-element.38.own_ref, f32[12,48,128]{2,1,0:T(8,128)S(1)} %get-tuple-element.41.xl_ref, f32[12,48,128]{2,1,0:T(8,128)S(1)} %get-tuple-element.42.xh_ref, f32[16,48,128]{2,1,0:T(8,128)S(1)} %get-tuple-element.35.dens_ref, ...), custom_call_target="tpu_custom_call" | custom-call | bytes 5400000 | tf_op jit(solution)/shard_map/pallas_call | solution.py:827
  18.2 0.0 collective-permute-done.3.even_ref
  18.2 1.4 %collective-permute-done.4.odd_ref = f32[360,128]{1,0:T(8,128)S(1)} collective-permute-done((f32[360,128]{1,0:T(8,128)S(1)}, f32[360,128]{1,0:T(8,128)S(1)}, u32[]{:S(2)}, u32[]{:S(2)}) %collective-permute-start.4) | collective-permute-done | bytes 184352 | tf_op jit(solution)/shard_map/ppermute | solution.py:764
  19.6 0.5 %shard_map.84 = (f32[360,128]{1,0:T(8,128)S(1)}, f32[360,128]{1,0:T(8,128)S(1)}, f32[72,128]{1,0:T(8,128)S(1)}, f32[72,128]{1,0:T(8,128)S(1)}, f32[24,128]{1,0:T(8,128)S(1)}, /*index=5*/f32[184,128]{1,0:T(8,128)S(1)}) custom-call(f32[3,24,128]{2,1,0:T(8,128)S(1)} %get-tuple-element.46.tx_ref, f32[91,8,128]{2,1,0:T(8,128)S(1)} %shard_map.83.zo_ref, ...), custom_call_target="tpu_custom_call" | custom-call | bytes 3600000 | tf_op jit(solution)/shard_map/pallas_call | solution.py:830
  20.1 0.6 %collective-permute-start.5 = (f32[184,128]{1,0:T(8,128)S(1)}, f32[184,128]{1,0:T(8,128)S(1)}, u32[]{:S(2)}, u32[]{:S(2)}) collective-permute-start(f32[184,128]{1,0:T(8,128)S(1)} %get-tuple-element.63), channel_id=1, source_target_pairs={{0,1},{2,3},{4,5},{6,7},{1,0},{3,2},{5,4},{7,6},{8,9},{10,11},{12,... | collective-permute-start | bytes 282632 | tf_op jit(solution)/shard_map/ppermute | solution.py:764
  20.7 1.8 %shard_map.85 = (f32[22,8,128]{2,1,0:T(8,128)S(1)}, f32[22,8,128]{2,1,0:T(8,128)S(1)}) custom-call(f32[51,48,128]{2,1,0:T(8,128)S(1)} %get-tuple-element.38.own_ref, f32[12,48,128]{2,1,0:T(8,128)S(1)} %get-tuple-element.41.xl_ref, f32[12,48,128]{2,1,0:T(8,128)S(1)} %get-tuple-element.42.xh_ref, f32[360,128]{1,0:T(8,128)S(1)} %get-tuple-element.50.lowy_ref, ...), custom_call_target="tpu_custom_call" | custom-call | bytes 8279999 | tf_op jit(solution)/shard_map/pallas_call | solution.py:839
  22.5 1.1 %shard_map.86.g_ref = f32[2,16,48,128]{3,2,1,0:T(8,128)S(1)} custom-call(f32[12,48,128]{2,1,0:T(8,128)S(1)} %get-tuple-element.37.ea_ref, f32[10,48,128]{2,1,0:T(8,128)S(1)} %shard_map.81.eb_ref, f32[22,8,128]{2,1,0:T(8,128)S(1)} %get-tuple-element.53.el_ref, f32[22,8,128]{2,1,0:T(8,128)S(1)} %get-tuple-element.54.eh_ref, ...), custom_call_target="tpu_custom_call" | custom-call | bytes 5400000 | tf_op jit(solution)/shard_map/pallas_call | solution.py:847
  23.6 1.3 %collective-permute-done.5.refs_0_ = f32[184,128]{1,0:T(8,128)S(1)} collective-permute-done((f32[184,128]{1,0:T(8,128)S(1)}, f32[184,128]{1,0:T(8,128)S(1)}, u32[]{:S(2)}, u32[]{:S(2)}) %collective-permute-start.5) | collective-permute-done | bytes 94240 | tf_op jit(solution)/shard_map/ppermute | solution.py:764
  24.9 2.2 %shard_map.87 = (f32[704,128]{1,0:T(8,128)}, f32[704,128]{1,0:T(8,128)}) custom-call(f32[2,16,48,128]{3,2,1,0:T(8,128)S(1)} %shard_map.86.g_ref, bf16[128,128]{1,0:T(8,128)(2,1)S(1)} %get-tuple-element.55.along_ref, bf16[256,2048]{1,0:T(8,128)(2,1)S(1)} %get-tuple-element.56.right_ref, f32[16,48,128]{2,1,0:T(8,128)S(1)} %get-tuple-element.57.rs_ref, ...), custom_call_target="tpu_custom_call" | custom-call | bytes 9000000 | tf_op jit(solution)/shard_map/pallas_call | solution.py:851
  (2 shorter events, 0.0 us)
Async XLA Ops:
  0.6 6.8 %copy-start = (f32[3,17,45,128]{3,2,1,0:T(8,128)S(1)}, f32[3,17,45,128]{3,2,1,0:T(8,128)}, u32[]{:S(2)}) copy-start(f32[3,17,45,128]{3,2,1,0:T(8,128)} %local_ref.3) | copy-start | bytes 3525124
  0.6 3.6 %copy-start.1 = (f32[16,44,128]{2,0,1:T(8,128)S(1)}, f32[16,44,128]{2,0,1:T(8,128)}, u32[]{:S(2)}) copy-start(f32[16,44,128]{2,0,1:T(8,128)} %param.10) | copy-start | bytes 1081348
  0.7 3.6 %copy-start.3 = (s32[1,1,1,8]{3,2,1,0:T(1,128)S(1)}, s32[1,1,1,8]{3,2,1,0:T(1,128)}, u32[]{:S(2)}) copy-start(s32[1,1,1,8]{3,2,1,0:T(1,128)} %param.9) | copy-start | bytes 100
  0.7 3.1 %copy-start.4 = (f32[3,512]{1,0:T(4,128)S(1)}, f32[3,512]{1,0:T(4,128)}, u32[]{:S(2)}) copy-start(f32[3,512]{1,0:T(4,128)} %param.8) | copy-start | bytes 18436
  0.7 3.6 %copy-start.2 = (f32[24,24]{1,0:T(8,128)S(1)}, f32[24,24]{1,0:T(8,128)}, u32[]{:S(2)}) copy-start(f32[24,24]{1,0:T(8,128)} %stiff_ref.1) | copy-start | bytes 6916
  2.1 10.0 %collective-permute-start.1 = (f32[688,128]{1,0:T(8,128)S(1)}, f32[688,128]{1,0:T(8,128)S(1)}, u32[]{:S(2)}, u32[]{:S(2)}) collective-permute-start(f32[688,128]{1,0:T(8,128)S(1)} %get-tuple-element.39), channel_id=1, source_target_pairs={{0,8},{2,10},{4,12},{6,14},{8,0},{10,2},{12,4},{14,6},{16,24},{18,... | collective-permute-start | bytes 1056776 | tf_op jit(solution)/shard_map/ppermute | solution.py:764
  3.7 9.7 %collective-permute-start.2 = (f32[688,128]{1,0:T(8,128)S(1)}, f32[688,128]{1,0:T(8,128)S(1)}, u32[]{:S(2)}, u32[]{:S(2)}) collective-permute-start(f32[688,128]{1,0:T(8,128)S(1)} %get-tuple-element.40), channel_id=1, source_target_pairs={{0,2},{2,0},{4,6},{6,4},{8,16},{10,18},{12,20},{14,22},{16,8},{18,... | collective-permute-start | bytes 1056776 | tf_op jit(solution)/shard_map/ppermute | solution.py:764
  3.7 3.7 %collective-permute-start = (f32[3,512]{1,0:T(4,128)S(1)}, f32[3,512]{1,0:T(4,128)S(1)}, u32[]{:S(2)}, u32[]{:S(2)}) collective-permute-start(f32[3,512]{1,0:T(4,128)S(1)} %copy-done.4), channel_id=1, source_target_pairs={{0,1},{1,0},{2,3},{3,2},{4,5},{5,4},{6,7},{7,6},{8,9},{9,8},{10,11... | collective-permute-start | bytes 18440 | tf_op jit(solution)/shard_map/ppermute | solution.py:772
  14.0 4.3 %collective-permute-start.3 = (f32[360,128]{1,0:T(8,128)S(1)}, f32[360,128]{1,0:T(8,128)S(1)}, u32[]{:S(2)}, u32[]{:S(2)}) collective-permute-start(f32[360,128]{1,0:T(8,128)S(1)} %get-tuple-element.48), channel_id=1, source_target_pairs={{0,2},{1,3},{2,0},{3,1},{4,6},{5,7},{6,4},{7,5},{8,10},{9,11},{10,... | collective-permute-start | bytes 552968 | tf_op jit(solution)/shard_map/ppermute | solution.py:764
  14.0 5.6 %collective-permute-start.4 = (f32[360,128]{1,0:T(8,128)S(1)}, f32[360,128]{1,0:T(8,128)S(1)}, u32[]{:S(2)}, u32[]{:S(2)}) collective-permute-start(f32[360,128]{1,0:T(8,128)S(1)} %get-tuple-element.49), channel_id=1, source_target_pairs={{0,1},{1,0},{2,4},{3,5},{4,2},{5,3},{6,7},{7,6},{8,9},{9,8},{10,12... | collective-permute-start | bytes 552968 | tf_op jit(solution)/shard_map/ppermute | solution.py:764
  20.1 4.8 %collective-permute-start.5 = (f32[184,128]{1,0:T(8,128)S(1)}, f32[184,128]{1,0:T(8,128)S(1)}, u32[]{:S(2)}, u32[]{:S(2)}) collective-permute-start(f32[184,128]{1,0:T(8,128)S(1)} %get-tuple-element.63), channel_id=1, source_target_pairs={{0,1},{2,3},{4,5},{6,7},{1,0},{3,2},{5,4},{7,6},{8,9},{10,11},{12,... | collective-permute-start | bytes 282632 | tf_op jit(solution)/shard_map/ppermute | solution.py:764

commit v8 on v7

--- a/solution.py
+++ b/solution.py
@@ -183,8 +183,8 @@
     return lax.axis_index(axis) % 2 == 1
 
 
-X_MESSAGE = 688
-X_DENSITY, X_TOP, X_DOFS = 576, 672, 684
+X_MESSAGE = 680
+X_DENSITY, X_TOP, X_DOFS = 576, 672, 678
 
 
 def third_rows():
@@ -212,9 +212,9 @@
         for i in range(NX):
             tops_ref[c, i : i + 1, 0:NY] = t_ref[c, i]
     for out_ref, flip in outs:
-        for c in range(3):
-            out_ref[X_TOP + 4 * c : X_TOP + 4 * c + 4, :] = jnp.where(
-                flip, tops_ref[c, 0:4, :], tops_ref[c, EX - RADIUS : EX - RADIUS + 4, :])
+        faces = [jnp.where(flip, tops_ref[c, 0:4, :], tops_ref[c, EX - RADIUS : EX - RADIUS + 4, :]) for c in range(3)]
+        faces = jnp.concatenate(faces, axis=0)
+        out_ref[X_TOP : X_TOP + 6, :] = faces[0:6] + pltpu.roll(faces[6:12], 64, 1)
         for j in range(3):
             value = jnp.where(flip, d_ref[pl.ds(j, EY, stride=EX), :], d_ref[pl.ds(EX - RADIUS + j, EY, stride=EX), :])
             if j < 2:
@@ -272,21 +272,24 @@
         rs_ref[x] = both / od_ref[x]
 
 
-def own_kernel(shared, local_ref, lhs_ref, dens_ref, coarse_ref, dofs_ref, own_ref, e_ref, up_ref, down_ref, *refs):
+def own_kernel(shared, local_ref, lhs_ref, dens_ref, coarse_ref, dofs_ref, own_ref, e_ref, even_ref, odd_ref, *refs):
     corners = corner_values(coarse_ref, dofs_ref[:, 0:1], shared)
     for c in range(3):
         edges = corner_rows(corners, c)
         for i in range(NX):
             own_ref[c * NX + i, 0:NY, :] = local_ref[c, i] + plane_interp(edges, i, NY)
             own_ref[c * NX + i, NY:ROWS, :] = jnp.zeros((ROWS - NY, EZ), F32)
-    for out_ref, first in ((up_ref, EY - RADIUS), (down_ref, 0)):
+    odd = odd_place("gy")
+    for out_ref, first, second in ((even_ref, EY - RADIUS, 0), (odd_ref, 0, EY - RADIUS)):
         out_ref[OWN_ROWS - 4 : OWN_ROWS, :] = jnp.zeros((4, EZ), F32)
         for p in range(4, 19):
             for c in range(3):
                 at = node_row(c, p)
-                out_ref[at : at + 4, :] = own_ref[c * NX + p - 3, first : first + 4, :]
+                plane = own_ref[c * NX + p - 3]
+                out_ref[at : at + 4, :] = jnp.where(odd, plane[second : second + 4], plane[first : first + 4])
         for x in range(3, 19):
-            out_ref[dens_row(x) : dens_row(x) + 3, :] = dens_ref[x - 3, first : first + 3, :]
+            plane = dens_ref[x - 3]
+            out_ref[dens_row(x) : dens_row(x) + 3, :] = jnp.where(odd, plane[second : second + 3], plane[first : first + 3])
     build_nodes(lambda c, p: own_ref[c * NX + p + 1], range(OWN + 1), ROWS, refs)
     blocks = [(p, r) for p in range(OWN) for r in range(1, EY - 1, 3)]
     energy_planes(lhs_ref[...], 3, refs, e_ref, 0, OWN, ROWS, blocks, 0)
@@ -390,7 +393,7 @@
             hd_ref[first + 2, row : row + count, :] = jnp.where(there, side(at, count), 0.0)
 
 
-def x_kernel(shared, own_ref, up_own_ref, down_own_ref, top_ref, even_ref, odd_ref, coarse_ref, dofs_ref,
+def x_kernel(shared, own_ref, even_own_ref, odd_own_ref, top_ref, even_ref, odd_ref, coarse_ref, dofs_ref,
              tx_ref, yeven_ref, yodd_ref, up_ref, down_ref, t_ref):
     sides = low_rows, high_rows = x_sides(even_ref, odd_ref)
     corners = corner_values(coarse_ref, dofs_ref[:, 0:1], shared)
@@ -414,8 +417,10 @@
     t_ref[...] = jnp.zeros(t_ref.shape, F32)
     for c in range(3):
         t_ref[0] = top_ref[c] + top_interp(corners, c, XR)
-        t_ref[1, 0:4, :] = low_rows(X_TOP + 4 * c, 4)
-        t_ref[2, 0:4, :] = high_rows(X_TOP + 4 * c, 4)
+        for side, side_rows in ((1, low_rows), (2, high_rows)):
+            both = side_rows(X_TOP, 6)
+            both = jnp.concatenate([both, pltpu.roll(both, 64, 1)], axis=0)
+            t_ref[side, 0:4, :] = both[4 * c : 4 * c + 4]
         t_low = t_ref[1, 0:8, :] + pltpu.roll(top_interp(corners_low, c, 24), 24 - (EX - RADIUS), 0)[0:8]
         t_high = t_ref[2, 0:8, :] + top_interp(corners_high, c, 8)
         first = average(lower, t_low[3:4], t_ref[0, 0:1, :], t_ref[0, 0:1, :])
@@ -436,8 +441,8 @@
             total = jnp.where((lane >= 4 * c) & (lane < 4 * c + 4), moved, total)
         out_ref[TOP_AT - OWN_ROWS :, :] = total[0:8] + pltpu.roll(total[8:16], 16, 1) + pltpu.roll(total[16:24], 32, 1)
     odd = odd_place("gy")
-    for mine, other, out_ref in ((up_own_ref, down_own_ref, yeven_ref), (down_own_ref, up_own_ref, yodd_ref)):
-        out_ref[0:OWN_ROWS, :] = jnp.where(odd, other[...], mine[...])
+    yeven_ref[0:OWN_ROWS, :] = even_own_ref[...]
+    yodd_ref[0:OWN_ROWS, :] = odd_own_ref[...]
     for mine, other, out_ref in ((up_ref, down_ref, yeven_ref), (down_ref, up_ref, yodd_ref)):
         out_ref[OWN_ROWS:, :] = jnp.where(odd, other[...], mine[...])
 
@@ -797,7 +802,7 @@
     )(element_stiffness, dens, corner_dofs.reshape(1, 8))
 
     own_part = ((OWN_ROWS, EZ), F32)
-    own, ea, up_own, down_own = call(
+    own, ea, even_own, odd_own = call(
         functools.partial(own_kernel, shared),
         [((3 * NX, ROWS, EZ), F32), ((OWN, ROWS, EZ), F32), own_part, own_part],
         [VM] * 5,
@@ -814,7 +819,7 @@
         [VM] * 8,
         [halo_part, halo_part, ((4, XR, EZ), F32)],
         micros=1.0,
-    )(own, up_own, down_own, tops, even_x, odd_x, coarse, dofs)
+    )(own, even_own, odd_own, tops, even_x, odd_x, coarse, dofs)
     even_y, odd_y = exchange("gy", "gz", even, odd)
 
     xl, xh, halo_dens = call(

time: 27.3 us -> 27.2 us (level)
  transfers between devices with their start and end apart: 6 -> 6, of which waited for: 5 -> 5; matrix products, arithmetic and copies ran while one was open for 0% -> 0% of each run, Pallas kernels for 39% -> 40%
where the time goes in v8:
time: 27.2 us; the launch traced here: 27.1 us
  Pallas kernels  15.4 us (57%)
  waiting for transfers between devices  7.54 us (28%)
  starting transfers between devices  3.31 us (12%)
  between operations  0.77 us (3%)
    ppermute x5, waiting for transfers between devices, exchange(): results.append(lax.ppermute(value, names, moves))  5.59 us
    pallas_call x1, Pallas kernels, local(): call(functools.partial(own_kernel, shared), [((3 * NX, ROWS, EZ), F32), (...  3.02 us
    ppermute x5, starting transfers between devices, exchange(): results.append(lax.ppermute(value, names, moves))  2.81 us
    pallas_call x1, Pallas kernels, local(): call(side_kernel, [((XE - OWN, ROWS, EZ), F32)], [VM] * 4, node_buffers((...  2.37 us
    pallas_call x1, Pallas kernels, local(): call(last_kernel, [((EY * EX, EZ), F32)] * 2, [VM] * (9 + len(received_z)...  2.25 us
    ppermute x1, waiting for transfers between devices, local(): other = lax.ppermute(coarse_solution, 'gz', [(0, 1), (1, 0)])  1.95 us
    pallas_call x1, Pallas kernels, local(): call(edge_kernel, [((XE, 8, EZ), F32)] * 2, [VM] * 6, node_buffers(XN * 8...  1.76 us
    pallas_call x1, Pallas kernels, local(): call(pack_kernel, [message, message, ((3, XR, EZ), F32)], [pltpu.HBM] * 4...  1.41 us
  transfers between devices with their start and end apart: 6, of which 5 were waited for; matrix products, arithmetic and copies ran while one was open for 0% of the time, Pallas kernels for 40%

profile of v8, /device:TPU:20, one launch (start us, length us, event | category | flops | bytes accessed | tf_op | source)
XLA Modules:
  0.0 27.1 jit_solution(8171489169637634212)
XLA Ops:
  0.6 0.0 copy-start
  0.6 0.0 copy-start.1
  0.7 0.0 copy-start.3
  0.7 0.0 copy-start.4
  0.7 0.0 copy-start.2
  0.7 1.4 %shard_map.79 = (f32[680,128]{1,0:T(8,128)S(1)}, f32[680,128]{1,0:T(8,128)S(1)}, f32[3,24,128]{2,1,0:T(8,128)S(1)}) custom-call(f32[3,17,45,128]{3,2,1,0:T(8,128)} %local_ref.3, f32[3,17,1,45]{3,2,1,0:T(1,128)} %bitcast.17, f32[704,128]{1,0:T(8,128)} %bitcast.13, s32[1,8]{1,0:T(1,128)} %bitcast.15), custom_call_target="tpu_custom_call" | custom-call | bytes 3600000 | tf_op jit(solution)/shard_map/pallas_call | solution.py:783
  2.1 1.6 %collective-permute-start.1 = (f32[680,128]{1,0:T(8,128)S(1)}, f32[680,128]{1,0:T(8,128)S(1)}, u32[]{:S(2)}, u32[]{:S(2)}) collective-permute-start(f32[680,128]{1,0:T(8,128)S(1)} %get-tuple-element.39), channel_id=1, source_target_pairs={{0,8},{2,10},{4,12},{6,14},{8,0},{10,2},{12,4},{14,6},{16,24},{18,... | collective-permute-start | bytes 1044488 | tf_op jit(solution)/shard_map/ppermute | solution.py:769
  3.7 0.0 collective-permute-start.2
  3.7 0.0 copy-done.4
  3.7 0.5 %collective-permute-start = (f32[3,512]{1,0:T(4,128)S(1)}, f32[3,512]{1,0:T(4,128)S(1)}, u32[]{:S(2)}, u32[]{:S(2)}) collective-permute-start(f32[3,512]{1,0:T(4,128)S(1)} %copy-done.4), channel_id=1, source_target_pairs={{0,1},{1,0},{2,3},{3,2},{4,5},{5,4},{6,7},{7,6},{8,9},{9,8},{10,11... | collective-permute-start | bytes 18440 | tf_op jit(solution)/shard_map/ppermute | solution.py:777
  4.3 0.0 copy-done.1
  4.3 0.0 copy-done.3
  4.3 0.0 copy-done.2
  4.3 1.2 %shard_map.77 = (bf16[96,192]{1,0:T(8,128)(2,1)S(1)}, bf16[128,256]{1,0:T(8,128)(2,1)S(1)}, bf16[128,256]{1,0:T(8,128)(2,1)S(1)}, f32[16,48,128]{2,1,0:T(8,128)S...) custom-call(f32[24,24]{1,0:T(8,128)S(1)} %copy-done.2, ...), custom_call_target="tpu_custom_call" | custom-call | bytes 3600000 | tf_op jit(solution)/shard_map/pallas_call | solution.py:796
  5.4 1.9 %collective-permute-done = f32[3,512]{1,0:T(4,128)S(1)} collective-permute-done((f32[3,512]{1,0:T(4,128)S(1)}, f32[3,512]{1,0:T(4,128)S(1)}, u32[]{:S(2)}, u32[]{:S(2)}) %collective-permute-start) | collective-permute-done | bytes 6176 | tf_op jit(solution)/shard_map/ppermute | solution.py:777
  7.4 3.0 %shard_map.78 = (f32[51,48,128]{2,1,0:T(8,128)S(1)}, f32[12,48,128]{2,1,0:T(8,128)S(1)}, f32[232,128]{1,0:T(8,128)S(1)}, f32[232,128]{1,0:T(8,128)S(1)}) custom-call(f32[3,17,45,128]{3,2,1,0:T(8,128)S(1)} %copy-done, bf16[96,192]{1,0:T(8,128)(2,1)S(1)} %get-tuple-element.34.lhs_ref, f32[16,48,128]{2,1,0:T(8,128)S(1)} %get-tuple-element.35.dens_ref, ...), custom_call_target="tpu_custom_call" | custom-call | bytes 21600000 | tf_op jit(solution)/shard_map/pallas_call | solution.py:805
  10.4 1.6 %collective-permute-done.1.even_ref = f32[680,128]{1,0:T(8,128)S(1)} collective-permute-done((f32[680,128]{1,0:T(8,128)S(1)}, f32[680,128]{1,0:T(8,128)S(1)}, u32[]{:S(2)}, u32[]{:S(2)}) %collective-permute-start.1) | collective-permute-done | bytes 348192 | tf_op jit(solution)/shard_map/ppermute | solution.py:769
  12.1 1.3 %collective-permute-done.2.odd_ref = f32[680,128]{1,0:T(8,128)S(1)} collective-permute-done((f32[680,128]{1,0:T(8,128)S(1)}, f32[680,128]{1,0:T(8,128)S(1)}, u32[]{:S(2)}, u32[]{:S(2)}) %collective-permute-start.2) | collective-permute-done | bytes 348192 | tf_op jit(solution)/shard_map/ppermute | solution.py:769
  13.3 0.5 %shard_map.82 = (f32[3,24,128]{2,1,0:T(8,128)S(1)}, f32[360,128]{1,0:T(8,128)S(1)}, f32[360,128]{1,0:T(8,128)S(1)}) custom-call(f32[51,48,128]{2,1,0:T(8,128)S(1)} %get-tuple-element.38.own_ref, f32[232,128]{1,0:T(8,128)S(1)} %get-tuple-element.43.even_own_ref, f32[232,128]{1,0:T(8,128)S(1)} %get-tuple-element.44.odd_own_ref, ...), custom_call_target="tpu_custom_call" | custom-call | bytes 3600000 | tf_op jit(solution)/shard_map/pallas_call | solution.py:816
  13.9 0.0 collective-permute-start.3
  13.9 0.6 %collective-permute-start.4 = (f32[360,128]{1,0:T(8,128)S(1)}, f32[360,128]{1,0:T(8,128)S(1)}, u32[]{:S(2)}, u32[]{:S(2)}) collective-permute-start(f32[360,128]{1,0:T(8,128)S(1)} %get-tuple-element.49), channel_id=1, source_target_pairs={{0,1},{1,0},{2,4},{3,5},{4,2},{5,3},{6,7},{7,6},{8,9},{9,8},{10,12... | collective-permute-start | bytes 552968 | tf_op jit(solution)/shard_map/ppermute | solution.py:769
  14.5 0.4 %shard_map.80 = (f32[12,48,128]{2,1,0:T(8,128)S(1)}, f32[12,48,128]{2,1,0:T(8,128)S(1)}, f32[6,48,128]{2,1,0:T(8,128)S(1)}) custom-call(f32[51,48,128]{2,1,0:T(8,128)S(1)} %get-tuple-element.38.own_ref, f32[680,128]{1,0:T(8,128)S(1)} %collective-permute-done.1.even_ref, f32[680,128]{1,0:T(8,128)S(1)} %collective-permute-done.2.odd_ref, ...), custom_call_target="tpu_custom_call" | custom-call | bytes 2520000 | tf_op jit(solution)/shard_map/pallas_call | solution.py:825
  14.8 2.4 %shard_map.81.eb_ref = f32[10,48,128]{2,1,0:T(8,128)S(1)} custom-call(f32[51,48,128]{2,1,0:T(8,128)S(1)} %get-tuple-element.38.own_ref, f32[12,48,128]{2,1,0:T(8,128)S(1)} %get-tuple-element.41.xl_ref, f32[12,48,128]{2,1,0:T(8,128)S(1)} %get-tuple-element.42.xh_ref, bf16[96,192]{1,0:T(8,128)(2,1)S(1)} %get-tuple-element.34.lhs_ref), custom_call_target="tpu_custom_call" | custom-call | bytes 9360000 | tf_op jit(solution)/shard_map/pallas_call | solution.py:828
  17.2 0.9 %shard_map.83.zo_ref = f32[91,8,128]{2,1,0:T(8,128)S(1)} custom-call(f32[51,48,128]{2,1,0:T(8,128)S(1)} %get-tuple-element.38.own_ref, f32[12,48,128]{2,1,0:T(8,128)S(1)} %get-tuple-element.41.xl_ref, f32[12,48,128]{2,1,0:T(8,128)S(1)} %get-tuple-element.42.xh_ref, f32[16,48,128]{2,1,0:T(8,128)S(1)} %get-tuple-element.35.dens_ref, ...), custom_call_target="tpu_custom_call" | custom-call | bytes 5400000 | tf_op jit(solution)/shard_map/pallas_call | solution.py:832
  18.1 0.0 collective-permute-done.3.even_ref
  18.1 1.4 %collective-permute-done.4.odd_ref = f32[360,128]{1,0:T(8,128)S(1)} collective-permute-done((f32[360,128]{1,0:T(8,128)S(1)}, f32[360,128]{1,0:T(8,128)S(1)}, u32[]{:S(2)}, u32[]{:S(2)}) %collective-permute-start.4) | collective-permute-done | bytes 184352 | tf_op jit(solution)/shard_map/ppermute | solution.py:769
  19.5 0.5 %shard_map.84 = (f32[360,128]{1,0:T(8,128)S(1)}, f32[360,128]{1,0:T(8,128)S(1)}, f32[72,128]{1,0:T(8,128)S(1)}, f32[72,128]{1,0:T(8,128)S(1)}, f32[24,128]{1,0:T(8,128)S(1)}, /*index=5*/f32[184,128]{1,0:T(8,128)S(1)}) custom-call(f32[3,24,128]{2,1,0:T(8,128)S(1)} %get-tuple-element.46.tx_ref, f32[91,8,128]{2,1,0:T(8,128)S(1)} %shard_map.83.zo_ref, ...), custom_call_target="tpu_custom_call" | custom-call | bytes 3600000 | tf_op jit(solution)/shard_map/pallas_call | solution.py:835
  20.0 0.6 %collective-permute-start.5 = (f32[184,128]{1,0:T(8,128)S(1)}, f32[184,128]{1,0:T(8,128)S(1)}, u32[]{:S(2)}, u32[]{:S(2)}) collective-permute-start(f32[184,128]{1,0:T(8,128)S(1)} %get-tuple-element.63), channel_id=1, source_target_pairs={{0,1},{2,3},{4,5},{6,7},{1,0},{3,2},{5,4},{7,6},{8,9},{10,11},{12,... | collective-permute-start | bytes 282632 | tf_op jit(solution)/shard_map/ppermute | solution.py:769
  20.6 1.8 %shard_map.85 = (f32[22,8,128]{2,1,0:T(8,128)S(1)}, f32[22,8,128]{2,1,0:T(8,128)S(1)}) custom-call(f32[51,48,128]{2,1,0:T(8,128)S(1)} %get-tuple-element.38.own_ref, f32[12,48,128]{2,1,0:T(8,128)S(1)} %get-tuple-element.41.xl_ref, f32[12,48,128]{2,1,0:T(8,128)S(1)} %get-tuple-element.42.xh_ref, f32[360,128]{1,0:T(8,128)S(1)} %get-tuple-element.50.lowy_ref, ...), custom_call_target="tpu_custom_call" | custom-call | bytes 8279999 | tf_op jit(solution)/shard_map/pallas_call | solution.py:844
  22.4 1.1 %shard_map.86.g_ref = f32[2,16,48,128]{3,2,1,0:T(8,128)S(1)} custom-call(f32[12,48,128]{2,1,0:T(8,128)S(1)} %get-tuple-element.37.ea_ref, f32[10,48,128]{2,1,0:T(8,128)S(1)} %shard_map.81.eb_ref, f32[22,8,128]{2,1,0:T(8,128)S(1)} %get-tuple-element.53.el_ref, f32[22,8,128]{2,1,0:T(8,128)S(1)} %get-tuple-element.54.eh_ref, ...), custom_call_target="tpu_custom_call" | custom-call | bytes 5400000 | tf_op jit(solution)/shard_map/pallas_call | solution.py:852
  23.5 1.3 %collective-permute-done.5.refs_0_ = f32[184,128]{1,0:T(8,128)S(1)} collective-permute-done((f32[184,128]{1,0:T(8,128)S(1)}, f32[184,128]{1,0:T(8,128)S(1)}, u32[]{:S(2)}, u32[]{:S(2)}) %collective-permute-start.5) | collective-permute-done | bytes 94240 | tf_op jit(solution)/shard_map/ppermute | solution.py:769
  24.8 2.2 %shard_map.87 = (f32[704,128]{1,0:T(8,128)}, f32[704,128]{1,0:T(8,128)}) custom-call(f32[2,16,48,128]{3,2,1,0:T(8,128)S(1)} %shard_map.86.g_ref, bf16[128,128]{1,0:T(8,128)(2,1)S(1)} %get-tuple-element.55.along_ref, bf16[256,2048]{1,0:T(8,128)(2,1)S(1)} %get-tuple-element.56.right_ref, f32[16,48,128]{2,1,0:T(8,128)S(1)} %get-tuple-element.57.rs_ref, ...), custom_call_target="tpu_custom_call" | custom-call | bytes 9000000 | tf_op jit(solution)/shard_map/pallas_call | solution.py:856
  (2 shorter events, 0.0 us)
Async XLA Ops:
  0.6 6.8 %copy-start = (f32[3,17,45,128]{3,2,1,0:T(8,128)S(1)}, f32[3,17,45,128]{3,2,1,0:T(8,128)}, u32[]{:S(2)}) copy-start(f32[3,17,45,128]{3,2,1,0:T(8,128)} %local_ref.3) | copy-start | bytes 3525124
  0.6 3.6 %copy-start.1 = (f32[16,44,128]{2,0,1:T(8,128)S(1)}, f32[16,44,128]{2,0,1:T(8,128)}, u32[]{:S(2)}) copy-start(f32[16,44,128]{2,0,1:T(8,128)} %param.10) | copy-start | bytes 1081348
  0.7 3.6 %copy-start.3 = (s32[1,1,1,8]{3,2,1,0:T(1,128)S(1)}, s32[1,1,1,8]{3,2,1,0:T(1,128)}, u32[]{:S(2)}) copy-start(s32[1,1,1,8]{3,2,1,0:T(1,128)} %param.9) | copy-start | bytes 100
  0.7 3.1 %copy-start.4 = (f32[3,512]{1,0:T(4,128)S(1)}, f32[3,512]{1,0:T(4,128)}, u32[]{:S(2)}) copy-start(f32[3,512]{1,0:T(4,128)} %param.8) | copy-start | bytes 18436
  0.7 3.6 %copy-start.2 = (f32[24,24]{1,0:T(8,128)S(1)}, f32[24,24]{1,0:T(8,128)}, u32[]{:S(2)}) copy-start(f32[24,24]{1,0:T(8,128)} %stiff_ref.1) | copy-start | bytes 6916
  2.1 10.0 %collective-permute-start.1 = (f32[680,128]{1,0:T(8,128)S(1)}, f32[680,128]{1,0:T(8,128)S(1)}, u32[]{:S(2)}, u32[]{:S(2)}) collective-permute-start(f32[680,128]{1,0:T(8,128)S(1)} %get-tuple-element.39), channel_id=1, source_target_pairs={{0,8},{2,10},{4,12},{6,14},{8,0},{10,2},{12,4},{14,6},{16,24},{18,... | collective-permute-start | bytes 1044488 | tf_op jit(solution)/shard_map/ppermute | solution.py:769
  3.7 9.6 %collective-permute-start.2 = (f32[680,128]{1,0:T(8,128)S(1)}, f32[680,128]{1,0:T(8,128)S(1)}, u32[]{:S(2)}, u32[]{:S(2)}) collective-permute-start(f32[680,128]{1,0:T(8,128)S(1)} %get-tuple-element.40), channel_id=1, source_target_pairs={{0,2},{2,0},{4,6},{6,4},{8,16},{10,18},{12,20},{14,22},{16,8},{18,... | collective-permute-start | bytes 1044488 | tf_op jit(solution)/shard_map/ppermute | solution.py:769
  3.7 3.7 %collective-permute-start = (f32[3,512]{1,0:T(4,128)S(1)}, f32[3,512]{1,0:T(4,128)S(1)}, u32[]{:S(2)}, u32[]{:S(2)}) collective-permute-start(f32[3,512]{1,0:T(4,128)S(1)} %copy-done.4), channel_id=1, source_target_pairs={{0,1},{1,0},{2,3},{3,2},{4,5},{5,4},{6,7},{7,6},{8,9},{9,8},{10,11... | collective-permute-start | bytes 18440 | tf_op jit(solution)/shard_map/ppermute | solution.py:777
  13.9 4.3 %collective-permute-start.3 = (f32[360,128]{1,0:T(8,128)S(1)}, f32[360,128]{1,0:T(8,128)S(1)}, u32[]{:S(2)}, u32[]{:S(2)}) collective-permute-start(f32[360,128]{1,0:T(8,128)S(1)} %get-tuple-element.48), channel_id=1, source_target_pairs={{0,2},{1,3},{2,0},{3,1},{4,6},{5,7},{6,4},{7,5},{8,10},{9,11},{10,... | collective-permute-start | bytes 552968 | tf_op jit(solution)/shard_map/ppermute | solution.py:769
  13.9 5.6 %collective-permute-start.4 = (f32[360,128]{1,0:T(8,128)S(1)}, f32[360,128]{1,0:T(8,128)S(1)}, u32[]{:S(2)}, u32[]{:S(2)}) collective-permute-start(f32[360,128]{1,0:T(8,128)S(1)} %get-tuple-element.49), channel_id=1, source_target_pairs={{0,1},{1,0},{2,4},{3,5},{4,2},{5,3},{6,7},{7,6},{8,9},{9,8},{10,12... | collective-permute-start | bytes 552968 | tf_op jit(solution)/shard_map/ppermute | solution.py:769
  20.0 4.8 %collective-permute-start.5 = (f32[184,128]{1,0:T(8,128)S(1)}, f32[184,128]{1,0:T(8,128)S(1)}, u32[]{:S(2)}, u32[]{:S(2)}) collective-permute-start(f32[184,128]{1,0:T(8,128)S(1)} %get-tuple-element.63), channel_id=1, source_target_pairs={{0,1},{2,3},{4,5},{6,7},{1,0},{3,2},{5,4},{7,6},{8,9},{10,11},{12,... | collective-permute-start | bytes 282632 | tf_op jit(solution)/shard_map/ppermute | solution.py:769

commit v9 on v8

--- a/solution.py
+++ b/solution.py
@@ -504,7 +504,7 @@
 def y_kernel(tx_ref, zo_ref, eb_ref, even_ref, odd_ref,
              low_ref, high_ref, oa_ref, ob_ref, od_ref, *refs):
     del eb_ref
-    z_ref, d_ref, up_ref, down_ref = refs[-4:]
+    z_ref, d_ref = refs[-2:]
     sort_sides("gy", even_ref, odd_ref, low_ref, high_ref)
     lower, upper = has_lower("gy"), has_upper("gy")
     clear(z_ref)
@@ -561,18 +561,13 @@
     oa_ref[...] = pack(nodes(0), top)
     ob_ref[...] = pack(nodes(1), nodes(7))
     od_ref[...] = pack(dens(0), dens(7))
-    up_ref[0:72, :] = pack(nodes(5), nodes(6))
-    up_ref[72:144, :] = pack(nodes(7), top)
-    up_ref[144:168, :] = pack(dens(5), dens(6))
-    up_ref[168:184, :] = fold(dens(7))
-    down_ref[0:72, :] = pack(nodes(0), nodes(1))
-    down_ref[72:144, :] = pack(nodes(2), nodes(3))
-    down_ref[144:168, :] = pack(dens(0), dens(1))
-    down_ref[168:184, :] = fold(dens(2))
     odd = odd_place("gz")
-    refs[0][...] = jnp.where(odd, down_ref[...], up_ref[...])
-    if len(refs) > 5:
-        refs[1][...] = jnp.where(odd, up_ref[...], down_ref[...])
+    for out_ref, down in zip(refs[:-2], (odd, jnp.logical_not(odd))):
+        first = jnp.where(down, 0, 5)
+        out_ref[0:72, :] = pack(nodes(first), nodes(first + 1))
+        out_ref[72:144, :] = pack(nodes(first + 2), jnp.where(down, nodes(3), top))
+        out_ref[144:168, :] = pack(dens(first), dens(first + 1))
+        out_ref[168:184, :] = fold(dens(first + 2))
 
 
 def edge_kernel(own_ref, xl_ref, xh_ref, lowy_ref, highy_ref, lhs_ref, el_ref, eh_ref, *refs):
@@ -836,7 +831,7 @@
         y_kernel,
         [y_message, y_message, ((72, EZ), F32), ((72, EZ), F32), ((XR, EZ), F32)] + [z_message] * (1 if shared else 2),
         [VM] * 5,
-        [((8 * 3 * XR, EZ), F32), ((8 * XR, EZ), F32), z_message, z_message],
+        [((8 * 3 * XR, EZ), F32), ((8 * XR, EZ), F32)],
         micros=1.0,
     )(tx, zo, eb, even_y, odd_y)
     received_z = exchange("gz", "gy", *messages)

time: 27.2 us -> 27.2 us (level)
  the two profiles are of different devices: /device:TPU:20 before, /device:TPU:16 now
where the time goes in v9:
time: 27.2 us; the launch traced here: 27 us
  Pallas kernels  15.4 us (57%)
  starting transfers between devices  6.35 us (23%)
  waiting for transfers between devices  4.5 us (17%)
  between operations  0.77 us (3%)
    ppermute x5, starting transfers between devices, exchange(): results.append(lax.ppermute(value, names, moves))  4.83 us
    ppermute x5, waiting for transfers between devices, exchange(): results.append(lax.ppermute(value, names, moves))  3.56 us
    pallas_call x1, Pallas kernels, local(): call(functools.partial(own_kernel, shared), [((3 * NX, ROWS, EZ), F32), (...  3.02 us
    pallas_call x1, Pallas kernels, local(): call(side_kernel, [((XE - OWN, ROWS, EZ), F32)], [VM] * 4, node_buffers((...  2.38 us
    pallas_call x1, Pallas kernels, local(): call(last_kernel, [((EY * EX, EZ), F32)] * 2, [VM] * (9 + len(received_z)...  2.25 us
    pallas_call x1, Pallas kernels, local(): call(edge_kernel, [((XE, 8, EZ), F32)] * 2, [VM] * 6, node_buffers(XN * 8...  1.75 us
    ppermute x1, starting transfers between devices, local(): other = lax.ppermute(coarse_solution, 'gz', [(0, 1), (1, 0)])  1.52 us
    pallas_call x1, Pallas kernels, local(): call(pack_kernel, [message, message, ((3, XR, EZ), F32)], [pltpu.HBM] * 4...  1.41 us
  transfers between devices with their start and end apart: 6, of which 5 were waited for; matrix products, arithmetic and copies ran while one was open for 0% of the time, Pallas kernels for 40%

profile of v9, /device:TPU:16, one launch (start us, length us, event | category | flops | bytes accessed | tf_op | source)
XLA Modules:
  0.0 27.0 jit_solution(11002163535209726227)
XLA Ops:
  0.6 0.0 copy-start
  0.6 0.0 copy-start.1
  0.7 0.0 copy-start.3
  0.7 0.0 copy-start.4
  0.7 0.0 copy-start.2
  0.7 1.4 %shard_map.79 = (f32[680,128]{1,0:T(8,128)S(1)}, f32[680,128]{1,0:T(8,128)S(1)}, f32[3,24,128]{2,1,0:T(8,128)S(1)}) custom-call(f32[3,17,45,128]{3,2,1,0:T(8,128)} %local_ref.3, f32[3,17,1,45]{3,2,1,0:T(1,128)} %bitcast.17, f32[704,128]{1,0:T(8,128)} %bitcast.13, s32[1,8]{1,0:T(1,128)} %bitcast.15), custom_call_target="tpu_custom_call" | custom-call | bytes 3600000 | tf_op jit(solution)/shard_map/pallas_call | solution.py:778
  2.1 1.6 %collective-permute-start.1 = (f32[680,128]{1,0:T(8,128)S(1)}, f32[680,128]{1,0:T(8,128)S(1)}, u32[]{:S(2)}, u32[]{:S(2)}) collective-permute-start(f32[680,128]{1,0:T(8,128)S(1)} %get-tuple-element.39), channel_id=1, source_target_pairs={{0,8},{2,10},{4,12},{6,14},{8,0},{10,2},{12,4},{14,6},{16,24},{18,... | collective-permute-start | bytes 1044488 | tf_op jit(solution)/shard_map/ppermute | solution.py:764
  3.7 0.0 collective-permute-start.2
  3.7 0.0 copy-done.4
  3.7 1.5 %collective-permute-start = (f32[3,512]{1,0:T(4,128)S(1)}, f32[3,512]{1,0:T(4,128)S(1)}, u32[]{:S(2)}, u32[]{:S(2)}) collective-permute-start(f32[3,512]{1,0:T(4,128)S(1)} %copy-done.4), channel_id=1, source_target_pairs={{0,1},{1,0},{2,3},{3,2},{4,5},{5,4},{6,7},{7,6},{8,9},{9,8},{10,11... | collective-permute-start | bytes 18440 | tf_op jit(solution)/shard_map/ppermute | solution.py:772
  5.3 0.0 copy-done.1
  5.3 0.0 copy-done.3
  5.3 0.0 copy-done.2
  5.3 1.2 %shard_map.77 = (bf16[96,192]{1,0:T(8,128)(2,1)S(1)}, bf16[128,256]{1,0:T(8,128)(2,1)S(1)}, bf16[128,256]{1,0:T(8,128)(2,1)S(1)}, f32[16,48,128]{2,1,0:T(8,128)S...) custom-call(f32[24,24]{1,0:T(8,128)S(1)} %copy-done.2, ...), custom_call_target="tpu_custom_call" | custom-call | bytes 3600000 | tf_op jit(solution)/shard_map/pallas_call | solution.py:791
  6.5 0.9 %collective-permute-done = f32[3,512]{1,0:T(4,128)S(1)} collective-permute-done((f32[3,512]{1,0:T(4,128)S(1)}, f32[3,512]{1,0:T(4,128)S(1)}, u32[]{:S(2)}, u32[]{:S(2)}) %collective-permute-start) | collective-permute-done | bytes 6176 | tf_op jit(solution)/shard_map/ppermute | solution.py:772
  7.4 3.0 %shard_map.78 = (f32[51,48,128]{2,1,0:T(8,128)S(1)}, f32[12,48,128]{2,1,0:T(8,128)S(1)}, f32[232,128]{1,0:T(8,128)S(1)}, f32[232,128]{1,0:T(8,128)S(1)}) custom-call(f32[3,17,45,128]{3,2,1,0:T(8,128)S(1)} %copy-done, bf16[96,192]{1,0:T(8,128)(2,1)S(1)} %get-tuple-element.34.lhs_ref, f32[16,48,128]{2,1,0:T(8,128)S(1)} %get-tuple-element.35.dens_ref, ...), custom_call_target="tpu_custom_call" | custom-call | bytes 21600000 | tf_op jit(solution)/shard_map/pallas_call | solution.py:800
  10.4 1.6 %collective-permute-done.1.even_ref = f32[680,128]{1,0:T(8,128)S(1)} collective-permute-done((f32[680,128]{1,0:T(8,128)S(1)}, f32[680,128]{1,0:T(8,128)S(1)}, u32[]{:S(2)}, u32[]{:S(2)}) %collective-permute-start.1) | collective-permute-done | bytes 348192 | tf_op jit(solution)/shard_map/ppermute | solution.py:764
  12.1 1.3 %collective-permute-done.2.odd_ref = f32[680,128]{1,0:T(8,128)S(1)} collective-permute-done((f32[680,128]{1,0:T(8,128)S(1)}, f32[680,128]{1,0:T(8,128)S(1)}, u32[]{:S(2)}, u32[]{:S(2)}) %collective-permute-start.2) | collective-permute-done | bytes 348192 | tf_op jit(solution)/shard_map/ppermute | solution.py:764
  13.3 0.5 %shard_map.82 = (f32[3,24,128]{2,1,0:T(8,128)S(1)}, f32[360,128]{1,0:T(8,128)S(1)}, f32[360,128]{1,0:T(8,128)S(1)}) custom-call(f32[51,48,128]{2,1,0:T(8,128)S(1)} %get-tuple-element.38.own_ref, f32[232,128]{1,0:T(8,128)S(1)} %get-tuple-element.43.even_own_ref, f32[232,128]{1,0:T(8,128)S(1)} %get-tuple-element.44.odd_own_ref, ...), custom_call_target="tpu_custom_call" | custom-call | bytes 3600000 | tf_op jit(solution)/shard_map/pallas_call | solution.py:811
  13.9 0.0 collective-permute-start.3
  13.9 1.6 %collective-permute-start.4 = (f32[360,128]{1,0:T(8,128)S(1)}, f32[360,128]{1,0:T(8,128)S(1)}, u32[]{:S(2)}, u32[]{:S(2)}) collective-permute-start(f32[360,128]{1,0:T(8,128)S(1)} %get-tuple-element.49), channel_id=1, source_target_pairs={{0,1},{1,0},{2,4},{3,5},{4,2},{5,3},{6,7},{7,6},{8,9},{9,8},{10,12... | collective-permute-start | bytes 552968 | tf_op jit(solution)/shard_map/ppermute | solution.py:764
  15.5 0.4 %shard_map.80 = (f32[12,48,128]{2,1,0:T(8,128)S(1)}, f32[12,48,128]{2,1,0:T(8,128)S(1)}, f32[6,48,128]{2,1,0:T(8,128)S(1)}) custom-call(f32[51,48,128]{2,1,0:T(8,128)S(1)} %get-tuple-element.38.own_ref, f32[680,128]{1,0:T(8,128)S(1)} %collective-permute-done.1.even_ref, f32[680,128]{1,0:T(8,128)S(1)} %collective-permute-done.2.odd_ref, ...), custom_call_target="tpu_custom_call" | custom-call | bytes 2520000 | tf_op jit(solution)/shard_map/pallas_call | solution.py:820
  15.8 2.4 %shard_map.81.eb_ref = f32[10,48,128]{2,1,0:T(8,128)S(1)} custom-call(f32[51,48,128]{2,1,0:T(8,128)S(1)} %get-tuple-element.38.own_ref, f32[12,48,128]{2,1,0:T(8,128)S(1)} %get-tuple-element.41.xl_ref, f32[12,48,128]{2,1,0:T(8,128)S(1)} %get-tuple-element.42.xh_ref, bf16[96,192]{1,0:T(8,128)(2,1)S(1)} %get-tuple-element.34.lhs_ref), custom_call_target="tpu_custom_call" | custom-call | bytes 9360000 | tf_op jit(solution)/shard_map/pallas_call | solution.py:823
  18.2 0.9 %shard_map.83.zo_ref = f32[91,8,128]{2,1,0:T(8,128)S(1)} custom-call(f32[51,48,128]{2,1,0:T(8,128)S(1)} %get-tuple-element.38.own_ref, f32[12,48,128]{2,1,0:T(8,128)S(1)} %get-tuple-element.41.xl_ref, f32[12,48,128]{2,1,0:T(8,128)S(1)} %get-tuple-element.42.xh_ref, f32[16,48,128]{2,1,0:T(8,128)S(1)} %get-tuple-element.35.dens_ref, ...), custom_call_target="tpu_custom_call" | custom-call | bytes 5400000 | tf_op jit(solution)/shard_map/pallas_call | solution.py:827
  19.1 0.0 collective-permute-done.3.even_ref
  19.2 0.3 %collective-permute-done.4.odd_ref = f32[360,128]{1,0:T(8,128)S(1)} collective-permute-done((f32[360,128]{1,0:T(8,128)S(1)}, f32[360,128]{1,0:T(8,128)S(1)}, u32[]{:S(2)}, u32[]{:S(2)}) %collective-permute-start.4) | collective-permute-done | bytes 184352 | tf_op jit(solution)/shard_map/ppermute | solution.py:764
  19.5 0.5 %shard_map.84 = (f32[360,128]{1,0:T(8,128)S(1)}, f32[360,128]{1,0:T(8,128)S(1)}, f32[72,128]{1,0:T(8,128)S(1)}, f32[72,128]{1,0:T(8,128)S(1)}, f32[24,128]{1,0:T(8,128)S(1)}, /*index=5*/f32[184,128]{1,0:T(8,128)S(1)}) custom-call(f32[3,24,128]{2,1,0:T(8,128)S(1)} %get-tuple-element.46.tx_ref, f32[91,8,128]{2,1,0:T(8,128)S(1)} %shard_map.83.zo_ref, ...), custom_call_target="tpu_custom_call" | custom-call | bytes 3600000 | tf_op jit(solution)/shard_map/pallas_call | solution.py:830
  20.0 1.6 %collective-permute-start.5 = (f32[184,128]{1,0:T(8,128)S(1)}, f32[184,128]{1,0:T(8,128)S(1)}, u32[]{:S(2)}, u32[]{:S(2)}) collective-permute-start(f32[184,128]{1,0:T(8,128)S(1)} %get-tuple-element.63), channel_id=1, source_target_pairs={{0,1},{2,3},{4,5},{6,7},{1,0},{3,2},{5,4},{7,6},{8,9},{10,11},{12,... | collective-permute-start | bytes 282632 | tf_op jit(solution)/shard_map/ppermute | solution.py:764
  21.6 1.8 %shard_map.85 = (f32[22,8,128]{2,1,0:T(8,128)S(1)}, f32[22,8,128]{2,1,0:T(8,128)S(1)}) custom-call(f32[51,48,128]{2,1,0:T(8,128)S(1)} %get-tuple-element.38.own_ref, f32[12,48,128]{2,1,0:T(8,128)S(1)} %get-tuple-element.41.xl_ref, f32[12,48,128]{2,1,0:T(8,128)S(1)} %get-tuple-element.42.xh_ref, f32[360,128]{1,0:T(8,128)S(1)} %get-tuple-element.50.lowy_ref, ...), custom_call_target="tpu_custom_call" | custom-call | bytes 8279999 | tf_op jit(solution)/shard_map/pallas_call | solution.py:839
  23.4 1.1 %shard_map.86.g_ref = f32[2,16,48,128]{3,2,1,0:T(8,128)S(1)} custom-call(f32[12,48,128]{2,1,0:T(8,128)S(1)} %get-tuple-element.37.ea_ref, f32[10,48,128]{2,1,0:T(8,128)S(1)} %shard_map.81.eb_ref, f32[22,8,128]{2,1,0:T(8,128)S(1)} %get-tuple-element.53.el_ref, f32[22,8,128]{2,1,0:T(8,128)S(1)} %get-tuple-element.54.eh_ref, ...), custom_call_target="tpu_custom_call" | custom-call | bytes 5400000 | tf_op jit(solution)/shard_map/pallas_call | solution.py:847
  24.5 0.3 %collective-permute-done.5.refs_0_ = f32[184,128]{1,0:T(8,128)S(1)} collective-permute-done((f32[184,128]{1,0:T(8,128)S(1)}, f32[184,128]{1,0:T(8,128)S(1)}, u32[]{:S(2)}, u32[]{:S(2)}) %collective-permute-start.5) | collective-permute-done | bytes 94240 | tf_op jit(solution)/shard_map/ppermute | solution.py:764
  24.8 2.2 %shard_map.87 = (f32[704,128]{1,0:T(8,128)}, f32[704,128]{1,0:T(8,128)}) custom-call(f32[2,16,48,128]{3,2,1,0:T(8,128)S(1)} %shard_map.86.g_ref, bf16[128,128]{1,0:T(8,128)(2,1)S(1)} %get-tuple-element.55.along_ref, bf16[256,2048]{1,0:T(8,128)(2,1)S(1)} %get-tuple-element.56.right_ref, f32[16,48,128]{2,1,0:T(8,128)S(1)} %get-tuple-element.57.rs_ref, ...), custom_call_target="tpu_custom_call" | custom-call | bytes 9000000 | tf_op jit(solution)/shard_map/pallas_call | solution.py:851
  (2 shorter events, 0.0 us)
Async XLA Ops:
  0.6 6.8 %copy-start = (f32[3,17,45,128]{3,2,1,0:T(8,128)S(1)}, f32[3,17,45,128]{3,2,1,0:T(8,128)}, u32[]{:S(2)}) copy-start(f32[3,17,45,128]{3,2,1,0:T(8,128)} %local_ref.3) | copy-start | bytes 3525124
  0.6 4.6 %copy-start.1 = (f32[16,44,128]{2,0,1:T(8,128)S(1)}, f32[16,44,128]{2,0,1:T(8,128)}, u32[]{:S(2)}) copy-start(f32[16,44,128]{2,0,1:T(8,128)} %param.10) | copy-start | bytes 1081348
  0.7 4.6 %copy-start.3 = (s32[1,1,1,8]{3,2,1,0:T(1,128)S(1)}, s32[1,1,1,8]{3,2,1,0:T(1,128)}, u32[]{:S(2)}) copy-start(s32[1,1,1,8]{3,2,1,0:T(1,128)} %param.9) | copy-start | bytes 100
  0.7 3.1 %copy-start.4 = (f32[3,512]{1,0:T(4,128)S(1)}, f32[3,512]{1,0:T(4,128)}, u32[]{:S(2)}) copy-start(f32[3,512]{1,0:T(4,128)} %param.8) | copy-start | bytes 18436
  0.7 4.6 %copy-start.2 = (f32[24,24]{1,0:T(8,128)S(1)}, f32[24,24]{1,0:T(8,128)}, u32[]{:S(2)}) copy-start(f32[24,24]{1,0:T(8,128)} %stiff_ref.1) | copy-start | bytes 6916
  2.1 10.0 %collective-permute-start.1 = (f32[680,128]{1,0:T(8,128)S(1)}, f32[680,128]{1,0:T(8,128)S(1)}, u32[]{:S(2)}, u32[]{:S(2)}) collective-permute-start(f32[680,128]{1,0:T(8,128)S(1)} %get-tuple-element.39), channel_id=1, source_target_pairs={{0,8},{2,10},{4,12},{6,14},{8,0},{10,2},{12,4},{14,6},{16,24},{18,... | collective-permute-start | bytes 1044488 | tf_op jit(solution)/shard_map/ppermute | solution.py:764
  3.7 9.6 %collective-permute-start.2 = (f32[680,128]{1,0:T(8,128)S(1)}, f32[680,128]{1,0:T(8,128)S(1)}, u32[]{:S(2)}, u32[]{:S(2)}) collective-permute-start(f32[680,128]{1,0:T(8,128)S(1)} %get-tuple-element.40), channel_id=1, source_target_pairs={{0,2},{2,0},{4,6},{6,4},{8,16},{10,18},{12,20},{14,22},{16,8},{18,... | collective-permute-start | bytes 1044488 | tf_op jit(solution)/shard_map/ppermute | solution.py:764
  3.7 3.7 %collective-permute-start = (f32[3,512]{1,0:T(4,128)S(1)}, f32[3,512]{1,0:T(4,128)S(1)}, u32[]{:S(2)}, u32[]{:S(2)}) collective-permute-start(f32[3,512]{1,0:T(4,128)S(1)} %copy-done.4), channel_id=1, source_target_pairs={{0,1},{1,0},{2,3},{3,2},{4,5},{5,4},{6,7},{7,6},{8,9},{9,8},{10,11... | collective-permute-start | bytes 18440 | tf_op jit(solution)/shard_map/ppermute | solution.py:772
  13.9 5.3 %collective-permute-start.3 = (f32[360,128]{1,0:T(8,128)S(1)}, f32[360,128]{1,0:T(8,128)S(1)}, u32[]{:S(2)}, u32[]{:S(2)}) collective-permute-start(f32[360,128]{1,0:T(8,128)S(1)} %get-tuple-element.48), channel_id=1, source_target_pairs={{0,2},{1,3},{2,0},{3,1},{4,6},{5,7},{6,4},{7,5},{8,10},{9,11},{10,... | collective-permute-start | bytes 552968 | tf_op jit(solution)/shard_map/ppermute | solution.py:764
  13.9 5.6 %collective-permute-start.4 = (f32[360,128]{1,0:T(8,128)S(1)}, f32[360,128]{1,0:T(8,128)S(1)}, u32[]{:S(2)}, u32[]{:S(2)}) collective-permute-start(f32[360,128]{1,0:T(8,128)S(1)} %get-tuple-element.49), channel_id=1, source_target_pairs={{0,1},{1,0},{2,4},{3,5},{4,2},{5,3},{6,7},{7,6},{8,9},{9,8},{10,12... | collective-permute-start | bytes 552968 | tf_op jit(solution)/shard_map/ppermute | solution.py:764
  20.0 4.8 %collective-permute-start.5 = (f32[184,128]{1,0:T(8,128)S(1)}, f32[184,128]{1,0:T(8,128)S(1)}, u32[]{:S(2)}, u32[]{:S(2)}) collective-permute-start(f32[184,128]{1,0:T(8,128)S(1)} %get-tuple-element.63), channel_id=1, source_target_pairs={{0,1},{2,3},{4,5},{6,7},{1,0},{3,2},{5,4},{7,6},{8,9},{10,11},{12,... | collective-permute-start | bytes 282632 | tf_op jit(solution)/shard_map/ppermute | solution.py:764
